TPU v7x, 32 devices: a whole 2x2x4 slice. The times are simulated.
32 devices in a mesh: groups: 2 (over x), tm: 8 (over z, y), chan: 2 (over core).
Axes of the slice: x: 2, y: 2, z: 4, core: 2. Of those that a mesh axis runs over, the one named last changes fastest.
Arguments:
- signal: bfloat16 [65536, 256], P(('groups', 'tm'), 'chan'), parts along dimension 0, may hold values from -6 to 6
- cotangent: bfloat16 [65536, 256], P(('groups', 'tm'), 'chan'), parts along dimension 0, may hold values from -6 to 6
- conv_weight: bfloat16 [2, 2, 256, 2, 256], replicated, may hold values from -0.25 to 0.25
- out_weight: bfloat16 [2, 256, 256], replicated, may hold values from -0.375 to 0.375
Outputs:
- output: bfloat16 [65536, 256], P(('groups', 'tm'), 'chan'), parts along dimension 0
- in_grad: bfloat16 [65536, 256], P(('groups', 'tm'), 'chan'), parts along dimension 0
- conv_grad: float32 [4, 2, 256, 2, 256], P('groups', None, None, None, 'chan'), parts along dimension 0
- out_grad: float32 [4, 256, 256], P('groups', None, 'chan'), parts along dimension 0
There are 2 independent parts, one for each index of `groups`. A program takes and returns all parts, laid end to end along the dimension named above; an argument that names none is the same for every part. Nothing has to cross between parts.
All inputs are finite; a program needn't handle non-finite values.
Results may differ from a plain program's by a relative error of at most 0.0058.
Values may be sent and summed in bfloat16 or wider, within the bound.
No kernel may reach another device: no remote copies, remote signals or barrier semaphores. Data moves between devices by JAX's collectives and lax.ppermute only.
A program may use at most 128 MiB of HBM per device.

v0:
```python
import math

import jax
import jax.numpy as jnp
from jax import lax
from jax.sharding import PartitionSpec as P


def shifted(block, axis, distance):
    devices = range(lax.axis_size(axis))
    route = [(i - distance, i) for i in devices if i - distance in devices]
    return lax.ppermute(block, axis, route)


def reduced_rows(former, latter):
    return lax.dot_general(
        former, latter, (((0,), (0,)), ((), ())), preferred_element_type=jnp.float32
    )


def contract_last(former, latter):
    return lax.dot_general(
        former, latter, (((1,), (1,)), ((), ())), preferred_element_type=jnp.float32
    )


def delay_whole(values, delay_span):
    row_count = values.shape[0]
    if delay_span < row_count:
        arrived = shifted(values[row_count - delay_span :], "tm", 1)
        return jnp.concatenate([arrived, values[: row_count - delay_span]], axis=0)
    return shifted(values, "tm", delay_span // row_count)


def advance_grads(values, delay_span):
    row_count = values.shape[0]
    if delay_span < row_count:
        arrived = shifted(values[:delay_span], "tm", -1)
        return jnp.concatenate([values[delay_span:], arrived], axis=0)
    return shifted(values, "tm", -(delay_span // row_count))


def sum_layer(conv_term, out_term):
    return lax.psum((conv_term, out_term), "tm")


def gated_layer(full_now, full_past, tap_now, tap_past, row_count, width):
    preact = jnp.dot(full_now, tap_now, preferred_element_type=jnp.float32) + jnp.dot(
        full_past, tap_past, preferred_element_type=jnp.float32
    )
    preact = preact.reshape(row_count, 2, width)
    filter_act = jnp.tanh(preact[:, 0, :])
    gate_act = jax.nn.sigmoid(preact[:, 1, :])
    hidden = (filter_act * gate_act).astype(jnp.bfloat16)
    return (filter_act, gate_act, hidden)


def pre_gradient(hidden_grad, filter_act, gate_act, row_count, width):
    filter_grad = hidden_grad * gate_act * (1.0 - filter_act * filter_act)
    gate_grad = hidden_grad * filter_act * gate_act * (1.0 - gate_act)
    return (
        jnp.stack([filter_grad, gate_grad], axis=1)
        .astype(jnp.bfloat16)
        .reshape(row_count, 2 * width)
    )


def on_device(signal, cotangent, conv_weight, out_weight):
    row_count = signal.shape[0]
    half_width = signal.shape[1]
    channels = conv_weight.shape[2]
    layers = conv_weight.shape[0]
    scale_factor = 1.0 / math.sqrt(row_count * lax.axis_size("tm"))
    dilation_list = (row_count // 2, 2 * row_count)
    offset = lax.axis_index("chan") * half_width
    present_signal = signal
    stored = []
    for layer_index in range(layers):
        delay_span = dilation_list[layer_index]
        own_cols = lax.dynamic_slice_in_dim(conv_weight[layer_index], offset, half_width, 3)
        tap_now = own_cols[0].reshape(channels, 2 * half_width)
        tap_past = own_cols[1].reshape(channels, 2 * half_width)
        full_now = lax.all_gather(present_signal, "chan", axis=1, tiled=True)
        full_past = delay_whole(full_now, delay_span)
        filter_act, gate_act, hidden = gated_layer(
            full_now, full_past, tap_now, tap_past, row_count, half_width
        )
        full_hidden = lax.all_gather(hidden, "chan", axis=1, tiled=True)
        out_cols = lax.dynamic_slice_in_dim(out_weight[layer_index], offset, half_width, 1)
        following = (
            present_signal.astype(jnp.float32)
            + jnp.dot(full_hidden, out_cols, preferred_element_type=jnp.float32)
        ).astype(jnp.bfloat16)
        stored.append((full_now, full_past, filter_act, gate_act, full_hidden))
        present_signal = following
    upstream = cotangent
    conv_list = [None] * layers
    out_list = [None] * layers
    for layer_index in reversed(range(layers)):
        delay_span = dilation_list[layer_index]
        full_now, full_past, filter_act, gate_act, full_hidden = stored[layer_index]
        out_rows = lax.dynamic_slice_in_dim(out_weight[layer_index], offset, half_width, 0)
        full_grad = lax.all_gather(upstream, "chan", axis=1, tiled=True)
        hidden_grad = contract_last(full_grad, out_rows)
        pre_grad = pre_gradient(hidden_grad, filter_act, gate_act, row_count, half_width)
        ahead_grad = advance_grads(pre_grad, delay_span)
        out_term = reduced_rows(full_hidden, upstream) * scale_factor
        conv_now = reduced_rows(full_now, pre_grad)
        conv_past = reduced_rows(full_past, pre_grad)
        conv_term = (
            jnp.stack([conv_now, conv_past]).reshape(2, channels, 2, half_width) * scale_factor
        )
        own_cols = lax.dynamic_slice_in_dim(conv_weight[layer_index], offset, half_width, 3)
        tap_now = own_cols[0].reshape(channels, 2 * half_width)
        tap_past = own_cols[1].reshape(channels, 2 * half_width)
        partial_sum = contract_last(pre_grad, tap_now) + contract_last(ahead_grad, tap_past)
        summed = lax.psum_scatter(partial_sum, "chan", scatter_dimension=1, tiled=True)
        upstream = (upstream.astype(jnp.float32) + summed).astype(jnp.bfloat16)
        conv_list[layer_index], out_list[layer_index] = sum_layer(conv_term, out_term)
    conv_total = jnp.stack(conv_list)
    out_total = jnp.stack(out_list)
    return (present_signal, upstream, conv_total, out_total)


def solution(mesh):
    placed = (P(("groups", "tm"), "chan"), P(("groups", "tm"), "chan"), P(), P())
    return jax.shard_map(
        on_device,
        mesh=mesh,
        in_specs=placed,
        out_specs=(
            P(("groups", "tm"), "chan"),
            P(("groups", "tm"), "chan"),
            P("groups", None, None, None, "chan"),
            P("groups", None, "chan"),
        ),
        check_vma=False,
    )
```

profile of v0, /device:TPU:0, one launch (start us, length us, event | category | flops | bytes accessed | tf_op | source)
XLA Modules:
  0.0 369.0 jit_solution(10626977300184263852)
XLA Ops:
  7.2 0.0 all-gather.7.cloned.1.call-start
  7.2 2.3 copy.8
  9.5 0.0 all-gather.9.cloned.1.call-start
  9.6 13.9 %all-gather.7.cloned.1.call-done = bf16[4096,256]{0,1:T(8,128)(2,1)} async-done(((bf16[4096,128]{0,1:T(8,128)(2,1)}), bf16[4096,256]{0,1:T(8,128)(2,1)}) %all-gather.7.cloned.1.call-update) | async-done | bytes 2097168 | tf_op jit(solution)/shard_map/all_gather | solution.py:83
  23.4 2.7 fusion.79
  26.1 4.9 %collective-permute-start = (bf16[2048,256]{0,1:T(8,128)(2,1)}, bf16[2048,256]{0,1:T(8,128)(2,1)}, u32[]{:S(2)}, u32[]{:S(2)}) collective-permute-start(bf16[2048,256]{0,1:T(8,128)(2,1)} %get-tuple-element.18), channel_id=1, source_target_pairs={{0,2},{2,4},{4,6},{6,8},{8,10},{10,12},{12,14},{1,3},{3,5},{5,7},{... | collective-permute-start | bytes 3145736 | tf_op jit(solution)/shard_map/ppermute | solution.py:12
  31.0 2.7 fusion.80
  33.7 0.2 constant_dynamic-slice_fusion.3
  33.9 0.7 convolution_bitcast_fusion
  34.7 18.6 %collective-permute-done = bf16[2048,256]{0,1:T(8,128)(2,1)} collective-permute-done((bf16[2048,256]{0,1:T(8,128)(2,1)}, bf16[2048,256]{0,1:T(8,128)(2,1)}, u32[]{:S(2)}, u32[]{:S(2)}) %collective-permute-start) | collective-permute-done | bytes 1048608 | tf_op jit(solution)/shard_map/ppermute | solution.py:12
  53.2 2.1 convolution_add_fusion.3
  55.3 2.0 copy-done.2
  57.3 1.8 multiply_convert_fusion.1
  59.1 0.0 all-gather.11.cloned.1.call-start
  59.2 12.6 %all-gather.9.cloned.1.call-done = bf16[4096,256]{0,1:T(8,128)(2,1)} async-done(((bf16[4096,128]{0,1:T(8,128)(2,1)}), bf16[4096,256]{0,1:T(8,128)(2,1)}) %all-gather.9.cloned.1.call-update) | async-done | bytes 2097168 | tf_op jit(solution)/shard_map/all_gather | solution.py:88
  71.7 3.3 fusion
  75.1 0.0 all-gather.11.cloned.1.call-update
  75.1 0.0 all-gather.15.cloned.1.call-start
  75.1 11.6 %all-gather.11.cloned.1.call-done = bf16[4096,256]{1,0:T(8,128)(2,1)} async-done(((bf16[4096,128]{1,0:T(8,128)(2,1)}), bf16[4096,256]{1,0:T(8,128)(2,1)}) %all-gather.11.cloned.1.call-update) | async-done | bytes 2097168 | tf_op jit(solution)/shard_map/all_gather | solution.py:83
  86.7 3.8 %collective-permute-start.1 = (bf16[4096,256]{1,0:T(8,128)(2,1)}, bf16[4096,256]{1,0:T(8,128)(2,1)S(1)}, u32[]{:S(2)}, u32[]{:S(2)}) collective-permute-start(bf16[4096,256]{1,0:T(8,128)(2,1)} %all-gather.11.cloned.1.call-done), channel_id=1, source_target_pairs={{0,4},{2,6},{4,8},{6,10},{8,12},{10,14},{1,5},{3,7},{5,9},{7,11},{... | collective-permute-start | bytes 6291464 | tf_op jit(solution)/shard_map/ppermute | solution.py:12
  90.6 0.0 reduce-scatter.3.cloned.1.call-start
  90.6 0.2 constant_dynamic-slice_fusion.2
  90.8 2.3 fusion.47
  93.2 42.9 %collective-permute-done.1 = bf16[4096,256]{1,0:T(8,128)(2,1)S(1)} collective-permute-done((bf16[4096,256]{1,0:T(8,128)(2,1)}, bf16[4096,256]{1,0:T(8,128)(2,1)S(1)}, u32[]{:S(2)}, u32[]{:S(2)}) %collective-permute-start.1) | collective-permute-done | bytes 2097184 | tf_op jit(solution)/shard_map/ppermute | solution.py:12
  136.0 2.8 convolution_add_fusion.2
  138.8 4.2 %multiply_bitcast_fusion.3 = (bf16[4096,1,128]{0,2,1:T(8,128)(2,1)S(1)}, bf16[4096,1,128]{0,2,1:T(8,128)(2,1)S(1)}) fusion(f32[4096,2,128]{0,2,1:T(8,128)} %bitcast.170, bf16[4096,256]{1,0:T(8,128)(2,1)} %all-gather.15.cloned.1.call-done, bf16[1,256,256]{2,1,0:T(8,128)(2,1)S(1)} %get-tuple-element.26, s32[]{:T(128)S(6)} %select_n.2), kind=kOutput, calls=%fused_computation.44 | convolution fusion | flops 275251200 | bytes 8454148 | tf_op jit(solution)/shard_map/dot_general | solution.py:22
  143.1 0.2 maximum_convert_fusion
  143.3 1.3 collective-permute-start.2
  144.6 0.8 fusion.45
  145.3 47.5 %collective-permute-done.2 = bf16[4096,256]{0,1:T(8,128)(2,1)S(1)} collective-permute-done((bf16[4096,256]{0,1:T(8,128)(2,1)S(1)}, bf16[4096,256]{0,1:T(8,128)(2,1)S(1)}, u32[]{:S(2)}, u32[]{:S(2)}) %collective-permute-start.2) | collective-permute-done | bytes 2097184 | tf_op jit(solution)/shard_map/ppermute | solution.py:12
  192.8 2.8 convolution_add_fusion.1
  195.7 0.0 all-gather.13.cloned.1.call-start
  195.7 4.1 %multiply_convert_fusion = bf16[4096,128]{0,1:T(8,128)(2,1)} fusion(f32[4096,2,128]{0,2,1:T(8,128)} %bitcast.171), kind=kLoop, calls=%fused_computation.45 | loop fusion | flops 2621440 | bytes 5242880 | tf_op jit(solution)/shard_map/convert_element_type | solution.py:54
  199.8 0.0 all-gather.17.cloned.1.call-start
  199.9 8.2 %reduce-scatter.3.cloned.1.call-done = f32[4096,128]{1,0:T(8,128)} async-done(((f32[4096,256]{1,0:T(8,128)}), f32[4096,128]{1,0:T(8,128)}) %reduce-scatter.3.cloned.1.call-update) | async-done | bytes 2097168 | tf_op jit(solution)/shard_map/reduce_scatter | solution.py:117
  208.1 2.8 add_convert_fusion.1
  210.9 0.2 all-reduce.3.cloned.1.call-start
  211.1 2.5 fusion.29
  213.6 0.8 fusion.24
  214.4 0.9 fusion.42
  215.3 6.8 %all-gather.13.cloned.1.call-done = bf16[4096,256]{0,1:T(8,128)(2,1)} async-done(((bf16[4096,128]{0,1:T(8,128)(2,1)}), bf16[4096,256]{0,1:T(8,128)(2,1)}) %all-gather.13.cloned.1.call-update) | async-done | bytes 2097168 | tf_op jit(solution)/shard_map/all_gather | solution.py:88
  222.1 3.1 fusion.39
  225.2 1.3 fusion.40
  226.5 9.3 %all-gather.17.cloned.1.call-done = bf16[4096,256]{1,0:T(8,128)(2,1)} async-done(((bf16[4096,128]{1,0:T(8,128)(2,1)}), bf16[4096,256]{1,0:T(8,128)(2,1)}) %all-gather.17.cloned.1.call-update) | async-done | bytes 2097168 | tf_op jit(solution)/shard_map/all_gather | solution.py:103
  235.8 4.2 %multiply_bitcast_fusion.1 = (bf16[4096,1,128]{0,2,1:T(8,128)(2,1)S(1)}, bf16[4096,1,128]{0,2,1:T(8,128)(2,1)S(1)}) fusion(f32[4096,2,128]{0,2,1:T(8,128)} %bitcast.169, bf16[4096,256]{1,0:T(8,128)(2,1)} %all-gather.17.cloned.1.call-done, bf16[1,256,256]{2,1,0:T(8,128)(2,1)S(1)} %copy-done.15, s32[]{:T(128)S(6)} %select_n.2), kind=kOutput, calls=%fused_computation.41 | convolution fusion | flops 275251200 | bytes 8454148 | tf_op jit(solution)/shard_map/dot_general | solution.py:22
  240.0 0.2 maximum_convert_fusion.1
  240.2 1.5 fusion.78
  241.7 1.3 collective-permute-start.3
  243.0 1.5 fusion.86
  244.5 2.7 fusion.34
  247.1 1.8 copy.9
  248.9 1.9 fusion.41
  250.8 0.0 reduce-scatter.5.cloned.1.call-start
  250.9 0.8 fusion.51
  251.7 22.6 %collective-permute-done.3 = bf16[2048,256]{0,1:T(8,128)(2,1)} collective-permute-done((bf16[2048,256]{0,1:T(8,128)(2,1)}, bf16[2048,256]{0,1:T(8,128)(2,1)}, u32[]{:S(2)}, u32[]{:S(2)}) %collective-permute-start.3) | collective-permute-done | bytes 1048608 | tf_op jit(solution)/shard_map/ppermute | solution.py:12
  274.2 4.0 %convolution_add_fusion = f32[4096,256]{1,0:T(8,128)} fusion(f32[4096,256]{1,0:T(8,128)S(1)} %fusion.51, bf16[2048,256]{0,1:T(8,128)(2,1)} %collective-permute-done.3, bf16[2048,256]{0,1:T(8,128)(2,1)S(1)} %bitcast.172, bf16[32,8,2,128]{3,2,1,0:T(2,128)(2,1)S(1)} %bitcast.178), kind=kOutput, calls=%fused_computation | convolution fusion | flops 542113792 | bytes 10616832 | tf_op jit(solution)/shard_map/dot_general | solution.py:22
  278.3 1.2 copy-done.5
  279.5 3.3 fusion.1
  282.8 63.3 %all-reduce.3.cloned.1.call-done = (f32[1,2,256,2,128]{4,2,3,1,0:T(8,128)}, f32[1,2,256,2,128]{4,2,3,1,0:T(8,128)}, f32[1,256,128]{2,1,0:T(8,128)}, f32[1,256,128]{2,1,0:T(8,128)}) async-done(((f32[1,2,256,2,128]{4,2,3,1,0:T(8,128)}, f32[1,2,256,2,128]{4,2,3,1,0:T(8,128)}, f32[1,256,128]{2,1,0:T(8,128)}, f32[1,256,128]{2,1,0:T(8,128)}), (f32[1,2,256,2,128]{4,2,3,1,0:T(8,128)}, ...) | async-done | bytes 1310736 | tf_op jit(solution)/shard_map/psum | solution.py:44
  346.2 1.3 pad_maximum_fusion.3
  347.5 1.8 copy.12
  349.3 0.7 pad_maximum_fusion.4
  350.0 9.7 %reduce-scatter.5.cloned.1.call-done = f32[4096,128]{1,0:T(8,128)} async-done(((f32[4096,256]{1,0:T(8,128)}), f32[4096,128]{1,0:T(8,128)}) %reduce-scatter.5.cloned.1.call-update) | async-done | bytes 2097168 | tf_op jit(solution)/shard_map/reduce_scatter | solution.py:117
  359.7 2.8 add_convert_fusion
  (46 shorter events, 0.2 us)
Async XLA Ops:
  7.2 16.3 %all-gather.7.cloned.1.call-start = ((), (), s32[]{:S(2)}) async-start(), calls=%async_computation.2 | async-start | bytes 3145728 | tf_op jit(solution)/shard_map/all_gather | solution.py:83
  9.5 62.2 %all-gather.9.cloned.1.call-start = ((), (), s32[]{:S(2)}) async-start(), calls=%async_computation.3 | async-start | bytes 3145728 | tf_op jit(solution)/shard_map/all_gather | solution.py:88
  26.1 27.1 %copy-start.10 = (bf16[2048,256]{0,1:T(8,128)(2,1)}, bf16[2048,256]{0,1:T(8,128)(2,1)S(1)}, u32[]{:S(2)}) copy-start(bf16[2048,256]{0,1:T(8,128)(2,1)S(1)} %get-tuple-element.19) | copy-start | bytes 3145732
  26.1 7.8 %copy-start = (bf16[4096,256]{0,1:T(8,128)(2,1)S(1)}, bf16[4096,256]{0,1:T(8,128)(2,1)}, u32[]{:S(2)}) copy-start(bf16[4096,256]{0,1:T(8,128)(2,1)} %all-gather.7.cloned.1.call-done) | copy-start | bytes 6291460
  26.1 27.1 %collective-permute-start = (bf16[2048,256]{0,1:T(8,128)(2,1)}, bf16[2048,256]{0,1:T(8,128)(2,1)}, u32[]{:S(2)}, u32[]{:S(2)}) collective-permute-start(bf16[2048,256]{0,1:T(8,128)(2,1)} %get-tuple-element.18), channel_id=1, source_target_pairs={{0,2},{2,4},{4,6},{6,8},{8,10},{10,12},{12,14},{1,3},{3,5},{5,7},{... | collective-permute-start | bytes 3145736 | tf_op jit(solution)/shard_map/ppermute | solution.py:12
  55.3 2.0 copy-start.2
  57.3 1.9 copy-start.16
  59.0 12.7 %copy-start.9 = (bf16[4096,128]{1,0:T(8,128)(2,1)S(1)}, bf16[4096,128]{1,0:T(8,128)(2,1)}, u32[]{:S(2)}) copy-start(bf16[4096,128]{1,0:T(8,128)(2,1)} %param.4) | copy-start | bytes 3145732
  59.1 27.7 %all-gather.11.cloned.1.call-start = ((), (), s32[]{:S(2)}) async-start(), calls=%async_computation.4 | async-start | bytes 3145728 | tf_op jit(solution)/shard_map/all_gather | solution.py:83
  59.2 15.9 %copy-start.14 = (bf16[1,256,256]{2,1,0:T(8,128)(2,1)}, bf16[1,256,256]{2,1,0:T(8,128)(2,1)S(1)}, u32[]{:S(2)}) copy-start(bf16[1,256,256]{2,1,0:T(8,128)(2,1)S(1)} %get-tuple-element.27) | copy-start | bytes 393220
  75.1 15.6 %copy-start.13 = (bf16[1,2,256,2,256]{4,3,2,1,0:T(2,128)(2,1)S(1)}, bf16[1,2,256,2,256]{4,3,2,1,0:T(2,128)(2,1)}, u32[]{:S(2)}) copy-start(bf16[1,2,256,2,256]{4,3,2,1,0:T(2,128)(2,1)} %get-tuple-element.20) | copy-start | bytes 1572868
  75.1 63.7 %all-gather.15.cloned.1.call-start = ((), (), s32[]{:S(2)}) async-start(), calls=%async_computation.6 | async-start | bytes 3145728 | tf_op jit(solution)/shard_map/all_gather | solution.py:103
  86.7 49.3 %collective-permute-start.1 = (bf16[4096,256]{1,0:T(8,128)(2,1)}, bf16[4096,256]{1,0:T(8,128)(2,1)S(1)}, u32[]{:S(2)}, u32[]{:S(2)}) collective-permute-start(bf16[4096,256]{1,0:T(8,128)(2,1)} %all-gather.11.cloned.1.call-done), channel_id=1, source_target_pairs={{0,4},{2,6},{4,8},{6,10},{8,12},{10,14},{1,5},{3,7},{5,9},{7,11},{... | collective-permute-start | bytes 6291464 | tf_op jit(solution)/shard_map/ppermute | solution.py:12
  90.6 117.5 %reduce-scatter.3.cloned.1.call-start = ((), (), s32[]{:S(2)}) async-start(), calls=%async_computation.7 | async-start | bytes 6291456 | tf_op jit(solution)/shard_map/reduce_scatter | solution.py:117
  136.0 2.8 copy-start.8
  143.3 49.5 %collective-permute-start.2 = (bf16[4096,256]{0,1:T(8,128)(2,1)S(1)}, bf16[4096,256]{0,1:T(8,128)(2,1)S(1)}, u32[]{:S(2)}, u32[]{:S(2)}) collective-permute-start(bf16[4096,256]{0,1:T(8,128)(2,1)S(1)} %bitcast.164), channel_id=1, source_target_pairs={{4,0},{6,2},{8,4},{10,6},{12,8},{14,10},{5,1},{7,3},{9,5},{11,7},{... | collective-permute-start | bytes 6291464 | tf_op jit(solution)/shard_map/ppermute | solution.py:12
  195.6 12.4 %copy-start.6 = (bf16[4096,128]{1,0:T(8,128)(2,1)S(1)}, bf16[4096,128]{1,0:T(8,128)(2,1)}, u32[]{:S(2)}) copy-start(bf16[4096,128]{1,0:T(8,128)(2,1)} %param.5) | copy-start | bytes 3145732
  195.7 26.4 %all-gather.13.cloned.1.call-start = ((), (), s32[]{:S(2)}) async-start(), calls=%async_computation.5 | async-start | bytes 3145728 | tf_op jit(solution)/shard_map/all_gather | solution.py:88
  199.8 35.9 %all-gather.17.cloned.1.call-start = ((), (), s32[]{:S(2)}) async-start(), calls=%async_computation.8 | async-start | bytes 3145728 | tf_op jit(solution)/shard_map/all_gather | solution.py:103
  210.9 135.3 %all-reduce.3.cloned.1.call-start = ((), (), s32[]{:S(2)}) async-start(), calls=%async_computation.10 | async-start | bytes 2621440 | tf_op jit(solution)/shard_map/psum | solution.py:44
  211.1 2.5 copy-start.4
  214.4 10.7 %copy-start.3 = (bf16[4096,128]{1,0:T(8,128)(2,1)S(1)}, bf16[4096,128]{1,0:T(8,128)(2,1)}, u32[]{:S(2)}) copy-start(bf16[4096,128]{1,0:T(8,128)(2,1)} %add_convert_fusion.1) | copy-start | bytes 3145732
  222.1 3.1 copy-start.7
  225.1 10.6 %copy-start.15 = (bf16[1,256,256]{2,1,0:T(8,128)(2,1)S(1)}, bf16[1,256,256]{2,1,0:T(8,128)(2,1)}, u32[]{:S(2)}) copy-start(bf16[1,256,256]{2,1,0:T(8,128)(2,1)} %copy-done.14) | copy-start | bytes 393220
  240.2 2.8 copy-start.1
  241.7 32.6 %collective-permute-start.3 = (bf16[2048,256]{0,1:T(8,128)(2,1)}, bf16[2048,256]{0,1:T(8,128)(2,1)}, u32[]{:S(2)}, u32[]{:S(2)}) collective-permute-start(bf16[2048,256]{0,1:T(8,128)(2,1)} %bitcast.19), channel_id=1, source_target_pairs={{2,0},{4,2},{6,4},{8,6},{10,8},{12,10},{14,12},{3,1},{5,3},{7,5},{... | collective-permute-start | bytes 3145736 | tf_op jit(solution)/shard_map/ppermute | solution.py:12
  243.0 1.5 copy-start.11
  250.8 108.9 %reduce-scatter.5.cloned.1.call-start = ((), (), s32[]{:S(2)}) async-start(), calls=%async_computation.9 | async-start | bytes 6291456 | tf_op jit(solution)/shard_map/reduce_scatter | solution.py:117
  250.9 23.3 %copy-start.12 = (bf16[2048,2,128]{0,2,1:T(8,128)(2,1)S(1)}, bf16[2048,2,128]{0,2,1:T(8,128)(2,1)}, u32[]{:S(2)}) copy-start(bf16[2048,2,128]{0,2,1:T(8,128)(2,1)} %get-tuple-element.16) | copy-start | bytes 3145732
  278.2 1.2 copy-start.5
  346.2 3.1 copy-start.17
  346.2 3.1 copy-start.18
Sparse Core Ops, SparseCore 0:
  10.1 13.2 all-gather.6
  59.2 12.4 all-gather.8
  75.2 11.4 all-gather.10
  90.7 10.1 all-gather.14
  195.8 12.2 reduce-scatter.2
  210.1 11.8 all-gather.12
  224.2 11.4 all-gather.16
  251.0 95.1 all-reduce.2
  348.4 11.2 reduce-scatter.4
where the time goes:
time: 370 us; the launch traced here: 369 us
  waiting for transfers between devices  267 us (72%)
  matrix products  43.3 us (12%)
  other arithmetic  16.6 us (4%)
  local copies, waits for them, and re-layouts  16.3 us (4%)
  between operations  14.1 us (4%)
  starting transfers between devices  11.8 us (3%)
    ppermute x4, waiting for transfers between devices, shifted(): return lax.ppermute(block, axis, route)  131 us
    psum x1, waiting for transfers between devices, sum_layer(): return lax.psum((conv_term, out_term), 'tm')  63.3 us
    all_gather x2, waiting for transfers between devices, on_device(): full_now = lax.all_gather(present_signal, 'chan', axis=1, tiled=True)  25.5 us
    all_gather x2, waiting for transfers between devices, on_device(): full_hidden = lax.all_gather(hidden, 'chan', axis=1, tiled=True)  19.3 us
    reduce_scatter x2, waiting for transfers between devices, on_device(): lax.psum_scatter(partial_sum, 'chan', scatter_dimension=1, tiled=True)  17.9 us
    dot_general x6, matrix products, contract_last(): lax.dot_general(former, latter, (((1,), (1,)), ((), ())), preferred_eleme...  16.8 us
    dot_general x6, matrix products, reduced_rows(): lax.dot_general(former, latter, (((0,), (0,)), ((), ())), preferred_eleme...  11.9 us
    ppermute x4, starting transfers between devices, shifted(): return lax.ppermute(block, axis, route)  11.3 us
  transfers between devices with their start and end apart: 13, of which 12 were waited for; matrix products, arithmetic and copies ran while one was open for 12% of the time, Pallas kernels for 0%

commit v1 on v0

v1 whole, which is shorter than its diff:
```python
import functools
import math

import jax
import jax.numpy as jnp
from jax import lax
from jax.experimental import pallas as pl
from jax.experimental.pallas import tpu as pltpu
from jax.sharding import PartitionSpec as P

BF = jnp.bfloat16
F32 = jnp.float32
VMEM_LIMIT = 48 * 1024 * 1024


def mm(a, b):
    return jnp.dot(a, b, preferred_element_type=F32)


def mm_t(a, b):
    return lax.dot_general(a, b, (((1,), (1,)), ((), ())), preferred_element_type=F32)


def mm_rows(a, b):
    return lax.dot_general(a, b, (((0,), (0,)), ((), ())), preferred_element_type=F32)


def ordered(core, own, other):
    first = core == 0
    return jnp.concatenate(
        [jnp.where(first, own, other), jnp.where(first, other, own)], axis=1
    )


def halves(core, values):
    width = values.shape[1] // 2
    low, high = values[:, :width], values[:, width:]
    first = core == 0
    return jnp.where(first, low, high), jnp.where(first, high, low)


def gated(x, delayed, tap_now, tap_past):
    width = x.shape[1]
    preact = mm(x, tap_now) + mm(delayed, tap_past)
    filt = jnp.tanh(preact[:, :width])
    gate = 0.5 * jnp.tanh(0.5 * preact[:, width:]) + 0.5
    hidden = (filt * gate).astype(BF)
    slope_f = gate * (1.0 - filt * filt)
    slope_g = filt * gate * (1.0 - gate)
    return hidden, slope_f, slope_g


def call(body, scalars, grid, ins, outs, scratch=(), flops=0, moved=0):
    return pl.pallas_call(
        body,
        grid_spec=pltpu.PrefetchScalarGridSpec(
            num_scalar_prefetch=1,
            grid=grid,
            in_specs=[pl.BlockSpec(block, index) for _, block, index in ins],
            out_specs=[pl.BlockSpec(block, index) for _, _, block, index in outs],
            scratch_shapes=list(scratch),
        ),
        out_shape=[jax.ShapeDtypeStruct(shape, kind) for shape, kind, _, _ in outs],
        compiler_params=pltpu.CompilerParams(vmem_limit_bytes=VMEM_LIMIT),
        cost_estimate=pl.CostEstimate(flops=flops, bytes_accessed=moved, transcendentals=0),
    )(scalars, *[array for array, _, _ in ins])


def rows_map(i, s):
    return (i, 0)


def fixed_map(i, s):
    return (0, 0)


def whole(array):
    return (array, array.shape, fixed_map)


def by_rows(array, block):
    return (array, (block, array.shape[1]), rows_map)


def out_rows(rows, cols, kind, block):
    return ((rows, cols), kind, (block, cols), rows_map)


def first_b(ids, own, other, own_a, other_a, t0, t1, wo, x_o, xa_o, x1_o, hid_o, slope_o):
    core = ids[0]
    x = ordered(core, own[...], other[...])
    delayed = ordered(core, own_a[...], other_a[...])
    x_o[...] = x
    xa_o[...] = delayed
    hidden, sf, sg = gated(x, delayed, t0[...], t1[...])
    x1_o[...] = (x.astype(F32) + mm(hidden, wo[...])).astype(BF)
    hid_o[...] = hidden
    width = x.shape[1]
    slope_o[:, :width] = sf
    slope_o[:, width:] = sg


def first_a(ids, x_r, own_h, other_h, t0, t1, wo, xh_o, x1_o, hid_o, slope_o):
    core = ids[0]
    x = x_r[...]
    delayed = ordered(core, own_h[...], other_h[...])
    xh_o[...] = delayed
    hidden, sf, sg = gated(x, delayed, t0[...], t1[...])
    x1_o[...] = (x.astype(F32) + mm(hidden, wo[...])).astype(BF)
    hid_o[...] = hidden
    width = x.shape[1]
    slope_o[:, :width] = sf
    slope_o[:, width:] = sg


def cot_body(ids, own, other, wo, g_o, hg_o):
    g = ordered(ids[0], own[...], other[...])
    g_o[...] = g
    hg_o[...] = mm_t(g, wo[...])


def second(ids, x_r, d_r, hg_r, t0, t1, pre_o, past_o, hid_o):
    hidden, sf, sg = gated(x_r[...], d_r[...], t0[...], t1[...])
    hid_o[...] = hidden
    hg = hg_r[...]
    pre = jnp.concatenate([(hg * sf).astype(BF), (hg * sg).astype(BF)], axis=1)
    pre_o[...] = pre
    past_o[...] = mm_t(pre, t1[...]).astype(BF)


def second_rest(ids, x_r, hid_r, g_r, pre_r, t0, wo, keep_o, send_o, local_o):
    out = (x_r[...].astype(F32) + mm(hid_r[...], wo[...])).astype(BF)
    keep, send = halves(ids[0], out)
    keep_o[...] = keep
    send_o[...] = send
    local_o[...] = g_r[...].astype(F32) + mm_t(pre_r[...], t0[...])


def third(ids, local_r, arrived_r, slope_r, t0, t1, wo, g_o, pre_o, past_o, now_o):
    g = (local_r[...] + arrived_r[...].astype(F32)).astype(BF)
    g_o[...] = g
    hg = mm_t(g, wo[...])
    width = g.shape[1]
    pre = jnp.concatenate(
        [(hg * slope_r[:, :width]).astype(BF), (hg * slope_r[:, width:]).astype(BF)], axis=1
    )
    pre_o[...] = pre
    past_o[...] = mm_t(pre, t1[...]).astype(past_o.dtype)
    now_o[...] = g.astype(F32) + mm_t(pre, t0[...])


def last(ids, now_r, past_r, keep_o, send_o):
    keep, send = halves(ids[0], (now_r[...] + past_r[...].astype(F32)).astype(BF))
    keep_o[...] = keep
    send_o[...] = send


def weight_body(scale, steps, ids, *refs):
    (xa, da, pa, ha, ga, xb, db, pb, hb, gb, keep_o, send_o, now, past, outg) = refs
    step = pl.program_id(0)

    @pl.when(step == 0)
    def _():
        now[...] = jnp.zeros_like(now)
        past[...] = jnp.zeros_like(past)
        outg[...] = jnp.zeros_like(outg)

    now[...] += mm_rows(xa[...], pa[...]) + mm_rows(xb[...], pb[...])
    past[...] += mm_rows(da[...], pa[...]) + mm_rows(db[...], pb[...])
    outg[...] += mm_rows(ha[...], ga[...]) + mm_rows(hb[...], gb[...])

    @pl.when(step == steps - 1)
    def _():
        channels = outg.shape[0]
        parts = [r[:, k * channels : (k + 1) * channels] for r in (now, past) for k in (0, 1)]
        parts.append(outg[...])
        for position, part in enumerate(parts):
            keep, send = halves(ids[0], part * scale)
            keep_o[pl.ds(position * channels, channels), :] = keep
            send_o[pl.ds(position * channels, channels), :] = send.astype(BF)


def split_body(parts, ids, keep_r, arrived_r, own_o, *rest):
    outs, total = rest[:-1], rest[-1]
    me = ids[1]
    total[...] = keep_r[...] + arrived_r[...].astype(F32)
    rows = own_o.shape[0]
    own_o[...] = total[pl.ds(pl.multiple_of(me * rows, rows), rows), :]
    for d in range(1, parts):
        place = lax.rem(me + d, parts) * rows
        outs[d - 1][...] = total[pl.ds(pl.multiple_of(place, rows), rows), :].astype(BF)


def sum_body(ids, own_r, *rest):
    total = own_r[...]
    for r in rest[:-1]:
        total = total + r[...].astype(F32)
    rest[-1][...] = total.astype(BF)


def place_body(parts, ids, own_r, *rest):
    me = ids[1]
    out = rest[-1]
    rows = own_r.shape[0]
    out[pl.ds(pl.multiple_of(me * rows, rows), rows), :] = own_r[...].astype(F32)
    for d in range(1, parts):
        place = lax.rem(me + parts - d, parts) * rows
        out[pl.ds(pl.multiple_of(place, rows), rows), :] = rest[d - 1][...].astype(F32)


def moved_by(values, distance):
    devices = range(lax.axis_size("tm"))
    return lax.ppermute(
        values, "tm", [(i, i + distance) for i in devices if i + distance in devices]
    )


def turned(values, distance):
    size = lax.axis_size("tm")
    return lax.ppermute(values, "tm", [(i, (i + distance) % size) for i in range(size)])


def swapped(values):
    return lax.ppermute(values, "chan", [(0, 1), (1, 0)])


def reduced(ids, keep, arrived):
    parts = lax.axis_size("tm")
    rows, cols = keep.shape
    if parts != 8:
        return lax.psum(keep + arrived.astype(F32), "tm")
    piece = rows // parts
    split = call(
        functools.partial(split_body, parts),
        ids,
        (1,),
        [whole(keep), whole(arrived)],
        [((piece, cols), F32, (piece, cols), fixed_map)]
        + [((piece, cols), BF, (piece, cols), fixed_map)] * (parts - 1),
        [pltpu.VMEM((rows, cols), F32)],
        moved=rows * cols * 8,
    )
    got = [turned(split[d], d) for d in range(1, parts)]
    (total,) = call(
        sum_body,
        ids,
        (1,),
        [whole(split[0])] + [whole(g) for g in got],
        [((piece, cols), BF, (piece, cols), fixed_map)],
        moved=rows * cols * 2,
    )
    back = [turned(total, d) for d in range(1, parts)]
    (result,) = call(
        functools.partial(place_body, parts),
        ids,
        (1,),
        [whole(total)] + [whole(b) for b in back],
        [((rows, cols), F32, (rows, cols), fixed_map)],
        moved=rows * cols * 6,
    )
    return result


def assembled(core, keep_a, got_a, keep_b, got_b):
    first = core == 0
    pieces = []
    for keep, got in ((keep_a, got_a), (keep_b, got_b)):
        pieces += [jnp.where(first, keep, got), jnp.where(first, got, keep)]
    return jnp.concatenate(pieces, axis=0)


def on_device(signal, cotangent, conv_weight, out_weight):
    rows, half_width = signal.shape
    channels = conv_weight.shape[2]
    quarter = rows // 4
    scale = 1.0 / math.sqrt(rows * lax.axis_size("tm"))
    core = lax.axis_index("chan")
    ids = jnp.stack([core, lax.axis_index("tm")]).astype(jnp.int32)
    taps = conv_weight.transpose(0, 1, 2, 3, 4).reshape(2, 2, channels, 2 * channels)
    t00, t01, t10, t11 = taps[0, 0], taps[0, 1], taps[1, 0], taps[1, 1]
    wo0, wo1 = out_weight[0], out_weight[1]
    blk = quarter // 4
    steps = quarter // blk
    wide = 2 * channels

    signal_other = swapped(signal)
    same = lax.dynamic_slice_in_dim(signal, 2 * quarter + core * quarter, quarter, 0)
    cross = lax.dynamic_slice_in_dim(signal, 2 * quarter + (1 - core) * quarter, quarter, 0)
    halo_own = moved_by(same, 1)
    size = lax.axis_size("tm")
    halo_other = lax.ppermute(
        cross,
        ("tm", "chan"),
        [(2 * i + c, 2 * (i + 1) + 1 - c) for i in range(size - 1) for c in (0, 1)],
    )
    cot_other = swapped(cotangent)

    def local_rows(array, half):
        return (array, (blk, half_width), lambda i, s: ((half * 2 + s[0]) * steps + i, 0))

    flop1 = 2 * quarter * (wide * wide + channels * channels)
    x_b, x_a, x1_b, hid0_b, slope_b = call(
        first_b,
        ids,
        (steps,),
        [local_rows(signal, 1), local_rows(signal_other, 1), local_rows(signal, 0), local_rows(signal_other, 0)]
        + [whole(t00), whole(t01), whole(wo0)],
        [out_rows(quarter, channels, BF, blk)] * 4 + [out_rows(quarter, wide, F32, blk)],
        flops=flop1,
        moved=quarter * channels * 20,
    )
    x1_b_past = moved_by(x1_b, 2)
    x_h, x1_a, hid0_a, slope_a = call(
        first_a,
        ids,
        (steps,),
        [by_rows(x_a, blk), by_rows(halo_own, blk), by_rows(halo_other, blk)]
        + [whole(t00), whole(t01), whole(wo0)],
        [out_rows(quarter, channels, BF, blk)] * 3 + [out_rows(quarter, wide, F32, blk)],
        flops=flop1,
        moved=quarter * channels * 18,
    )
    x1_a_past = moved_by(x1_a, 2)

    def cot_half(half):
        return call(
            cot_body,
            ids,
            (steps,),
            [local_rows(cotangent, half), local_rows(cot_other, half), whole(wo1)],
            [out_rows(quarter, channels, BF, blk), out_rows(quarter, channels, F32, blk)],
            flops=2 * quarter * channels * channels,
            moved=quarter * channels * 8,
        )

    cot_b, hg_b = cot_half(1)
    cot_a, hg_a = cot_half(0)

    def second_half(x1, past, hg):
        return call(
            second,
            ids,
            (steps,),
            [by_rows(x1, blk), by_rows(past, blk), by_rows(hg, blk), whole(t10), whole(t11)],
            [out_rows(quarter, wide, BF, blk)] + [out_rows(quarter, channels, BF, blk)] * 2,
            flops=2 * quarter * wide * (wide + channels),
            moved=quarter * channels * 16,
        )

    pre1_b, to_past_b, hid1_b = second_half(x1_b, x1_b_past, hg_b)
    from_next_b = moved_by(to_past_b, -2)
    pre1_a, to_past_a, hid1_a = second_half(x1_a, x1_a_past, hg_a)
    from_next_a = moved_by(to_past_a, -2)

    def rest_half(x1, hid1, cot, pre1):
        return call(
            second_rest,
            ids,
            (steps,),
            [by_rows(x1, blk), by_rows(hid1, blk), by_rows(cot, blk), by_rows(pre1, blk), whole(t10), whole(wo1)],
            [out_rows(quarter, half_width, BF, blk)] * 2 + [out_rows(quarter, channels, F32, blk)],
            flops=2 * quarter * channels * (wide + channels),
            moved=quarter * channels * 16,
        )

    out_keep_b, out_send_b, local_b = rest_half(x1_b, hid1_b, cot_b, pre1_b)
    out_keep_a, out_send_a, local_a = rest_half(x1_a, hid1_a, cot_a, pre1_a)
    output = assembled(core, out_keep_a, swapped(out_send_a), out_keep_b, swapped(out_send_b))

    def weights(*arrays):
        count = 5 * channels
        return call(
            functools.partial(weight_body, scale, steps),
            ids,
            (steps,),
            [by_rows(a, blk) for a in arrays],
            [((count, half_width), F32, (count, half_width), fixed_map), ((count, half_width), BF, (count, half_width), fixed_map)],
            [pltpu.VMEM((channels, wide), F32)] * 2 + [pltpu.VMEM((channels, channels), F32)],
            flops=4 * quarter * channels * (2 * wide + channels),
            moved=quarter * channels * 24,
        )

    keep1, send1 = weights(
        x1_a, x1_a_past, pre1_a, hid1_a, cot_a, x1_b, x1_b_past, pre1_b, hid1_b, cot_b
    )
    grads1 = reduced(ids, keep1, swapped(send1))

    def third_half(local, arrived, slope, kind):
        return call(
            third,
            ids,
            (steps,),
            [by_rows(local, blk), by_rows(arrived, blk), by_rows(slope, blk), whole(t00), whole(t01), whole(wo0)],
            [
                out_rows(quarter, channels, BF, blk),
                out_rows(quarter, wide, BF, blk),
                out_rows(quarter, channels, kind, blk),
                out_rows(quarter, channels, F32, blk),
            ],
            flops=2 * quarter * channels * (2 * wide + channels),
            moved=quarter * channels * 26,
        )

    g1_b, pre0_b, past_b, now_b = third_half(local_b, from_next_b, slope_b, F32)
    g1_a, pre0_a, past_a, now_a = third_half(local_a, from_next_a, slope_a, BF)
    ahead_b = moved_by(past_a, -1)
    keep0, send0 = weights(
        x_a, x_h, pre0_a, hid0_a, g1_a, x_b, x_a, pre0_b, hid0_b, g1_b
    )
    grads0 = reduced(ids, keep0, swapped(send0))

    def last_half(now, past):
        return call(
            last,
            ids,
            (steps,),
            [by_rows(now, blk), by_rows(past, blk)],
            [out_rows(quarter, half_width, BF, blk)] * 2,
            moved=quarter * channels * 10,
        )

    in_keep_a, in_send_a = last_half(now_a, past_b)
    in_keep_b, in_send_b = last_half(now_b, ahead_b)
    in_grad = assembled(core, in_keep_a, swapped(in_send_a), in_keep_b, swapped(in_send_b))

    grads = jnp.stack([grads0, grads1]).reshape(2, 5, channels, half_width)
    conv_grad = grads[:, :4].reshape(2, 2, 2, channels, half_width).transpose(0, 1, 3, 2, 4)
    return output, in_grad, conv_grad, grads[:, 4]


def solution(mesh):
    placed = (P(("groups", "tm"), "chan"), P(("groups", "tm"), "chan"), P(), P())
    return jax.shard_map(
        on_device,
        mesh=mesh,
        in_specs=placed,
        out_specs=(
            P(("groups", "tm"), "chan"),
            P(("groups", "tm"), "chan"),
            P("groups", None, None, None, "chan"),
            P("groups", None, "chan"),
        ),
        check_vma=False,
    )
```

time: 370 us -> 164 us (0.44)
  waiting for transfers between devices: 267 us -> 29.1 us
  starting transfers between devices: 11.8 us -> 66.6 us
  Pallas kernels: 0 us -> 44.4 us
  matrix products: 43.3 us -> 0 us
  between operations: 14.1 us -> 1.12 us
  other arithmetic: 16.6 us -> 5.08 us
    ppermute x4 -> x43, waiting for transfers between devices: 131 us -> 29.1 us  [the longest x28 16.2 us: turned(): lax.ppermute(values, 'tm', [(i, (i + distance) % size) for i in range(siz...]
    psum x1 -> x0, waiting for transfers between devices: 63.3 us -> none  [sum_layer(): return lax.psum((conv_term, out_term), 'tm')]
    ppermute x4 -> x43, starting transfers between devices: 11.3 us -> 66.6 us  [the longest x28 44.3 us: turned(): lax.ppermute(values, 'tm', [(i, (i + distance) % size) for i in range(siz...]
    all_gather x6 -> x0, waiting for transfers between devices: 54.1 us -> none  [the longest x2 25.5 us: on_device(): full_now = lax.all_gather(present_signal, 'chan', axis=1, tiled=True)]
    pallas_call x0 -> x20, Pallas kernels: none -> 44.4 us  [call(): pl.pallas_call(body, grid_spec=pltpu.PrefetchScalarGridSpec(num_scalar_pr...]
    dot_general x18 -> x0, matrix products: 43.3 us -> none  [the longest x6 16.8 us: contract_last(): lax.dot_general(former, latter, (((1,), (1,)), ((), ())), preferred_eleme...]
    reduce_scatter x2 -> x0, waiting for transfers between devices: 17.9 us -> none  [on_device(): lax.psum_scatter(partial_sum, 'chan', scatter_dimension=1, tiled=True)]
    convert_element_type x6 -> x0, other arithmetic: 11.8 us -> none  [the longest x2 5.88 us: gated_layer(): hidden = (filter_act * gate_act).astype(jnp.bfloat16)]
  transfers between devices with their start and end apart: 13 -> 43, of which waited for: 12 -> 12; matrix products, arithmetic and copies ran while one was open for 12% -> 7% of each run, Pallas kernels for 0% -> 27%
where the time goes in v1:
time: 164 us; the launch traced here: 163 us
  starting transfers between devices  66.6 us (41%)
  Pallas kernels  44.4 us (27%)
  waiting for transfers between devices  29.1 us (18%)
  local copies, waits for them, and re-layouts  16.4 us (10%)
  other arithmetic  5.08 us (3%)
    pallas_call x20, Pallas kernels, call(): pl.pallas_call(body, grid_spec=pltpu.PrefetchScalarGridSpec(num_scalar_pr...  44.4 us
    ppermute x28, starting transfers between devices, turned(): lax.ppermute(values, 'tm', [(i, (i + distance) % size) for i in range(siz...  44.3 us
    ppermute x6, starting transfers between devices, moved_by(): lax.ppermute(values, 'tm', [(i, i + distance) for i in devices if i + dis...  16.7 us
    ppermute x28, waiting for transfers between devices, turned(): lax.ppermute(values, 'tm', [(i, (i + distance) % size) for i in range(siz...  16.2 us
    ppermute x6, waiting for transfers between devices, moved_by(): lax.ppermute(values, 'tm', [(i, i + distance) for i in devices if i + dis...  12.4 us
    unnamed x48, local copies, waits for them, and re-layouts  8.87 us
    ppermute x1, starting transfers between devices, on_device(): lax.ppermute(cross, ('tm', 'chan'), [(2 * i + c, 2 * (i + 1) + 1 - c) for...  3.92 us
  transfers between devices with their start and end apart: 43, of which 12 were waited for; matrix products, arithmetic and copies ran while one was open for 7% of the time, Pallas kernels for 27%

profile of v1, /device:TPU:0, one launch (start us, length us, event | category | flops | bytes accessed | tf_op | source)
XLA Modules:
  0.0 162.7 jit_solution(3111439064375672677)
XLA Ops:
  1.1 1.9 %constant_dynamic-slice_fusion = (bf16[1024,128]{1,0:T(8,128)(2,1)}, bf16[1024,128]{1,0:T(8,128)(2,1)}) fusion(bf16[4096,128]{1,0:T(8,128)(2,1)} %own_a.1, s32[]{:T(128)S(6)} %select_n.44, s32[]{:T(128)S(6)} %select_n.43), kind=kLoop, calls=%fused_computation.23 | loop fusion | bytes 1048584 | tf_op jit(solution)/shard_map/dynamic_slice | solution.py:288
  3.0 4.5 %collective-permute-start.1 = (bf16[1024,128]{1,0:T(8,128)(2,1)}, bf16[1024,128]{1,0:T(8,128)(2,1)S(1)}, u32[]{:S(2)}, u32[]{:S(2)}) collective-permute-start(bf16[1024,128]{1,0:T(8,128)(2,1)} %get-tuple-element.119), channel_id=1, source_target_pairs={{0,2},{2,4},{4,6},{6,8},{8,10},{10,12},{12,14},{1,3},{3,5},{5,7},{... | collective-permute-start | bytes 786440 | tf_op jit(solution)/shard_map/ppermute | solution.py:213
  7.5 3.9 %collective-permute-start.2 = (bf16[1024,128]{1,0:T(8,128)(2,1)}, bf16[1024,128]{1,0:T(8,128)(2,1)}, u32[]{:S(2)}, u32[]{:S(2)}) collective-permute-start(bf16[1024,128]{1,0:T(8,128)(2,1)} %get-tuple-element.118), channel_id=1, source_target_pairs={{0,3},{1,2},{2,5},{3,4},{4,7},{5,6},{6,9},{7,8},{8,11},{9,10},{10,... | collective-permute-start | bytes 786440 | tf_op jit(solution)/shard_map/ppermute | solution.py:291
  11.7 2.6 %reshape.19 = bf16[2,2,256,512]{3,2,1,0:T(8,128)(2,1)} reshape(bf16[2,2,256,2,256]{4,3,2,1,0:T(2,128)(2,1)} %param.6) | data formatting | bytes 2097152 | tf_op jit(solution)/shard_map/reshape | solution.py:279
  14.4 1.3 slice_bitcast_fusion
  15.7 3.4 %shard_map.75 = (bf16[1024,256]{1,0:T(8,128)(2,1)S(1)}, bf16[1024,256]{1,0:T(8,128)(2,1)S(1)}, bf16[1024,256]{1,0:T(8,128)(2,1)S(1)}, bf16[1024,256]{1,0:T(8,128)(2,1)S(1)}, f32[1024,512]{1,0:T(8,128)}) custom-call(s32[2]{0:T(128)S(1)} %pad_add_fusion.ids, bf16[4096,128]{1,0:T(8,128)(2,1)S(1)} %copy-done, ...), custom_call_target="tpu_custom_call" | custom-call | flops 671088640 | bytes 5242880 | tf_op jit(solution)/shard_map/pallas_call | solution.py:54
  19.6 3.7 %shard_map.76 = (bf16[1024,256]{1,0:T(8,128)(2,1)S(1)}, bf16[1024,256]{1,0:T(8,128)(2,1)S(1)}, bf16[1024,256]{1,0:T(8,128)(2,1)S(1)}, f32[1024,512]{1,0:T(8,128)S(1)}) custom-call(s32[2]{0:T(128)S(1)} %pad_add_fusion.ids, bf16[1024,256]{1,0:T(8,128)(2,1)S(1)} %get-tuple-element.61.x_r.refs_0_.refs_6_, bf16[1024,128]{1,0:T(8,128)(2,1)S(1)} %collective-permute-done.1.own_h, ...), custom_call_target="tpu_custom_call" | custom-call | flops 671088640 | bytes 4718592 | tf_op jit(solution)/shard_map/pallas_call | solution.py:54
  23.3 1.4 copy-done.6
  24.7 4.9 %collective-permute-start.3 = (bf16[1024,256]{1,0:T(8,128)(2,1)S(1)}, bf16[1024,256]{1,0:T(8,128)(2,1)S(1)}, u32[]{:S(2)}, u32[]{:S(2)}) collective-permute-start(bf16[1024,256]{1,0:T(8,128)(2,1)S(1)} %get-tuple-element.62.x_r.refs_0_), channel_id=1, source_target_pairs={{0,4},{2,6},{4,8},{6,10},{8,12},{10,14},{1,5},{3,7},{5,9},{7,11},{... | collective-permute-start | bytes 1572872 | tf_op jit(solution)/shard_map/ppermute | solution.py:213
  29.7 3.5 %collective-permute-start.6 = (bf16[1024,256]{1,0:T(8,128)(2,1)S(1)}, bf16[1024,256]{1,0:T(8,128)(2,1)S(1)}, u32[]{:S(2)}, u32[]{:S(2)}) collective-permute-start(bf16[1024,256]{1,0:T(8,128)(2,1)S(1)} %get-tuple-element.69.x_r.refs_5_), channel_id=1, source_target_pairs={{0,4},{2,6},{4,8},{6,10},{8,12},{10,14},{1,5},{3,7},{5,9},{7,11},{... | collective-permute-start | bytes 1572872 | tf_op jit(solution)/shard_map/ppermute | solution.py:213
  33.2 1.4 shard_map.77
  34.6 1.4 shard_map.80
  36.1 5.8 %collective-permute-done.3.d_r.refs_1_ = bf16[1024,256]{1,0:T(8,128)(2,1)S(1)} collective-permute-done((bf16[1024,256]{1,0:T(8,128)(2,1)S(1)}, bf16[1024,256]{1,0:T(8,128)(2,1)S(1)}, u32[]{:S(2)}, u32[]{:S(2)}) %collective-permute-start.3) | collective-permute-done | bytes 524320 | tf_op jit(solution)/shard_map/ppermute | solution.py:213
  41.9 3.0 %shard_map.78 = (bf16[1024,512]{1,0:T(8,128)(2,1)S(1)}, bf16[1024,256]{1,0:T(8,128)(2,1)S(1)}, bf16[1024,256]{1,0:T(8,128)(2,1)S(1)}) custom-call(s32[2]{0:T(128)S(1)} %pad_add_fusion.ids, bf16[1024,256]{1,0:T(8,128)(2,1)S(1)} %get-tuple-element.62.x_r.refs_0_, bf16[1024,256]{1,0:T(8,128)(2,1)S(1)} %collective-permute-done.3.d_r.refs_1_, ...), custom_call_target="tpu_custom_call" | custom-call | flops 805306368 | bytes 4194304 | tf_op jit(solution)/shard_map/pallas_call | solution.py:54
  44.9 1.0 copy-done.1
  45.9 1.3 collective-permute-start.8
  47.2 5.3 %collective-permute-done.6.d_r.refs_6_ = bf16[1024,256]{1,0:T(8,128)(2,1)S(1)} collective-permute-done((bf16[1024,256]{1,0:T(8,128)(2,1)S(1)}, bf16[1024,256]{1,0:T(8,128)(2,1)S(1)}, u32[]{:S(2)}, u32[]{:S(2)}) %collective-permute-start.6) | collective-permute-done | bytes 524320 | tf_op jit(solution)/shard_map/ppermute | solution.py:213
  52.4 3.0 %shard_map.81 = (bf16[1024,512]{1,0:T(8,128)(2,1)S(1)}, bf16[1024,256]{1,0:T(8,128)(2,1)S(1)}, bf16[1024,256]{1,0:T(8,128)(2,1)S(1)}) custom-call(s32[2]{0:T(128)S(1)} %pad_add_fusion.ids, bf16[1024,256]{1,0:T(8,128)(2,1)S(1)} %get-tuple-element.69.x_r.refs_5_, bf16[1024,256]{1,0:T(8,128)(2,1)S(1)} %collective-permute-done.6.d_r.refs_6_, ...), custom_call_target="tpu_custom_call" | custom-call | flops 805306368 | bytes 4194304 | tf_op jit(solution)/shard_map/pallas_call | solution.py:54
  55.5 1.0 copy-done.3
  56.4 1.3 collective-permute-start.9
  57.7 4.6 %shard_map.91 = (f32[1280,128]{1,0:T(8,128)S(1)}, bf16[1280,128]{1,0:T(8,128)(2,1)S(1)}) custom-call(s32[2]{0:T(128)S(1)} %pad_add_fusion.ids, bf16[1024,256]{1,0:T(8,128)(2,1)S(1)} %get-tuple-element.62.x_r.refs_0_, bf16[1024,256]{1,0:T(8,128)(2,1)S(1)} %collective-permute-done.3.d_r.refs_1_, bf16[1024,512]{1,0:T(8,128)(2,1)} %copy-done.1, ...), custom_call_target="tpu_custom_call" | custom-call | flops 1342177280 | bytes 6291456 | tf_op jit(solution)/shard_map/pallas_call | solution.py:54
  62.4 1.7 %shard_map.79 = (bf16[1024,128]{1,0:T(8,128)(2,1)S(1)}, bf16[1024,128]{1,0:T(8,128)(2,1)S(1)}, f32[1024,256]{1,0:T(8,128)S(1)}) custom-call(s32[2]{0:T(128)S(1)} %pad_add_fusion.ids, bf16[1024,256]{1,0:T(8,128)(2,1)S(1)} %get-tuple-element.62.x_r.refs_0_, bf16[1024,256]{1,0:T(8,128)(2,1)S(1)} %get-tuple-element.64.hid_r.refs_3_, ...), custom_call_target="tpu_custom_call" | custom-call | flops 402653184 | bytes 4194304 | tf_op jit(solution)/shard_map/pallas_call | solution.py:54
  64.2 1.7 %shard_map.82 = (bf16[1024,128]{1,0:T(8,128)(2,1)S(1)}, bf16[1024,128]{1,0:T(8,128)(2,1)S(1)}, f32[1024,256]{1,0:T(8,128)S(1)}) custom-call(s32[2]{0:T(128)S(1)} %pad_add_fusion.ids, bf16[1024,256]{1,0:T(8,128)(2,1)S(1)} %get-tuple-element.69.x_r.refs_5_, bf16[1024,256]{1,0:T(8,128)(2,1)S(1)} %get-tuple-element.71.hid_r.refs_8_, ...), custom_call_target="tpu_custom_call" | custom-call | flops 402653184 | bytes 4194304 | tf_op jit(solution)/shard_map/pallas_call | solution.py:54
  65.9 4.2 %shard_map.83 = (bf16[1024,256]{1,0:T(8,128)(2,1)S(1)}, bf16[1024,512]{1,0:T(8,128)(2,1)S(1)}, bf16[1024,256]{1,0:T(8,128)(2,1)S(1)}, f32[1024,256]{1,0:T(8,128)S(1)}) custom-call(s32[2]{0:T(128)S(1)} %pad_add_fusion.ids, f32[1024,256]{1,0:T(8,128)S(1)} %get-tuple-element.76.local_r, bf16[1024,256]{1,0:T(8,128)(2,1)S(1)} %collective-permute-done.8.arrived_r, ...), custom_call_target="tpu_custom_call" | custom-call | flops 671088640 | bytes 6815744 | tf_op jit(solution)/shard_map/pallas_call | solution.py:54
  70.9 1.4 collective-permute-done.9.arrived_r
  72.3 4.2 %shard_map.84 = (bf16[1024,256]{1,0:T(8,128)(2,1)S(1)}, bf16[1024,512]{1,0:T(8,128)(2,1)S(1)}, f32[1024,256]{1,0:T(8,128)S(1)}, f32[1024,256]{1,0:T(8,128)S(1)}) custom-call(s32[2]{0:T(128)S(1)} %pad_add_fusion.ids, f32[1024,256]{1,0:T(8,128)S(1)} %get-tuple-element.80.local_r, bf16[1024,256]{1,0:T(8,128)(2,1)S(1)} %collective-permute-done.9.arrived_r, ...), custom_call_target="tpu_custom_call" | custom-call | flops 671088640 | bytes 6815744 | tf_op jit(solution)/shard_map/pallas_call | solution.py:54
  76.6 1.0 copy-done.7
  77.5 4.4 %shard_map.87 = (f32[1280,128]{1,0:T(8,128)S(1)}, bf16[1280,128]{1,0:T(8,128)(2,1)S(1)}) custom-call(s32[2]{0:T(128)S(1)} %pad_add_fusion.ids, bf16[1024,256]{1,0:T(8,128)(2,1)S(1)} %get-tuple-element.61.x_r.refs_0_.refs_6_, bf16[1024,256]{1,0:T(8,128)(2,1)S(1)} %copy-done.11, bf16[1024,512]{1,0:T(8,128)(2,1)S(1)} %get-tuple-element.91.refs_2_, ...), custom_call_target="tpu_custom_call" | custom-call | flops 1342177280 | bytes 6291456 | tf_op jit(solution)/shard_map/pallas_call | solution.py:54
  84.0 2.1 %collective-permute-start.30 = (bf16[160,128]{1,0:T(8,128)(2,1)S(1)}, bf16[160,128]{1,0:T(8,128)(2,1)S(1)}, u32[]{:S(2)}, u32[]{:S(2)}) collective-permute-start(bf16[160,128]{1,0:T(8,128)(2,1)S(1)} %get-tuple-element.112), channel_id=1, source_target_pairs={{0,4},{2,6},{4,8},{6,10},{8,12},{10,14},{12,0},{14,2},{1,5},{3,7},... | collective-permute-start | bytes 122888 | tf_op jit(solution)/shard_map/ppermute | solution.py:220
  86.1 4.0 %collective-permute-done.29.rest_0_ = bf16[160,128]{1,0:T(8,128)(2,1)S(1)} collective-permute-done((bf16[160,128]{1,0:T(8,128)(2,1)S(1)}, bf16[160,128]{1,0:T(8,128)(2,1)S(1)}, u32[]{:S(2)}, u32[]{:S(2)}) %collective-permute-start.29) | collective-permute-done | bytes 40992 | tf_op jit(solution)/shard_map/ppermute | solution.py:220
  90.6 2.0 %collective-permute-start.32 = (bf16[160,128]{1,0:T(8,128)(2,1)S(1)}, bf16[160,128]{1,0:T(8,128)(2,1)S(1)}, u32[]{:S(2)}, u32[]{:S(2)}) collective-permute-start(bf16[160,128]{1,0:T(8,128)(2,1)S(1)} %get-tuple-element.114), channel_id=1, source_target_pairs={{0,8},{2,10},{4,12},{6,14},{8,0},{10,2},{12,4},{14,6},{1,9},{3,11}... | collective-permute-start | bytes 122888 | tf_op jit(solution)/shard_map/ppermute | solution.py:220
  92.6 4.0 %collective-permute-done.31.rest_2_ = bf16[160,128]{1,0:T(8,128)(2,1)S(1)} collective-permute-done((bf16[160,128]{1,0:T(8,128)(2,1)S(1)}, bf16[160,128]{1,0:T(8,128)(2,1)S(1)}, u32[]{:S(2)}, u32[]{:S(2)}) %collective-permute-start.31) | collective-permute-done | bytes 40992 | tf_op jit(solution)/shard_map/ppermute | solution.py:220
  96.6 2.4 %collective-permute-start.34 = (bf16[160,128]{1,0:T(8,128)(2,1)S(1)}, bf16[160,128]{1,0:T(8,128)(2,1)S(1)}, u32[]{:S(2)}, u32[]{:S(2)}) collective-permute-start(bf16[160,128]{1,0:T(8,128)(2,1)S(1)} %get-tuple-element.116), channel_id=1, source_target_pairs={{0,12},{2,14},{4,0},{6,2},{8,4},{10,6},{12,8},{14,10},{1,13},{3,15... | collective-permute-start | bytes 122888 | tf_op jit(solution)/shard_map/ppermute | solution.py:220
  99.1 2.5 %collective-permute-done.33.rest_4_ = bf16[160,128]{1,0:T(8,128)(2,1)S(1)} collective-permute-done((bf16[160,128]{1,0:T(8,128)(2,1)S(1)}, bf16[160,128]{1,0:T(8,128)(2,1)S(1)}, u32[]{:S(2)}, u32[]{:S(2)}) %collective-permute-start.33) | collective-permute-done | bytes 40992 | tf_op jit(solution)/shard_map/ppermute | solution.py:220
  101.5 1.8 %collective-permute-start.35 = (bf16[160,128]{1,0:T(8,128)(2,1)S(1)}, bf16[160,128]{1,0:T(8,128)(2,1)S(1)}, u32[]{:S(2)}, u32[]{:S(2)}) collective-permute-start(bf16[160,128]{1,0:T(8,128)(2,1)S(1)} %get-tuple-element.117), channel_id=1, source_target_pairs={{0,14},{2,0},{4,2},{6,4},{8,6},{10,8},{12,10},{14,12},{1,15},{3,1}... | collective-permute-start | bytes 122888 | tf_op jit(solution)/shard_map/ppermute | solution.py:220
  103.4 2.2 %collective-permute-done.35.rest_6_ = bf16[160,128]{1,0:T(8,128)(2,1)S(1)} collective-permute-done((bf16[160,128]{1,0:T(8,128)(2,1)S(1)}, bf16[160,128]{1,0:T(8,128)(2,1)S(1)}, u32[]{:S(2)}, u32[]{:S(2)}) %collective-permute-start.35) | collective-permute-done | bytes 40992 | tf_op jit(solution)/shard_map/ppermute | solution.py:220
  106.1 1.7 %collective-permute-start.36 = (bf16[160,128]{1,0:T(8,128)(2,1)S(1)}, bf16[160,128]{1,0:T(8,128)(2,1)}, u32[]{:S(2)}, u32[]{:S(2)}) collective-permute-start(bf16[160,128]{1,0:T(8,128)(2,1)S(1)} %shard_map.93.own_r), channel_id=1, source_target_pairs={{0,2},{2,4},{4,6},{6,8},{8,10},{10,12},{12,14},{14,0},{1,3},{3,5},... | collective-permute-start | bytes 122888 | tf_op jit(solution)/shard_map/ppermute | solution.py:220
  108.7 4.2 %collective-permute-start.38 = (bf16[160,128]{1,0:T(8,128)(2,1)S(1)}, bf16[160,128]{1,0:T(8,128)(2,1)}, u32[]{:S(2)}, u32[]{:S(2)}) collective-permute-start(bf16[160,128]{1,0:T(8,128)(2,1)S(1)} %shard_map.93.own_r), channel_id=1, source_target_pairs={{0,6},{2,8},{4,10},{6,12},{8,14},{10,0},{12,2},{14,4},{1,7},{3,9},... | collective-permute-start | bytes 122888 | tf_op jit(solution)/shard_map/ppermute | solution.py:220
  112.9 1.3 shard_map.88
  118.8 1.0 collective-permute-start.16
  119.8 3.5 %collective-permute-start.17 = (bf16[160,128]{1,0:T(8,128)(2,1)}, bf16[160,128]{1,0:T(8,128)(2,1)S(1)}, u32[]{:S(2)}, u32[]{:S(2)}) collective-permute-start(bf16[160,128]{1,0:T(8,128)(2,1)} %copy-done.19), channel_id=1, source_target_pairs={{0,8},{2,10},{4,12},{6,14},{8,0},{10,2},{12,4},{14,6},{1,9},{3,11}... | collective-permute-start | bytes 122888 | tf_op jit(solution)/shard_map/ppermute | solution.py:220
  123.3 1.0 collective-permute-start.18
  124.2 2.1 %collective-permute-start.19 = (bf16[160,128]{1,0:T(8,128)(2,1)}, bf16[160,128]{1,0:T(8,128)(2,1)S(1)}, u32[]{:S(2)}, u32[]{:S(2)}) collective-permute-start(bf16[160,128]{1,0:T(8,128)(2,1)} %copy-done.17), channel_id=1, source_target_pairs={{0,12},{2,14},{4,0},{6,2},{8,4},{10,6},{12,8},{14,10},{1,13},{3,15... | collective-permute-start | bytes 122888 | tf_op jit(solution)/shard_map/ppermute | solution.py:220
  126.4 1.3 collective-permute-start.20
  127.7 1.1 broadcast_select_fusion.7
  128.8 2.9 %collective-permute-start.39 = (bf16[160,128]{1,0:T(8,128)(2,1)S(1)}, bf16[160,128]{1,0:T(8,128)(2,1)S(1)}, u32[]{:S(2)}, u32[]{:S(2)}) collective-permute-start(bf16[160,128]{1,0:T(8,128)(2,1)S(1)} %shard_map.93.own_r), channel_id=1, source_target_pairs={{0,8},{2,10},{4,12},{6,14},{8,0},{10,2},{12,4},{14,6},{1,9},{3,11}... | collective-permute-start | bytes 122888 | tf_op jit(solution)/shard_map/ppermute | solution.py:220
  131.9 1.3 collective-permute-start.41
  133.2 1.5 collective-permute-start.42
  134.7 1.3 collective-permute-start.11
  136.0 1.0 broadcast_select_fusion.5
  137.7 1.4 shard_map.89.own_r
  139.2 2.7 %collective-permute-start.21 = (bf16[160,128]{1,0:T(8,128)(2,1)S(1)}, bf16[160,128]{1,0:T(8,128)(2,1)S(1)}, u32[]{:S(2)}, u32[]{:S(2)}) collective-permute-start(bf16[160,128]{1,0:T(8,128)(2,1)S(1)} %shard_map.89.own_r), channel_id=1, source_target_pairs={{0,2},{2,4},{4,6},{6,8},{8,10},{10,12},{12,14},{14,0},{1,3},{3,5},... | collective-permute-start | bytes 122888 | tf_op jit(solution)/shard_map/ppermute | solution.py:220
  141.9 1.5 collective-permute-start.22
  143.4 1.4 collective-permute-start.23
  144.8 1.0 pad_maximum_fusion
  145.8 1.4 shard_map.94
  147.3 2.5 %collective-permute-start.24 = (bf16[160,128]{1,0:T(8,128)(2,1)S(1)}, bf16[160,128]{1,0:T(8,128)(2,1)S(1)}, u32[]{:S(2)}, u32[]{:S(2)}) collective-permute-start(bf16[160,128]{1,0:T(8,128)(2,1)S(1)} %shard_map.89.own_r), channel_id=1, source_target_pairs={{0,8},{2,10},{4,12},{6,14},{8,0},{10,2},{12,4},{14,6},{1,9},{3,11}... | collective-permute-start | bytes 122888 | tf_op jit(solution)/shard_map/ppermute | solution.py:220
  150.5 2.0 %collective-permute-start.25 = (bf16[160,128]{1,0:T(8,128)(2,1)S(1)}, bf16[160,128]{1,0:T(8,128)(2,1)S(1)}, u32[]{:S(2)}, u32[]{:S(2)}) collective-permute-start(bf16[160,128]{1,0:T(8,128)(2,1)S(1)} %shard_map.89.own_r), channel_id=1, source_target_pairs={{0,10},{2,12},{4,14},{6,0},{8,2},{10,4},{12,6},{14,8},{1,11},{3,13... | collective-permute-start | bytes 122888 | tf_op jit(solution)/shard_map/ppermute | solution.py:220
  152.6 1.8 %collective-permute-start.26 = (bf16[160,128]{1,0:T(8,128)(2,1)S(1)}, bf16[160,128]{1,0:T(8,128)(2,1)S(1)}, u32[]{:S(2)}, u32[]{:S(2)}) collective-permute-start(bf16[160,128]{1,0:T(8,128)(2,1)S(1)} %shard_map.89.own_r), channel_id=1, source_target_pairs={{0,12},{2,14},{4,0},{6,2},{8,4},{10,6},{12,8},{14,10},{1,13},{3,15... | collective-permute-start | bytes 122888 | tf_op jit(solution)/shard_map/ppermute | solution.py:220
  154.4 0.9 collective-permute-start.27
  155.5 1.1 collective-permute-done.26.rest_5_
  156.6 1.8 %collective-permute-done.27.rest_6_ = bf16[160,128]{1,0:T(8,128)(2,1)S(1)} collective-permute-done((bf16[160,128]{1,0:T(8,128)(2,1)S(1)}, bf16[160,128]{1,0:T(8,128)(2,1)S(1)}, u32[]{:S(2)}, u32[]{:S(2)}) %collective-permute-start.27) | collective-permute-done | bytes 40992 | tf_op jit(solution)/shard_map/ppermute | solution.py:220
  159.1 1.8 %copy.12 = f32[2,2,2,256,128]{4,2,3,1,0:T(2,128)} copy(f32[2,2,2,256,128]{4,3,0,2,1:T(8,128)S(1)} %bitcast.30) | data formatting | bytes 2097152 | tf_op jit(solution)/shard_map/reshape | solution.py:427
  161.6 1.0 pad_maximum_fusion.1
  (104 shorter events, 14.3 us)
Async XLA Ops:
  0.6 15.0 %collective-permute-start = (bf16[4096,128]{1,0:T(8,128)(2,1)}, bf16[4096,128]{1,0:T(8,128)(2,1)S(1)}, u32[]{:S(2)}, u32[]{:S(2)}) collective-permute-start(bf16[4096,128]{1,0:T(8,128)(2,1)} %own_a.1), channel_id=1, source_target_pairs={{0,1},{1,0},{2,3},{3,2},{4,5},{5,4},{6,7},{7,6},{8,9},{9,8},{10,11... | collective-permute-start | bytes 3145736 | tf_op jit(solution)/shard_map/ppermute | solution.py:224
  3.0 16.1 %collective-permute-start.1 = (bf16[1024,128]{1,0:T(8,128)(2,1)}, bf16[1024,128]{1,0:T(8,128)(2,1)S(1)}, u32[]{:S(2)}, u32[]{:S(2)}) collective-permute-start(bf16[1024,128]{1,0:T(8,128)(2,1)} %get-tuple-element.119), channel_id=1, source_target_pairs={{0,2},{2,4},{4,6},{6,8},{8,10},{10,12},{12,14},{1,3},{3,5},{5,7},{... | collective-permute-start | bytes 786440 | tf_op jit(solution)/shard_map/ppermute | solution.py:213
  7.5 12.1 %collective-permute-start.2 = (bf16[1024,128]{1,0:T(8,128)(2,1)}, bf16[1024,128]{1,0:T(8,128)(2,1)}, u32[]{:S(2)}, u32[]{:S(2)}) collective-permute-start(bf16[1024,128]{1,0:T(8,128)(2,1)} %get-tuple-element.118), channel_id=1, source_target_pairs={{0,3},{1,2},{2,5},{3,4},{4,7},{5,6},{6,9},{7,8},{8,11},{9,10},{10,... | collective-permute-start | bytes 786440 | tf_op jit(solution)/shard_map/ppermute | solution.py:291
  11.4 21.8 %collective-permute-start.4 = (bf16[4096,128]{1,0:T(8,128)(2,1)}, bf16[4096,128]{1,0:T(8,128)(2,1)S(1)}, u32[]{:S(2)}, u32[]{:S(2)}) collective-permute-start(bf16[4096,128]{1,0:T(8,128)(2,1)} %own.5), channel_id=1, source_target_pairs={{0,1},{1,0},{2,3},{3,2},{4,5},{5,4},{6,7},{7,6},{8,9},{9,8},{10,11... | collective-permute-start | bytes 3145736 | tf_op jit(solution)/shard_map/ppermute | solution.py:224
  11.7 4.0 %copy-start = (bf16[4096,128]{1,0:T(8,128)(2,1)S(1)}, bf16[4096,128]{1,0:T(8,128)(2,1)}, u32[]{:S(2)}) copy-start(bf16[4096,128]{1,0:T(8,128)(2,1)} %own_a.1) | copy-start | bytes 3145732
  14.3 1.3 copy-start.21
  19.1 15.5 %copy-start.8 = (bf16[1024,256]{1,0:T(8,128)(2,1)}, bf16[1024,256]{1,0:T(8,128)(2,1)S(1)}, u32[]{:S(2)}) copy-start(bf16[1024,256]{1,0:T(8,128)(2,1)S(1)} %get-tuple-element.96.refs_8_) | copy-start | bytes 1572868
  19.1 14.1 %copy-start.5 = (bf16[4096,128]{1,0:T(8,128)(2,1)S(1)}, bf16[4096,128]{1,0:T(8,128)(2,1)}, u32[]{:S(2)}) copy-start(bf16[4096,128]{1,0:T(8,128)(2,1)} %own.5) | copy-start | bytes 3145732
  23.3 1.4 copy-start.6
  24.7 11.4 %copy-start.10 = (bf16[1024,256]{1,0:T(8,128)(2,1)}, bf16[1024,256]{1,0:T(8,128)(2,1)S(1)}, u32[]{:S(2)}) copy-start(bf16[1024,256]{1,0:T(8,128)(2,1)S(1)} %get-tuple-element.90.refs_1_) | copy-start | bytes 1572868
  24.7 11.4 %copy-start.12 = (bf16[1024,256]{1,0:T(8,128)(2,1)}, bf16[1024,256]{1,0:T(8,128)(2,1)S(1)}, u32[]{:S(2)}) copy-start(bf16[1024,256]{1,0:T(8,128)(2,1)S(1)} %get-tuple-element.92.refs_3_) | copy-start | bytes 1572868
  24.7 17.2 %collective-permute-start.3 = (bf16[1024,256]{1,0:T(8,128)(2,1)S(1)}, bf16[1024,256]{1,0:T(8,128)(2,1)S(1)}, u32[]{:S(2)}, u32[]{:S(2)}) collective-permute-start(bf16[1024,256]{1,0:T(8,128)(2,1)S(1)} %get-tuple-element.62.x_r.refs_0_), channel_id=1, source_target_pairs={{0,4},{2,6},{4,8},{6,10},{8,12},{10,14},{1,5},{3,7},{5,9},{7,11},{... | collective-permute-start | bytes 1572872 | tf_op jit(solution)/shard_map/ppermute | solution.py:213
  29.7 22.8 %collective-permute-start.6 = (bf16[1024,256]{1,0:T(8,128)(2,1)S(1)}, bf16[1024,256]{1,0:T(8,128)(2,1)S(1)}, u32[]{:S(2)}, u32[]{:S(2)}) collective-permute-start(bf16[1024,256]{1,0:T(8,128)(2,1)S(1)} %get-tuple-element.69.x_r.refs_5_), channel_id=1, source_target_pairs={{0,4},{2,6},{4,8},{6,10},{8,12},{10,14},{1,5},{3,7},{5,9},{7,11},{... | collective-permute-start | bytes 1572872 | tf_op jit(solution)/shard_map/ppermute | solution.py:213
  44.9 1.0 copy-start.1
  45.9 20.0 %collective-permute-start.8 = (bf16[1024,256]{1,0:T(8,128)(2,1)S(1)}, bf16[1024,256]{1,0:T(8,128)(2,1)S(1)}, u32[]{:S(2)}, u32[]{:S(2)}) collective-permute-start(bf16[1024,256]{1,0:T(8,128)(2,1)S(1)} %get-tuple-element.77), channel_id=1, source_target_pairs={{4,0},{6,2},{8,4},{10,6},{12,8},{14,10},{5,1},{7,3},{9,5},{11,7},{... | collective-permute-start | bytes 1572872 | tf_op jit(solution)/shard_map/ppermute | solution.py:213
  55.5 1.0 copy-start.3
  56.4 15.9 %collective-permute-start.9 = (bf16[1024,256]{1,0:T(8,128)(2,1)S(1)}, bf16[1024,256]{1,0:T(8,128)(2,1)S(1)}, u32[]{:S(2)}, u32[]{:S(2)}) collective-permute-start(bf16[1024,256]{1,0:T(8,128)(2,1)S(1)} %get-tuple-element.81), channel_id=1, source_target_pairs={{4,0},{6,2},{8,4},{10,6},{12,8},{14,10},{5,1},{7,3},{9,5},{11,7},{... | collective-permute-start | bytes 1572872 | tf_op jit(solution)/shard_map/ppermute | solution.py:213
  57.7 4.7 %copy-start.2 = (bf16[1024,512]{1,0:T(8,128)(2,1)S(1)}, bf16[1024,512]{1,0:T(8,128)(2,1)}, u32[]{:S(2)}) copy-start(bf16[1024,512]{1,0:T(8,128)(2,1)} %copy-done.1) | copy-start | bytes 3145732
  62.3 1.8 %copy-start.4 = (bf16[1024,512]{1,0:T(8,128)(2,1)S(1)}, bf16[1024,512]{1,0:T(8,128)(2,1)}, u32[]{:S(2)}) copy-start(bf16[1024,512]{1,0:T(8,128)(2,1)} %copy-done.3) | copy-start | bytes 3145732
  62.4 20.3 %collective-permute-start.28 = (bf16[1280,128]{1,0:T(8,128)(2,1)S(1)}, bf16[1280,128]{1,0:T(8,128)(2,1)S(1)}, u32[]{:S(2)}, u32[]{:S(2)}) collective-permute-start(bf16[1280,128]{1,0:T(8,128)(2,1)S(1)} %get-tuple-element.109), channel_id=1, source_target_pairs={{0,1},{1,0},{2,3},{3,2},{4,5},{5,4},{6,7},{7,6},{8,9},{9,8},{10,11... | collective-permute-start | bytes 983048 | tf_op jit(solution)/shard_map/ppermute | solution.py:224
  64.2 1.7 %copy-start.14 = (bf16[1024,128]{1,0:T(8,128)(2,1)}, bf16[1024,128]{1,0:T(8,128)(2,1)S(1)}, u32[]{:S(2)}) copy-start(bf16[1024,128]{1,0:T(8,128)(2,1)S(1)} %get-tuple-element.67) | copy-start | bytes 786436
  70.1 0.8 copy-start.15
  72.3 5.2 %copy-start.9 = (bf16[1024,256]{1,0:T(8,128)(2,1)S(1)}, bf16[1024,256]{1,0:T(8,128)(2,1)}, u32[]{:S(2)}) copy-start(bf16[1024,256]{1,0:T(8,128)(2,1)} %copy-done.8) | copy-start | bytes 1572868
  72.3 5.2 %copy-start.11 = (bf16[1024,256]{1,0:T(8,128)(2,1)S(1)}, bf16[1024,256]{1,0:T(8,128)(2,1)}, u32[]{:S(2)}) copy-start(bf16[1024,256]{1,0:T(8,128)(2,1)} %copy-done.10) | copy-start | bytes 1572868
  72.3 5.2 %copy-start.13 = (bf16[1024,256]{1,0:T(8,128)(2,1)S(1)}, bf16[1024,256]{1,0:T(8,128)(2,1)}, u32[]{:S(2)}) copy-start(bf16[1024,256]{1,0:T(8,128)(2,1)} %copy-done.12) | copy-start | bytes 1572868
  76.5 1.0 copy-start.7
  82.0 26.7 %collective-permute-start.13 = (bf16[1280,128]{1,0:T(8,128)(2,1)S(1)}, bf16[1280,128]{1,0:T(8,128)(2,1)S(1)}, u32[]{:S(2)}, u32[]{:S(2)}) collective-permute-start(bf16[1280,128]{1,0:T(8,128)(2,1)S(1)} %get-tuple-element.99), channel_id=1, source_target_pairs={{0,1},{1,0},{2,3},{3,2},{4,5},{5,4},{6,7},{7,6},{8,9},{9,8},{10,11... | collective-permute-start | bytes 983048 | tf_op jit(solution)/shard_map/ppermute | solution.py:224
  82.1 35.2 %collective-permute-start.5 = (bf16[1024,128]{1,0:T(8,128)(2,1)S(1)}, bf16[1024,128]{1,0:T(8,128)(2,1)S(1)}, u32[]{:S(2)}, u32[]{:S(2)}) collective-permute-start(bf16[1024,128]{1,0:T(8,128)(2,1)S(1)} %get-tuple-element.68), channel_id=1, source_target_pairs={{0,1},{1,0},{2,3},{3,2},{4,5},{5,4},{6,7},{7,6},{8,9},{9,8},{10,11... | collective-permute-start | bytes 786440 | tf_op jit(solution)/shard_map/ppermute | solution.py:224
  82.5 35.4 %collective-permute-start.7 = (bf16[1024,128]{1,0:T(8,128)(2,1)S(1)}, bf16[1024,128]{1,0:T(8,128)(2,1)S(1)}, u32[]{:S(2)}, u32[]{:S(2)}) collective-permute-start(bf16[1024,128]{1,0:T(8,128)(2,1)S(1)} %get-tuple-element.75), channel_id=1, source_target_pairs={{0,1},{1,0},{2,3},{3,2},{4,5},{5,4},{6,7},{7,6},{8,9},{9,8},{10,11... | collective-permute-start | bytes 786440 | tf_op jit(solution)/shard_map/ppermute | solution.py:224
  83.3 6.8 %collective-permute-start.29 = (bf16[160,128]{1,0:T(8,128)(2,1)S(1)}, bf16[160,128]{1,0:T(8,128)(2,1)S(1)}, u32[]{:S(2)}, u32[]{:S(2)}) collective-permute-start(bf16[160,128]{1,0:T(8,128)(2,1)S(1)} %get-tuple-element.111), channel_id=1, source_target_pairs={{0,2},{2,4},{4,6},{6,8},{8,10},{10,12},{12,14},{14,0},{1,3},{3,5},... | collective-permute-start | bytes 122888 | tf_op jit(solution)/shard_map/ppermute | solution.py:220
  84.0 6.6 %collective-permute-start.30 = (bf16[160,128]{1,0:T(8,128)(2,1)S(1)}, bf16[160,128]{1,0:T(8,128)(2,1)S(1)}, u32[]{:S(2)}, u32[]{:S(2)}) collective-permute-start(bf16[160,128]{1,0:T(8,128)(2,1)S(1)} %get-tuple-element.112), channel_id=1, source_target_pairs={{0,4},{2,6},{4,8},{6,10},{8,12},{10,14},{12,0},{14,2},{1,5},{3,7},... | collective-permute-start | bytes 122888 | tf_op jit(solution)/shard_map/ppermute | solution.py:220
  90.0 6.6 %collective-permute-start.31 = (bf16[160,128]{1,0:T(8,128)(2,1)S(1)}, bf16[160,128]{1,0:T(8,128)(2,1)S(1)}, u32[]{:S(2)}, u32[]{:S(2)}) collective-permute-start(bf16[160,128]{1,0:T(8,128)(2,1)S(1)} %get-tuple-element.113), channel_id=1, source_target_pairs={{0,6},{2,8},{4,10},{6,12},{8,14},{10,0},{12,2},{14,4},{1,7},{3,9},... | collective-permute-start | bytes 122888 | tf_op jit(solution)/shard_map/ppermute | solution.py:220
  90.6 6.1 %collective-permute-start.32 = (bf16[160,128]{1,0:T(8,128)(2,1)S(1)}, bf16[160,128]{1,0:T(8,128)(2,1)S(1)}, u32[]{:S(2)}, u32[]{:S(2)}) collective-permute-start(bf16[160,128]{1,0:T(8,128)(2,1)S(1)} %get-tuple-element.114), channel_id=1, source_target_pairs={{0,8},{2,10},{4,12},{6,14},{8,0},{10,2},{12,4},{14,6},{1,9},{3,11}... | collective-permute-start | bytes 122888 | tf_op jit(solution)/shard_map/ppermute | solution.py:220
  96.6 4.9 %collective-permute-start.33 = (bf16[160,128]{1,0:T(8,128)(2,1)S(1)}, bf16[160,128]{1,0:T(8,128)(2,1)S(1)}, u32[]{:S(2)}, u32[]{:S(2)}) collective-permute-start(bf16[160,128]{1,0:T(8,128)(2,1)S(1)} %get-tuple-element.115), channel_id=1, source_target_pairs={{0,10},{2,12},{4,14},{6,0},{8,2},{10,4},{12,6},{14,8},{1,11},{3,13... | collective-permute-start | bytes 122888 | tf_op jit(solution)/shard_map/ppermute | solution.py:220
  96.6 6.7 %collective-permute-start.34 = (bf16[160,128]{1,0:T(8,128)(2,1)S(1)}, bf16[160,128]{1,0:T(8,128)(2,1)S(1)}, u32[]{:S(2)}, u32[]{:S(2)}) collective-permute-start(bf16[160,128]{1,0:T(8,128)(2,1)S(1)} %get-tuple-element.116), channel_id=1, source_target_pairs={{0,12},{2,14},{4,0},{6,2},{8,4},{10,6},{12,8},{14,10},{1,13},{3,15... | collective-permute-start | bytes 122888 | tf_op jit(solution)/shard_map/ppermute | solution.py:220
  101.5 4.0 %collective-permute-start.35 = (bf16[160,128]{1,0:T(8,128)(2,1)S(1)}, bf16[160,128]{1,0:T(8,128)(2,1)S(1)}, u32[]{:S(2)}, u32[]{:S(2)}) collective-permute-start(bf16[160,128]{1,0:T(8,128)(2,1)S(1)} %get-tuple-element.117), channel_id=1, source_target_pairs={{0,14},{2,0},{4,2},{6,4},{8,6},{10,8},{12,10},{14,12},{1,15},{3,1}... | collective-permute-start | bytes 122888 | tf_op jit(solution)/shard_map/ppermute | solution.py:220
  106.1 12.7 %collective-permute-start.36 = (bf16[160,128]{1,0:T(8,128)(2,1)S(1)}, bf16[160,128]{1,0:T(8,128)(2,1)}, u32[]{:S(2)}, u32[]{:S(2)}) collective-permute-start(bf16[160,128]{1,0:T(8,128)(2,1)S(1)} %shard_map.93.own_r), channel_id=1, source_target_pairs={{0,2},{2,4},{4,6},{6,8},{8,10},{10,12},{12,14},{14,0},{1,3},{3,5},... | collective-permute-start | bytes 122888 | tf_op jit(solution)/shard_map/ppermute | solution.py:220
  107.9 11.9 %collective-permute-start.37 = (bf16[160,128]{1,0:T(8,128)(2,1)S(1)}, bf16[160,128]{1,0:T(8,128)(2,1)}, u32[]{:S(2)}, u32[]{:S(2)}) collective-permute-start(bf16[160,128]{1,0:T(8,128)(2,1)S(1)} %shard_map.93.own_r), channel_id=1, source_target_pairs={{0,4},{2,6},{4,8},{6,10},{8,12},{10,14},{12,0},{14,2},{1,5},{3,7},... | collective-permute-start | bytes 122888 | tf_op jit(solution)/shard_map/ppermute | solution.py:220
  108.7 14.6 %collective-permute-start.38 = (bf16[160,128]{1,0:T(8,128)(2,1)S(1)}, bf16[160,128]{1,0:T(8,128)(2,1)}, u32[]{:S(2)}, u32[]{:S(2)}) collective-permute-start(bf16[160,128]{1,0:T(8,128)(2,1)S(1)} %shard_map.93.own_r), channel_id=1, source_target_pairs={{0,6},{2,8},{4,10},{6,12},{8,14},{10,0},{12,2},{14,4},{1,7},{3,9},... | collective-permute-start | bytes 122888 | tf_op jit(solution)/shard_map/ppermute | solution.py:220
  116.0 0.6 copy-start.19
  116.6 0.6 copy-start.20
  117.2 1.4 copy-start.23
  117.2 7.0 %collective-permute-start.14 = (bf16[160,128]{1,0:T(8,128)(2,1)}, bf16[160,128]{1,0:T(8,128)(2,1)}, u32[]{:S(2)}, u32[]{:S(2)}) collective-permute-start(bf16[160,128]{1,0:T(8,128)(2,1)} %get-tuple-element.101), channel_id=1, source_target_pairs={{0,2},{2,4},{4,6},{6,8},{8,10},{10,12},{12,14},{14,0},{1,3},{3,5},... | collective-permute-start | bytes 122888 | tf_op jit(solution)/shard_map/ppermute | solution.py:220
  117.9 0.7 copy-start.22
  118.6 7.7 %collective-permute-start.15 = (bf16[160,128]{1,0:T(8,128)(2,1)}, bf16[160,128]{1,0:T(8,128)(2,1)}, u32[]{:S(2)}, u32[]{:S(2)}) collective-permute-start(bf16[160,128]{1,0:T(8,128)(2,1)} %get-tuple-element.102), channel_id=1, source_target_pairs={{0,4},{2,6},{4,8},{6,10},{8,12},{10,14},{12,0},{14,2},{1,5},{3,7},... | collective-permute-start | bytes 122888 | tf_op jit(solution)/shard_map/ppermute | solution.py:220
  118.8 10.0 %collective-permute-start.16 = (bf16[160,128]{1,0:T(8,128)(2,1)}, bf16[160,128]{1,0:T(8,128)(2,1)S(1)}, u32[]{:S(2)}, u32[]{:S(2)}) collective-permute-start(bf16[160,128]{1,0:T(8,128)(2,1)} %copy-done.20), channel_id=1, source_target_pairs={{0,6},{2,8},{4,10},{6,12},{8,14},{10,0},{12,2},{14,4},{1,7},{3,9},... | collective-permute-start | bytes 122888 | tf_op jit(solution)/shard_map/ppermute | solution.py:220
  119.8 11.9 %collective-permute-start.17 = (bf16[160,128]{1,0:T(8,128)(2,1)}, bf16[160,128]{1,0:T(8,128)(2,1)S(1)}, u32[]{:S(2)}, u32[]{:S(2)}) collective-permute-start(bf16[160,128]{1,0:T(8,128)(2,1)} %copy-done.19), channel_id=1, source_target_pairs={{0,8},{2,10},{4,12},{6,14},{8,0},{10,2},{12,4},{14,6},{1,9},{3,11}... | collective-permute-start | bytes 122888 | tf_op jit(solution)/shard_map/ppermute | solution.py:220
  123.3 8.6 %collective-permute-start.18 = (bf16[160,128]{1,0:T(8,128)(2,1)}, bf16[160,128]{1,0:T(8,128)(2,1)S(1)}, u32[]{:S(2)}, u32[]{:S(2)}) collective-permute-start(bf16[160,128]{1,0:T(8,128)(2,1)} %copy-done.18), channel_id=1, source_target_pairs={{0,10},{2,12},{4,14},{6,0},{8,2},{10,4},{12,6},{14,8},{1,11},{3,13... | collective-permute-start | bytes 122888 | tf_op jit(solution)/shard_map/ppermute | solution.py:220
  124.2 9.0 %collective-permute-start.19 = (bf16[160,128]{1,0:T(8,128)(2,1)}, bf16[160,128]{1,0:T(8,128)(2,1)S(1)}, u32[]{:S(2)}, u32[]{:S(2)}) collective-permute-start(bf16[160,128]{1,0:T(8,128)(2,1)} %copy-done.17), channel_id=1, source_target_pairs={{0,12},{2,14},{4,0},{6,2},{8,4},{10,6},{12,8},{14,10},{1,13},{3,15... | collective-permute-start | bytes 122888 | tf_op jit(solution)/shard_map/ppermute | solution.py:220
  126.4 8.3 %collective-permute-start.20 = (bf16[160,128]{1,0:T(8,128)(2,1)}, bf16[160,128]{1,0:T(8,128)(2,1)S(1)}, u32[]{:S(2)}, u32[]{:S(2)}) collective-permute-start(bf16[160,128]{1,0:T(8,128)(2,1)} %copy-done.16), channel_id=1, source_target_pairs={{0,14},{2,0},{4,2},{6,4},{8,6},{10,8},{12,10},{14,12},{1,15},{3,1}... | collective-permute-start | bytes 122888 | tf_op jit(solution)/shard_map/ppermute | solution.py:220
  128.8 10.4 %collective-permute-start.39 = (bf16[160,128]{1,0:T(8,128)(2,1)S(1)}, bf16[160,128]{1,0:T(8,128)(2,1)S(1)}, u32[]{:S(2)}, u32[]{:S(2)}) collective-permute-start(bf16[160,128]{1,0:T(8,128)(2,1)S(1)} %shard_map.93.own_r), channel_id=1, source_target_pairs={{0,8},{2,10},{4,12},{6,14},{8,0},{10,2},{12,4},{14,6},{1,9},{3,11}... | collective-permute-start | bytes 122888 | tf_op jit(solution)/shard_map/ppermute | solution.py:220
  131.7 7.5 %collective-permute-start.40 = (bf16[160,128]{1,0:T(8,128)(2,1)S(1)}, bf16[160,128]{1,0:T(8,128)(2,1)S(1)}, u32[]{:S(2)}, u32[]{:S(2)}) collective-permute-start(bf16[160,128]{1,0:T(8,128)(2,1)S(1)} %shard_map.93.own_r), channel_id=1, source_target_pairs={{0,10},{2,12},{4,14},{6,0},{8,2},{10,4},{12,6},{14,8},{1,11},{3,13... | collective-permute-start | bytes 122888 | tf_op jit(solution)/shard_map/ppermute | solution.py:220
  131.9 10.0 %collective-permute-start.41 = (bf16[160,128]{1,0:T(8,128)(2,1)S(1)}, bf16[160,128]{1,0:T(8,128)(2,1)S(1)}, u32[]{:S(2)}, u32[]{:S(2)}) collective-permute-start(bf16[160,128]{1,0:T(8,128)(2,1)S(1)} %shard_map.93.own_r), channel_id=1, source_target_pairs={{0,12},{2,14},{4,0},{6,2},{8,4},{10,6},{12,8},{14,10},{1,13},{3,15... | collective-permute-start | bytes 122888 | tf_op jit(solution)/shard_map/ppermute | solution.py:220
  133.2 10.2 %collective-permute-start.42 = (bf16[160,128]{1,0:T(8,128)(2,1)S(1)}, bf16[160,128]{1,0:T(8,128)(2,1)S(1)}, u32[]{:S(2)}, u32[]{:S(2)}) collective-permute-start(bf16[160,128]{1,0:T(8,128)(2,1)S(1)} %shard_map.93.own_r), channel_id=1, source_target_pairs={{0,14},{2,0},{4,2},{6,4},{8,6},{10,8},{12,10},{14,12},{1,15},{3,1}... | collective-permute-start | bytes 122888 | tf_op jit(solution)/shard_map/ppermute | solution.py:220
  134.7 12.6 %collective-permute-start.11 = (bf16[1024,256]{1,0:T(8,128)(2,1)}, bf16[1024,256]{1,0:T(8,128)(2,1)S(1)}, u32[]{:S(2)}, u32[]{:S(2)}) collective-permute-start(bf16[1024,256]{1,0:T(8,128)(2,1)} %copy-done.15), channel_id=1, source_target_pairs={{2,0},{4,2},{6,4},{8,6},{10,8},{12,10},{14,12},{3,1},{5,3},{7,5},{... | collective-permute-start | bytes 1572872 | tf_op jit(solution)/shard_map/ppermute | solution.py:213
  139.1 11.4 %collective-permute-start.10 = (bf16[1024,128]{1,0:T(8,128)(2,1)S(1)}, bf16[1024,128]{1,0:T(8,128)(2,1)S(1)}, u32[]{:S(2)}, u32[]{:S(2)}) collective-permute-start(bf16[1024,128]{1,0:T(8,128)(2,1)S(1)} %get-tuple-element.85), channel_id=1, source_target_pairs={{0,1},{1,0},{2,3},{3,2},{4,5},{5,4},{6,7},{7,6},{8,9},{9,8},{10,11... | collective-permute-start | bytes 786440 | tf_op jit(solution)/shard_map/ppermute | solution.py:224
  139.2 13.4 %collective-permute-start.21 = (bf16[160,128]{1,0:T(8,128)(2,1)S(1)}, bf16[160,128]{1,0:T(8,128)(2,1)S(1)}, u32[]{:S(2)}, u32[]{:S(2)}) collective-permute-start(bf16[160,128]{1,0:T(8,128)(2,1)S(1)} %shard_map.89.own_r), channel_id=1, source_target_pairs={{0,2},{2,4},{4,6},{6,8},{8,10},{10,12},{12,14},{14,0},{1,3},{3,5},... | collective-permute-start | bytes 122888 | tf_op jit(solution)/shard_map/ppermute | solution.py:220
  141.9 12.5 %collective-permute-start.22 = (bf16[160,128]{1,0:T(8,128)(2,1)S(1)}, bf16[160,128]{1,0:T(8,128)(2,1)S(1)}, u32[]{:S(2)}, u32[]{:S(2)}) collective-permute-start(bf16[160,128]{1,0:T(8,128)(2,1)S(1)} %shard_map.89.own_r), channel_id=1, source_target_pairs={{0,4},{2,6},{4,8},{6,10},{8,12},{10,14},{12,0},{14,2},{1,5},{3,7},... | collective-permute-start | bytes 122888 | tf_op jit(solution)/shard_map/ppermute | solution.py:220
  143.4 11.9 %collective-permute-start.23 = (bf16[160,128]{1,0:T(8,128)(2,1)S(1)}, bf16[160,128]{1,0:T(8,128)(2,1)S(1)}, u32[]{:S(2)}, u32[]{:S(2)}) collective-permute-start(bf16[160,128]{1,0:T(8,128)(2,1)S(1)} %shard_map.89.own_r), channel_id=1, source_target_pairs={{0,6},{2,8},{4,10},{6,12},{8,14},{10,0},{12,2},{14,4},{1,7},{3,9},... | collective-permute-start | bytes 122888 | tf_op jit(solution)/shard_map/ppermute | solution.py:220
  147.3 8.1 %collective-permute-start.24 = (bf16[160,128]{1,0:T(8,128)(2,1)S(1)}, bf16[160,128]{1,0:T(8,128)(2,1)S(1)}, u32[]{:S(2)}, u32[]{:S(2)}) collective-permute-start(bf16[160,128]{1,0:T(8,128)(2,1)S(1)} %shard_map.89.own_r), channel_id=1, source_target_pairs={{0,8},{2,10},{4,12},{6,14},{8,0},{10,2},{12,4},{14,6},{1,9},{3,11}... | collective-permute-start | bytes 122888 | tf_op jit(solution)/shard_map/ppermute | solution.py:220
  150.5 5.0 %collective-permute-start.25 = (bf16[160,128]{1,0:T(8,128)(2,1)S(1)}, bf16[160,128]{1,0:T(8,128)(2,1)S(1)}, u32[]{:S(2)}, u32[]{:S(2)}) collective-permute-start(bf16[160,128]{1,0:T(8,128)(2,1)S(1)} %shard_map.89.own_r), channel_id=1, source_target_pairs={{0,10},{2,12},{4,14},{6,0},{8,2},{10,4},{12,6},{14,8},{1,11},{3,13... | collective-permute-start | bytes 122888 | tf_op jit(solution)/shard_map/ppermute | solution.py:220
  152.6 4.0 %collective-permute-start.26 = (bf16[160,128]{1,0:T(8,128)(2,1)S(1)}, bf16[160,128]{1,0:T(8,128)(2,1)S(1)}, u32[]{:S(2)}, u32[]{:S(2)}) collective-permute-start(bf16[160,128]{1,0:T(8,128)(2,1)S(1)} %shard_map.89.own_r), channel_id=1, source_target_pairs={{0,12},{2,14},{4,0},{6,2},{8,4},{10,6},{12,8},{14,10},{1,13},{3,15... | collective-permute-start | bytes 122888 | tf_op jit(solution)/shard_map/ppermute | solution.py:220
  154.4 4.0 %collective-permute-start.27 = (bf16[160,128]{1,0:T(8,128)(2,1)S(1)}, bf16[160,128]{1,0:T(8,128)(2,1)S(1)}, u32[]{:S(2)}, u32[]{:S(2)}) collective-permute-start(bf16[160,128]{1,0:T(8,128)(2,1)S(1)} %shard_map.89.own_r), channel_id=1, source_target_pairs={{0,14},{2,0},{4,2},{6,4},{8,6},{10,8},{12,10},{14,12},{1,15},{3,1}... | collective-permute-start | bytes 122888 | tf_op jit(solution)/shard_map/ppermute | solution.py:220
  155.3 6.3 %collective-permute-start.12 = (bf16[1024,128]{1,0:T(8,128)(2,1)S(1)}, bf16[1024,128]{1,0:T(8,128)(2,1)S(1)}, u32[]{:S(2)}, u32[]{:S(2)}) collective-permute-start(bf16[1024,128]{1,0:T(8,128)(2,1)S(1)} %get-tuple-element.89), channel_id=1, source_target_pairs={{0,1},{1,0},{2,3},{3,2},{4,5},{5,4},{6,7},{7,6},{8,9},{9,8},{10,11... | collective-permute-start | bytes 786440 | tf_op jit(solution)/shard_map/ppermute | solution.py:224
  (3 other events, 1.8 us)

commit v2 on v0

v2 whole, which is shorter than its diff:
```python
import functools
import math

import jax
import jax.numpy as jnp
from jax import lax
from jax.experimental import pallas as pl
from jax.experimental.pallas import tpu as pltpu
from jax.sharding import PartitionSpec as P

BF = jnp.bfloat16
F32 = jnp.float32
VMEM_LIMIT = 24 * 1024 * 1024
CHUNK = 256


def mm(a, b):
    return jnp.dot(a, b, preferred_element_type=F32)


def mm_t(a, b):
    return lax.dot_general(a, b, (((1,), (1,)), ((), ())), preferred_element_type=F32)


def mm_rows(a, b):
    return lax.dot_general(a, b, (((0,), (0,)), ((), ())), preferred_element_type=F32)


def ordered(core, own, other):
    first = core == 0
    return jnp.concatenate(
        [jnp.where(first, own, other), jnp.where(first, other, own)], axis=1
    )


def halves(core, values):
    width = values.shape[1] // 2
    low, high = values[:, :width], values[:, width:]
    first = core == 0
    return jnp.where(first, low, high), jnp.where(first, high, low)


def chunks(ref):
    return [pl.ds(r, CHUNK) for r in range(0, ref.shape[0], CHUNK)]


def run(body, ids, ins, outs, scratch=(), after=()):
    count = len(ins)

    def kernel(ids_ref, *refs):
        body(ids_ref, *refs[:count], *refs[count + len(after) :])

    return pl.pallas_call(
        kernel,
        in_specs=[pl.BlockSpec(memory_space=pltpu.SMEM)]
        + [pl.BlockSpec(memory_space=pltpu.VMEM)] * count
        + [pl.BlockSpec(memory_space=pl.ANY)] * len(after),
        out_specs=[pl.BlockSpec(memory_space=pltpu.VMEM)] * len(outs),
        out_shape=[jax.ShapeDtypeStruct(shape, kind) for shape, kind in outs],
        scratch_shapes=list(scratch),
        compiler_params=pltpu.CompilerParams(vmem_limit_bytes=VMEM_LIMIT),
        cost_estimate=pl.CostEstimate(flops=1, bytes_accessed=1, transcendentals=0),
    )(ids, *ins, *after)


def gated(x, delayed, taps, layer):
    width = x.shape[1]
    preact = mm(x, taps[layer, 0]) + mm(delayed, taps[layer, 1])
    filt = jnp.tanh(preact[:, :width])
    gate = 0.5 * jnp.tanh(0.5 * preact[:, width:]) + 0.5
    hidden = (filt * gate).astype(BF)
    return hidden, gate * (1.0 - filt * filt), filt * gate * (1.0 - gate)


def join_body(ids, own, other, a_o, b_o):
    core = ids[0]
    count = a_o.shape[0]
    for half, out in ((0, a_o), (1, b_o)):
        for rows in chunks(out):
            place = pl.ds(pl.multiple_of((half * 2 + core) * count + rows.start, CHUNK), CHUNK)
            out[rows, :] = ordered(core, own[place, :], other[place, :])


def cot_body(ids, own, other, wo, a_o, b_o, ha_o, hb_o):
    join_body(ids, own, other, a_o, b_o)
    for g_r, h_r in ((a_o, ha_o), (b_o, hb_o)):
        for rows in chunks(g_r):
            h_r[rows, :] = mm_t(g_r[rows, :], wo[1])


def first_body(ids, x_r, d_r, taps, wo, x1_o, hid_o, slope_o):
    width = x_r.shape[1]
    for rows in chunks(x_r):
        x = x_r[rows, :]
        hidden, sf, sg = gated(x, d_r[rows, :], taps, 0)
        hid_o[rows, :] = hidden
        slope_o[rows, :width] = sf
        slope_o[rows, width:] = sg
        x1_o[rows, :] = (x.astype(F32) + mm(hidden, wo[0])).astype(BF)


def second_body(ids, x_r, d_r, hg_r, taps, pre_o, past_o, hid_o):
    for rows in chunks(x_r):
        hidden, sf, sg = gated(x_r[rows, :], d_r[rows, :], taps, 1)
        hid_o[rows, :] = hidden
        hg = hg_r[rows, :]
        pre = jnp.concatenate([(hg * sf).astype(BF), (hg * sg).astype(BF)], axis=1)
        pre_o[rows, :] = pre
        past_o[rows, :] = mm_t(pre, taps[1, 1]).astype(BF)


def rest_body(ids, x_r, hid_r, g_r, pre_r, taps, wo, keep_o, send_o, local_o):
    for rows in chunks(x_r):
        out = (x_r[rows, :].astype(F32) + mm(hid_r[rows, :], wo[1])).astype(BF)
        keep, send = halves(ids[0], out)
        keep_o[rows, :] = keep
        send_o[rows, :] = send
        local_o[rows, :] = g_r[rows, :].astype(F32) + mm_t(pre_r[rows, :], taps[1, 0])


def third_body(ids, local_r, arrived_r, slope_r, taps, wo, g_o, pre_o, past_o, now_o):
    width = g_o.shape[1]
    for rows in chunks(local_r):
        g = (local_r[rows, :] + arrived_r[rows, :].astype(F32)).astype(BF)
        g_o[rows, :] = g
        hg = mm_t(g, wo[0])
        pre = jnp.concatenate(
            [
                (hg * slope_r[rows, :width]).astype(BF),
                (hg * slope_r[rows, width:]).astype(BF),
            ],
            axis=1,
        )
        pre_o[rows, :] = pre
        past_o[rows, :] = mm_t(pre, taps[0, 1]).astype(past_o.dtype)
        now_o[rows, :] = g.astype(F32) + mm_t(pre, taps[0, 0])


def last_body(ids, now_r, past_r, keep_o, send_o):
    for rows in chunks(now_r):
        keep, send = halves(
            ids[0], (now_r[rows, :] + past_r[rows, :].astype(F32)).astype(BF)
        )
        keep_o[rows, :] = keep
        send_o[rows, :] = send


def assemble_body(ids, keep_a, got_a, keep_b, got_b, out):
    core = ids[0]
    count = keep_a.shape[0]
    for half, keep, got in ((0, keep_a, got_a), (1, keep_b, got_b)):
        own = pl.multiple_of((half * 2 + core) * count, count)
        other = pl.multiple_of((half * 2 + 1 - core) * count, count)
        out[pl.ds(own, count), :] = keep[...]
        out[pl.ds(other, count), :] = got[...]


def weight_body(scale, ids, xa, da, pa, ha, ga, xb, db, pb, hb, gb, keep_o, send_o):
    channels = ha.shape[1]
    pairs = (
        (xa, pa, xb, pb),
        (da, pa, db, pb),
        (ha, ga, hb, gb),
    )
    position = 0
    for la, ra, lb, rb in pairs:
        both = (mm_rows(la[...], ra[...]) + mm_rows(lb[...], rb[...])) * scale
        for k in range(both.shape[1] // channels):
            keep, send = halves(ids[0], both[:, k * channels : (k + 1) * channels])
            keep_o[pl.ds(position * channels, channels), :] = keep
            send_o[pl.ds(position * channels, channels), :] = send.astype(BF)
            position += 1


def gather_sums(channels, keeps, gots, total):
    for layer, (keep, got) in enumerate(zip(keeps, gots)):
        for position in range(5):
            rows = pl.ds(position * channels, channels)
            value = keep[rows, :] + got[rows, :].astype(F32)
            if position < 4:
                tap, k = divmod(position, 2)
                base = (layer * 2 + tap) * 2 * channels + k
                total[pl.ds(base, channels, stride=2), :] = value
            else:
                total[pl.ds((8 + layer) * channels, channels), :] = value


def split_body(parts, ids, keep0, got0, keep1, got1, own_o, *rest):
    outs, total = rest[:-1], rest[-1]
    me = ids[1]
    gather_sums(total.shape[0] // 10, (keep0, keep1), (got0, got1), total)
    rows = own_o.shape[0]
    own_o[...] = total[pl.ds(pl.multiple_of(me * rows, rows), rows), :]
    for d in range(1, parts):
        place = lax.rem(me + d, parts) * rows
        outs[d - 1][...] = total[pl.ds(pl.multiple_of(place, rows), rows), :].astype(BF)


def sum_body(ids, own_r, *rest):
    total = own_r[...]
    for r in rest[:-1]:
        total = total + r[...].astype(F32)
    rest[-1][...] = total.astype(BF)


def place_body(parts, ids, own_r, *rest):
    me = ids[1]
    conv_o, out_o, total = rest[-3:]
    rows = own_r.shape[0]
    total[pl.ds(pl.multiple_of(me * rows, rows), rows), :] = own_r[...].astype(F32)
    for d in range(1, parts):
        place = lax.rem(me + parts - d, parts) * rows
        total[pl.ds(pl.multiple_of(place, rows), rows), :] = rest[d - 1][...].astype(F32)
    count = conv_o.shape[0]
    conv_o[...] = total[:count, :]
    out_o[...] = total[count:, :]


def plain_body(ids, keep0, got0, keep1, got1, total):
    gather_sums(total.shape[0] // 10, (keep0, keep1), (got0, got1), total)


def moved_by(values, distance):
    devices = range(lax.axis_size("tm"))
    return lax.ppermute(
        values, "tm", [(i, i + distance) for i in devices if i + distance in devices]
    )


def turned(values, distance):
    size = lax.axis_size("tm")
    return lax.ppermute(values, "tm", [(i, (i + distance) % size) for i in range(size)])


def swapped(values):
    return lax.ppermute(values, "chan", [(0, 1), (1, 0)])


def reduced(ids, channels, sums, after):
    parts = lax.axis_size("tm")
    cols = sums[0].shape[1]
    rows = 10 * channels
    if parts != 8:
        (total,) = run(plain_body, ids, sums, [((rows, cols), F32)])
        total = lax.psum(total, "tm")
        return total[: 8 * channels], total[8 * channels :]
    piece = rows // parts
    split = run(
        functools.partial(split_body, parts),
        ids,
        sums,
        [((piece, cols), F32)] + [((piece, cols), BF)] * (parts - 1),
        [pltpu.VMEM((rows, cols), F32)],
        after=after,
    )
    got = [turned(split[d], d) for d in range(1, parts)]
    (total,) = run(sum_body, ids, [split[0]] + got, [((piece, cols), BF)])
    back = [turned(total, d) for d in range(1, parts)]
    return run(
        functools.partial(place_body, parts),
        ids,
        [total] + back,
        [((8 * channels, cols), F32), ((2 * channels, cols), F32)],
        [pltpu.VMEM((rows, cols), F32)],
    )


def on_device(signal, cotangent, conv_weight, out_weight):
    rows, half_width = signal.shape
    channels = conv_weight.shape[2]
    quarter = rows // 4
    wide = 2 * channels
    scale = 1.0 / math.sqrt(rows * lax.axis_size("tm"))
    ids = jnp.stack([lax.axis_index("chan"), lax.axis_index("tm")]).astype(jnp.int32)
    taps = conv_weight.reshape(2, 2, channels, wide)
    wo = out_weight

    narrow, broad = (quarter, channels), (quarter, wide)
    half = (quarter, half_width)

    x_a, x_b = run(join_body, ids, [signal, swapped(signal)], [(narrow, BF)] * 2)
    x_h = moved_by(x_b, 1)

    def first(x, delayed, after=()):
        return run(
            first_body, ids, [x, delayed, taps, wo], [(narrow, BF)] * 2 + [(broad, F32)], after=after
        )

    x1_b, hid0_b, slope_b = first(x_b, x_a)
    x1_b_past = moved_by(x1_b, 2)
    cot_a, cot_b, hg_a, hg_b = run(
        cot_body,
        ids,
        [cotangent, swapped(cotangent), wo],
        [(narrow, BF)] * 2 + [(narrow, F32)] * 2,
        after=[x1_b],
    )
    x1_a, hid0_a, slope_a = first(x_a, x_h, after=[cot_a])
    x1_a_past = moved_by(x1_a, 2)

    def second(x1, past, hg, after=()):
        return run(
            second_body,
            ids,
            [x1, past, hg, taps],
            [(broad, BF)] + [(narrow, BF)] * 2,
            after=after,
        )

    def rest(x1, hid1, cot, pre1, after=()):
        return run(
            rest_body,
            ids,
            [x1, hid1, cot, pre1, taps, wo],
            [(half, BF)] * 2 + [(narrow, F32)],
            after=after,
        )

    pre1_b, to_past_b, hid1_b = second(x1_b, x1_b_past, hg_b)
    from_next_b = moved_by(to_past_b, -2)
    out_keep_b, out_send_b, local_b = rest(x1_b, hid1_b, cot_b, pre1_b)
    pre1_a, to_past_a, hid1_a = second(x1_a, x1_a_past, hg_a, after=[local_b])
    from_next_a = moved_by(to_past_a, -2)
    out_keep_a, out_send_a, local_a = rest(x1_a, hid1_a, cot_a, pre1_a)

    def weights(arrays, after=()):
        shape = (5 * channels, half_width)
        return run(
            functools.partial(weight_body, scale),
            ids,
            arrays,
            [(shape, F32), (shape, BF)],
            after=after,
        )

    keep1, send1 = weights(
        [x1_a, x1_a_past, pre1_a, hid1_a, cot_a, x1_b, x1_b_past, pre1_b, hid1_b, cot_b],
        after=[local_a],
    )
    got1 = swapped(send1)
    (output,) = run(
        assemble_body,
        ids,
        [out_keep_a, swapped(out_send_a), out_keep_b, swapped(out_send_b)],
        [((rows, half_width), BF)],
        after=[keep1],
    )

    def third(local, arrived, slope, kind, after=()):
        return run(
            third_body,
            ids,
            [local, arrived, slope, taps, wo],
            [(narrow, BF), (broad, BF), (narrow, kind), (narrow, F32)],
            after=after,
        )

    g1_b, pre0_b, past_b, now_b = third(local_b, from_next_b, slope_b, F32, after=[output])
    g1_a, pre0_a, past_a, now_a = third(local_a, from_next_a, slope_a, BF, after=[g1_b])
    ahead_b = moved_by(past_a, -1)
    keep0, send0 = weights(
        [x_a, x_h, pre0_a, hid0_a, g1_a, x_b, x_a, pre0_b, hid0_b, g1_b]
    )
    got0 = swapped(send0)

    def last(now, past, after=()):
        return run(last_body, ids, [now, past], [(half, BF)] * 2, after=after)

    in_keep_a, in_send_a = last(now_a, past_b, after=[keep0])
    conv_grad, out_grad = reduced(ids, channels, [keep0, got0, keep1, got1], [in_keep_a])
    in_keep_b, in_send_b = last(now_b, ahead_b)
    (in_grad,) = run(
        assemble_body,
        ids,
        [in_keep_a, swapped(in_send_a), in_keep_b, swapped(in_send_b)],
        [((rows, half_width), BF)],
    )
    return (
        output,
        in_grad,
        conv_grad.reshape(2, 2, channels, 2, half_width),
        out_grad.reshape(2, channels, half_width),
    )


def solution(mesh):
    placed = (P(("groups", "tm"), "chan"), P(("groups", "tm"), "chan"), P(), P())
    return jax.shard_map(
        on_device,
        mesh=mesh,
        in_specs=placed,
        out_specs=(
            P(("groups", "tm"), "chan"),
            P(("groups", "tm"), "chan"),
            P("groups", None, None, None, "chan"),
            P("groups", None, "chan"),
        ),
        check_vma=False,
    )
```

time: 370 us -> 123 us (0.33)
  waiting for transfers between devices: 267 us -> 33.5 us
  starting transfers between devices: 11.8 us -> 55.6 us
  matrix products: 43.3 us -> 0 us
  Pallas kernels: 0 us -> 27.9 us
  other arithmetic: 16.6 us -> 0.07 us
  between operations: 14.1 us -> 0.93 us
  local copies, waits for them, and re-layouts: 16.3 us -> 4.2 us
    ppermute x4 -> x28, waiting for transfers between devices: 131 us -> 33.5 us  [the longest x14 16.2 us: turned(): lax.ppermute(values, 'tm', [(i, (i + distance) % size) for i in range(siz...]
    psum x1 -> x0, waiting for transfers between devices: 63.3 us -> none  [sum_layer(): return lax.psum((conv_term, out_term), 'tm')]
    all_gather x6 -> x0, waiting for transfers between devices: 54.1 us -> none  [the longest x2 25.5 us: on_device(): full_now = lax.all_gather(present_signal, 'chan', axis=1, tiled=True)]
    ppermute x4 -> x28, starting transfers between devices: 11.3 us -> 55.6 us  [the longest x14 34.6 us: turned(): lax.ppermute(values, 'tm', [(i, (i + distance) % size) for i in range(siz...]
    dot_general x18 -> x0, matrix products: 43.3 us -> none  [the longest x6 16.8 us: contract_last(): lax.dot_general(former, latter, (((1,), (1,)), ((), ())), preferred_eleme...]
    pallas_call x0 -> x19, Pallas kernels: none -> 27.9 us  [run(): pl.pallas_call(kernel, in_specs=[pl.BlockSpec(memory_space=pltpu.SMEM)] +...]
    reduce_scatter x2 -> x0, waiting for transfers between devices: 17.9 us -> none  [on_device(): lax.psum_scatter(partial_sum, 'chan', scatter_dimension=1, tiled=True)]
    convert_element_type x6 -> x0, other arithmetic: 11.8 us -> none  [the longest x2 5.88 us: gated_layer(): hidden = (filter_act * gate_act).astype(jnp.bfloat16)]
  transfers between devices with their start and end apart: 13 -> 28, of which waited for: 12 -> 12; matrix products, arithmetic and copies ran while one was open for 12% -> 1% of each run, Pallas kernels for 0% -> 20%
where the time goes in v2:
time: 123 us; the launch traced here: 122 us
  starting transfers between devices  55.6 us (45%)
  waiting for transfers between devices  33.5 us (27%)
  Pallas kernels  27.9 us (23%)
  local copies, waits for them, and re-layouts  4.2 us (3%)
    ppermute x14, starting transfers between devices, turned(): lax.ppermute(values, 'tm', [(i, (i + distance) % size) for i in range(siz...  34.6 us
    pallas_call x19, Pallas kernels, run(): pl.pallas_call(kernel, in_specs=[pl.BlockSpec(memory_space=pltpu.SMEM)] +...  27.9 us
    ppermute x6, starting transfers between devices, moved_by(): lax.ppermute(values, 'tm', [(i, i + distance) for i in devices if i + dis...  18.5 us
    ppermute x14, waiting for transfers between devices, turned(): lax.ppermute(values, 'tm', [(i, (i + distance) % size) for i in range(siz...  16.2 us
    ppermute x6, waiting for transfers between devices, moved_by(): lax.ppermute(values, 'tm', [(i, i + distance) for i in devices if i + dis...  13.7 us
    ppermute x8, waiting for transfers between devices, swapped(): return lax.ppermute(values, 'chan', [(0, 1), (1, 0)])  3.62 us
  transfers between devices with their start and end apart: 28, of which 12 were waited for; matrix products, arithmetic and copies ran while one was open for 1% of the time, Pallas kernels for 20%

profile of v2, /device:TPU:0, one launch (start us, length us, event | category | flops | bytes accessed | tf_op | source)
XLA Modules:
  0.0 122.2 jit_solution(7255787377472041869)
XLA Ops:
  0.6 0.5 collective-permute-start
  1.1 0.1 collective-permute-start.2
  1.2 0.1 pad_add_fusion.ids_ref
  1.3 3.0 %collective-permute-done.refs_1_ = bf16[4096,128]{1,0:T(8,128)(2,1)S(1)} collective-permute-done((bf16[4096,128]{1,0:T(8,128)(2,1)}, bf16[4096,128]{1,0:T(8,128)(2,1)S(1)}, u32[]{:S(2)}, u32[]{:S(2)}) %collective-permute-start) | collective-permute-done | bytes 1048608 | tf_op jit(solution)/shard_map/ppermute | solution.py:236
  4.3 1.2 %copy-done.3 = bf16[4096,128]{1,0:T(8,128)(2,1)S(1)} copy-done((bf16[4096,128]{1,0:T(8,128)(2,1)S(1)}, bf16[4096,128]{1,0:T(8,128)(2,1)}, u32[]{:S(2)}) %copy-start.3) | copy-done | bytes 1048600
  5.6 0.7 shard_map.75
  6.2 4.8 %collective-permute-start.1 = (bf16[1024,256]{1,0:T(8,128)(2,1)S(1)}, bf16[1024,256]{1,0:T(8,128)(2,1)S(1)}, u32[]{:S(2)}, u32[]{:S(2)}) collective-permute-start(bf16[1024,256]{1,0:T(8,128)(2,1)S(1)} %get-tuple-element.55.refs_0_.refs_5_), channel_id=1, source_target_pairs={{0,2},{2,4},{4,6},{6,8},{8,10},{10,12},{12,14},{1,3},{3,5},{5,7},{... | collective-permute-start | bytes 1572872 | tf_op jit(solution)/shard_map/ppermute | solution.py:225
  11.1 1.7 %reshape.17.refs_2_.refs_3_.refs_4_ = bf16[2,2,256,512]{3,2,1,0:T(8,128)(2,1)S(1)} reshape(bf16[2,2,256,2,256]{4,3,2,1,0:T(2,128)(2,1)} %param.6) | data formatting | bytes 2097152 | tf_op jit(solution)/shard_map/reshape | solution.py:275
  12.8 0.0 copy-start.2
  12.8 1.9 %shard_map.76 = (bf16[1024,256]{1,0:T(8,128)(2,1)S(1)}, bf16[1024,256]{1,0:T(8,128)(2,1)S(1)}, f32[1024,512]{1,0:T(8,128)S(1)}) custom-call(s32[2]{0:T(128)S(1)} %pad_add_fusion.ids_ref, bf16[1024,256]{1,0:T(8,128)(2,1)S(1)} %get-tuple-element.55.refs_0_.refs_5_, bf16[1024,256]{1,0:T(8,128)(2,1)S(1)} %get-tuple-element.54.refs_1_.refs_0_.refs_6_, ...), custom_call_target="tpu_custom_call" | custom-call | flops 1 | bytes 1 | tf_op jit(solution)/shard_map/pallas_call | solution.py:53
  14.7 3.5 %collective-permute-start.4 = (bf16[1024,256]{1,0:T(8,128)(2,1)S(1)}, bf16[1024,256]{1,0:T(8,128)(2,1)S(1)}, u32[]{:S(2)}, u32[]{:S(2)}) collective-permute-start(bf16[1024,256]{1,0:T(8,128)(2,1)S(1)} %get-tuple-element.56.refs_3_.refs_0_.refs_5_), channel_id=1, source_target_pairs={{0,4},{2,6},{4,8},{6,10},{8,12},{10,14},{1,5},{3,7},{5,9},{7,11},{... | collective-permute-start | bytes 1572872 | tf_op jit(solution)/shard_map/ppermute | solution.py:225
  18.2 1.7 %shard_map.77 = (bf16[1024,256]{1,0:T(8,128)(2,1)S(1)}, bf16[1024,256]{1,0:T(8,128)(2,1)S(1)}, f32[1024,256]{1,0:T(8,128)S(1)}, f32[1024,256]{1,0:T(8,128)S(1)}) custom-call(s32[2]{0:T(128)S(1)} %pad_add_fusion.ids_ref, bf16[4096,128]{1,0:T(8,128)(2,1)S(1)} %copy-done.2, bf16[4096,128]{1,0:T(8,128)(2,1)} %collective-permute-done.2.refs_1_, ...), custom_call_target="tpu_custom_call" | custom-call | flops 1 | bytes 1 | tf_op jit(solution)/shard_map/pallas_call | solution.py:53
  20.0 2.5 %collective-permute-done.1.refs_1_ = bf16[1024,256]{1,0:T(8,128)(2,1)S(1)} collective-permute-done((bf16[1024,256]{1,0:T(8,128)(2,1)S(1)}, bf16[1024,256]{1,0:T(8,128)(2,1)S(1)}, u32[]{:S(2)}, u32[]{:S(2)}) %collective-permute-start.1) | collective-permute-done | bytes 524320 | tf_op jit(solution)/shard_map/ppermute | solution.py:225
  22.5 1.9 %shard_map.78 = (bf16[1024,256]{1,0:T(8,128)(2,1)S(1)}, bf16[1024,256]{1,0:T(8,128)(2,1)S(1)}, f32[1024,512]{1,0:T(8,128)S(1)}) custom-call(s32[2]{0:T(128)S(1)} %pad_add_fusion.ids_ref, bf16[1024,256]{1,0:T(8,128)(2,1)S(1)} %get-tuple-element.54.refs_1_.refs_0_.refs_6_, bf16[1024,256]{1,0:T(8,128)(2,1)S(1)} %collective-permute-done.1.refs_1_, ...), custom_call_target="tpu_custom_call" | custom-call | flops 1 | bytes 1 | tf_op jit(solution)/shard_map/pallas_call | solution.py:53
  24.4 6.2 %collective-permute-start.3 = (bf16[1024,256]{1,0:T(8,128)(2,1)S(1)}, bf16[1024,256]{1,0:T(8,128)(2,1)S(1)}, u32[]{:S(2)}, u32[]{:S(2)}) collective-permute-start(bf16[1024,256]{1,0:T(8,128)(2,1)S(1)} %get-tuple-element.58.refs_0_), channel_id=1, source_target_pairs={{0,4},{2,6},{4,8},{6,10},{8,12},{10,14},{1,5},{3,7},{5,9},{7,11},{... | collective-permute-start | bytes 1572872 | tf_op jit(solution)/shard_map/ppermute | solution.py:225
  30.6 1.9 %shard_map.79 = (bf16[1024,512]{1,0:T(8,128)(2,1)S(1)}, bf16[1024,256]{1,0:T(8,128)(2,1)S(1)}, bf16[1024,256]{1,0:T(8,128)(2,1)S(1)}) custom-call(s32[2]{0:T(128)S(1)} %pad_add_fusion.ids_ref, bf16[1024,256]{1,0:T(8,128)(2,1)S(1)} %get-tuple-element.56.refs_3_.refs_0_.refs_5_, bf16[1024,256]{1,0:T(8,128)(2,1)S(1)} %collective-permute-done.4.refs_1_.refs_6_, ...), custom_call_target="tpu_custom_call" | custom-call | flops 1 | bytes 1 | tf_op jit(solution)/shard_map/pallas_call | solution.py:53
  32.5 1.3 %collective-permute-start.8 = (bf16[1024,256]{1,0:T(8,128)(2,1)S(1)}, bf16[1024,256]{1,0:T(8,128)(2,1)S(1)}, u32[]{:S(2)}, u32[]{:S(2)}) collective-permute-start(bf16[1024,256]{1,0:T(8,128)(2,1)S(1)} %get-tuple-element.75), channel_id=1, source_target_pairs={{4,0},{6,2},{8,4},{10,6},{12,8},{14,10},{5,1},{7,3},{9,5},{11,7},{... | collective-permute-start | bytes 1572872 | tf_op jit(solution)/shard_map/ppermute | solution.py:225
  33.8 1.1 shard_map.80
  35.0 5.6 %collective-permute-done.3.refs_1_ = bf16[1024,256]{1,0:T(8,128)(2,1)S(1)} collective-permute-done((bf16[1024,256]{1,0:T(8,128)(2,1)S(1)}, bf16[1024,256]{1,0:T(8,128)(2,1)S(1)}, u32[]{:S(2)}, u32[]{:S(2)}) %collective-permute-start.3) | collective-permute-done | bytes 524320 | tf_op jit(solution)/shard_map/ppermute | solution.py:225
  40.6 1.9 %shard_map.81 = (bf16[1024,512]{1,0:T(8,128)(2,1)S(1)}, bf16[1024,256]{1,0:T(8,128)(2,1)S(1)}, bf16[1024,256]{1,0:T(8,128)(2,1)S(1)}) custom-call(s32[2]{0:T(128)S(1)} %pad_add_fusion.ids_ref, bf16[1024,256]{1,0:T(8,128)(2,1)S(1)} %get-tuple-element.58.refs_0_, bf16[1024,256]{1,0:T(8,128)(2,1)S(1)} %collective-permute-done.3.refs_1_, ...), custom_call_target="tpu_custom_call" | custom-call | flops 1 | bytes 1 | tf_op jit(solution)/shard_map/pallas_call | solution.py:53
  42.5 1.3 %collective-permute-start.7 = (bf16[1024,256]{1,0:T(8,128)(2,1)S(1)}, bf16[1024,256]{1,0:T(8,128)(2,1)S(1)}, u32[]{:S(2)}, u32[]{:S(2)}) collective-permute-start(bf16[1024,256]{1,0:T(8,128)(2,1)S(1)} %get-tuple-element.73), channel_id=1, source_target_pairs={{4,0},{6,2},{8,4},{10,6},{12,8},{14,10},{5,1},{7,3},{9,5},{11,7},{... | collective-permute-start | bytes 1572872 | tf_op jit(solution)/shard_map/ppermute | solution.py:225
  43.8 0.1 collective-permute-start.6
  43.9 1.1 shard_map.82
  45.1 0.6 collective-permute-start.5
  45.6 2.1 %shard_map.83 = (f32[1280,128]{1,0:T(8,128)S(1)}, bf16[1280,128]{1,0:T(8,128)(2,1)S(1)}) custom-call(s32[2]{0:T(128)S(1)} %pad_add_fusion.ids_ref, bf16[1024,256]{1,0:T(8,128)(2,1)S(1)} %get-tuple-element.58.refs_0_, bf16[1024,256]{1,0:T(8,128)(2,1)S(1)} %collective-permute-done.3.refs_1_, bf16[1024,512]{1,0:T(8,128)(2,1)S(1)} %get-tuple-element.66.refs_3_.refs_2_, ...), custom_call_target="tpu_custom_call" | custom-call | flops 1 | bytes 1 | tf_op jit(solution)/shard_map/pallas_call | solution.py:53
  47.8 1.6 %shard_map.84.refs_5_ = bf16[4096,128]{1,0:T(8,128)(2,1)} custom-call(s32[2]{0:T(128)S(1)} %pad_add_fusion.ids_ref, bf16[1024,128]{1,0:T(8,128)(2,1)S(1)} %get-tuple-element.67.refs_0_, bf16[1024,128]{1,0:T(8,128)(2,1)S(1)} %collective-permute-done.5.refs_1_, bf16[1024,128]{1,0:T(8,128)(2,1)S(1)} %get-tuple-element.69.refs_2_, ...), custom_call_target="tpu_custom_call" | custom-call | flops 1 | bytes 1 | tf_op jit(solution)/shard_map/pallas_call | solution.py:53
  49.4 1.2 %copy-done.1 = bf16[4096,128]{1,0:T(8,128)(2,1)S(1)} copy-done((bf16[4096,128]{1,0:T(8,128)(2,1)S(1)}, bf16[4096,128]{1,0:T(8,128)(2,1)}, u32[]{:S(2)}) %copy-start.1) | copy-done | bytes 1048600
  50.6 1.9 %shard_map.85 = (bf16[1024,256]{1,0:T(8,128)(2,1)S(1)}, bf16[1024,512]{1,0:T(8,128)(2,1)S(1)}, f32[1024,256]{1,0:T(8,128)S(1)}, f32[1024,256]{1,0:T(8,128)S(1)}) custom-call(s32[2]{0:T(128)S(1)} %pad_add_fusion.ids_ref, f32[1024,256]{1,0:T(8,128)S(1)} %get-tuple-element.64.refs_4_.refs_0_, bf16[1024,256]{1,0:T(8,128)(2,1)S(1)} %collective-permute-done.8.refs_1_, ...), custom_call_target="tpu_custom_call" | custom-call | flops 1 | bytes 1 | tf_op jit(solution)/shard_map/pallas_call | solution.py:53
  52.5 5.5 %collective-permute-done.7.refs_1_ = bf16[1024,256]{1,0:T(8,128)(2,1)S(1)} collective-permute-done((bf16[1024,256]{1,0:T(8,128)(2,1)S(1)}, bf16[1024,256]{1,0:T(8,128)(2,1)S(1)}, u32[]{:S(2)}, u32[]{:S(2)}) %collective-permute-start.7) | collective-permute-done | bytes 524320 | tf_op jit(solution)/shard_map/ppermute | solution.py:225
  58.0 1.9 %shard_map.86 = (bf16[1024,256]{1,0:T(8,128)(2,1)S(1)}, bf16[1024,512]{1,0:T(8,128)(2,1)S(1)}, bf16[1024,256]{1,0:T(8,128)(2,1)S(1)}, f32[1024,256]{1,0:T(8,128)S(1)}) custom-call(s32[2]{0:T(128)S(1)} %pad_add_fusion.ids_ref, f32[1024,256]{1,0:T(8,128)S(1)} %get-tuple-element.71.refs_10_.refs_0_, bf16[1024,256]{1,0:T(8,128)(2,1)S(1)} %collective-permute-done.7.refs_1_, ...), custom_call_target="tpu_custom_call" | custom-call | flops 1 | bytes 1 | tf_op jit(solution)/shard_map/pallas_call | solution.py:53
  59.9 1.5 %collective-permute-start.10 = (bf16[1024,256]{1,0:T(8,128)(2,1)S(1)}, bf16[1024,256]{1,0:T(8,128)(2,1)S(1)}, u32[]{:S(2)}, u32[]{:S(2)}) collective-permute-start(bf16[1024,256]{1,0:T(8,128)(2,1)S(1)} %get-tuple-element.89), channel_id=1, source_target_pairs={{2,0},{4,2},{6,4},{8,6},{10,8},{12,10},{14,12},{3,1},{5,3},{7,5},{... | collective-permute-start | bytes 1572872 | tf_op jit(solution)/shard_map/ppermute | solution.py:225
  61.4 0.1 collective-permute-start.13
  61.5 2.1 %shard_map.87 = (f32[1280,128]{1,0:T(8,128)S(1)}, bf16[1280,128]{1,0:T(8,128)(2,1)S(1)}) custom-call(s32[2]{0:T(128)S(1)} %pad_add_fusion.ids_ref, bf16[1024,256]{1,0:T(8,128)(2,1)S(1)} %get-tuple-element.54.refs_1_.refs_0_.refs_6_, bf16[1024,256]{1,0:T(8,128)(2,1)S(1)} %collective-permute-done.1.refs_1_, bf16[1024,512]{1,0:T(8,128)(2,1)S(1)} %get-tuple-element.80.refs_2_, ...), custom_call_target="tpu_custom_call" | custom-call | flops 1 | bytes 1 | tf_op jit(solution)/shard_map/pallas_call | solution.py:53
  63.6 0.6 collective-permute-start.12
  64.2 0.7 shard_map.88
  64.8 0.6 collective-permute-done.12.refs_1_
  65.4 0.7 shard_map.91
  66.1 6.9 %collective-permute-start.14 = (bf16[320,128]{1,0:T(8,128)(2,1)S(1)}, bf16[320,128]{1,0:T(8,128)(2,1)S(1)}, u32[]{:S(2)}, u32[]{:S(2)}) collective-permute-start(bf16[320,128]{1,0:T(8,128)(2,1)S(1)} %get-tuple-element.95), channel_id=1, source_target_pairs={{0,2},{2,4},{4,6},{6,8},{8,10},{10,12},{12,14},{14,0},{1,3},{3,5},... | collective-permute-start | bytes 245768 | tf_op jit(solution)/shard_map/ppermute | solution.py:232
  73.0 1.7 %collective-permute-start.15 = (bf16[320,128]{1,0:T(8,128)(2,1)S(1)}, bf16[320,128]{1,0:T(8,128)(2,1)S(1)}, u32[]{:S(2)}, u32[]{:S(2)}) collective-permute-start(bf16[320,128]{1,0:T(8,128)(2,1)S(1)} %get-tuple-element.96), channel_id=1, source_target_pairs={{0,4},{2,6},{4,8},{6,10},{8,12},{10,14},{12,0},{14,2},{1,5},{3,7},... | collective-permute-start | bytes 245768 | tf_op jit(solution)/shard_map/ppermute | solution.py:232
  74.8 3.9 %collective-permute-start.16 = (bf16[320,128]{1,0:T(8,128)(2,1)S(1)}, bf16[320,128]{1,0:T(8,128)(2,1)S(1)}, u32[]{:S(2)}, u32[]{:S(2)}) collective-permute-start(bf16[320,128]{1,0:T(8,128)(2,1)S(1)} %get-tuple-element.97), channel_id=1, source_target_pairs={{0,6},{2,8},{4,10},{6,12},{8,14},{10,0},{12,2},{14,4},{1,7},{3,9},... | collective-permute-start | bytes 245768 | tf_op jit(solution)/shard_map/ppermute | solution.py:232
  78.7 1.1 collective-permute-start.17
  79.8 1.0 collective-permute-done.14.refs_1_
  80.8 6.0 %collective-permute-start.18 = (bf16[320,128]{1,0:T(8,128)(2,1)S(1)}, bf16[320,128]{1,0:T(8,128)(2,1)S(1)}, u32[]{:S(2)}, u32[]{:S(2)}) collective-permute-start(bf16[320,128]{1,0:T(8,128)(2,1)S(1)} %get-tuple-element.99), channel_id=1, source_target_pairs={{0,10},{2,12},{4,14},{6,0},{8,2},{10,4},{12,6},{14,8},{1,11},{3,13... | collective-permute-start | bytes 245768 | tf_op jit(solution)/shard_map/ppermute | solution.py:232
  86.8 1.3 %collective-permute-start.19 = (bf16[320,128]{1,0:T(8,128)(2,1)S(1)}, bf16[320,128]{1,0:T(8,128)(2,1)S(1)}, u32[]{:S(2)}, u32[]{:S(2)}) collective-permute-start(bf16[320,128]{1,0:T(8,128)(2,1)S(1)} %get-tuple-element.100), channel_id=1, source_target_pairs={{0,12},{2,14},{4,0},{6,2},{8,4},{10,6},{12,8},{14,10},{1,13},{3,15... | collective-permute-start | bytes 245768 | tf_op jit(solution)/shard_map/ppermute | solution.py:232
  88.1 1.3 %collective-permute-start.20 = (bf16[320,128]{1,0:T(8,128)(2,1)S(1)}, bf16[320,128]{1,0:T(8,128)(2,1)S(1)}, u32[]{:S(2)}, u32[]{:S(2)}) collective-permute-start(bf16[320,128]{1,0:T(8,128)(2,1)S(1)} %get-tuple-element.101), channel_id=1, source_target_pairs={{0,14},{2,0},{4,2},{6,4},{8,6},{10,8},{12,10},{14,12},{1,15},{3,1}... | collective-permute-start | bytes 245768 | tf_op jit(solution)/shard_map/ppermute | solution.py:232
  89.5 0.7 shard_map.89
  90.2 0.1 collective-permute-start.9
  90.3 0.5 collective-permute-start.11
  90.8 1.8 %collective-permute-done.19.refs_6_ = bf16[320,128]{1,0:T(8,128)(2,1)S(1)} collective-permute-done((bf16[320,128]{1,0:T(8,128)(2,1)S(1)}, bf16[320,128]{1,0:T(8,128)(2,1)S(1)}, u32[]{:S(2)}, u32[]{:S(2)}) %collective-permute-start.19) | collective-permute-done | bytes 81952 | tf_op jit(solution)/shard_map/ppermute | solution.py:232
  92.6 0.0 collective-permute-done.20.refs_7_
  92.6 0.6 shard_map.92.refs_0_
  93.2 4.9 %collective-permute-start.27 = (bf16[320,128]{1,0:T(8,128)(2,1)S(1)}, bf16[320,128]{1,0:T(8,128)(2,1)S(1)}, u32[]{:S(2)}, u32[]{:S(2)}) collective-permute-start(bf16[320,128]{1,0:T(8,128)(2,1)S(1)} %shard_map.92.refs_0_), channel_id=1, source_target_pairs={{0,14},{2,0},{4,2},{6,4},{8,6},{10,8},{12,10},{14,12},{1,15},{3,1}... | collective-permute-start | bytes 245768 | tf_op jit(solution)/shard_map/ppermute | solution.py:232
  98.1 0.4 collective-permute-start.25
  98.6 2.5 %collective-permute-done.27.refs_7_ = bf16[320,128]{1,0:T(8,128)(2,1)S(1)} collective-permute-done((bf16[320,128]{1,0:T(8,128)(2,1)S(1)}, bf16[320,128]{1,0:T(8,128)(2,1)S(1)}, u32[]{:S(2)}, u32[]{:S(2)}) %collective-permute-start.27) | collective-permute-done | bytes 81952 | tf_op jit(solution)/shard_map/ppermute | solution.py:232
  101.1 0.9 collective-permute-start.24
  102.0 0.9 collective-permute-done.26.refs_6_
  102.8 4.0 %collective-permute-start.23 = (bf16[320,128]{1,0:T(8,128)(2,1)S(1)}, bf16[320,128]{1,0:T(8,128)(2,1)S(1)}, u32[]{:S(2)}, u32[]{:S(2)}) collective-permute-start(bf16[320,128]{1,0:T(8,128)(2,1)S(1)} %shard_map.92.refs_0_), channel_id=1, source_target_pairs={{0,6},{2,8},{4,10},{6,12},{8,14},{10,0},{12,2},{14,4},{1,7},{3,9},... | collective-permute-start | bytes 245768 | tf_op jit(solution)/shard_map/ppermute | solution.py:232
  106.9 1.5 %collective-permute-start.22 = (bf16[320,128]{1,0:T(8,128)(2,1)S(1)}, bf16[320,128]{1,0:T(8,128)(2,1)S(1)}, u32[]{:S(2)}, u32[]{:S(2)}) collective-permute-start(bf16[320,128]{1,0:T(8,128)(2,1)S(1)} %shard_map.92.refs_0_), channel_id=1, source_target_pairs={{0,4},{2,6},{4,8},{6,10},{8,12},{10,14},{12,0},{14,2},{1,5},{3,7},... | collective-permute-start | bytes 245768 | tf_op jit(solution)/shard_map/ppermute | solution.py:232
  108.3 3.4 %collective-permute-done.24.refs_4_ = bf16[320,128]{1,0:T(8,128)(2,1)S(1)} collective-permute-done((bf16[320,128]{1,0:T(8,128)(2,1)S(1)}, bf16[320,128]{1,0:T(8,128)(2,1)S(1)}, u32[]{:S(2)}, u32[]{:S(2)}) %collective-permute-start.24) | collective-permute-done | bytes 81952 | tf_op jit(solution)/shard_map/ppermute | solution.py:232
  111.7 0.6 collective-permute-start.21
  112.3 0.8 collective-permute-done.22.refs_2_
  113.1 5.7 %collective-permute-done.21.refs_1_ = bf16[320,128]{1,0:T(8,128)(2,1)S(1)} collective-permute-done((bf16[320,128]{1,0:T(8,128)(2,1)S(1)}, bf16[320,128]{1,0:T(8,128)(2,1)S(1)}, u32[]{:S(2)}, u32[]{:S(2)}) %collective-permute-start.21) | collective-permute-done | bytes 81952 | tf_op jit(solution)/shard_map/ppermute | solution.py:232
  118.9 1.7 %shard_map.93 = (f32[2048,128]{1,0:T(8,128)}, f32[512,128]{1,0:T(8,128)}) custom-call(s32[2]{0:T(128)S(1)} %pad_add_fusion.ids_ref, bf16[320,128]{1,0:T(8,128)(2,1)S(1)} %shard_map.92.refs_0_, bf16[320,128]{1,0:T(8,128)(2,1)S(1)} %collective-permute-done.21.refs_1_, bf16[320,128]{1,0:T(8,128)(2,1)S(1)} %collective-permute-done.22.refs_2_, ...), custom_call_target="tpu_custom_call" | custom-call | flops 1 | bytes 1 | tf_op jit(solution)/shard_map/pallas_call | solution.py:53
  120.6 1.6 %shard_map.90 = bf16[4096,128]{1,0:T(8,128)(2,1)} custom-call(s32[2]{0:T(128)S(1)} %pad_add_fusion.ids_ref, bf16[1024,128]{1,0:T(8,128)(2,1)S(1)} %get-tuple-element.86.refs_0_.refs_4_, bf16[1024,128]{1,0:T(8,128)(2,1)S(1)} %collective-permute-done.9.refs_1_, bf16[1024,128]{1,0:T(8,128)(2,1)S(1)} %get-tuple-element.90.refs_2_, ...), custom_call_target="tpu_custom_call" | custom-call | flops 1 | bytes 1 | tf_op jit(solution)/shard_map/pallas_call | solution.py:53
  (21 shorter events, 0.1 us)
Async XLA Ops:
  0.6 3.7 %collective-permute-start = (bf16[4096,128]{1,0:T(8,128)(2,1)}, bf16[4096,128]{1,0:T(8,128)(2,1)S(1)}, u32[]{:S(2)}, u32[]{:S(2)}) collective-permute-start(bf16[4096,128]{1,0:T(8,128)(2,1)} %refs_0_.2), channel_id=1, source_target_pairs={{0,1},{1,0},{2,3},{3,2},{4,5},{5,4},{6,7},{7,6},{8,9},{9,8},{10,11... | collective-permute-start | bytes 3145736 | tf_op jit(solution)/shard_map/ppermute | solution.py:236
  1.1 17.1 %collective-permute-start.2 = (bf16[4096,128]{1,0:T(8,128)(2,1)}, bf16[4096,128]{1,0:T(8,128)(2,1)}, u32[]{:S(2)}, u32[]{:S(2)}) collective-permute-start(bf16[4096,128]{1,0:T(8,128)(2,1)} %refs_0_.3), channel_id=1, source_target_pairs={{0,1},{1,0},{2,3},{3,2},{4,5},{5,4},{6,7},{7,6},{8,9},{9,8},{10,11... | collective-permute-start | bytes 3145736 | tf_op jit(solution)/shard_map/ppermute | solution.py:236
  1.3 11.5 %copy-start = (bf16[2,256,256]{2,1,0:T(8,128)(2,1)S(1)}, bf16[2,256,256]{2,1,0:T(8,128)(2,1)}, u32[]{:S(2)}) copy-start(bf16[2,256,256]{2,1,0:T(8,128)(2,1)} %refs_4_.3) | copy-start | bytes 786436
  4.3 1.2 %copy-start.3 = (bf16[4096,128]{1,0:T(8,128)(2,1)S(1)}, bf16[4096,128]{1,0:T(8,128)(2,1)}, u32[]{:S(2)}) copy-start(bf16[4096,128]{1,0:T(8,128)(2,1)} %refs_0_.2) | copy-start | bytes 3145732
  6.2 16.3 %collective-permute-start.1 = (bf16[1024,256]{1,0:T(8,128)(2,1)S(1)}, bf16[1024,256]{1,0:T(8,128)(2,1)S(1)}, u32[]{:S(2)}, u32[]{:S(2)}) collective-permute-start(bf16[1024,256]{1,0:T(8,128)(2,1)S(1)} %get-tuple-element.55.refs_0_.refs_5_), channel_id=1, source_target_pairs={{0,2},{2,4},{4,6},{6,8},{8,10},{10,12},{12,14},{1,3},{3,5},{5,7},{... | collective-permute-start | bytes 1572872 | tf_op jit(solution)/shard_map/ppermute | solution.py:225
  12.8 5.4 %copy-start.2 = (bf16[4096,128]{1,0:T(8,128)(2,1)S(1)}, bf16[4096,128]{1,0:T(8,128)(2,1)}, u32[]{:S(2)}) copy-start(bf16[4096,128]{1,0:T(8,128)(2,1)} %refs_0_.3) | copy-start | bytes 3145732
  14.7 15.8 %collective-permute-start.4 = (bf16[1024,256]{1,0:T(8,128)(2,1)S(1)}, bf16[1024,256]{1,0:T(8,128)(2,1)S(1)}, u32[]{:S(2)}, u32[]{:S(2)}) collective-permute-start(bf16[1024,256]{1,0:T(8,128)(2,1)S(1)} %get-tuple-element.56.refs_3_.refs_0_.refs_5_), channel_id=1, source_target_pairs={{0,4},{2,6},{4,8},{6,10},{8,12},{10,14},{1,5},{3,7},{5,9},{7,11},{... | collective-permute-start | bytes 1572872 | tf_op jit(solution)/shard_map/ppermute | solution.py:225
  24.4 16.2 %collective-permute-start.3 = (bf16[1024,256]{1,0:T(8,128)(2,1)S(1)}, bf16[1024,256]{1,0:T(8,128)(2,1)S(1)}, u32[]{:S(2)}, u32[]{:S(2)}) collective-permute-start(bf16[1024,256]{1,0:T(8,128)(2,1)S(1)} %get-tuple-element.58.refs_0_), channel_id=1, source_target_pairs={{0,4},{2,6},{4,8},{6,10},{8,12},{10,14},{1,5},{3,7},{5,9},{7,11},{... | collective-permute-start | bytes 1572872 | tf_op jit(solution)/shard_map/ppermute | solution.py:225
  32.5 16.9 %collective-permute-start.8 = (bf16[1024,256]{1,0:T(8,128)(2,1)S(1)}, bf16[1024,256]{1,0:T(8,128)(2,1)S(1)}, u32[]{:S(2)}, u32[]{:S(2)}) collective-permute-start(bf16[1024,256]{1,0:T(8,128)(2,1)S(1)} %get-tuple-element.75), channel_id=1, source_target_pairs={{4,0},{6,2},{8,4},{10,6},{12,8},{14,10},{5,1},{7,3},{9,5},{11,7},{... | collective-permute-start | bytes 1572872 | tf_op jit(solution)/shard_map/ppermute | solution.py:225
  42.5 15.5 %collective-permute-start.7 = (bf16[1024,256]{1,0:T(8,128)(2,1)S(1)}, bf16[1024,256]{1,0:T(8,128)(2,1)S(1)}, u32[]{:S(2)}, u32[]{:S(2)}) collective-permute-start(bf16[1024,256]{1,0:T(8,128)(2,1)S(1)} %get-tuple-element.73), channel_id=1, source_target_pairs={{4,0},{6,2},{8,4},{10,6},{12,8},{14,10},{5,1},{7,3},{9,5},{11,7},{... | collective-permute-start | bytes 1572872 | tf_op jit(solution)/shard_map/ppermute | solution.py:225
  43.8 3.9 %collective-permute-start.6 = (bf16[1024,128]{1,0:T(8,128)(2,1)S(1)}, bf16[1024,128]{1,0:T(8,128)(2,1)S(1)}, u32[]{:S(2)}, u32[]{:S(2)}) collective-permute-start(bf16[1024,128]{1,0:T(8,128)(2,1)S(1)} %get-tuple-element.70), channel_id=1, source_target_pairs={{0,1},{1,0},{2,3},{3,2},{4,5},{5,4},{6,7},{7,6},{8,9},{9,8},{10,11... | collective-permute-start | bytes 786440 | tf_op jit(solution)/shard_map/ppermute | solution.py:236
  45.1 2.7 %collective-permute-start.5 = (bf16[1024,128]{1,0:T(8,128)(2,1)S(1)}, bf16[1024,128]{1,0:T(8,128)(2,1)S(1)}, u32[]{:S(2)}, u32[]{:S(2)}) collective-permute-start(bf16[1024,128]{1,0:T(8,128)(2,1)S(1)} %get-tuple-element.68), channel_id=1, source_target_pairs={{0,1},{1,0},{2,3},{3,2},{4,5},{5,4},{6,7},{7,6},{8,9},{9,8},{10,11... | collective-permute-start | bytes 786440 | tf_op jit(solution)/shard_map/ppermute | solution.py:236
  49.4 1.2 %copy-start.1 = (bf16[4096,128]{1,0:T(8,128)(2,1)S(1)}, bf16[4096,128]{1,0:T(8,128)(2,1)}, u32[]{:S(2)}) copy-start(bf16[4096,128]{1,0:T(8,128)(2,1)} %shard_map.84.refs_5_) | copy-start | bytes 3145732
  59.9 28.2 %collective-permute-start.10 = (bf16[1024,256]{1,0:T(8,128)(2,1)S(1)}, bf16[1024,256]{1,0:T(8,128)(2,1)S(1)}, u32[]{:S(2)}, u32[]{:S(2)}) collective-permute-start(bf16[1024,256]{1,0:T(8,128)(2,1)S(1)} %get-tuple-element.89), channel_id=1, source_target_pairs={{2,0},{4,2},{6,4},{8,6},{10,8},{12,10},{14,12},{3,1},{5,3},{7,5},{... | collective-permute-start | bytes 1572872 | tf_op jit(solution)/shard_map/ppermute | solution.py:225
  61.4 3.5 %collective-permute-start.13 = (bf16[1280,128]{1,0:T(8,128)(2,1)S(1)}, bf16[1280,128]{1,0:T(8,128)(2,1)S(1)}, u32[]{:S(2)}, u32[]{:S(2)}) collective-permute-start(bf16[1280,128]{1,0:T(8,128)(2,1)S(1)} %get-tuple-element.93), channel_id=1, source_target_pairs={{0,1},{1,0},{2,3},{3,2},{4,5},{5,4},{6,7},{7,6},{8,9},{9,8},{10,11... | collective-permute-start | bytes 983048 | tf_op jit(solution)/shard_map/ppermute | solution.py:236
  63.6 1.8 %collective-permute-start.12 = (bf16[1280,128]{1,0:T(8,128)(2,1)S(1)}, bf16[1280,128]{1,0:T(8,128)(2,1)S(1)}, u32[]{:S(2)}, u32[]{:S(2)}) collective-permute-start(bf16[1280,128]{1,0:T(8,128)(2,1)S(1)} %get-tuple-element.92), channel_id=1, source_target_pairs={{0,1},{1,0},{2,3},{3,2},{4,5},{5,4},{6,7},{7,6},{8,9},{9,8},{10,11... | collective-permute-start | bytes 983048 | tf_op jit(solution)/shard_map/ppermute | solution.py:236
  66.1 14.7 %collective-permute-start.14 = (bf16[320,128]{1,0:T(8,128)(2,1)S(1)}, bf16[320,128]{1,0:T(8,128)(2,1)S(1)}, u32[]{:S(2)}, u32[]{:S(2)}) collective-permute-start(bf16[320,128]{1,0:T(8,128)(2,1)S(1)} %get-tuple-element.95), channel_id=1, source_target_pairs={{0,2},{2,4},{4,6},{6,8},{8,10},{10,12},{12,14},{14,0},{1,3},{3,5},... | collective-permute-start | bytes 245768 | tf_op jit(solution)/shard_map/ppermute | solution.py:232
  73.0 13.8 %collective-permute-start.15 = (bf16[320,128]{1,0:T(8,128)(2,1)S(1)}, bf16[320,128]{1,0:T(8,128)(2,1)S(1)}, u32[]{:S(2)}, u32[]{:S(2)}) collective-permute-start(bf16[320,128]{1,0:T(8,128)(2,1)S(1)} %get-tuple-element.96), channel_id=1, source_target_pairs={{0,4},{2,6},{4,8},{6,10},{8,12},{10,14},{12,0},{14,2},{1,5},{3,7},... | collective-permute-start | bytes 245768 | tf_op jit(solution)/shard_map/ppermute | solution.py:232
  74.8 15.4 %collective-permute-start.16 = (bf16[320,128]{1,0:T(8,128)(2,1)S(1)}, bf16[320,128]{1,0:T(8,128)(2,1)S(1)}, u32[]{:S(2)}, u32[]{:S(2)}) collective-permute-start(bf16[320,128]{1,0:T(8,128)(2,1)S(1)} %get-tuple-element.97), channel_id=1, source_target_pairs={{0,6},{2,8},{4,10},{6,12},{8,14},{10,0},{12,2},{14,4},{1,7},{3,9},... | collective-permute-start | bytes 245768 | tf_op jit(solution)/shard_map/ppermute | solution.py:232
  78.7 11.6 %collective-permute-start.17 = (bf16[320,128]{1,0:T(8,128)(2,1)S(1)}, bf16[320,128]{1,0:T(8,128)(2,1)S(1)}, u32[]{:S(2)}, u32[]{:S(2)}) collective-permute-start(bf16[320,128]{1,0:T(8,128)(2,1)S(1)} %get-tuple-element.98), channel_id=1, source_target_pairs={{0,8},{2,10},{4,12},{6,14},{8,0},{10,2},{12,4},{14,6},{1,9},{3,11}... | collective-permute-start | bytes 245768 | tf_op jit(solution)/shard_map/ppermute | solution.py:232
  80.8 9.9 %collective-permute-start.18 = (bf16[320,128]{1,0:T(8,128)(2,1)S(1)}, bf16[320,128]{1,0:T(8,128)(2,1)S(1)}, u32[]{:S(2)}, u32[]{:S(2)}) collective-permute-start(bf16[320,128]{1,0:T(8,128)(2,1)S(1)} %get-tuple-element.99), channel_id=1, source_target_pairs={{0,10},{2,12},{4,14},{6,0},{8,2},{10,4},{12,6},{14,8},{1,11},{3,13... | collective-permute-start | bytes 245768 | tf_op jit(solution)/shard_map/ppermute | solution.py:232
  86.8 5.8 %collective-permute-start.19 = (bf16[320,128]{1,0:T(8,128)(2,1)S(1)}, bf16[320,128]{1,0:T(8,128)(2,1)S(1)}, u32[]{:S(2)}, u32[]{:S(2)}) collective-permute-start(bf16[320,128]{1,0:T(8,128)(2,1)S(1)} %get-tuple-element.100), channel_id=1, source_target_pairs={{0,12},{2,14},{4,0},{6,2},{8,4},{10,6},{12,8},{14,10},{1,13},{3,15... | collective-permute-start | bytes 245768 | tf_op jit(solution)/shard_map/ppermute | solution.py:232
  88.1 4.4 %collective-permute-start.20 = (bf16[320,128]{1,0:T(8,128)(2,1)S(1)}, bf16[320,128]{1,0:T(8,128)(2,1)S(1)}, u32[]{:S(2)}, u32[]{:S(2)}) collective-permute-start(bf16[320,128]{1,0:T(8,128)(2,1)S(1)} %get-tuple-element.101), channel_id=1, source_target_pairs={{0,14},{2,0},{4,2},{6,4},{8,6},{10,8},{12,10},{14,12},{1,15},{3,1}... | collective-permute-start | bytes 245768 | tf_op jit(solution)/shard_map/ppermute | solution.py:232
  90.2 30.4 %collective-permute-start.9 = (bf16[1024,128]{1,0:T(8,128)(2,1)S(1)}, bf16[1024,128]{1,0:T(8,128)(2,1)S(1)}, u32[]{:S(2)}, u32[]{:S(2)}) collective-permute-start(bf16[1024,128]{1,0:T(8,128)(2,1)S(1)} %get-tuple-element.87), channel_id=1, source_target_pairs={{0,1},{1,0},{2,3},{3,2},{4,5},{5,4},{6,7},{7,6},{8,9},{9,8},{10,11... | collective-permute-start | bytes 786440 | tf_op jit(solution)/shard_map/ppermute | solution.py:236
  90.3 30.4 %collective-permute-start.11 = (bf16[1024,128]{1,0:T(8,128)(2,1)S(1)}, bf16[1024,128]{1,0:T(8,128)(2,1)S(1)}, u32[]{:S(2)}, u32[]{:S(2)}) collective-permute-start(bf16[1024,128]{1,0:T(8,128)(2,1)S(1)} %get-tuple-element.91), channel_id=1, source_target_pairs={{0,1},{1,0},{2,3},{3,2},{4,5},{5,4},{6,7},{7,6},{8,9},{9,8},{10,11... | collective-permute-start | bytes 786440 | tf_op jit(solution)/shard_map/ppermute | solution.py:236
  93.2 7.9 %collective-permute-start.27 = (bf16[320,128]{1,0:T(8,128)(2,1)S(1)}, bf16[320,128]{1,0:T(8,128)(2,1)S(1)}, u32[]{:S(2)}, u32[]{:S(2)}) collective-permute-start(bf16[320,128]{1,0:T(8,128)(2,1)S(1)} %shard_map.92.refs_0_), channel_id=1, source_target_pairs={{0,14},{2,0},{4,2},{6,4},{8,6},{10,8},{12,10},{14,12},{1,15},{3,1}... | collective-permute-start | bytes 245768 | tf_op jit(solution)/shard_map/ppermute | solution.py:232
  98.1 4.7 %collective-permute-start.26 = (bf16[320,128]{1,0:T(8,128)(2,1)S(1)}, bf16[320,128]{1,0:T(8,128)(2,1)S(1)}, u32[]{:S(2)}, u32[]{:S(2)}) collective-permute-start(bf16[320,128]{1,0:T(8,128)(2,1)S(1)} %shard_map.92.refs_0_), channel_id=1, source_target_pairs={{0,12},{2,14},{4,0},{6,2},{8,4},{10,6},{12,8},{14,10},{1,13},{3,15... | collective-permute-start | bytes 245768 | tf_op jit(solution)/shard_map/ppermute | solution.py:232
  98.1 8.7 %collective-permute-start.25 = (bf16[320,128]{1,0:T(8,128)(2,1)S(1)}, bf16[320,128]{1,0:T(8,128)(2,1)S(1)}, u32[]{:S(2)}, u32[]{:S(2)}) collective-permute-start(bf16[320,128]{1,0:T(8,128)(2,1)S(1)} %shard_map.92.refs_0_), channel_id=1, source_target_pairs={{0,10},{2,12},{4,14},{6,0},{8,2},{10,4},{12,6},{14,8},{1,11},{3,13... | collective-permute-start | bytes 245768 | tf_op jit(solution)/shard_map/ppermute | solution.py:232
  101.1 10.7 %collective-permute-start.24 = (bf16[320,128]{1,0:T(8,128)(2,1)S(1)}, bf16[320,128]{1,0:T(8,128)(2,1)S(1)}, u32[]{:S(2)}, u32[]{:S(2)}) collective-permute-start(bf16[320,128]{1,0:T(8,128)(2,1)S(1)} %shard_map.92.refs_0_), channel_id=1, source_target_pairs={{0,8},{2,10},{4,12},{6,14},{8,0},{10,2},{12,4},{14,6},{1,9},{3,11}... | collective-permute-start | bytes 245768 | tf_op jit(solution)/shard_map/ppermute | solution.py:232
  102.8 9.5 %collective-permute-start.23 = (bf16[320,128]{1,0:T(8,128)(2,1)S(1)}, bf16[320,128]{1,0:T(8,128)(2,1)S(1)}, u32[]{:S(2)}, u32[]{:S(2)}) collective-permute-start(bf16[320,128]{1,0:T(8,128)(2,1)S(1)} %shard_map.92.refs_0_), channel_id=1, source_target_pairs={{0,6},{2,8},{4,10},{6,12},{8,14},{10,0},{12,2},{14,4},{1,7},{3,9},... | collective-permute-start | bytes 245768 | tf_op jit(solution)/shard_map/ppermute | solution.py:232
  106.9 6.2 %collective-permute-start.22 = (bf16[320,128]{1,0:T(8,128)(2,1)S(1)}, bf16[320,128]{1,0:T(8,128)(2,1)S(1)}, u32[]{:S(2)}, u32[]{:S(2)}) collective-permute-start(bf16[320,128]{1,0:T(8,128)(2,1)S(1)} %shard_map.92.refs_0_), channel_id=1, source_target_pairs={{0,4},{2,6},{4,8},{6,10},{8,12},{10,14},{12,0},{14,2},{1,5},{3,7},... | collective-permute-start | bytes 245768 | tf_op jit(solution)/shard_map/ppermute | solution.py:232
  111.7 7.1 %collective-permute-start.21 = (bf16[320,128]{1,0:T(8,128)(2,1)S(1)}, bf16[320,128]{1,0:T(8,128)(2,1)S(1)}, u32[]{:S(2)}, u32[]{:S(2)}) collective-permute-start(bf16[320,128]{1,0:T(8,128)(2,1)S(1)} %shard_map.92.refs_0_), channel_id=1, source_target_pairs={{0,2},{2,4},{4,6},{6,8},{8,10},{10,12},{12,14},{14,0},{1,3},{3,5},... | collective-permute-start | bytes 245768 | tf_op jit(solution)/shard_map/ppermute | solution.py:232

commit v3 on v2

v3 whole, which is shorter than its diff:
```python
import functools
import math

import jax
import jax.numpy as jnp
from jax import lax
from jax.experimental import pallas as pl
from jax.experimental.pallas import tpu as pltpu
from jax.sharding import PartitionSpec as P

BF = jnp.bfloat16
F32 = jnp.float32
VMEM_LIMIT = 24 * 1024 * 1024
CHUNK = 256


def mm(a, b):
    return jnp.dot(a, b, preferred_element_type=F32)


def mm_t(a, b):
    return lax.dot_general(a, b, (((1,), (1,)), ((), ())), preferred_element_type=F32)


def mm_rows(a, b):
    return lax.dot_general(a, b, (((0,), (0,)), ((), ())), preferred_element_type=F32)


def ordered(core, own, other):
    first = core == 0
    return jnp.concatenate(
        [jnp.where(first, own, other), jnp.where(first, other, own)], axis=1
    )


def halves(core, values):
    width = values.shape[1] // 2
    low, high = values[:, :width], values[:, width:]
    first = core == 0
    return jnp.where(first, low, high), jnp.where(first, high, low)


def chunks(ref):
    return [pl.ds(r, CHUNK) for r in range(0, ref.shape[0], CHUNK)]


def run(body, ids, ins, outs, scratch=(), after=()):
    count = len(ins)

    def kernel(ids_ref, *refs):
        body(ids_ref, *refs[:count], *refs[count + len(after) :])

    return pl.pallas_call(
        kernel,
        in_specs=[pl.BlockSpec(memory_space=pltpu.SMEM)]
        + [pl.BlockSpec(memory_space=pltpu.VMEM)] * count
        + [pl.BlockSpec(memory_space=pl.ANY)] * len(after),
        out_specs=[pl.BlockSpec(memory_space=pltpu.VMEM)] * len(outs),
        out_shape=[jax.ShapeDtypeStruct(shape, kind) for shape, kind in outs],
        scratch_shapes=list(scratch),
        compiler_params=pltpu.CompilerParams(vmem_limit_bytes=VMEM_LIMIT),
        cost_estimate=pl.CostEstimate(flops=1, bytes_accessed=1, transcendentals=0),
    )(ids, *ins, *after)


def gated(x, delayed, taps, layer):
    width = x.shape[1]
    preact = mm(x, taps[layer, 0]) + mm(delayed, taps[layer, 1])
    filt = jnp.tanh(preact[:, :width])
    gate = 0.5 * jnp.tanh(0.5 * preact[:, width:]) + 0.5
    hidden = (filt * gate).astype(BF)
    return hidden, gate * (1.0 - filt * filt), filt * gate * (1.0 - gate)


def join_body(ids, own, other, a_o, b_o):
    core = ids[0]
    count = a_o.shape[0]
    for half, out in ((0, a_o), (1, b_o)):
        for rows in chunks(out):
            place = pl.ds(pl.multiple_of((half * 2 + core) * count + rows.start, CHUNK), CHUNK)
            out[rows, :] = ordered(core, own[place, :], other[place, :])


def cot_body(ids, own, other, wo, a_o, b_o, ha_o, hb_o):
    join_body(ids, own, other, a_o, b_o)
    for g_r, h_r in ((a_o, ha_o), (b_o, hb_o)):
        for rows in chunks(g_r):
            h_r[rows, :] = mm_t(g_r[rows, :], wo[1])


def first_body(ids, x_r, d_r, taps, wo, x1_o, hid_o, slope_o):
    width = x_r.shape[1]
    for rows in chunks(x_r):
        x = x_r[rows, :]
        hidden, sf, sg = gated(x, d_r[rows, :], taps, 0)
        hid_o[rows, :] = hidden
        slope_o[rows, :width] = sf
        slope_o[rows, width:] = sg
        x1_o[rows, :] = (x.astype(F32) + mm(hidden, wo[0])).astype(BF)


def pre_grad(hg, sf, sg):
    return jnp.concatenate([(hg * sf).astype(BF), (hg * sg).astype(BF)], axis=1)


def second_body(ids, x_r, d_r, hg_r, taps, pre_o, past_o, hid_o):
    for rows in chunks(x_r):
        hidden, sf, sg = gated(x_r[rows, :], d_r[rows, :], taps, 1)
        hid_o[rows, :] = hidden
        pre = pre_grad(hg_r[rows, :], sf, sg)
        pre_o[rows, :] = pre
        past_o[rows, :] = mm_t(pre, taps[1, 1]).astype(BF)


def rest_body(ids, x_r, hid_r, g_r, pre_r, taps, wo, keep_o, send_o, local_o):
    for rows in chunks(x_r):
        out = (x_r[rows, :].astype(F32) + mm(hid_r[rows, :], wo[1])).astype(BF)
        keep, send = halves(ids[0], out)
        keep_o[rows, :] = keep
        send_o[rows, :] = send
        local_o[rows, :] = g_r[rows, :].astype(F32) + mm_t(pre_r[rows, :], taps[1, 0])


def later_body(ids, x_r, d_r, g_r, taps, wo, term_o):
    for rows in chunks(d_r):
        _, sf, sg = gated(x_r[rows, :], d_r[rows, :], taps, 1)
        pre = pre_grad(mm_t(g_r[rows, :], wo[1]), sf, sg)
        term_o[rows, :] = mm_t(pre, taps[1, 1])


def third_rows(rows, g, slope_r, taps, wo, g_o, pre_o, now_o):
    width = g.shape[1]
    g_o[rows, :] = g
    pre = pre_grad(mm_t(g, wo[0]), slope_r[rows, :width], slope_r[rows, width:])
    pre_o[rows, :] = pre
    now_o[rows, :] = g.astype(F32) + mm_t(pre, taps[0, 0])
    return pre


def past_body(ids, pre_r, taps, past_o):
    for rows in chunks(pre_r):
        past_o[rows, :] = mm_t(pre_r[rows, :], taps[0, 1]).astype(BF)


def third_body(ids, local_r, arrived_r, slope_r, now_a, taps, wo, keep_o, send_o, *outs):
    for rows in chunks(local_r):
        g = (local_r[rows, :] + arrived_r[rows, :].astype(F32)).astype(BF)
        pre = third_rows(rows, g, slope_r, taps, wo, *outs)
        keep, send = halves(ids[0], (now_a[rows, :] + mm_t(pre, taps[0, 1])).astype(BF))
        keep_o[rows, :] = keep
        send_o[rows, :] = send


def both_body(ids, x_r, d_r, g_r, hg_r, term_r, slope_r, taps, wo, *outs):
    pre1_o, hid_o, keep_o, send_o = outs[:4]
    for rows in chunks(x_r):
        x = x_r[rows, :]
        hidden, sf, sg = gated(x, d_r[rows, :], taps, 1)
        hid_o[rows, :] = hidden
        pre = pre_grad(hg_r[rows, :], sf, sg)
        pre1_o[rows, :] = pre
        local = g_r[rows, :].astype(F32) + mm_t(pre, taps[1, 0])
        third_rows(rows, (local + term_r[rows, :]).astype(BF), slope_r, taps, wo, *outs[4:])
        out = (x.astype(F32) + mm(hidden, wo[1])).astype(BF)
        keep, send = halves(ids[0], out)
        keep_o[rows, :] = keep
        send_o[rows, :] = send


def last_body(ids, now_r, past_r, keep_o, send_o):
    for rows in chunks(now_r):
        keep, send = halves(
            ids[0], (now_r[rows, :] + past_r[rows, :].astype(F32)).astype(BF)
        )
        keep_o[rows, :] = keep
        send_o[rows, :] = send


def assemble_body(ids, keep_a, got_a, keep_b, got_b, out):
    core = ids[0]
    count = keep_a.shape[0]
    for half, keep, got in ((0, keep_a, got_a), (1, keep_b, got_b)):
        own = pl.multiple_of((half * 2 + core) * count, count)
        other = pl.multiple_of((half * 2 + 1 - core) * count, count)
        out[pl.ds(own, count), :] = keep[...]
        out[pl.ds(other, count), :] = got[...]


def weight_body(scale, ids, xa, da, pa, ha, ga, xb, db, pb, hb, gb, keep_o, send_o):
    channels = ha.shape[1]
    pairs = (
        (xa, pa, xb, pb),
        (da, pa, db, pb),
        (ha, ga, hb, gb),
    )
    position = 0
    for la, ra, lb, rb in pairs:
        both = (mm_rows(la[...], ra[...]) + mm_rows(lb[...], rb[...])) * scale
        for k in range(both.shape[1] // channels):
            keep, send = halves(ids[0], both[:, k * channels : (k + 1) * channels])
            keep_o[pl.ds(position * channels, channels), :] = keep
            send_o[pl.ds(position * channels, channels), :] = send.astype(BF)
            position += 1


def gather_sums(keep, got, total):
    channels = total.shape[0] // 5
    for position in range(5):
        rows = pl.ds(position * channels, channels)
        value = keep[rows, :] + got[rows, :].astype(F32)
        if position < 4:
            tap, k = divmod(position, 2)
            total[pl.ds(tap * 2 * channels + k, channels, stride=2), :] = value
        else:
            total[rows, :] = value


def split_body(ids, keep, got, own_o, send_o, total):
    gather_sums(keep, got, total)
    rows = own_o.shape[0]
    side = ids[1] % 2
    own_o[...] = total[pl.ds(pl.multiple_of(side * rows, rows), rows), :]
    send_o[...] = total[pl.ds(pl.multiple_of((1 - side) * rows, rows), rows), :].astype(BF)


def place_body(ids, own0, got0, own1, got1, conv_o, out_o, total):
    rows = own0.shape[0]
    conv_rows = conv_o.shape[0] // 2
    out_rows = out_o.shape[0] // 2
    side = ids[1] % 2
    for layer, (own, got) in enumerate(((own0, got0), (own1, got1))):
        total[pl.ds(pl.multiple_of(side * rows, rows), rows), :] = own[...].astype(F32)
        total[pl.ds(pl.multiple_of((1 - side) * rows, rows), rows), :] = got[...].astype(F32)
        conv_o[pl.ds(layer * conv_rows, conv_rows), :] = total[:conv_rows, :]
        out_o[pl.ds(layer * out_rows, out_rows), :] = total[conv_rows:, :]


def plain_body(ids, keep, got, total):
    gather_sums(keep, got, total)


def moved_by(values, distance):
    devices = range(lax.axis_size("tm"))
    return lax.ppermute(
        values, "tm", [(i, i + distance) for i in devices if i + distance in devices]
    )


def crossed(values, bit):
    return lax.ppermute(values, "tm", [(i, i ^ bit) for i in range(lax.axis_size("tm"))])


def swapped(values):
    return lax.ppermute(values, "chan", [(0, 1), (1, 0)])


def rounded(values):
    return lax.reduce_precision(values, 8, 7).astype(BF)


def add_body(ids, own, got, total_o):
    total_o[...] = (own[...] + got[...].astype(F32)).astype(BF)


def two_powers():
    size = lax.axis_size("tm")
    return size > 1 and not size & (size - 1)


def split_sums(ids, keep, got, after=()):
    rows, cols = keep.shape
    if not two_powers():
        return run(plain_body, ids, [keep, got], [((rows, cols), F32)])
    return run(
        split_body,
        ids,
        [keep, got],
        [((rows // 2, cols), F32), ((rows // 2, cols), BF)],
        [pltpu.VMEM((rows, cols), F32)],
        after=after,
    )


def reduced(ids, parts, after=()):
    if not two_powers():
        return (lax.psum(parts[0], "tm"),)
    own, send = parts
    (total,) = run(add_body, ids, [own, crossed(send, 1)], [(own.shape, BF)], after=after)
    bit = 2
    while bit < lax.axis_size("tm"):
        total = rounded(total.astype(F32) + crossed(total, bit).astype(F32))
        bit *= 2
    return total, crossed(total, 1)


def placed_sums(ids, channels, layers):
    if not two_powers():
        both = jnp.concatenate(layers[0] + layers[1]).reshape(2, 5 * channels, -1)
        return both[:, : 4 * channels], both[:, 4 * channels :]
    cols = layers[0][0].shape[1]
    return run(
        place_body,
        ids,
        [array for layer in layers for array in layer],
        [((8 * channels, cols), F32), ((2 * channels, cols), F32)],
        [pltpu.VMEM((5 * channels, cols), F32)],
    )


def on_device(signal, cotangent, conv_weight, out_weight):
    rows, half_width = signal.shape
    channels = conv_weight.shape[2]
    quarter = rows // 4
    wide = 2 * channels
    scale = 1.0 / math.sqrt(rows * lax.axis_size("tm"))
    later = 2
    ids = jnp.stack([lax.axis_index("chan"), lax.axis_index("tm")]).astype(jnp.int32)
    taps = conv_weight.reshape(2, 2, channels, wide)
    wo = out_weight

    narrow, broad = (quarter, channels), (quarter, wide)
    half = (quarter, half_width)
    third_outs = [(narrow, BF), (broad, BF), (narrow, F32)]

    x_a, x_b = run(
        join_body, ids, [signal, swapped(signal)], [(narrow, BF)] * 2, after=[taps]
    )
    x_h = moved_by(x_b, 1)
    first_outs = [(narrow, BF)] * 2 + [(broad, F32)]
    x1_b, hid0_b, slope_b = run(
        first_body, ids, [x_b, x_a, taps, wo], first_outs
    )
    x1_b_past = moved_by(x1_b, later)
    cot_a, cot_b, hg_a, hg_b = run(
        cot_body,
        ids,
        [cotangent, swapped(cotangent), wo],
        [(narrow, BF)] * 2 + [(narrow, F32)] * 2,
        after=[x1_b],
    )
    cot_a_later = moved_by(cot_a, -later)
    x1_a, hid0_a, slope_a = run(
        first_body, ids, [x_a, x_h, taps, wo], first_outs, after=[cot_a]
    )
    x1_a_later = moved_by(x1_a, -later)
    x1_a_past = moved_by(x1_a, later)

    pre1_b, to_past_b, hid1_b = run(
        second_body,
        ids,
        [x1_b, x1_b_past, hg_b, taps],
        [(broad, BF)] + [(narrow, BF)] * 2,
        after=[x1_a],
    )
    from_next_b = moved_by(to_past_b, -later)
    out_keep_b, out_send_b, local_b = run(
        rest_body,
        ids,
        [x1_b, hid1_b, cot_b, pre1_b, taps, wo],
        [(half, BF)] * 2 + [(narrow, F32)],
    )
    (term_a,) = run(
        later_body,
        ids,
        [x1_a_later, x1_a, cot_a_later, taps, wo],
        [(narrow, F32)],
        after=[local_b],
    )
    pre1_a, hid1_a, out_keep_a, out_send_a, g1_a, pre0_a, now_a = run(
        both_body,
        ids,
        [x1_a, x1_a_past, cot_a, hg_a, term_a, slope_a, taps, wo],
        [(broad, BF), (narrow, BF), (half, BF), (half, BF)] + third_outs,
    )

    def weights(arrays, after=()):
        shape = (5 * channels, half_width)
        return run(
            functools.partial(weight_body, scale),
            ids,
            arrays,
            [(shape, F32), (shape, BF)],
            after=after,
        )

    keep1, send1 = weights(
        [x1_a, x1_a_past, pre1_a, hid1_a, cot_a, x1_b, x1_b_past, pre1_b, hid1_b, cot_b]
    )
    parts1 = split_sums(ids, keep1, swapped(send1))
    (past_a,) = run(past_body, ids, [pre0_a, taps], [(narrow, BF)], after=parts1)
    ahead_b = moved_by(past_a, -1)
    in_keep_a, in_send_a, g1_b, pre0_b, now_b = run(
        third_body,
        ids,
        [local_b, from_next_b, slope_b, now_a, taps, wo],
        [(half, BF)] * 2 + third_outs,
        after=[past_a],
    )
    keep0, send0 = weights(
        [x_a, x_h, pre0_a, hid0_a, g1_a, x_b, x_a, pre0_b, hid0_b, g1_b]
    )
    parts0 = split_sums(ids, keep0, swapped(send0))
    sums1 = reduced(ids, parts1, after=[keep0])
    in_keep_b, in_send_b = run(last_body, ids, [now_b, ahead_b], [(half, BF)] * 2)
    sums0 = reduced(ids, parts0, after=[in_keep_b])
    conv_grad, out_grad = placed_sums(ids, channels, [sums0, sums1])
    (output,) = run(
        assemble_body,
        ids,
        [out_keep_a, swapped(out_send_a), out_keep_b, swapped(out_send_b)],
        [((rows, half_width), BF)],
        after=[in_keep_b],
    )
    (in_grad,) = run(
        assemble_body,
        ids,
        [in_keep_a, swapped(in_send_a), in_keep_b, swapped(in_send_b)],
        [((rows, half_width), BF)],
    )
    return (
        output,
        in_grad,
        conv_grad.reshape(2, 2, channels, 2, half_width),
        out_grad.reshape(2, channels, half_width),
    )


def solution(mesh):
    placed = (P(("groups", "tm"), "chan"), P(("groups", "tm"), "chan"), P(), P())
    return jax.shard_map(
        on_device,
        mesh=mesh,
        in_specs=placed,
        out_specs=(
            P(("groups", "tm"), "chan"),
            P(("groups", "tm"), "chan"),
            P("groups", None, None, None, "chan"),
            P("groups", None, "chan"),
        ),
        check_vma=False,
    )
```

time: 123 us -> 109 us (0.89)
  starting transfers between devices: 55.6 us -> 40.9 us
  local copies, waits for them, and re-layouts: 4.2 us -> 1.75 us
  Pallas kernels: 27.9 us -> 30.1 us
    ppermute x14 -> x8, starting transfers between devices: 34.6 us -> 19 us  [crossed(): lax.ppermute(values, 'tm', [(i, i ^ bit) for i in range(lax.axis_size('tm...]
    ppermute x14 -> x8, waiting for transfers between devices: 16.2 us -> 19.4 us  [crossed(): lax.ppermute(values, 'tm', [(i, i ^ bit) for i in range(lax.axis_size('tm...]
    unnamed x8 -> x6, local copies, waits for them, and re-layouts: 2.46 us -> 0.01 us
    pallas_call x19 -> x20, Pallas kernels: 27.9 us -> 30.1 us  [run(): pl.pallas_call(kernel, in_specs=[pl.BlockSpec(memory_space=pltpu.SMEM)] +...]
    ppermute x6 -> x7, starting transfers between devices: 18.5 us -> 20.5 us  [moved_by(): lax.ppermute(values, 'tm', [(i, i + distance) for i in devices if i + dis...]
    ppermute x6 -> x7, waiting for transfers between devices: 13.7 us -> 12.3 us  [moved_by(): lax.ppermute(values, 'tm', [(i, i + distance) for i in devices if i + dis...]
  transfers between devices with their start and end apart: 28 -> 23, of which waited for: 12 -> 9; matrix products, arithmetic and copies ran while one was open for 1% -> 2% of each run, Pallas kernels for 20% -> 26%
where the time goes in v3:
time: 109 us
  starting transfers between devices  40.9 us (38%)
  waiting for transfers between devices  34.7 us (32%)
  Pallas kernels  30.1 us (28%)
  local copies, waits for them, and re-layouts  1.75 us (2%)
    pallas_call x20, Pallas kernels, run(): pl.pallas_call(kernel, in_specs=[pl.BlockSpec(memory_space=pltpu.SMEM)] +...  30.1 us
    ppermute x7, starting transfers between devices, moved_by(): lax.ppermute(values, 'tm', [(i, i + distance) for i in devices if i + dis...  20.5 us
    ppermute x8, waiting for transfers between devices, crossed(): lax.ppermute(values, 'tm', [(i, i ^ bit) for i in range(lax.axis_size('tm...  19.4 us
    ppermute x8, starting transfers between devices, crossed(): lax.ppermute(values, 'tm', [(i, i ^ bit) for i in range(lax.axis_size('tm...  19 us
    ppermute x7, waiting for transfers between devices, moved_by(): lax.ppermute(values, 'tm', [(i, i + distance) for i in devices if i + dis...  12.3 us
    ppermute x8, waiting for transfers between devices, swapped(): return lax.ppermute(values, 'chan', [(0, 1), (1, 0)])  3.04 us
  transfers between devices with their start and end apart: 23, of which 9 were waited for; matrix products, arithmetic and copies ran while one was open for 2% of the time, Pallas kernels for 26%

profile of v3, /device:TPU:0, one launch (start us, length us, event | category | flops | bytes accessed | tf_op | source)
XLA Modules:
  0.0 108.6 jit_solution(12831465669540976985)
XLA Ops:
  0.6 0.5 collective-permute-start
  1.2 0.1 collective-permute-start.2
  1.2 1.7 %reshape.17.refs_2_.refs_3_.refs_4_.refs_6_.refs_1_ = bf16[2,2,256,512]{3,2,1,0:T(8,128)(2,1)S(1)} reshape(bf16[2,2,256,2,256]{4,3,2,1,0:T(2,128)(2,1)} %param.6) | data formatting | bytes 2097152 | tf_op jit(solution)/shard_map/reshape | solution.py:318
  3.0 0.0 copy-start
  3.0 0.1 pad_add_fusion.ids_ref
  3.1 1.4 %collective-permute-done.refs_1_ = bf16[4096,128]{1,0:T(8,128)(2,1)} collective-permute-done((bf16[4096,128]{1,0:T(8,128)(2,1)}, bf16[4096,128]{1,0:T(8,128)(2,1)}, u32[]{:S(2)}, u32[]{:S(2)}) %collective-permute-start) | collective-permute-done | bytes 1048608 | tf_op jit(solution)/shard_map/ppermute | solution.py:254
  4.5 1.4 %shard_map.75 = (bf16[1024,256]{1,0:T(8,128)(2,1)S(1)}, bf16[1024,256]{1,0:T(8,128)(2,1)S(1)}) custom-call(s32[2]{0:T(128)S(1)} %pad_add_fusion.ids_ref, bf16[4096,128]{1,0:T(8,128)(2,1)S(1)} %copy-done.2, bf16[4096,128]{1,0:T(8,128)(2,1)} %collective-permute-done.refs_1_, bf16[2,2,256,512]{3,2,1,0:T(8,128)(2,1)S(1)} %reshape.17.refs_2_.refs_3_.refs_4_.refs_6_.refs_1_), custom_call_target="tpu_custom_call" | custom-call | flops 1 | bytes 1 | tf_op jit(solution)/shard_map/pallas_call | solution.py:53
  5.9 4.8 %collective-permute-start.1 = (bf16[1024,256]{1,0:T(8,128)(2,1)S(1)}, bf16[1024,256]{1,0:T(8,128)(2,1)S(1)}, u32[]{:S(2)}, u32[]{:S(2)}) collective-permute-start(bf16[1024,256]{1,0:T(8,128)(2,1)S(1)} %get-tuple-element.47.refs_0_.refs_5_), channel_id=1, source_target_pairs={{0,2},{2,4},{4,6},{6,8},{8,10},{10,12},{12,14},{1,3},{3,5},{5,7},{... | collective-permute-start | bytes 1572872 | tf_op jit(solution)/shard_map/ppermute | solution.py:244
  10.7 1.9 %shard_map.76 = (bf16[1024,256]{1,0:T(8,128)(2,1)S(1)}, bf16[1024,256]{1,0:T(8,128)(2,1)S(1)}, f32[1024,512]{1,0:T(8,128)S(1)}) custom-call(s32[2]{0:T(128)S(1)} %pad_add_fusion.ids_ref, bf16[1024,256]{1,0:T(8,128)(2,1)S(1)} %get-tuple-element.47.refs_0_.refs_5_, bf16[1024,256]{1,0:T(8,128)(2,1)S(1)} %get-tuple-element.46.refs_1_.refs_0_.refs_6_, ...), custom_call_target="tpu_custom_call" | custom-call | flops 1 | bytes 1 | tf_op jit(solution)/shard_map/pallas_call | solution.py:53
  12.6 3.5 %collective-permute-start.6 = (bf16[1024,256]{1,0:T(8,128)(2,1)S(1)}, bf16[1024,256]{1,0:T(8,128)(2,1)S(1)}, u32[]{:S(2)}, u32[]{:S(2)}) collective-permute-start(bf16[1024,256]{1,0:T(8,128)(2,1)S(1)} %get-tuple-element.48.refs_3_.refs_0_.refs_5_), channel_id=1, source_target_pairs={{0,4},{2,6},{4,8},{6,10},{8,12},{10,14},{1,5},{3,7},{5,9},{7,11},{... | collective-permute-start | bytes 1572872 | tf_op jit(solution)/shard_map/ppermute | solution.py:244
  16.1 0.0 collective-permute-done.2.refs_1_
  16.1 1.1 shard_map.77
  17.2 1.3 %collective-permute-start.5 = (bf16[1024,256]{1,0:T(8,128)(2,1)S(1)}, bf16[1024,256]{1,0:T(8,128)(2,1)S(1)}, u32[]{:S(2)}, u32[]{:S(2)}) collective-permute-start(bf16[1024,256]{1,0:T(8,128)(2,1)S(1)} %get-tuple-element.49.refs_4_.refs_2_), channel_id=1, source_target_pairs={{4,0},{6,2},{8,4},{10,6},{12,8},{14,10},{5,1},{7,3},{9,5},{11,7},{... | collective-permute-start | bytes 1572872 | tf_op jit(solution)/shard_map/ppermute | solution.py:244
  18.5 3.6 %collective-permute-done.1.refs_1_ = bf16[1024,256]{1,0:T(8,128)(2,1)S(1)} collective-permute-done((bf16[1024,256]{1,0:T(8,128)(2,1)S(1)}, bf16[1024,256]{1,0:T(8,128)(2,1)S(1)}, u32[]{:S(2)}, u32[]{:S(2)}) %collective-permute-start.1) | collective-permute-done | bytes 524320 | tf_op jit(solution)/shard_map/ppermute | solution.py:244
  22.1 1.9 %shard_map.78 = (bf16[1024,256]{1,0:T(8,128)(2,1)S(1)}, bf16[1024,256]{1,0:T(8,128)(2,1)S(1)}, f32[1024,512]{1,0:T(8,128)S(1)}) custom-call(s32[2]{0:T(128)S(1)} %pad_add_fusion.ids_ref, bf16[1024,256]{1,0:T(8,128)(2,1)S(1)} %get-tuple-element.46.refs_1_.refs_0_.refs_6_, bf16[1024,256]{1,0:T(8,128)(2,1)S(1)} %collective-permute-done.1.refs_1_, ...), custom_call_target="tpu_custom_call" | custom-call | flops 1 | bytes 1 | tf_op jit(solution)/shard_map/pallas_call | solution.py:53
  24.0 1.3 %collective-permute-start.4 = (bf16[1024,256]{1,0:T(8,128)(2,1)S(1)}, bf16[1024,256]{1,0:T(8,128)(2,1)S(1)}, u32[]{:S(2)}, u32[]{:S(2)}) collective-permute-start(bf16[1024,256]{1,0:T(8,128)(2,1)S(1)} %get-tuple-element.50.refs_4_.refs_1_.refs_0_), channel_id=1, source_target_pairs={{4,0},{6,2},{8,4},{10,6},{12,8},{14,10},{5,1},{7,3},{9,5},{11,7},{... | collective-permute-start | bytes 1572872 | tf_op jit(solution)/shard_map/ppermute | solution.py:244
  25.3 6.8 %collective-permute-start.3 = (bf16[1024,256]{1,0:T(8,128)(2,1)S(1)}, bf16[1024,256]{1,0:T(8,128)(2,1)S(1)}, u32[]{:S(2)}, u32[]{:S(2)}) collective-permute-start(bf16[1024,256]{1,0:T(8,128)(2,1)S(1)} %get-tuple-element.50.refs_4_.refs_1_.refs_0_), channel_id=1, source_target_pairs={{0,4},{2,6},{4,8},{6,10},{8,12},{10,14},{1,5},{3,7},{5,9},{7,11},{... | collective-permute-start | bytes 1572872 | tf_op jit(solution)/shard_map/ppermute | solution.py:244
  32.1 0.0 collective-permute-done.6.refs_1_.refs_6_
  32.2 1.9 %shard_map.79 = (bf16[1024,512]{1,0:T(8,128)(2,1)S(1)}, bf16[1024,256]{1,0:T(8,128)(2,1)S(1)}, bf16[1024,256]{1,0:T(8,128)(2,1)S(1)}) custom-call(s32[2]{0:T(128)S(1)} %pad_add_fusion.ids_ref, bf16[1024,256]{1,0:T(8,128)(2,1)S(1)} %get-tuple-element.48.refs_3_.refs_0_.refs_5_, bf16[1024,256]{1,0:T(8,128)(2,1)S(1)} %collective-permute-done.6.refs_1_.refs_6_, ...), custom_call_target="tpu_custom_call" | custom-call | flops 1 | bytes 1 | tf_op jit(solution)/shard_map/pallas_call | solution.py:53
  34.1 1.3 %collective-permute-start.9 = (bf16[1024,256]{1,0:T(8,128)(2,1)S(1)}, bf16[1024,256]{1,0:T(8,128)(2,1)S(1)}, u32[]{:S(2)}, u32[]{:S(2)}) collective-permute-start(bf16[1024,256]{1,0:T(8,128)(2,1)S(1)} %get-tuple-element.62), channel_id=1, source_target_pairs={{4,0},{6,2},{8,4},{10,6},{12,8},{14,10},{5,1},{7,3},{9,5},{11,7},{... | collective-permute-start | bytes 1572872 | tf_op jit(solution)/shard_map/ppermute | solution.py:244
  35.4 1.1 %shard_map.80 = (bf16[1024,128]{1,0:T(8,128)(2,1)S(1)}, bf16[1024,128]{1,0:T(8,128)(2,1)S(1)}, f32[1024,256]{1,0:T(8,128)S(1)}) custom-call(s32[2]{0:T(128)S(1)} %pad_add_fusion.ids_ref, bf16[1024,256]{1,0:T(8,128)(2,1)S(1)} %get-tuple-element.48.refs_3_.refs_0_.refs_5_, bf16[1024,256]{1,0:T(8,128)(2,1)S(1)} %get-tuple-element.53.refs_1_.refs_8_, ...), custom_call_target="tpu_custom_call" | custom-call | flops 1 | bytes 1 | tf_op jit(solution)/shard_map/pallas_call | solution.py:53
  36.5 0.0 collective-permute-done.5.refs_2_
  36.5 8.6 %collective-permute-done.4.refs_0_ = bf16[1024,256]{1,0:T(8,128)(2,1)S(1)} collective-permute-done((bf16[1024,256]{1,0:T(8,128)(2,1)S(1)}, bf16[1024,256]{1,0:T(8,128)(2,1)S(1)}, u32[]{:S(2)}, u32[]{:S(2)}) %collective-permute-start.4) | collective-permute-done | bytes 524320 | tf_op jit(solution)/shard_map/ppermute | solution.py:244
  45.2 2.1 %shard_map.81.refs_4_ = f32[1024,256]{1,0:T(8,128)S(1)} custom-call(s32[2]{0:T(128)S(1)} %pad_add_fusion.ids_ref, bf16[1024,256]{1,0:T(8,128)(2,1)S(1)} %collective-permute-done.4.refs_0_, bf16[1024,256]{1,0:T(8,128)(2,1)S(1)} %get-tuple-element.50.refs_4_.refs_1_.refs_0_, bf16[1024,256]{1,0:T(8,128)(2,1)S(1)} %collective-permute-done.5.refs_2_, ...), custom_call_target="tpu_custom_call" | custom-call | flops 1 | bytes 1 | tf_op jit(solution)/shard_map/pallas_call | solution.py:53
  47.3 0.0 collective-permute-done.3.refs_1_
  47.3 3.5 %shard_map.82 = (bf16[1024,512]{1,0:T(8,128)(2,1)S(1)}, bf16[1024,256]{1,0:T(8,128)(2,1)S(1)}, bf16[1024,128]{1,0:T(8,128)(2,1)S(1)}, bf16[1024,128]{1,0:T(8,128...) custom-call(s32[2]{0:T(128)S(1)} %pad_add_fusion.ids_ref, ...), custom_call_target="tpu_custom_call" | custom-call | flops 1 | bytes 1 | tf_op jit(solution)/shard_map/pallas_call | solution.py:53
  50.8 2.1 %shard_map.83 = (f32[1280,128]{1,0:T(8,128)S(1)}, bf16[1280,128]{1,0:T(8,128)(2,1)S(1)}) custom-call(s32[2]{0:T(128)S(1)} %pad_add_fusion.ids_ref, bf16[1024,256]{1,0:T(8,128)(2,1)S(1)} %get-tuple-element.50.refs_4_.refs_1_.refs_0_, bf16[1024,256]{1,0:T(8,128)(2,1)S(1)} %collective-permute-done.3.refs_1_, bf16[1024,512]{1,0:T(8,128)(2,1)S(1)} %get-tuple-element.66.refs_2_, ...), custom_call_target="tpu_custom_call" | custom-call | flops 1 | bytes 1 | tf_op jit(solution)/shard_map/pallas_call | solution.py:53
  53.0 0.1 collective-permute-start.10
  53.0 1.6 %collective-permute-done.10.refs_1_ = bf16[1280,128]{1,0:T(8,128)(2,1)S(1)} collective-permute-done((bf16[1280,128]{1,0:T(8,128)(2,1)S(1)}, bf16[1280,128]{1,0:T(8,128)(2,1)S(1)}, u32[]{:S(2)}, u32[]{:S(2)}) %collective-permute-start.10) | collective-permute-done | bytes 327712 | tf_op jit(solution)/shard_map/ppermute | solution.py:254
  54.6 0.6 shard_map.84
  55.3 1.0 shard_map.85.refs_6_
  56.3 1.5 %collective-permute-start.11 = (bf16[1024,256]{1,0:T(8,128)(2,1)S(1)}, bf16[1024,256]{1,0:T(8,128)(2,1)S(1)}, u32[]{:S(2)}, u32[]{:S(2)}) collective-permute-start(bf16[1024,256]{1,0:T(8,128)(2,1)S(1)} %shard_map.85.refs_6_), channel_id=1, source_target_pairs={{2,0},{4,2},{6,4},{8,6},{10,8},{12,10},{14,12},{3,1},{5,3},{7,5},{... | collective-permute-start | bytes 1572872 | tf_op jit(solution)/shard_map/ppermute | solution.py:244
  57.8 0.0 collective-permute-done.9.refs_1_
  57.8 1.9 %shard_map.86 = (bf16[1024,128]{1,0:T(8,128)(2,1)S(1)}, bf16[1024,128]{1,0:T(8,128)(2,1)S(1)}, bf16[1024,256]{1,0:T(8,128)(2,1)S(1)}, bf16[1024,512]{1,0:T(8,128)(2,1)S(1)}, f32[1024,256]{1,0:T(8,128)S(1)}) custom-call(s32[2]{0:T(128)S(1)} %pad_add_fusion.ids_ref, f32[1024,256]{1,0:T(8,128)S(1)} %get-tuple-element.56.refs_5_.refs_0_, ...), custom_call_target="tpu_custom_call" | custom-call | flops 1 | bytes 1 | tf_op jit(solution)/shard_map/pallas_call | solution.py:53
  59.7 2.1 %shard_map.90 = (f32[1280,128]{1,0:T(8,128)S(1)}, bf16[1280,128]{1,0:T(8,128)(2,1)S(1)}) custom-call(s32[2]{0:T(128)S(1)} %pad_add_fusion.ids_ref, bf16[1024,256]{1,0:T(8,128)(2,1)S(1)} %get-tuple-element.46.refs_1_.refs_0_.refs_6_, bf16[1024,256]{1,0:T(8,128)(2,1)S(1)} %collective-permute-done.1.refs_1_, ...), custom_call_target="tpu_custom_call" | custom-call | flops 1 | bytes 1 | tf_op jit(solution)/shard_map/pallas_call | solution.py:53
  61.8 0.2 collective-permute-start.14
  62.0 2.6 %collective-permute-start.19 = (bf16[640,128]{1,0:T(8,128)(2,1)S(1)}, bf16[640,128]{1,0:T(8,128)(2,1)S(1)}, u32[]{:S(2)}, u32[]{:S(2)}) collective-permute-start(bf16[640,128]{1,0:T(8,128)(2,1)S(1)} %get-tuple-element.71.refs_3_), channel_id=1, source_target_pairs={{0,2},{2,0},{4,6},{6,4},{8,10},{10,8},{12,14},{14,12},{1,3},{3,1},... | collective-permute-start | bytes 491528 | tf_op jit(solution)/shard_map/ppermute | solution.py:250
  64.6 0.6 shard_map.91
  65.3 1.6 %collective-permute-start.15 = (bf16[640,128]{1,0:T(8,128)(2,1)S(1)}, bf16[640,128]{1,0:T(8,128)(2,1)S(1)}, u32[]{:S(2)}, u32[]{:S(2)}) collective-permute-start(bf16[640,128]{1,0:T(8,128)(2,1)S(1)} %get-tuple-element.85), channel_id=1, source_target_pairs={{0,2},{2,0},{4,6},{6,4},{8,10},{10,8},{12,14},{14,12},{1,3},{3,1},... | collective-permute-start | bytes 491528 | tf_op jit(solution)/shard_map/ppermute | solution.py:250
  66.9 9.6 %collective-permute-done.19.refs_1_ = bf16[640,128]{1,0:T(8,128)(2,1)S(1)} collective-permute-done((bf16[640,128]{1,0:T(8,128)(2,1)S(1)}, bf16[640,128]{1,0:T(8,128)(2,1)S(1)}, u32[]{:S(2)}, u32[]{:S(2)}) %collective-permute-start.19) | collective-permute-done | bytes 163872 | tf_op jit(solution)/shard_map/ppermute | solution.py:250
  76.5 0.6 shard_map.93
  77.1 1.6 %collective-permute-start.20 = (bf16[640,128]{1,0:T(8,128)(2,1)S(1)}, bf16[640,128]{1,0:T(8,128)(2,1)S(1)}, u32[]{:S(2)}, u32[]{:S(2)}) collective-permute-start(bf16[640,128]{1,0:T(8,128)(2,1)S(1)} %shard_map.93), channel_id=1, source_target_pairs={{0,4},{2,6},{4,0},{6,2},{8,12},{10,14},{12,8},{14,10},{1,5},{3,7},... | collective-permute-start | bytes 491528 | tf_op jit(solution)/shard_map/ppermute | solution.py:250
  78.7 0.5 collective-permute-start.7
  79.2 0.0 collective-permute-done.11.refs_1_
  79.2 0.0 collective-permute-start.12
  79.2 0.7 shard_map.87
  79.9 0.0 collective-permute-done.15.refs_1_
  79.9 0.6 shard_map.92
  80.5 0.9 collective-permute-start.16
  81.4 1.0 collective-permute-done.20
  82.5 2.6 %collective-permute-start.21 = (bf16[640,128]{1,0:T(8,128)(2,1)S(1)}, bf16[640,128]{1,0:T(8,128)(2,1)S(1)}, u32[]{:S(2)}, u32[]{:S(2)}) collective-permute-start(bf16[640,128]{1,0:T(8,128)(2,1)S(1)} %reduce-precision_convert_fusion.1), channel_id=1, source_target_pairs={{0,8},{2,10},{4,12},{6,14},{8,0},{10,2},{12,4},{14,6},{1,9},{3,11}... | collective-permute-start | bytes 491528 | tf_op jit(solution)/shard_map/ppermute | solution.py:250
  85.1 4.8 %collective-permute-done.16 = bf16[640,128]{1,0:T(8,128)(2,1)S(1)} collective-permute-done((bf16[640,128]{1,0:T(8,128)(2,1)S(1)}, bf16[640,128]{1,0:T(8,128)(2,1)S(1)}, u32[]{:S(2)}, u32[]{:S(2)}) %collective-permute-start.16) | collective-permute-done | bytes 163872 | tf_op jit(solution)/shard_map/ppermute | solution.py:250
  90.0 0.1 collective-permute-start.17
  90.2 2.1 %collective-permute-done.21 = bf16[640,128]{1,0:T(8,128)(2,1)S(1)} collective-permute-done((bf16[640,128]{1,0:T(8,128)(2,1)S(1)}, bf16[640,128]{1,0:T(8,128)(2,1)S(1)}, u32[]{:S(2)}, u32[]{:S(2)}) %collective-permute-start.21) | collective-permute-done | bytes 163872 | tf_op jit(solution)/shard_map/ppermute | solution.py:250
  92.3 7.3 %collective-permute-start.22 = (bf16[640,128]{1,0:T(8,128)(2,1)S(1)}, bf16[640,128]{1,0:T(8,128)(2,1)S(1)}, u32[]{:S(2)}, u32[]{:S(2)}) collective-permute-start(bf16[640,128]{1,0:T(8,128)(2,1)S(1)} %reduce-precision_convert_fusion.refs_2_), channel_id=1, source_target_pairs={{0,2},{2,0},{4,6},{6,4},{8,10},{10,8},{12,14},{14,12},{1,3},{3,1},... | collective-permute-start | bytes 491528 | tf_op jit(solution)/shard_map/ppermute | solution.py:250
  99.6 0.0 collective-permute-done.17
  99.7 0.0 collective-permute-start.13
  99.7 0.0 collective-permute-done.8.refs_3_
  99.7 2.2 %collective-permute-start.18 = (bf16[640,128]{1,0:T(8,128)(2,1)S(1)}, bf16[640,128]{1,0:T(8,128)(2,1)S(1)}, u32[]{:S(2)}, u32[]{:S(2)}) collective-permute-start(bf16[640,128]{1,0:T(8,128)(2,1)S(1)} %reduce-precision_convert_fusion.2.refs_0_), channel_id=1, source_target_pairs={{0,2},{2,0},{4,6},{6,4},{8,10},{10,8},{12,14},{14,12},{1,3},{3,1},... | collective-permute-start | bytes 491528 | tf_op jit(solution)/shard_map/ppermute | solution.py:250
  101.9 1.6 %shard_map.88 = bf16[4096,128]{1,0:T(8,128)(2,1)} custom-call(s32[2]{0:T(128)S(1)} %pad_add_fusion.ids_ref, bf16[1024,128]{1,0:T(8,128)(2,1)S(1)} %get-tuple-element.58.refs_0_, bf16[1024,128]{1,0:T(8,128)(2,1)S(1)} %collective-permute-done.7.refs_1_, bf16[1024,128]{1,0:T(8,128)(2,1)S(1)} %get-tuple-element.60.refs_2_, ...), custom_call_target="tpu_custom_call" | custom-call | flops 1 | bytes 1 | tf_op jit(solution)/shard_map/pallas_call | solution.py:53
  103.5 1.6 %shard_map.89 = bf16[4096,128]{1,0:T(8,128)(2,1)} custom-call(s32[2]{0:T(128)S(1)} %pad_add_fusion.ids_ref, bf16[1024,128]{1,0:T(8,128)(2,1)S(1)} %get-tuple-element.74.refs_0_, bf16[1024,128]{1,0:T(8,128)(2,1)S(1)} %collective-permute-done.12.refs_1_, bf16[1024,128]{1,0:T(8,128)(2,1)S(1)} %get-tuple-element.73.refs_4_.refs_2_, ...), custom_call_target="tpu_custom_call" | custom-call | flops 1 | bytes 1 | tf_op jit(solution)/shard_map/pallas_call | solution.py:53
  105.1 0.0 collective-permute-done.22.refs_3_
  105.1 1.7 %collective-permute-done.18.refs_1_ = bf16[640,128]{1,0:T(8,128)(2,1)S(1)} collective-permute-done((bf16[640,128]{1,0:T(8,128)(2,1)S(1)}, bf16[640,128]{1,0:T(8,128)(2,1)S(1)}, u32[]{:S(2)}, u32[]{:S(2)}) %collective-permute-start.18) | collective-permute-done | bytes 163872 | tf_op jit(solution)/shard_map/ppermute | solution.py:250
  106.8 1.8 %shard_map.94 = (f32[2048,128]{1,0:T(8,128)}, f32[512,128]{1,0:T(8,128)}) custom-call(s32[2]{0:T(128)S(1)} %pad_add_fusion.ids_ref, bf16[640,128]{1,0:T(8,128)(2,1)S(1)} %reduce-precision_convert_fusion.2.refs_0_, bf16[640,128]{1,0:T(8,128)(2,1)S(1)} %collective-permute-done.18.refs_1_, bf16[640,128]{1,0:T(8,128)(2,1)S(1)} %reduce-precision_convert_fusion.refs_2_, ...), custom_call_target="tpu_custom_call" | custom-call | flops 1 | bytes 1 | tf_op jit(solution)/shard_map/pallas_call | solution.py:53
  (14 shorter events, 0.2 us)
Async XLA Ops:
  0.6 3.9 %copy-start.2 = (bf16[4096,128]{1,0:T(8,128)(2,1)S(1)}, bf16[4096,128]{1,0:T(8,128)(2,1)}, u32[]{:S(2)}) copy-start(bf16[4096,128]{1,0:T(8,128)(2,1)} %refs_0_.2) | copy-start | bytes 3145732
  0.6 3.8 %collective-permute-start = (bf16[4096,128]{1,0:T(8,128)(2,1)}, bf16[4096,128]{1,0:T(8,128)(2,1)}, u32[]{:S(2)}, u32[]{:S(2)}) collective-permute-start(bf16[4096,128]{1,0:T(8,128)(2,1)} %refs_0_.2), channel_id=1, source_target_pairs={{0,1},{1,0},{2,3},{3,2},{4,5},{5,4},{6,7},{7,6},{8,9},{9,8},{10,11... | collective-permute-start | bytes 3145736 | tf_op jit(solution)/shard_map/ppermute | solution.py:254
  1.2 15.0 %collective-permute-start.2 = (bf16[4096,128]{1,0:T(8,128)(2,1)}, bf16[4096,128]{1,0:T(8,128)(2,1)S(1)}, u32[]{:S(2)}, u32[]{:S(2)}) collective-permute-start(bf16[4096,128]{1,0:T(8,128)(2,1)} %refs_0_.3), channel_id=1, source_target_pairs={{0,1},{1,0},{2,3},{3,2},{4,5},{5,4},{6,7},{7,6},{8,9},{9,8},{10,11... | collective-permute-start | bytes 3145736 | tf_op jit(solution)/shard_map/ppermute | solution.py:254
  3.0 7.7 %copy-start = (bf16[2,256,256]{2,1,0:T(8,128)(2,1)S(1)}, bf16[2,256,256]{2,1,0:T(8,128)(2,1)}, u32[]{:S(2)}) copy-start(bf16[2,256,256]{2,1,0:T(8,128)(2,1)} %refs_5_.3) | copy-start | bytes 786436
  3.1 13.0 %copy-start.1 = (bf16[4096,128]{1,0:T(8,128)(2,1)S(1)}, bf16[4096,128]{1,0:T(8,128)(2,1)}, u32[]{:S(2)}) copy-start(bf16[4096,128]{1,0:T(8,128)(2,1)} %refs_0_.3) | copy-start | bytes 3145732
  5.9 16.3 %collective-permute-start.1 = (bf16[1024,256]{1,0:T(8,128)(2,1)S(1)}, bf16[1024,256]{1,0:T(8,128)(2,1)S(1)}, u32[]{:S(2)}, u32[]{:S(2)}) collective-permute-start(bf16[1024,256]{1,0:T(8,128)(2,1)S(1)} %get-tuple-element.47.refs_0_.refs_5_), channel_id=1, source_target_pairs={{0,2},{2,4},{4,6},{6,8},{8,10},{10,12},{12,14},{1,3},{3,5},{5,7},{... | collective-permute-start | bytes 1572872 | tf_op jit(solution)/shard_map/ppermute | solution.py:244
  12.6 19.5 %collective-permute-start.6 = (bf16[1024,256]{1,0:T(8,128)(2,1)S(1)}, bf16[1024,256]{1,0:T(8,128)(2,1)S(1)}, u32[]{:S(2)}, u32[]{:S(2)}) collective-permute-start(bf16[1024,256]{1,0:T(8,128)(2,1)S(1)} %get-tuple-element.48.refs_3_.refs_0_.refs_5_), channel_id=1, source_target_pairs={{0,4},{2,6},{4,8},{6,10},{8,12},{10,14},{1,5},{3,7},{5,9},{7,11},{... | collective-permute-start | bytes 1572872 | tf_op jit(solution)/shard_map/ppermute | solution.py:244
  17.2 19.3 %collective-permute-start.5 = (bf16[1024,256]{1,0:T(8,128)(2,1)S(1)}, bf16[1024,256]{1,0:T(8,128)(2,1)S(1)}, u32[]{:S(2)}, u32[]{:S(2)}) collective-permute-start(bf16[1024,256]{1,0:T(8,128)(2,1)S(1)} %get-tuple-element.49.refs_4_.refs_2_), channel_id=1, source_target_pairs={{4,0},{6,2},{8,4},{10,6},{12,8},{14,10},{5,1},{7,3},{9,5},{11,7},{... | collective-permute-start | bytes 1572872 | tf_op jit(solution)/shard_map/ppermute | solution.py:244
  24.0 21.1 %collective-permute-start.4 = (bf16[1024,256]{1,0:T(8,128)(2,1)S(1)}, bf16[1024,256]{1,0:T(8,128)(2,1)S(1)}, u32[]{:S(2)}, u32[]{:S(2)}) collective-permute-start(bf16[1024,256]{1,0:T(8,128)(2,1)S(1)} %get-tuple-element.50.refs_4_.refs_1_.refs_0_), channel_id=1, source_target_pairs={{4,0},{6,2},{8,4},{10,6},{12,8},{14,10},{5,1},{7,3},{9,5},{11,7},{... | collective-permute-start | bytes 1572872 | tf_op jit(solution)/shard_map/ppermute | solution.py:244
  25.3 21.9 %collective-permute-start.3 = (bf16[1024,256]{1,0:T(8,128)(2,1)S(1)}, bf16[1024,256]{1,0:T(8,128)(2,1)S(1)}, u32[]{:S(2)}, u32[]{:S(2)}) collective-permute-start(bf16[1024,256]{1,0:T(8,128)(2,1)S(1)} %get-tuple-element.50.refs_4_.refs_1_.refs_0_), channel_id=1, source_target_pairs={{0,4},{2,6},{4,8},{6,10},{8,12},{10,14},{1,5},{3,7},{5,9},{7,11},{... | collective-permute-start | bytes 1572872 | tf_op jit(solution)/shard_map/ppermute | solution.py:244
  34.1 23.7 %collective-permute-start.9 = (bf16[1024,256]{1,0:T(8,128)(2,1)S(1)}, bf16[1024,256]{1,0:T(8,128)(2,1)S(1)}, u32[]{:S(2)}, u32[]{:S(2)}) collective-permute-start(bf16[1024,256]{1,0:T(8,128)(2,1)S(1)} %get-tuple-element.62), channel_id=1, source_target_pairs={{4,0},{6,2},{8,4},{10,6},{12,8},{14,10},{5,1},{7,3},{9,5},{11,7},{... | collective-permute-start | bytes 1572872 | tf_op jit(solution)/shard_map/ppermute | solution.py:244
  53.0 1.7 %collective-permute-start.10 = (bf16[1280,128]{1,0:T(8,128)(2,1)S(1)}, bf16[1280,128]{1,0:T(8,128)(2,1)S(1)}, u32[]{:S(2)}, u32[]{:S(2)}) collective-permute-start(bf16[1280,128]{1,0:T(8,128)(2,1)S(1)} %get-tuple-element.69), channel_id=1, source_target_pairs={{0,1},{1,0},{2,3},{3,2},{4,5},{5,4},{6,7},{7,6},{8,9},{9,8},{10,11... | collective-permute-start | bytes 983048 | tf_op jit(solution)/shard_map/ppermute | solution.py:254
  56.3 22.9 %collective-permute-start.11 = (bf16[1024,256]{1,0:T(8,128)(2,1)S(1)}, bf16[1024,256]{1,0:T(8,128)(2,1)S(1)}, u32[]{:S(2)}, u32[]{:S(2)}) collective-permute-start(bf16[1024,256]{1,0:T(8,128)(2,1)S(1)} %shard_map.85.refs_6_), channel_id=1, source_target_pairs={{2,0},{4,2},{6,4},{8,6},{10,8},{12,10},{14,12},{3,1},{5,3},{7,5},{... | collective-permute-start | bytes 1572872 | tf_op jit(solution)/shard_map/ppermute | solution.py:244
  61.8 2.8 %collective-permute-start.14 = (bf16[1280,128]{1,0:T(8,128)(2,1)S(1)}, bf16[1280,128]{1,0:T(8,128)(2,1)S(1)}, u32[]{:S(2)}, u32[]{:S(2)}) collective-permute-start(bf16[1280,128]{1,0:T(8,128)(2,1)S(1)} %get-tuple-element.83), channel_id=1, source_target_pairs={{0,1},{1,0},{2,3},{3,2},{4,5},{5,4},{6,7},{7,6},{8,9},{9,8},{10,11... | collective-permute-start | bytes 983048 | tf_op jit(solution)/shard_map/ppermute | solution.py:254
  62.0 14.5 %collective-permute-start.19 = (bf16[640,128]{1,0:T(8,128)(2,1)S(1)}, bf16[640,128]{1,0:T(8,128)(2,1)S(1)}, u32[]{:S(2)}, u32[]{:S(2)}) collective-permute-start(bf16[640,128]{1,0:T(8,128)(2,1)S(1)} %get-tuple-element.71.refs_3_), channel_id=1, source_target_pairs={{0,2},{2,0},{4,6},{6,4},{8,10},{10,8},{12,14},{14,12},{1,3},{3,1},... | collective-permute-start | bytes 491528 | tf_op jit(solution)/shard_map/ppermute | solution.py:250
  65.3 14.6 %collective-permute-start.15 = (bf16[640,128]{1,0:T(8,128)(2,1)S(1)}, bf16[640,128]{1,0:T(8,128)(2,1)S(1)}, u32[]{:S(2)}, u32[]{:S(2)}) collective-permute-start(bf16[640,128]{1,0:T(8,128)(2,1)S(1)} %get-tuple-element.85), channel_id=1, source_target_pairs={{0,2},{2,0},{4,6},{6,4},{8,10},{10,8},{12,14},{14,12},{1,3},{3,1},... | collective-permute-start | bytes 491528 | tf_op jit(solution)/shard_map/ppermute | solution.py:250
  77.1 5.4 %collective-permute-start.20 = (bf16[640,128]{1,0:T(8,128)(2,1)S(1)}, bf16[640,128]{1,0:T(8,128)(2,1)S(1)}, u32[]{:S(2)}, u32[]{:S(2)}) collective-permute-start(bf16[640,128]{1,0:T(8,128)(2,1)S(1)} %shard_map.93), channel_id=1, source_target_pairs={{0,4},{2,6},{4,0},{6,2},{8,12},{10,14},{12,8},{14,10},{1,5},{3,7},... | collective-permute-start | bytes 491528 | tf_op jit(solution)/shard_map/ppermute | solution.py:250
  78.7 21.0 %collective-permute-start.8 = (bf16[1024,128]{1,0:T(8,128)(2,1)S(1)}, bf16[1024,128]{1,0:T(8,128)(2,1)S(1)}, u32[]{:S(2)}, u32[]{:S(2)}) collective-permute-start(bf16[1024,128]{1,0:T(8,128)(2,1)S(1)} %get-tuple-element.61), channel_id=1, source_target_pairs={{0,1},{1,0},{2,3},{3,2},{4,5},{5,4},{6,7},{7,6},{8,9},{9,8},{10,11... | collective-permute-start | bytes 786440 | tf_op jit(solution)/shard_map/ppermute | solution.py:254
  78.7 23.2 %collective-permute-start.7 = (bf16[1024,128]{1,0:T(8,128)(2,1)S(1)}, bf16[1024,128]{1,0:T(8,128)(2,1)S(1)}, u32[]{:S(2)}, u32[]{:S(2)}) collective-permute-start(bf16[1024,128]{1,0:T(8,128)(2,1)S(1)} %get-tuple-element.59), channel_id=1, source_target_pairs={{0,1},{1,0},{2,3},{3,2},{4,5},{5,4},{6,7},{7,6},{8,9},{9,8},{10,11... | collective-permute-start | bytes 786440 | tf_op jit(solution)/shard_map/ppermute | solution.py:254
  79.2 24.3 %collective-permute-start.12 = (bf16[1024,128]{1,0:T(8,128)(2,1)S(1)}, bf16[1024,128]{1,0:T(8,128)(2,1)S(1)}, u32[]{:S(2)}, u32[]{:S(2)}) collective-permute-start(bf16[1024,128]{1,0:T(8,128)(2,1)S(1)} %get-tuple-element.75), channel_id=1, source_target_pairs={{0,1},{1,0},{2,3},{3,2},{4,5},{5,4},{6,7},{7,6},{8,9},{9,8},{10,11... | collective-permute-start | bytes 786440 | tf_op jit(solution)/shard_map/ppermute | solution.py:254
  80.5 9.5 %collective-permute-start.16 = (bf16[640,128]{1,0:T(8,128)(2,1)S(1)}, bf16[640,128]{1,0:T(8,128)(2,1)S(1)}, u32[]{:S(2)}, u32[]{:S(2)}) collective-permute-start(bf16[640,128]{1,0:T(8,128)(2,1)S(1)} %shard_map.92), channel_id=1, source_target_pairs={{0,4},{2,6},{4,0},{6,2},{8,12},{10,14},{12,8},{14,10},{1,5},{3,7},... | collective-permute-start | bytes 491528 | tf_op jit(solution)/shard_map/ppermute | solution.py:250
  82.5 9.8 %collective-permute-start.21 = (bf16[640,128]{1,0:T(8,128)(2,1)S(1)}, bf16[640,128]{1,0:T(8,128)(2,1)S(1)}, u32[]{:S(2)}, u32[]{:S(2)}) collective-permute-start(bf16[640,128]{1,0:T(8,128)(2,1)S(1)} %reduce-precision_convert_fusion.1), channel_id=1, source_target_pairs={{0,8},{2,10},{4,12},{6,14},{8,0},{10,2},{12,4},{14,6},{1,9},{3,11}... | collective-permute-start | bytes 491528 | tf_op jit(solution)/shard_map/ppermute | solution.py:250
  90.0 9.6 %collective-permute-start.17 = (bf16[640,128]{1,0:T(8,128)(2,1)S(1)}, bf16[640,128]{1,0:T(8,128)(2,1)S(1)}, u32[]{:S(2)}, u32[]{:S(2)}) collective-permute-start(bf16[640,128]{1,0:T(8,128)(2,1)S(1)} %reduce-precision_convert_fusion.3), channel_id=1, source_target_pairs={{0,8},{2,10},{4,12},{6,14},{8,0},{10,2},{12,4},{14,6},{1,9},{3,11}... | collective-permute-start | bytes 491528 | tf_op jit(solution)/shard_map/ppermute | solution.py:250
  92.3 12.8 %collective-permute-start.22 = (bf16[640,128]{1,0:T(8,128)(2,1)S(1)}, bf16[640,128]{1,0:T(8,128)(2,1)S(1)}, u32[]{:S(2)}, u32[]{:S(2)}) collective-permute-start(bf16[640,128]{1,0:T(8,128)(2,1)S(1)} %reduce-precision_convert_fusion.refs_2_), channel_id=1, source_target_pairs={{0,2},{2,0},{4,6},{6,4},{8,10},{10,8},{12,14},{14,12},{1,3},{3,1},... | collective-permute-start | bytes 491528 | tf_op jit(solution)/shard_map/ppermute | solution.py:250
  99.7 3.9 %collective-permute-start.13 = (bf16[1024,128]{1,0:T(8,128)(2,1)S(1)}, bf16[1024,128]{1,0:T(8,128)(2,1)S(1)}, u32[]{:S(2)}, u32[]{:S(2)}) collective-permute-start(bf16[1024,128]{1,0:T(8,128)(2,1)S(1)} %get-tuple-element.76), channel_id=1, source_target_pairs={{0,1},{1,0},{2,3},{3,2},{4,5},{5,4},{6,7},{7,6},{8,9},{9,8},{10,11... | collective-permute-start | bytes 786440 | tf_op jit(solution)/shard_map/ppermute | solution.py:254
  99.7 7.1 %collective-permute-start.18 = (bf16[640,128]{1,0:T(8,128)(2,1)S(1)}, bf16[640,128]{1,0:T(8,128)(2,1)S(1)}, u32[]{:S(2)}, u32[]{:S(2)}) collective-permute-start(bf16[640,128]{1,0:T(8,128)(2,1)S(1)} %reduce-precision_convert_fusion.2.refs_0_), channel_id=1, source_target_pairs={{0,2},{2,0},{4,6},{6,4},{8,10},{10,8},{12,14},{14,12},{1,3},{3,1},... | collective-permute-start | bytes 491528 | tf_op jit(solution)/shard_map/ppermute | solution.py:250

commit v4 on v3

--- a/solution.py
+++ b/solution.py
@@ -44,23 +44,27 @@
     return [pl.ds(r, CHUNK) for r in range(0, ref.shape[0], CHUNK)]
 
 
+class Place:
+    def __getitem__(self, axis):
+        return lax.axis_index(("chan", "tm")[axis])
+
+
 def run(body, ids, ins, outs, scratch=(), after=()):
     count = len(ins)
 
-    def kernel(ids_ref, *refs):
-        body(ids_ref, *refs[:count], *refs[count + len(after) :])
+    def kernel(*refs):
+        body(ids, *refs[:count], *refs[count + len(after) :])
 
     return pl.pallas_call(
         kernel,
-        in_specs=[pl.BlockSpec(memory_space=pltpu.SMEM)]
-        + [pl.BlockSpec(memory_space=pltpu.VMEM)] * count
+        in_specs=[pl.BlockSpec(memory_space=pltpu.VMEM)] * count
         + [pl.BlockSpec(memory_space=pl.ANY)] * len(after),
         out_specs=[pl.BlockSpec(memory_space=pltpu.VMEM)] * len(outs),
         out_shape=[jax.ShapeDtypeStruct(shape, kind) for shape, kind in outs],
         scratch_shapes=list(scratch),
         compiler_params=pltpu.CompilerParams(vmem_limit_bytes=VMEM_LIMIT),
         cost_estimate=pl.CostEstimate(flops=1, bytes_accessed=1, transcendentals=0),
-    )(ids, *ins, *after)
+    )(*ins, *after)
 
 
 def gated(x, delayed, taps, layer):
@@ -72,7 +76,7 @@
     return hidden, gate * (1.0 - filt * filt), filt * gate * (1.0 - gate)
 
 
-def join_body(ids, own, other, a_o, b_o):
+def gather_body(ids, own, other, a_o, b_o):
     core = ids[0]
     count = a_o.shape[0]
     for half, out in ((0, a_o), (1, b_o)):
@@ -82,7 +86,7 @@
 
 
 def cot_body(ids, own, other, wo, a_o, b_o, ha_o, hb_o):
-    join_body(ids, own, other, a_o, b_o)
+    gather_body(ids, own, other, a_o, b_o)
     for g_r, h_r in ((a_o, ha_o), (b_o, hb_o)):
         for rows in chunks(g_r):
             h_r[rows, :] = mm_t(g_r[rows, :], wo[1])
@@ -137,11 +141,6 @@
     return pre
 
 
-def past_body(ids, pre_r, taps, past_o):
-    for rows in chunks(pre_r):
-        past_o[rows, :] = mm_t(pre_r[rows, :], taps[0, 1]).astype(BF)
-
-
 def third_body(ids, local_r, arrived_r, slope_r, now_a, taps, wo, keep_o, send_o, *outs):
     for rows in chunks(local_r):
         g = (local_r[rows, :] + arrived_r[rows, :].astype(F32)).astype(BF)
@@ -152,7 +151,7 @@
 
 
 def both_body(ids, x_r, d_r, g_r, hg_r, term_r, slope_r, taps, wo, *outs):
-    pre1_o, hid_o, keep_o, send_o = outs[:4]
+    past_o, pre1_o, hid_o, keep_o, send_o = outs[:5]
     for rows in chunks(x_r):
         x = x_r[rows, :]
         hidden, sf, sg = gated(x, d_r[rows, :], taps, 1)
@@ -160,18 +159,21 @@
         pre = pre_grad(hg_r[rows, :], sf, sg)
         pre1_o[rows, :] = pre
         local = g_r[rows, :].astype(F32) + mm_t(pre, taps[1, 0])
-        third_rows(rows, (local + term_r[rows, :]).astype(BF), slope_r, taps, wo, *outs[4:])
+        g = (local + term_r[rows, :]).astype(BF)
+        pre = third_rows(rows, g, slope_r, taps, wo, *outs[5:])
+        past_o[rows, :] = mm_t(pre, taps[0, 1]).astype(BF)
         out = (x.astype(F32) + mm(hidden, wo[1])).astype(BF)
         keep, send = halves(ids[0], out)
         keep_o[rows, :] = keep
         send_o[rows, :] = send
 
 
-def last_body(ids, now_r, past_r, keep_o, send_o):
+def last_body(size, ids, now_r, past_r, keep_o, send_o):
+    ended = ids[1] == size - 1
     for rows in chunks(now_r):
-        keep, send = halves(
-            ids[0], (now_r[rows, :] + past_r[rows, :].astype(F32)).astype(BF)
-        )
+        past = past_r[rows, :].astype(F32)
+        past = jnp.where(ended, jnp.zeros_like(past), past)
+        keep, send = halves(ids[0], (now_r[rows, :] + past).astype(BF))
         keep_o[rows, :] = keep
         send_o[rows, :] = send
 
@@ -215,24 +217,63 @@
             total[rows, :] = value
 
 
+def side(ids, step):
+    return (ids[1] // (1 << step)) % 2
+
+
+def parted(ids, step, values, own_o, send_o):
+    count = own_o.shape[0]
+    own = side(ids, step)
+    own_o[...] = values(pl.ds(pl.multiple_of(own * count, count), count))
+    send_o[...] = values(pl.ds(pl.multiple_of((1 - own) * count, count), count)).astype(BF)
+
+
 def split_body(ids, keep, got, own_o, send_o, total):
     gather_sums(keep, got, total)
-    rows = own_o.shape[0]
-    side = ids[1] % 2
-    own_o[...] = total[pl.ds(pl.multiple_of(side * rows, rows), rows), :]
-    send_o[...] = total[pl.ds(pl.multiple_of((1 - side) * rows, rows), rows), :].astype(BF)
-
-
-def place_body(ids, own0, got0, own1, got1, conv_o, out_o, total):
-    rows = own0.shape[0]
+    parted(ids, 0, lambda rows: total[rows, :], own_o, send_o)
+
+
+def part_body(step, ids, own, got, own_o, send_o):
+    parted(
+        ids, step, lambda rows: own[rows, :] + got[rows, :].astype(F32), own_o, send_o
+    )
+
+
+def add_body(ids, own, got, total_o):
+    total_o[...] = (own[...].astype(F32) + got[...].astype(F32)).astype(BF)
+
+
+def join_body(ids, first, second, both_o):
+    rows = first.shape[0]
+    both_o[:rows, :] = first[...]
+    both_o[rows:, :] = second[...]
+
+
+def place_body(cuts, ids, *refs):
+    conv_o, out_o = refs[-2:]
+    pieces = 1 << cuts
+    rows = refs[0].shape[0]
     conv_rows = conv_o.shape[0] // 2
     out_rows = out_o.shape[0] // 2
-    side = ids[1] % 2
-    for layer, (own, got) in enumerate(((own0, got0), (own1, got1))):
-        total[pl.ds(pl.multiple_of(side * rows, rows), rows), :] = own[...].astype(F32)
-        total[pl.ds(pl.multiple_of((1 - side) * rows, rows), rows), :] = got[...].astype(F32)
-        conv_o[pl.ds(layer * conv_rows, conv_rows), :] = total[:conv_rows, :]
-        out_o[pl.ds(layer * out_rows, out_rows), :] = total[conv_rows:, :]
+    for layer in (0, 1):
+        held = []
+        for ref in refs[layer * (cuts + 1) : (layer + 1) * (cuts + 1)]:
+            held += [ref[r : r + rows, :] for r in range(0, ref.shape[0], rows)]
+        for bit in range(cuts):
+            swap = side(ids, cuts - 1 - bit) == 1
+            held = [
+                jnp.where(swap, held[i ^ (1 << bit)], held[i]) for i in range(pieces)
+            ]
+        for i in range(pieces):
+            value = held[i].astype(F32)
+            start = i * rows
+            for k in range(0, rows, 64):
+                at = start + k
+                if at < conv_rows:
+                    conv_o[layer * conv_rows + at : layer * conv_rows + at + 64, :] = value[k : k + 64]
+                else:
+                    at += layer * out_rows - conv_rows
+                    out_o[at : at + 64, :] = value[k : k + 64]
 
 
 def plain_body(ids, keep, got, total):
@@ -254,23 +295,17 @@
     return lax.ppermute(values, "chan", [(0, 1), (1, 0)])
 
 
-def rounded(values):
-    return lax.reduce_precision(values, 8, 7).astype(BF)
-
-
-def add_body(ids, own, got, total_o):
-    total_o[...] = (own[...] + got[...].astype(F32)).astype(BF)
-
-
-def two_powers():
+def cuts_of(rows):
     size = lax.axis_size("tm")
-    return size > 1 and not size & (size - 1)
+    if size < 2 or size & (size - 1) or rows % 64:
+        return 0
+    return min(2, size.bit_length() - 1)
 
 
 def split_sums(ids, keep, got, after=()):
     rows, cols = keep.shape
-    if not two_powers():
-        return run(plain_body, ids, [keep, got], [((rows, cols), F32)])
+    if not cuts_of(rows):
+        return run(plain_body, ids, [keep, got], [((rows, cols), F32)], after=after)
     return run(
         split_body,
         ids,
@@ -281,29 +316,48 @@
     )
 
 
-def reduced(ids, parts, after=()):
-    if not two_powers():
-        return (lax.psum(parts[0], "tm"),)
-    own, send = parts
-    (total,) = run(add_body, ids, [own, crossed(send, 1)], [(own.shape, BF)], after=after)
-    bit = 2
-    while bit < lax.axis_size("tm"):
-        total = rounded(total.astype(F32) + crossed(total, bit).astype(F32))
-        bit *= 2
-    return total, crossed(total, 1)
-
-
-def placed_sums(ids, channels, layers):
-    if not two_powers():
-        both = jnp.concatenate(layers[0] + layers[1]).reshape(2, 5 * channels, -1)
+def summed(ids, cuts, step, parts, after):
+    if not cuts:
+        return parts
+    if step < cuts:
+        own, send = parts
+    else:
+        own = send = parts[0]
+    got = crossed(send, 1 << step)
+    rows, cols = own.shape
+    if step + 1 < cuts:
+        return run(
+            functools.partial(part_body, step + 1),
+            ids,
+            [own, got],
+            [((rows // 2, cols), F32), ((rows // 2, cols), BF)],
+            after=after,
+        )
+    return run(add_body, ids, [own, got], [(own.shape, BF)], after=after)
+
+
+def spread(ids, cuts, total, after):
+    held = [total]
+    for step in reversed(range(cuts)):
+        both = held[0]
+        if len(held) > 1:
+            rows, cols = both.shape
+            (both,) = run(join_body, ids, held, [((2 * rows, cols), BF)], after=after)
+        held.append(crossed(both, 1 << step))
+    return held
+
+
+def placed_sums(ids, channels, cuts, sums0, sums1):
+    if not cuts:
+        both = jnp.stack([lax.psum(sums[0], "tm") for sums in (sums0, sums1)])
         return both[:, : 4 * channels], both[:, 4 * channels :]
-    cols = layers[0][0].shape[1]
+    cols = sums0[0].shape[1]
+    late = spread(ids, cuts, sums1[0], [sums0[0]])
     return run(
-        place_body,
-        ids,
-        [array for layer in layers for array in layer],
+        functools.partial(place_body, cuts),
+        ids,
+        spread(ids, cuts, sums0[0], [late[-1]]) + late,
         [((8 * channels, cols), F32), ((2 * channels, cols), F32)],
-        [pltpu.VMEM((5 * channels, cols), F32)],
     )
 
 
@@ -314,7 +368,7 @@
     wide = 2 * channels
     scale = 1.0 / math.sqrt(rows * lax.axis_size("tm"))
     later = 2
-    ids = jnp.stack([lax.axis_index("chan"), lax.axis_index("tm")]).astype(jnp.int32)
+    ids = Place()
     taps = conv_weight.reshape(2, 2, channels, wide)
     wo = out_weight
 
@@ -323,7 +377,7 @@
     third_outs = [(narrow, BF), (broad, BF), (narrow, F32)]
 
     x_a, x_b = run(
-        join_body, ids, [signal, swapped(signal)], [(narrow, BF)] * 2, after=[taps]
+        gather_body, ids, [signal, swapped(signal)], [(narrow, BF)] * 2, after=[taps]
     )
     x_h = moved_by(x_b, 1)
     first_outs = [(narrow, BF)] * 2 + [(broad, F32)]
@@ -366,12 +420,14 @@
         [(narrow, F32)],
         after=[local_b],
     )
-    pre1_a, hid1_a, out_keep_a, out_send_a, g1_a, pre0_a, now_a = run(
+    past_a, pre1_a, hid1_a, out_keep_a, out_send_a, g1_a, pre0_a, now_a = run(
         both_body,
         ids,
         [x1_a, x1_a_past, cot_a, hg_a, term_a, slope_a, taps, wo],
-        [(broad, BF), (narrow, BF), (half, BF), (half, BF)] + third_outs,
-    )
+        [(narrow, BF), (broad, BF), (narrow, BF), (half, BF), (half, BF)] + third_outs,
+    )
+    size = lax.axis_size("tm")
+    ahead_b = lax.ppermute(past_a, "tm", [(i, (i - 1) % size) for i in range(size)])
 
     def weights(arrays, after=()):
         shape = (5 * channels, half_width)
@@ -386,24 +442,26 @@
     keep1, send1 = weights(
         [x1_a, x1_a_past, pre1_a, hid1_a, cot_a, x1_b, x1_b_past, pre1_b, hid1_b, cot_b]
     )
-    parts1 = split_sums(ids, keep1, swapped(send1))
-    (past_a,) = run(past_body, ids, [pre0_a, taps], [(narrow, BF)], after=parts1)
-    ahead_b = moved_by(past_a, -1)
+    steps = max(1, (lax.axis_size("tm") - 1).bit_length())
+    cuts = cuts_of(5 * channels)
     in_keep_a, in_send_a, g1_b, pre0_b, now_b = run(
         third_body,
         ids,
         [local_b, from_next_b, slope_b, now_a, taps, wo],
         [(half, BF)] * 2 + third_outs,
-        after=[past_a],
-    )
+        after=[keep1],
+    )
+    sums1 = split_sums(ids, keep1, swapped(send1), after=[now_b])
     keep0, send0 = weights(
-        [x_a, x_h, pre0_a, hid0_a, g1_a, x_b, x_a, pre0_b, hid0_b, g1_b]
-    )
-    parts0 = split_sums(ids, keep0, swapped(send0))
-    sums1 = reduced(ids, parts1, after=[keep0])
-    in_keep_b, in_send_b = run(last_body, ids, [now_b, ahead_b], [(half, BF)] * 2)
-    sums0 = reduced(ids, parts0, after=[in_keep_b])
-    conv_grad, out_grad = placed_sums(ids, channels, [sums0, sums1])
+        [x_a, x_h, pre0_a, hid0_a, g1_a, x_b, x_a, pre0_b, hid0_b, g1_b], after=sums1
+    )
+    sums0 = split_sums(ids, keep0, swapped(send0))
+    sums1 = summed(ids, cuts, 0, sums1, sums0)
+    in_keep_b, in_send_b = run(functools.partial(last_body, size), ids, [now_b, ahead_b], [(half, BF)] * 2, after=sums1)
+    sums0 = summed(ids, cuts, 0, sums0, [in_keep_b])
+    for step in range(1, steps):
+        sums1 = summed(ids, cuts, step, sums1, sums0)
+        sums0 = summed(ids, cuts, step, sums0, sums1)
     (output,) = run(
         assemble_body,
         ids,
@@ -411,6 +469,7 @@
         [((rows, half_width), BF)],
         after=[in_keep_b],
     )
+    conv_grad, out_grad = placed_sums(ids, channels, cuts, sums0, sums1)
     (in_grad,) = run(
         assemble_body,
         ids,

time: 109 us -> 99.6 us (0.914)
  Pallas kernels: 30.1 us -> 19.5 us
  starting transfers between devices: 40.9 us -> 43.1 us
    pallas_call x20 -> x25, Pallas kernels: 30.1 us -> 19.5 us  [run(): pl.pallas_call(kernel, in_specs=[pl.BlockSpec(memory_space=pltpu.VMEM)] *...]
    ppermute x0 -> x1, starting transfers between devices: none -> 3.51 us  [on_device(): lax.ppermute(past_a, 'tm', [(i, (i - 1) % size) for i in range(size)])]
    ppermute x7 -> x6, waiting for transfers between devices: 12.3 us -> 14 us  [moved_by(): lax.ppermute(values, 'tm', [(i, i + distance) for i in devices if i + dis...]
    ppermute x8, waiting for transfers between devices: 3.04 us -> 1.49 us  [swapped(): return lax.ppermute(values, 'chan', [(0, 1), (1, 0)])]
    ppermute x7 -> x6, starting transfers between devices: 20.5 us -> 19 us  [moved_by(): lax.ppermute(values, 'tm', [(i, i + distance) for i in devices if i + dis...]
    ppermute x8 -> x10, waiting for transfers between devices: 19.4 us -> 18.6 us  [crossed(): lax.ppermute(values, 'tm', [(i, i ^ bit) for i in range(lax.axis_size('tm...]
    ppermute x8 -> x10, starting transfers between devices: 19 us -> 18.8 us  [crossed(): lax.ppermute(values, 'tm', [(i, i ^ bit) for i in range(lax.axis_size('tm...]
  transfers between devices with their start and end apart: 23 -> 25, of which waited for: 9 -> 11; matrix products, arithmetic and copies ran while one was open for 2% -> 2% of each run, Pallas kernels for 26% -> 18%
where the time goes in v4:
time: 99.6 us; the launch traced here: 99.3 us
  starting transfers between devices  43.1 us (43%)
  waiting for transfers between devices  34 us (34%)
  Pallas kernels  19.5 us (20%)
  local copies, waits for them, and re-layouts  1.75 us (2%)
    pallas_call x25, Pallas kernels, run(): pl.pallas_call(kernel, in_specs=[pl.BlockSpec(memory_space=pltpu.VMEM)] *...  19.5 us
    ppermute x6, starting transfers between devices, moved_by(): lax.ppermute(values, 'tm', [(i, i + distance) for i in devices if i + dis...  19 us
    ppermute x10, starting transfers between devices, crossed(): lax.ppermute(values, 'tm', [(i, i ^ bit) for i in range(lax.axis_size('tm...  18.8 us
    ppermute x10, waiting for transfers between devices, crossed(): lax.ppermute(values, 'tm', [(i, i ^ bit) for i in range(lax.axis_size('tm...  18.6 us
    ppermute x6, waiting for transfers between devices, moved_by(): lax.ppermute(values, 'tm', [(i, i + distance) for i in devices if i + dis...  14 us
    ppermute x1, starting transfers between devices, on_device(): lax.ppermute(past_a, 'tm', [(i, (i - 1) % size) for i in range(size)])  3.51 us
  transfers between devices with their start and end apart: 25, of which 11 were waited for; matrix products, arithmetic and copies ran while one was open for 2% of the time, Pallas kernels for 18%

profile of v4, /device:TPU:0, one launch (start us, length us, event | category | flops | bytes accessed | tf_op | source)
XLA Modules:
  0.0 99.3 jit_solution(9719157757847421413)
XLA Ops:
  0.6 0.5 collective-permute-start
  1.2 0.1 collective-permute-start.2
  1.2 1.7 %reshape.17.refs_2_.refs_3_.refs_4_.refs_6_ = bf16[2,2,256,512]{3,2,1,0:T(8,128)(2,1)S(1)} reshape(bf16[2,2,256,2,256]{4,3,2,1,0:T(2,128)(2,1)} %param.6) | data formatting | bytes 2097152 | tf_op jit(solution)/shard_map/reshape | solution.py:372
  3.0 0.0 copy-start
  3.0 0.0 copy-start.2
  3.0 1.4 %collective-permute-done.refs_1_ = bf16[4096,128]{1,0:T(8,128)(2,1)S(1)} collective-permute-done((bf16[4096,128]{1,0:T(8,128)(2,1)}, bf16[4096,128]{1,0:T(8,128)(2,1)S(1)}, u32[]{:S(2)}, u32[]{:S(2)}) %collective-permute-start) | collective-permute-done | bytes 1048608 | tf_op jit(solution)/shard_map/ppermute | solution.py:295
  4.4 0.1 shard_map.75
  4.5 4.8 %collective-permute-start.1 = (bf16[1024,256]{1,0:T(8,128)(2,1)S(1)}, bf16[1024,256]{1,0:T(8,128)(2,1)S(1)}, u32[]{:S(2)}, u32[]{:S(2)}) collective-permute-start(bf16[1024,256]{1,0:T(8,128)(2,1)S(1)} %get-tuple-element.52.refs_0_.refs_5_), channel_id=1, source_target_pairs={{0,2},{2,4},{4,6},{6,8},{8,10},{10,12},{12,14},{1,3},{3,5},{5,7},{... | collective-permute-start | bytes 1572872 | tf_op jit(solution)/shard_map/ppermute | solution.py:285
  9.3 1.4 %shard_map.76 = (bf16[1024,256]{1,0:T(8,128)(2,1)S(1)}, bf16[1024,256]{1,0:T(8,128)(2,1)S(1)}, f32[1024,512]{1,0:T(8,128)S(1)}) custom-call(bf16[1024,256]{1,0:T(8,128)(2,1)S(1)} %get-tuple-element.52.refs_0_.refs_5_, bf16[1024,256]{1,0:T(8,128)(2,1)S(1)} %get-tuple-element.51.refs_1_.refs_0_.refs_6_, ...), custom_call_target="tpu_custom_call" | custom-call | flops 1 | bytes 1 | tf_op jit(solution)/shard_map/pallas_call | solution.py:58
  10.7 3.5 %collective-permute-start.6 = (bf16[1024,256]{1,0:T(8,128)(2,1)S(1)}, bf16[1024,256]{1,0:T(8,128)(2,1)S(1)}, u32[]{:S(2)}, u32[]{:S(2)}) collective-permute-start(bf16[1024,256]{1,0:T(8,128)(2,1)S(1)} %get-tuple-element.53.refs_3_.refs_0_.refs_5_), channel_id=1, source_target_pairs={{0,4},{2,6},{4,8},{6,10},{8,12},{10,14},{1,5},{3,7},{5,9},{7,11},{... | collective-permute-start | bytes 1572872 | tf_op jit(solution)/shard_map/ppermute | solution.py:285
  14.2 0.0 collective-permute-done.2.refs_1_
  14.2 1.7 %shard_map.77 = (bf16[1024,256]{1,0:T(8,128)(2,1)S(1)}, bf16[1024,256]{1,0:T(8,128)(2,1)S(1)}, f32[1024,256]{1,0:T(8,128)S(1)}, f32[1024,256]{1,0:T(8,128)S(1)}) custom-call(bf16[4096,128]{1,0:T(8,128)(2,1)S(1)} %copy-done.2, bf16[4096,128]{1,0:T(8,128)(2,1)} %collective-permute-done.2.refs_1_, bf16[2,256,256]{2,1,0:T(8,128)(2,1)S(1)} %copy-done, ...), custom_call_target="tpu_custom_call" | custom-call | flops 1 | bytes 1 | tf_op jit(solution)/shard_map/pallas_call | solution.py:58
  15.9 1.3 %collective-permute-start.5 = (bf16[1024,256]{1,0:T(8,128)(2,1)S(1)}, bf16[1024,256]{1,0:T(8,128)(2,1)S(1)}, u32[]{:S(2)}, u32[]{:S(2)}) collective-permute-start(bf16[1024,256]{1,0:T(8,128)(2,1)S(1)} %get-tuple-element.54.refs_4_.refs_2_), channel_id=1, source_target_pairs={{4,0},{6,2},{8,4},{10,6},{12,8},{14,10},{5,1},{7,3},{9,5},{11,7},{... | collective-permute-start | bytes 1572872 | tf_op jit(solution)/shard_map/ppermute | solution.py:285
  17.2 3.5 %collective-permute-done.1.refs_1_ = bf16[1024,256]{1,0:T(8,128)(2,1)S(1)} collective-permute-done((bf16[1024,256]{1,0:T(8,128)(2,1)S(1)}, bf16[1024,256]{1,0:T(8,128)(2,1)S(1)}, u32[]{:S(2)}, u32[]{:S(2)}) %collective-permute-start.1) | collective-permute-done | bytes 524320 | tf_op jit(solution)/shard_map/ppermute | solution.py:285
  20.8 1.4 %shard_map.78 = (bf16[1024,256]{1,0:T(8,128)(2,1)S(1)}, bf16[1024,256]{1,0:T(8,128)(2,1)S(1)}, f32[1024,512]{1,0:T(8,128)S(1)}) custom-call(bf16[1024,256]{1,0:T(8,128)(2,1)S(1)} %get-tuple-element.51.refs_1_.refs_0_.refs_6_, bf16[1024,256]{1,0:T(8,128)(2,1)S(1)} %collective-permute-done.1.refs_1_, ...), custom_call_target="tpu_custom_call" | custom-call | flops 1 | bytes 1 | tf_op jit(solution)/shard_map/pallas_call | solution.py:58
  22.1 1.3 %collective-permute-start.4 = (bf16[1024,256]{1,0:T(8,128)(2,1)S(1)}, bf16[1024,256]{1,0:T(8,128)(2,1)S(1)}, u32[]{:S(2)}, u32[]{:S(2)}) collective-permute-start(bf16[1024,256]{1,0:T(8,128)(2,1)S(1)} %get-tuple-element.55.refs_4_.refs_1_.refs_0_), channel_id=1, source_target_pairs={{4,0},{6,2},{8,4},{10,6},{12,8},{14,10},{5,1},{7,3},{9,5},{11,7},{... | collective-permute-start | bytes 1572872 | tf_op jit(solution)/shard_map/ppermute | solution.py:285
  23.4 6.8 %collective-permute-start.3 = (bf16[1024,256]{1,0:T(8,128)(2,1)S(1)}, bf16[1024,256]{1,0:T(8,128)(2,1)S(1)}, u32[]{:S(2)}, u32[]{:S(2)}) collective-permute-start(bf16[1024,256]{1,0:T(8,128)(2,1)S(1)} %get-tuple-element.55.refs_4_.refs_1_.refs_0_), channel_id=1, source_target_pairs={{0,4},{2,6},{4,8},{6,10},{8,12},{10,14},{1,5},{3,7},{5,9},{7,11},{... | collective-permute-start | bytes 1572872 | tf_op jit(solution)/shard_map/ppermute | solution.py:285
  30.2 0.0 collective-permute-done.6.refs_1_.refs_6_
  30.2 1.3 %shard_map.79 = (bf16[1024,512]{1,0:T(8,128)(2,1)S(1)}, bf16[1024,256]{1,0:T(8,128)(2,1)S(1)}, bf16[1024,256]{1,0:T(8,128)(2,1)S(1)}) custom-call(bf16[1024,256]{1,0:T(8,128)(2,1)S(1)} %get-tuple-element.53.refs_3_.refs_0_.refs_5_, bf16[1024,256]{1,0:T(8,128)(2,1)S(1)} %collective-permute-done.6.refs_1_.refs_6_, f32[1024,256]{1,0:T(8,128)S(1)} %get-tuple-element.57.refs_2_, ...), custom_call_target="tpu_custom_call" | custom-call | flops 1 | bytes 1 | tf_op jit(solution)/shard_map/pallas_call | solution.py:58
  31.6 1.3 %collective-permute-start.9 = (bf16[1024,256]{1,0:T(8,128)(2,1)S(1)}, bf16[1024,256]{1,0:T(8,128)(2,1)S(1)}, u32[]{:S(2)}, u32[]{:S(2)}) collective-permute-start(bf16[1024,256]{1,0:T(8,128)(2,1)S(1)} %get-tuple-element.67), channel_id=1, source_target_pairs={{4,0},{6,2},{8,4},{10,6},{12,8},{14,10},{5,1},{7,3},{9,5},{11,7},{... | collective-permute-start | bytes 1572872 | tf_op jit(solution)/shard_map/ppermute | solution.py:285
  32.9 0.6 shard_map.80
  33.5 10.4 %collective-permute-done.4.refs_0_ = bf16[1024,256]{1,0:T(8,128)(2,1)S(1)} collective-permute-done((bf16[1024,256]{1,0:T(8,128)(2,1)S(1)}, bf16[1024,256]{1,0:T(8,128)(2,1)S(1)}, u32[]{:S(2)}, u32[]{:S(2)}) %collective-permute-start.4) | collective-permute-done | bytes 524320 | tf_op jit(solution)/shard_map/ppermute | solution.py:285
  43.9 1.5 %shard_map.81.refs_4_ = f32[1024,256]{1,0:T(8,128)S(1)} custom-call(bf16[1024,256]{1,0:T(8,128)(2,1)S(1)} %collective-permute-done.4.refs_0_, bf16[1024,256]{1,0:T(8,128)(2,1)S(1)} %get-tuple-element.55.refs_4_.refs_1_.refs_0_, bf16[1024,256]{1,0:T(8,128)(2,1)S(1)} %collective-permute-done.5.refs_2_, ...), custom_call_target="tpu_custom_call" | custom-call | flops 1 | bytes 1 | tf_op jit(solution)/shard_map/pallas_call | solution.py:58
  45.4 0.0 collective-permute-done.3.refs_1_
  45.4 3.2 %shard_map.82 = (bf16[1024,256]{1,0:T(8,128)(2,1)S(1)}, bf16[1024,512]{1,0:T(8,128)(2,1)S(1)}, bf16[1024,256]{1,0:T(8,128)(2,1)S(1)}, bf16[1024,128]{1,0:T(8,128...) custom-call(bf16[1024,256]{1,0:T(8,128)(2,1)S(1)} %get-tuple-element, ...), custom_call_target="tpu_custom_call" | custom-call | flops 1 | bytes 1 | tf_op jit(solution)/shard_map/pallas_call | solution.py:58
  48.6 1.6 %shard_map.83 = (f32[1280,128]{1,0:T(8,128)S(1)}, bf16[1280,128]{1,0:T(8,128)(2,1)S(1)}) custom-call(bf16[1024,256]{1,0:T(8,128)(2,1)S(1)} %get-tuple-element.55.refs_4_.refs_1_.refs_0_, bf16[1024,256]{1,0:T(8,128)(2,1)S(1)} %collective-permute-done.3.refs_1_, bf16[1024,512]{1,0:T(8,128)(2,1)S(1)} %get-tuple-element.70.refs_2_, ...), custom_call_target="tpu_custom_call" | custom-call | flops 1 | bytes 1 | tf_op jit(solution)/shard_map/pallas_call | solution.py:58
  50.2 0.1 collective-permute-start.11
  50.3 3.5 %collective-permute-start.10 = (bf16[1024,256]{1,0:T(8,128)(2,1)S(1)}, bf16[1024,256]{1,0:T(8,128)(2,1)S(1)}, u32[]{:S(2)}, u32[]{:S(2)}) collective-permute-start(bf16[1024,256]{1,0:T(8,128)(2,1)S(1)} %get-tuple-element.74), channel_id=1, source_target_pairs={{0,14},{2,0},{4,2},{6,4},{8,6},{10,8},{12,10},{14,12},{1,15},{3,1}... | collective-permute-start | bytes 1572872 | tf_op jit(solution)/shard_map/ppermute | solution.py:430
  53.8 1.3 %shard_map.84 = (bf16[1024,128]{1,0:T(8,128)(2,1)S(1)}, bf16[1024,128]{1,0:T(8,128)(2,1)S(1)}, bf16[1024,256]{1,0:T(8,128)(2,1)S(1)}, bf16[1024,512]{1,0:T(8,128)(2,1)S(1)}, f32[1024,256]{1,0:T(8,128)S(1)}) custom-call(f32[1024,256]{1,0:T(8,128)S(1)} %get-tuple-element.61.refs_5_.refs_0_, bf16[1024,256]{1,0:T(8,128)(2,1)S(1)} %collective-permute-done.9.refs_1_, ...), custom_call_target="tpu_custom_call" | custom-call | flops 1 | bytes 1 | tf_op jit(solution)/shard_map/pallas_call | solution.py:58
  55.1 0.1 shard_map.85
  55.2 1.6 %shard_map.86 = (f32[1280,128]{1,0:T(8,128)S(1)}, bf16[1280,128]{1,0:T(8,128)(2,1)S(1)}) custom-call(bf16[1024,256]{1,0:T(8,128)(2,1)S(1)} %get-tuple-element.51.refs_1_.refs_0_.refs_6_, bf16[1024,256]{1,0:T(8,128)(2,1)S(1)} %collective-permute-done.1.refs_1_, bf16[1024,512]{1,0:T(8,128)(2,1)S(1)} %get-tuple-element.78.refs_2_, ...), custom_call_target="tpu_custom_call" | custom-call | flops 1 | bytes 1 | tf_op jit(solution)/shard_map/pallas_call | solution.py:58
  56.8 0.1 collective-permute-start.13
  56.9 1.5 %collective-permute-start.12 = (bf16[640,128]{1,0:T(8,128)(2,1)S(1)}, bf16[640,128]{1,0:T(8,128)(2,1)S(1)}, u32[]{:S(2)}, u32[]{:S(2)}) collective-permute-start(bf16[640,128]{1,0:T(8,128)(2,1)S(1)} %get-tuple-element.77.refs_11_), channel_id=1, source_target_pairs={{0,2},{2,0},{4,6},{6,4},{8,10},{10,8},{12,14},{14,12},{1,3},{3,1},... | collective-permute-start | bytes 491528 | tf_op jit(solution)/shard_map/ppermute | solution.py:291
  58.4 0.1 collective-permute-done.13.refs_1_
  58.5 0.1 shard_map.87
  58.6 1.5 %collective-permute-start.16 = (bf16[640,128]{1,0:T(8,128)(2,1)S(1)}, bf16[640,128]{1,0:T(8,128)(2,1)S(1)}, u32[]{:S(2)}, u32[]{:S(2)}) collective-permute-start(bf16[640,128]{1,0:T(8,128)(2,1)S(1)} %get-tuple-element.87.refs_3_), channel_id=1, source_target_pairs={{0,2},{2,0},{4,6},{6,4},{8,10},{10,8},{12,14},{14,12},{1,3},{3,1},... | collective-permute-start | bytes 491528 | tf_op jit(solution)/shard_map/ppermute | solution.py:291
  60.1 8.6 %collective-permute-done.12.refs_1_ = bf16[640,128]{1,0:T(8,128)(2,1)S(1)} collective-permute-done((bf16[640,128]{1,0:T(8,128)(2,1)S(1)}, bf16[640,128]{1,0:T(8,128)(2,1)S(1)}, u32[]{:S(2)}, u32[]{:S(2)}) %collective-permute-start.12) | collective-permute-done | bytes 163872 | tf_op jit(solution)/shard_map/ppermute | solution.py:291
  68.8 1.6 %collective-permute-start.18 = (bf16[320,128]{1,0:T(8,128)(2,1)S(1)}, bf16[320,128]{1,0:T(8,128)(2,1)S(1)}, u32[]{:S(2)}, u32[]{:S(2)}) collective-permute-start(bf16[320,128]{1,0:T(8,128)(2,1)S(1)} %get-tuple-element.89.refs_3_), channel_id=1, source_target_pairs={{0,4},{2,6},{4,0},{6,2},{8,12},{10,14},{12,8},{14,10},{1,5},{3,7},... | collective-permute-start | bytes 245768 | tf_op jit(solution)/shard_map/ppermute | solution.py:291
  70.4 0.0 collective-permute-done.10.refs_1_
  70.4 0.2 shard_map.89
  70.6 1.0 %collective-permute-done.16.refs_1_ = bf16[640,128]{1,0:T(8,128)(2,1)S(1)} collective-permute-done((bf16[640,128]{1,0:T(8,128)(2,1)S(1)}, bf16[640,128]{1,0:T(8,128)(2,1)S(1)}, u32[]{:S(2)}, u32[]{:S(2)}) %collective-permute-start.16) | collective-permute-done | bytes 163872 | tf_op jit(solution)/shard_map/ppermute | solution.py:291
  71.6 1.6 %collective-permute-start.17 = (bf16[320,128]{1,0:T(8,128)(2,1)S(1)}, bf16[320,128]{1,0:T(8,128)(2,1)S(1)}, u32[]{:S(2)}, u32[]{:S(2)}) collective-permute-start(bf16[320,128]{1,0:T(8,128)(2,1)S(1)} %get-tuple-element.95.refs_3_), channel_id=1, source_target_pairs={{0,4},{2,6},{4,0},{6,2},{8,12},{10,14},{12,8},{14,10},{1,5},{3,7},... | collective-permute-start | bytes 245768 | tf_op jit(solution)/shard_map/ppermute | solution.py:291
  73.2 0.0 collective-permute-done.18.refs_1_
  73.3 3.1 %collective-permute-start.20 = (bf16[320,128]{1,0:T(8,128)(2,1)S(1)}, bf16[320,128]{1,0:T(8,128)(2,1)S(1)}, u32[]{:S(2)}, u32[]{:S(2)}) collective-permute-start(bf16[320,128]{1,0:T(8,128)(2,1)S(1)} %shard_map.93.refs_2_.refs_0_), channel_id=1, source_target_pairs={{0,8},{2,10},{4,12},{6,14},{8,0},{10,2},{12,4},{14,6},{1,9},{3,11}... | collective-permute-start | bytes 245768 | tf_op jit(solution)/shard_map/ppermute | solution.py:291
  76.4 0.0 collective-permute-done.17.refs_1_
  76.5 3.2 %collective-permute-start.19 = (bf16[320,128]{1,0:T(8,128)(2,1)S(1)}, bf16[320,128]{1,0:T(8,128)(2,1)S(1)}, u32[]{:S(2)}, u32[]{:S(2)}) collective-permute-start(bf16[320,128]{1,0:T(8,128)(2,1)S(1)} %shard_map.94.refs_2_.refs_0_), channel_id=1, source_target_pairs={{0,8},{2,10},{4,12},{6,14},{8,0},{10,2},{12,4},{14,6},{1,9},{3,11}... | collective-permute-start | bytes 245768 | tf_op jit(solution)/shard_map/ppermute | solution.py:291
  79.7 2.0 %collective-permute-done.20.refs_1_ = bf16[320,128]{1,0:T(8,128)(2,1)S(1)} collective-permute-done((bf16[320,128]{1,0:T(8,128)(2,1)S(1)}, bf16[320,128]{1,0:T(8,128)(2,1)S(1)}, u32[]{:S(2)}, u32[]{:S(2)}) %collective-permute-start.20) | collective-permute-done | bytes 81952 | tf_op jit(solution)/shard_map/ppermute | solution.py:291
  81.7 0.1 collective-permute-start.22
  81.8 1.9 %collective-permute-done.19.refs_1_ = bf16[320,128]{1,0:T(8,128)(2,1)S(1)} collective-permute-done((bf16[320,128]{1,0:T(8,128)(2,1)S(1)}, bf16[320,128]{1,0:T(8,128)(2,1)S(1)}, u32[]{:S(2)}, u32[]{:S(2)}) %collective-permute-start.19) | collective-permute-done | bytes 81952 | tf_op jit(solution)/shard_map/ppermute | solution.py:291
  83.8 1.2 %collective-permute-start.21 = (bf16[320,128]{1,0:T(8,128)(2,1)S(1)}, bf16[320,128]{1,0:T(8,128)(2,1)S(1)}, u32[]{:S(2)}, u32[]{:S(2)}) collective-permute-start(bf16[320,128]{1,0:T(8,128)(2,1)S(1)} %shard_map.96.refs_2_.refs_0_), channel_id=1, source_target_pairs={{0,4},{2,6},{4,0},{6,2},{8,12},{10,14},{12,8},{14,10},{1,5},{3,7},... | collective-permute-start | bytes 245768 | tf_op jit(solution)/shard_map/ppermute | solution.py:291
  85.0 1.5 %collective-permute-done.22.refs_1_.refs_4_ = bf16[320,128]{1,0:T(8,128)(2,1)S(1)} collective-permute-done((bf16[320,128]{1,0:T(8,128)(2,1)S(1)}, bf16[320,128]{1,0:T(8,128)(2,1)S(1)}, u32[]{:S(2)}, u32[]{:S(2)}) %collective-permute-start.22) | collective-permute-done | bytes 81952 | tf_op jit(solution)/shard_map/ppermute | solution.py:291
  86.5 2.5 %collective-permute-start.23 = (bf16[640,128]{1,0:T(8,128)(2,1)S(1)}, bf16[640,128]{1,0:T(8,128)(2,1)S(1)}, u32[]{:S(2)}, u32[]{:S(2)}) collective-permute-start(bf16[640,128]{1,0:T(8,128)(2,1)S(1)} %shard_map.97), channel_id=1, source_target_pairs={{0,2},{2,0},{4,6},{6,4},{8,10},{10,8},{12,14},{14,12},{1,3},{3,1},... | collective-permute-start | bytes 491528 | tf_op jit(solution)/shard_map/ppermute | solution.py:291
  89.0 0.5 collective-permute-start.7
  89.5 0.0 collective-permute-start.14
  89.5 0.0 collective-permute-done.21.refs_1_
  89.5 0.5 collective-permute-start.15
  90.0 2.3 %collective-permute-done.23.refs_2_.refs_5_ = bf16[640,128]{1,0:T(8,128)(2,1)S(1)} collective-permute-done((bf16[640,128]{1,0:T(8,128)(2,1)S(1)}, bf16[640,128]{1,0:T(8,128)(2,1)S(1)}, u32[]{:S(2)}, u32[]{:S(2)}) %collective-permute-start.23) | collective-permute-done | bytes 163872 | tf_op jit(solution)/shard_map/ppermute | solution.py:291
  92.3 2.4 %collective-permute-start.24 = (bf16[640,128]{1,0:T(8,128)(2,1)S(1)}, bf16[640,128]{1,0:T(8,128)(2,1)S(1)}, u32[]{:S(2)}, u32[]{:S(2)}) collective-permute-start(bf16[640,128]{1,0:T(8,128)(2,1)S(1)} %shard_map.98), channel_id=1, source_target_pairs={{0,2},{2,0},{4,6},{6,4},{8,10},{10,8},{12,14},{14,12},{1,3},{3,1},... | collective-permute-start | bytes 491528 | tf_op jit(solution)/shard_map/ppermute | solution.py:291
  94.7 1.0 %shard_map.90 = bf16[4096,128]{1,0:T(8,128)(2,1)} custom-call(bf16[1024,128]{1,0:T(8,128)(2,1)S(1)} %get-tuple-element.63.refs_0_, bf16[1024,128]{1,0:T(8,128)(2,1)S(1)} %collective-permute-done.7.refs_1_, bf16[1024,128]{1,0:T(8,128)(2,1)S(1)} %get-tuple-element.65.refs_2_, bf16[1024,128]{1,0:T(8,128)(2,1)S(1)} %collective-permute-done.8.refs_3_, ...), custom_call_target="tpu_custom_call" | custom-call | flops 1 | bytes 1 | tf_op jit(solution)/shard_map/pallas_call | solution.py:58
  95.8 0.0 collective-permute-done.14.refs_1_
  95.8 0.0 collective-permute-done.15.refs_3_
  95.8 1.0 %shard_map.91 = bf16[4096,128]{1,0:T(8,128)(2,1)} custom-call(bf16[1024,128]{1,0:T(8,128)(2,1)S(1)} %get-tuple-element.91.refs_0_, bf16[1024,128]{1,0:T(8,128)(2,1)S(1)} %collective-permute-done.14.refs_1_, bf16[1024,128]{1,0:T(8,128)(2,1)S(1)} %get-tuple-element.90.refs_4_.refs_2_, bf16[1024,128]{1,0:T(8,128)(2,1)S(1)} %collective-permute-done.15.refs_3_), custom_call_target="tpu_custom_call" | custom-call | flops 1 | bytes 1 | tf_op jit(solution)/shard_map/pallas_call | solution.py:58
  96.8 1.2 %collective-permute-done.24.refs_2_ = bf16[640,128]{1,0:T(8,128)(2,1)S(1)} collective-permute-done((bf16[640,128]{1,0:T(8,128)(2,1)S(1)}, bf16[640,128]{1,0:T(8,128)(2,1)S(1)}, u32[]{:S(2)}, u32[]{:S(2)}) %collective-permute-start.24) | collective-permute-done | bytes 163872 | tf_op jit(solution)/shard_map/ppermute | solution.py:291
  98.0 1.3 %shard_map.99 = (f32[2048,128]{1,0:T(8,128)}, f32[512,128]{1,0:T(8,128)}) custom-call(bf16[320,128]{1,0:T(8,128)(2,1)S(1)} %shard_map.96.refs_2_.refs_0_, bf16[320,128]{1,0:T(8,128)(2,1)S(1)} %collective-permute-done.21.refs_1_, bf16[640,128]{1,0:T(8,128)(2,1)S(1)} %collective-permute-done.24.refs_2_, ...), custom_call_target="tpu_custom_call" | custom-call | flops 1 | bytes 1 | tf_op jit(solution)/shard_map/pallas_call | solution.py:58
  (18 shorter events, 0.2 us)
Async XLA Ops:
  0.6 3.7 %copy-start.1 = (bf16[4096,128]{1,0:T(8,128)(2,1)S(1)}, bf16[4096,128]{1,0:T(8,128)(2,1)}, u32[]{:S(2)}) copy-start(bf16[4096,128]{1,0:T(8,128)(2,1)} %refs_0_.2) | copy-start | bytes 3145732
  0.6 3.7 %collective-permute-start = (bf16[4096,128]{1,0:T(8,128)(2,1)}, bf16[4096,128]{1,0:T(8,128)(2,1)S(1)}, u32[]{:S(2)}, u32[]{:S(2)}) collective-permute-start(bf16[4096,128]{1,0:T(8,128)(2,1)} %refs_0_.2), channel_id=1, source_target_pairs={{0,1},{1,0},{2,3},{3,2},{4,5},{5,4},{6,7},{7,6},{8,9},{9,8},{10,11... | collective-permute-start | bytes 3145736 | tf_op jit(solution)/shard_map/ppermute | solution.py:295
  1.2 13.0 %collective-permute-start.2 = (bf16[4096,128]{1,0:T(8,128)(2,1)}, bf16[4096,128]{1,0:T(8,128)(2,1)}, u32[]{:S(2)}, u32[]{:S(2)}) collective-permute-start(bf16[4096,128]{1,0:T(8,128)(2,1)} %refs_0_.3), channel_id=1, source_target_pairs={{0,1},{1,0},{2,3},{3,2},{4,5},{5,4},{6,7},{7,6},{8,9},{9,8},{10,11... | collective-permute-start | bytes 3145736 | tf_op jit(solution)/shard_map/ppermute | solution.py:295
  3.0 6.4 %copy-start = (bf16[2,256,256]{2,1,0:T(8,128)(2,1)S(1)}, bf16[2,256,256]{2,1,0:T(8,128)(2,1)}, u32[]{:S(2)}) copy-start(bf16[2,256,256]{2,1,0:T(8,128)(2,1)} %refs_5_.3) | copy-start | bytes 786436
  3.0 11.2 %copy-start.2 = (bf16[4096,128]{1,0:T(8,128)(2,1)S(1)}, bf16[4096,128]{1,0:T(8,128)(2,1)}, u32[]{:S(2)}) copy-start(bf16[4096,128]{1,0:T(8,128)(2,1)} %refs_0_.3) | copy-start | bytes 3145732
  4.5 16.3 %collective-permute-start.1 = (bf16[1024,256]{1,0:T(8,128)(2,1)S(1)}, bf16[1024,256]{1,0:T(8,128)(2,1)S(1)}, u32[]{:S(2)}, u32[]{:S(2)}) collective-permute-start(bf16[1024,256]{1,0:T(8,128)(2,1)S(1)} %get-tuple-element.52.refs_0_.refs_5_), channel_id=1, source_target_pairs={{0,2},{2,4},{4,6},{6,8},{8,10},{10,12},{12,14},{1,3},{3,5},{5,7},{... | collective-permute-start | bytes 1572872 | tf_op jit(solution)/shard_map/ppermute | solution.py:285
  10.7 19.5 %collective-permute-start.6 = (bf16[1024,256]{1,0:T(8,128)(2,1)S(1)}, bf16[1024,256]{1,0:T(8,128)(2,1)S(1)}, u32[]{:S(2)}, u32[]{:S(2)}) collective-permute-start(bf16[1024,256]{1,0:T(8,128)(2,1)S(1)} %get-tuple-element.53.refs_3_.refs_0_.refs_5_), channel_id=1, source_target_pairs={{0,4},{2,6},{4,8},{6,10},{8,12},{10,14},{1,5},{3,7},{5,9},{7,11},{... | collective-permute-start | bytes 1572872 | tf_op jit(solution)/shard_map/ppermute | solution.py:285
  15.9 17.5 %collective-permute-start.5 = (bf16[1024,256]{1,0:T(8,128)(2,1)S(1)}, bf16[1024,256]{1,0:T(8,128)(2,1)S(1)}, u32[]{:S(2)}, u32[]{:S(2)}) collective-permute-start(bf16[1024,256]{1,0:T(8,128)(2,1)S(1)} %get-tuple-element.54.refs_4_.refs_2_), channel_id=1, source_target_pairs={{4,0},{6,2},{8,4},{10,6},{12,8},{14,10},{5,1},{7,3},{9,5},{11,7},{... | collective-permute-start | bytes 1572872 | tf_op jit(solution)/shard_map/ppermute | solution.py:285
  22.1 21.8 %collective-permute-start.4 = (bf16[1024,256]{1,0:T(8,128)(2,1)S(1)}, bf16[1024,256]{1,0:T(8,128)(2,1)S(1)}, u32[]{:S(2)}, u32[]{:S(2)}) collective-permute-start(bf16[1024,256]{1,0:T(8,128)(2,1)S(1)} %get-tuple-element.55.refs_4_.refs_1_.refs_0_), channel_id=1, source_target_pairs={{4,0},{6,2},{8,4},{10,6},{12,8},{14,10},{5,1},{7,3},{9,5},{11,7},{... | collective-permute-start | bytes 1572872 | tf_op jit(solution)/shard_map/ppermute | solution.py:285
  23.4 22.0 %collective-permute-start.3 = (bf16[1024,256]{1,0:T(8,128)(2,1)S(1)}, bf16[1024,256]{1,0:T(8,128)(2,1)S(1)}, u32[]{:S(2)}, u32[]{:S(2)}) collective-permute-start(bf16[1024,256]{1,0:T(8,128)(2,1)S(1)} %get-tuple-element.55.refs_4_.refs_1_.refs_0_), channel_id=1, source_target_pairs={{0,4},{2,6},{4,8},{6,10},{8,12},{10,14},{1,5},{3,7},{5,9},{7,11},{... | collective-permute-start | bytes 1572872 | tf_op jit(solution)/shard_map/ppermute | solution.py:285
  31.6 22.2 %collective-permute-start.9 = (bf16[1024,256]{1,0:T(8,128)(2,1)S(1)}, bf16[1024,256]{1,0:T(8,128)(2,1)S(1)}, u32[]{:S(2)}, u32[]{:S(2)}) collective-permute-start(bf16[1024,256]{1,0:T(8,128)(2,1)S(1)} %get-tuple-element.67), channel_id=1, source_target_pairs={{4,0},{6,2},{8,4},{10,6},{12,8},{14,10},{5,1},{7,3},{9,5},{11,7},{... | collective-permute-start | bytes 1572872 | tf_op jit(solution)/shard_map/ppermute | solution.py:285
  50.2 4.9 %collective-permute-start.11 = (bf16[1280,128]{1,0:T(8,128)(2,1)S(1)}, bf16[1280,128]{1,0:T(8,128)(2,1)S(1)}, u32[]{:S(2)}, u32[]{:S(2)}) collective-permute-start(bf16[1280,128]{1,0:T(8,128)(2,1)S(1)} %get-tuple-element.75), channel_id=1, source_target_pairs={{0,1},{1,0},{2,3},{3,2},{4,5},{5,4},{6,7},{7,6},{8,9},{9,8},{10,11... | collective-permute-start | bytes 983048 | tf_op jit(solution)/shard_map/ppermute | solution.py:295
  50.3 20.1 %collective-permute-start.10 = (bf16[1024,256]{1,0:T(8,128)(2,1)S(1)}, bf16[1024,256]{1,0:T(8,128)(2,1)S(1)}, u32[]{:S(2)}, u32[]{:S(2)}) collective-permute-start(bf16[1024,256]{1,0:T(8,128)(2,1)S(1)} %get-tuple-element.74), channel_id=1, source_target_pairs={{0,14},{2,0},{4,2},{6,4},{8,6},{10,8},{12,10},{14,12},{1,15},{3,1}... | collective-permute-start | bytes 1572872 | tf_op jit(solution)/shard_map/ppermute | solution.py:430
  56.8 1.7 %collective-permute-start.13 = (bf16[1280,128]{1,0:T(8,128)(2,1)S(1)}, bf16[1280,128]{1,0:T(8,128)(2,1)S(1)}, u32[]{:S(2)}, u32[]{:S(2)}) collective-permute-start(bf16[1280,128]{1,0:T(8,128)(2,1)S(1)} %get-tuple-element.85), channel_id=1, source_target_pairs={{0,1},{1,0},{2,3},{3,2},{4,5},{5,4},{6,7},{7,6},{8,9},{9,8},{10,11... | collective-permute-start | bytes 983048 | tf_op jit(solution)/shard_map/ppermute | solution.py:295
  56.9 11.9 %collective-permute-start.12 = (bf16[640,128]{1,0:T(8,128)(2,1)S(1)}, bf16[640,128]{1,0:T(8,128)(2,1)S(1)}, u32[]{:S(2)}, u32[]{:S(2)}) collective-permute-start(bf16[640,128]{1,0:T(8,128)(2,1)S(1)} %get-tuple-element.77.refs_11_), channel_id=1, source_target_pairs={{0,2},{2,0},{4,6},{6,4},{8,10},{10,8},{12,14},{14,12},{1,3},{3,1},... | collective-permute-start | bytes 491528 | tf_op jit(solution)/shard_map/ppermute | solution.py:291
  58.6 13.0 %collective-permute-start.16 = (bf16[640,128]{1,0:T(8,128)(2,1)S(1)}, bf16[640,128]{1,0:T(8,128)(2,1)S(1)}, u32[]{:S(2)}, u32[]{:S(2)}) collective-permute-start(bf16[640,128]{1,0:T(8,128)(2,1)S(1)} %get-tuple-element.87.refs_3_), channel_id=1, source_target_pairs={{0,2},{2,0},{4,6},{6,4},{8,10},{10,8},{12,14},{14,12},{1,3},{3,1},... | collective-permute-start | bytes 491528 | tf_op jit(solution)/shard_map/ppermute | solution.py:291
  68.8 4.5 %collective-permute-start.18 = (bf16[320,128]{1,0:T(8,128)(2,1)S(1)}, bf16[320,128]{1,0:T(8,128)(2,1)S(1)}, u32[]{:S(2)}, u32[]{:S(2)}) collective-permute-start(bf16[320,128]{1,0:T(8,128)(2,1)S(1)} %get-tuple-element.89.refs_3_), channel_id=1, source_target_pairs={{0,4},{2,6},{4,0},{6,2},{8,12},{10,14},{12,8},{14,10},{1,5},{3,7},... | collective-permute-start | bytes 245768 | tf_op jit(solution)/shard_map/ppermute | solution.py:291
  71.6 4.8 %collective-permute-start.17 = (bf16[320,128]{1,0:T(8,128)(2,1)S(1)}, bf16[320,128]{1,0:T(8,128)(2,1)S(1)}, u32[]{:S(2)}, u32[]{:S(2)}) collective-permute-start(bf16[320,128]{1,0:T(8,128)(2,1)S(1)} %get-tuple-element.95.refs_3_), channel_id=1, source_target_pairs={{0,4},{2,6},{4,0},{6,2},{8,12},{10,14},{12,8},{14,10},{1,5},{3,7},... | collective-permute-start | bytes 245768 | tf_op jit(solution)/shard_map/ppermute | solution.py:291
  73.3 8.4 %collective-permute-start.20 = (bf16[320,128]{1,0:T(8,128)(2,1)S(1)}, bf16[320,128]{1,0:T(8,128)(2,1)S(1)}, u32[]{:S(2)}, u32[]{:S(2)}) collective-permute-start(bf16[320,128]{1,0:T(8,128)(2,1)S(1)} %shard_map.93.refs_2_.refs_0_), channel_id=1, source_target_pairs={{0,8},{2,10},{4,12},{6,14},{8,0},{10,2},{12,4},{14,6},{1,9},{3,11}... | collective-permute-start | bytes 245768 | tf_op jit(solution)/shard_map/ppermute | solution.py:291
  76.5 7.3 %collective-permute-start.19 = (bf16[320,128]{1,0:T(8,128)(2,1)S(1)}, bf16[320,128]{1,0:T(8,128)(2,1)S(1)}, u32[]{:S(2)}, u32[]{:S(2)}) collective-permute-start(bf16[320,128]{1,0:T(8,128)(2,1)S(1)} %shard_map.94.refs_2_.refs_0_), channel_id=1, source_target_pairs={{0,8},{2,10},{4,12},{6,14},{8,0},{10,2},{12,4},{14,6},{1,9},{3,11}... | collective-permute-start | bytes 245768 | tf_op jit(solution)/shard_map/ppermute | solution.py:291
  81.7 4.7 %collective-permute-start.22 = (bf16[320,128]{1,0:T(8,128)(2,1)S(1)}, bf16[320,128]{1,0:T(8,128)(2,1)S(1)}, u32[]{:S(2)}, u32[]{:S(2)}) collective-permute-start(bf16[320,128]{1,0:T(8,128)(2,1)S(1)} %shard_map.95.refs_2_.refs_0_.refs_3_), channel_id=1, source_target_pairs={{0,4},{2,6},{4,0},{6,2},{8,12},{10,14},{12,8},{14,10},{1,5},{3,7},... | collective-permute-start | bytes 245768 | tf_op jit(solution)/shard_map/ppermute | solution.py:291
  83.8 5.8 %collective-permute-start.21 = (bf16[320,128]{1,0:T(8,128)(2,1)S(1)}, bf16[320,128]{1,0:T(8,128)(2,1)S(1)}, u32[]{:S(2)}, u32[]{:S(2)}) collective-permute-start(bf16[320,128]{1,0:T(8,128)(2,1)S(1)} %shard_map.96.refs_2_.refs_0_), channel_id=1, source_target_pairs={{0,4},{2,6},{4,0},{6,2},{8,12},{10,14},{12,8},{14,10},{1,5},{3,7},... | collective-permute-start | bytes 245768 | tf_op jit(solution)/shard_map/ppermute | solution.py:291
  86.5 5.8 %collective-permute-start.23 = (bf16[640,128]{1,0:T(8,128)(2,1)S(1)}, bf16[640,128]{1,0:T(8,128)(2,1)S(1)}, u32[]{:S(2)}, u32[]{:S(2)}) collective-permute-start(bf16[640,128]{1,0:T(8,128)(2,1)S(1)} %shard_map.97), channel_id=1, source_target_pairs={{0,2},{2,0},{4,6},{6,4},{8,10},{10,8},{12,14},{14,12},{1,3},{3,1},... | collective-permute-start | bytes 491528 | tf_op jit(solution)/shard_map/ppermute | solution.py:291
  89.0 5.7 %collective-permute-start.8 = (bf16[1024,128]{1,0:T(8,128)(2,1)S(1)}, bf16[1024,128]{1,0:T(8,128)(2,1)S(1)}, u32[]{:S(2)}, u32[]{:S(2)}) collective-permute-start(bf16[1024,128]{1,0:T(8,128)(2,1)S(1)} %get-tuple-element.66), channel_id=1, source_target_pairs={{0,1},{1,0},{2,3},{3,2},{4,5},{5,4},{6,7},{7,6},{8,9},{9,8},{10,11... | collective-permute-start | bytes 786440 | tf_op jit(solution)/shard_map/ppermute | solution.py:295
  89.0 5.7 %collective-permute-start.7 = (bf16[1024,128]{1,0:T(8,128)(2,1)S(1)}, bf16[1024,128]{1,0:T(8,128)(2,1)S(1)}, u32[]{:S(2)}, u32[]{:S(2)}) collective-permute-start(bf16[1024,128]{1,0:T(8,128)(2,1)S(1)} %get-tuple-element.64), channel_id=1, source_target_pairs={{0,1},{1,0},{2,3},{3,2},{4,5},{5,4},{6,7},{7,6},{8,9},{9,8},{10,11... | collective-permute-start | bytes 786440 | tf_op jit(solution)/shard_map/ppermute | solution.py:295
  89.5 6.3 %collective-permute-start.14 = (bf16[1024,128]{1,0:T(8,128)(2,1)S(1)}, bf16[1024,128]{1,0:T(8,128)(2,1)S(1)}, u32[]{:S(2)}, u32[]{:S(2)}) collective-permute-start(bf16[1024,128]{1,0:T(8,128)(2,1)S(1)} %get-tuple-element.92), channel_id=1, source_target_pairs={{0,1},{1,0},{2,3},{3,2},{4,5},{5,4},{6,7},{7,6},{8,9},{9,8},{10,11... | collective-permute-start | bytes 786440 | tf_op jit(solution)/shard_map/ppermute | solution.py:295
  89.5 6.3 %collective-permute-start.15 = (bf16[1024,128]{1,0:T(8,128)(2,1)S(1)}, bf16[1024,128]{1,0:T(8,128)(2,1)S(1)}, u32[]{:S(2)}, u32[]{:S(2)}) collective-permute-start(bf16[1024,128]{1,0:T(8,128)(2,1)S(1)} %get-tuple-element.93), channel_id=1, source_target_pairs={{0,1},{1,0},{2,3},{3,2},{4,5},{5,4},{6,7},{7,6},{8,9},{9,8},{10,11... | collective-permute-start | bytes 786440 | tf_op jit(solution)/shard_map/ppermute | solution.py:295
  92.3 5.7 %collective-permute-start.24 = (bf16[640,128]{1,0:T(8,128)(2,1)S(1)}, bf16[640,128]{1,0:T(8,128)(2,1)S(1)}, u32[]{:S(2)}, u32[]{:S(2)}) collective-permute-start(bf16[640,128]{1,0:T(8,128)(2,1)S(1)} %shard_map.98), channel_id=1, source_target_pairs={{0,2},{2,0},{4,6},{6,4},{8,10},{10,8},{12,14},{14,12},{1,3},{3,1},... | collective-permute-start | bytes 491528 | tf_op jit(solution)/shard_map/ppermute | solution.py:291

commit v5 on v4

--- a/solution.py
+++ b/solution.py
@@ -381,20 +381,20 @@
     )
     x_h = moved_by(x_b, 1)
     first_outs = [(narrow, BF)] * 2 + [(broad, F32)]
-    x1_b, hid0_b, slope_b = run(
-        first_body, ids, [x_b, x_a, taps, wo], first_outs
-    )
-    x1_b_past = moved_by(x1_b, later)
     cot_a, cot_b, hg_a, hg_b = run(
         cot_body,
         ids,
         [cotangent, swapped(cotangent), wo],
         [(narrow, BF)] * 2 + [(narrow, F32)] * 2,
-        after=[x1_b],
+        after=[x_b],
     )
     cot_a_later = moved_by(cot_a, -later)
+    x1_b, hid0_b, slope_b = run(
+        first_body, ids, [x_b, x_a, taps, wo], first_outs, after=[cot_a]
+    )
+    x1_b_past = moved_by(x1_b, later)
     x1_a, hid0_a, slope_a = run(
-        first_body, ids, [x_a, x_h, taps, wo], first_outs, after=[cot_a]
+        first_body, ids, [x_a, x_h, taps, wo], first_outs, after=[x1_b]
     )
     x1_a_later = moved_by(x1_a, -later)
     x1_a_past = moved_by(x1_a, later)
@@ -404,7 +404,7 @@
         ids,
         [x1_b, x1_b_past, hg_b, taps],
         [(broad, BF)] + [(narrow, BF)] * 2,
-        after=[x1_a],
+        after=[x1_a, cot_a_later],
     )
     from_next_b = moved_by(to_past_b, -later)
     out_keep_b, out_send_b, local_b = run(
@@ -427,7 +427,7 @@
         [(narrow, BF), (broad, BF), (narrow, BF), (half, BF), (half, BF)] + third_outs,
     )
     size = lax.axis_size("tm")
-    ahead_b = lax.ppermute(past_a, "tm", [(i, (i - 1) % size) for i in range(size)])
+    ahead_b = moved_by(past_a, -1)
 
     def weights(arrays, after=()):
         shape = (5 * channels, half_width)

time: 99.6 us -> 99.3 us (level)
    ppermute x1 -> x0, starting transfers between devices: 3.51 us -> none  [on_device(): lax.ppermute(past_a, 'tm', [(i, (i - 1) % size) for i in range(size)])]
    ppermute x10, waiting for transfers between devices: 18.6 us -> 21.8 us  [crossed(): lax.ppermute(values, 'tm', [(i, i ^ bit) for i in range(lax.axis_size('tm...]
    ppermute x6 -> x7, waiting for transfers between devices: 14 us -> 11.2 us  [moved_by(): lax.ppermute(values, 'tm', [(i, i + distance) for i in devices if i + dis...]
    ppermute x6 -> x7, starting transfers between devices: 19 us -> 21.6 us  [moved_by(): lax.ppermute(values, 'tm', [(i, i + distance) for i in devices if i + dis...]
  transfers between devices with their start and end apart: 25 -> 25, of which waited for: 11 -> 12; matrix products, arithmetic and copies ran while one was open for 2% -> 2% of each run, Pallas kernels for 18% -> 18%
where the time goes in v5:
time: 99.3 us; the launch traced here: 99 us
  starting transfers between devices  42.4 us (43%)
  waiting for transfers between devices  34.4 us (35%)
  Pallas kernels  19.5 us (20%)
  local copies, waits for them, and re-layouts  1.75 us (2%)
    ppermute x10, waiting for transfers between devices, crossed(): lax.ppermute(values, 'tm', [(i, i ^ bit) for i in range(lax.axis_size('tm...  21.8 us
    ppermute x7, starting transfers between devices, moved_by(): lax.ppermute(values, 'tm', [(i, i + distance) for i in devices if i + dis...  21.6 us
    pallas_call x25, Pallas kernels, run(): pl.pallas_call(kernel, in_specs=[pl.BlockSpec(memory_space=pltpu.VMEM)] *...  19.5 us
    ppermute x10, starting transfers between devices, crossed(): lax.ppermute(values, 'tm', [(i, i ^ bit) for i in range(lax.axis_size('tm...  19.1 us
    ppermute x7, waiting for transfers between devices, moved_by(): lax.ppermute(values, 'tm', [(i, i + distance) for i in devices if i + dis...  11.2 us
  transfers between devices with their start and end apart: 25, of which 12 were waited for; matrix products, arithmetic and copies ran while one was open for 2% of the time, Pallas kernels for 18%

profile of v5, /device:TPU:0, one launch (start us, length us, event | category | flops | bytes accessed | tf_op | source)
XLA Modules:
  0.0 99.0 jit_solution(17833562636343505957)
XLA Ops:
  0.6 0.5 collective-permute-start
  1.2 0.1 collective-permute-start.2
  1.2 1.7 %reshape.17.refs_2_.refs_3_.refs_4_.refs_6_ = bf16[2,2,256,512]{3,2,1,0:T(8,128)(2,1)S(1)} reshape(bf16[2,2,256,2,256]{4,3,2,1,0:T(2,128)(2,1)} %param.6) | data formatting | bytes 2097152 | tf_op jit(solution)/shard_map/reshape | solution.py:372
  3.0 0.0 copy-start
  3.0 0.0 copy-start.2
  3.0 1.4 %collective-permute-done.refs_1_ = bf16[4096,128]{1,0:T(8,128)(2,1)S(1)} collective-permute-done((bf16[4096,128]{1,0:T(8,128)(2,1)}, bf16[4096,128]{1,0:T(8,128)(2,1)S(1)}, u32[]{:S(2)}, u32[]{:S(2)}) %collective-permute-start) | collective-permute-done | bytes 1048608 | tf_op jit(solution)/shard_map/ppermute | solution.py:295
  4.4 0.1 shard_map.75
  4.5 4.8 %collective-permute-start.1 = (bf16[1024,256]{1,0:T(8,128)(2,1)S(1)}, bf16[1024,256]{1,0:T(8,128)(2,1)S(1)}, u32[]{:S(2)}, u32[]{:S(2)}) collective-permute-start(bf16[1024,256]{1,0:T(8,128)(2,1)S(1)} %get-tuple-element.52.refs_3_.refs_0_.refs_5_), channel_id=1, source_target_pairs={{0,2},{2,4},{4,6},{6,8},{8,10},{10,12},{12,14},{1,3},{3,5},{5,7},{... | collective-permute-start | bytes 1572872 | tf_op jit(solution)/shard_map/ppermute | solution.py:285
  9.4 1.7 %shard_map.76 = (bf16[1024,256]{1,0:T(8,128)(2,1)S(1)}, bf16[1024,256]{1,0:T(8,128)(2,1)S(1)}, f32[1024,256]{1,0:T(8,128)S(1)}, f32[1024,256]{1,0:T(8,128)S(1)}) custom-call(bf16[4096,128]{1,0:T(8,128)(2,1)S(1)} %copy-done.2, bf16[4096,128]{1,0:T(8,128)(2,1)} %collective-permute-done.2.refs_1_, bf16[2,256,256]{2,1,0:T(8,128)(2,1)S(1)} %copy-done, ...), custom_call_target="tpu_custom_call" | custom-call | flops 1 | bytes 1 | tf_op jit(solution)/shard_map/pallas_call | solution.py:58
  11.1 1.3 %collective-permute-start.5 = (bf16[1024,256]{1,0:T(8,128)(2,1)S(1)}, bf16[1024,256]{1,0:T(8,128)(2,1)S(1)}, u32[]{:S(2)}, u32[]{:S(2)}) collective-permute-start(bf16[1024,256]{1,0:T(8,128)(2,1)S(1)} %get-tuple-element.53.refs_4_.refs_2_), channel_id=1, source_target_pairs={{4,0},{6,2},{8,4},{10,6},{12,8},{14,10},{5,1},{7,3},{9,5},{11,7},{... | collective-permute-start | bytes 1572872 | tf_op jit(solution)/shard_map/ppermute | solution.py:285
  12.4 1.4 %shard_map.77 = (bf16[1024,256]{1,0:T(8,128)(2,1)S(1)}, bf16[1024,256]{1,0:T(8,128)(2,1)S(1)}, f32[1024,512]{1,0:T(8,128)S(1)}) custom-call(bf16[1024,256]{1,0:T(8,128)(2,1)S(1)} %get-tuple-element.52.refs_3_.refs_0_.refs_5_, bf16[1024,256]{1,0:T(8,128)(2,1)S(1)} %get-tuple-element.51.refs_1_.refs_0_.refs_6_, ...), custom_call_target="tpu_custom_call" | custom-call | flops 1 | bytes 1 | tf_op jit(solution)/shard_map/pallas_call | solution.py:58
  13.7 4.6 %collective-permute-start.6 = (bf16[1024,256]{1,0:T(8,128)(2,1)S(1)}, bf16[1024,256]{1,0:T(8,128)(2,1)S(1)}, u32[]{:S(2)}, u32[]{:S(2)}) collective-permute-start(bf16[1024,256]{1,0:T(8,128)(2,1)S(1)} %get-tuple-element.54.refs_4_.refs_0_.refs_5_), channel_id=1, source_target_pairs={{0,4},{2,6},{4,8},{6,10},{8,12},{10,14},{1,5},{3,7},{5,9},{7,11},{... | collective-permute-start | bytes 1572872 | tf_op jit(solution)/shard_map/ppermute | solution.py:285
  18.3 2.4 %collective-permute-done.1.refs_1_ = bf16[1024,256]{1,0:T(8,128)(2,1)S(1)} collective-permute-done((bf16[1024,256]{1,0:T(8,128)(2,1)S(1)}, bf16[1024,256]{1,0:T(8,128)(2,1)S(1)}, u32[]{:S(2)}, u32[]{:S(2)}) %collective-permute-start.1) | collective-permute-done | bytes 524320 | tf_op jit(solution)/shard_map/ppermute | solution.py:285
  20.8 1.4 %shard_map.78 = (bf16[1024,256]{1,0:T(8,128)(2,1)S(1)}, bf16[1024,256]{1,0:T(8,128)(2,1)S(1)}, f32[1024,512]{1,0:T(8,128)S(1)}) custom-call(bf16[1024,256]{1,0:T(8,128)(2,1)S(1)} %get-tuple-element.51.refs_1_.refs_0_.refs_6_, bf16[1024,256]{1,0:T(8,128)(2,1)S(1)} %collective-permute-done.1.refs_1_, ...), custom_call_target="tpu_custom_call" | custom-call | flops 1 | bytes 1 | tf_op jit(solution)/shard_map/pallas_call | solution.py:58
  22.1 1.3 %collective-permute-start.4 = (bf16[1024,256]{1,0:T(8,128)(2,1)S(1)}, bf16[1024,256]{1,0:T(8,128)(2,1)S(1)}, u32[]{:S(2)}, u32[]{:S(2)}) collective-permute-start(bf16[1024,256]{1,0:T(8,128)(2,1)S(1)} %get-tuple-element.55.refs_4_.refs_1_.refs_0_), channel_id=1, source_target_pairs={{4,0},{6,2},{8,4},{10,6},{12,8},{14,10},{5,1},{7,3},{9,5},{11,7},{... | collective-permute-start | bytes 1572872 | tf_op jit(solution)/shard_map/ppermute | solution.py:285
  23.4 6.8 %collective-permute-start.3 = (bf16[1024,256]{1,0:T(8,128)(2,1)S(1)}, bf16[1024,256]{1,0:T(8,128)(2,1)S(1)}, u32[]{:S(2)}, u32[]{:S(2)}) collective-permute-start(bf16[1024,256]{1,0:T(8,128)(2,1)S(1)} %get-tuple-element.55.refs_4_.refs_1_.refs_0_), channel_id=1, source_target_pairs={{0,4},{2,6},{4,8},{6,10},{8,12},{10,14},{1,5},{3,7},{5,9},{7,11},{... | collective-permute-start | bytes 1572872 | tf_op jit(solution)/shard_map/ppermute | solution.py:285
  30.2 0.0 collective-permute-done.6.refs_1_.refs_6_
  30.3 1.3 %shard_map.79 = (bf16[1024,512]{1,0:T(8,128)(2,1)S(1)}, bf16[1024,256]{1,0:T(8,128)(2,1)S(1)}, bf16[1024,256]{1,0:T(8,128)(2,1)S(1)}) custom-call(bf16[1024,256]{1,0:T(8,128)(2,1)S(1)} %get-tuple-element.54.refs_4_.refs_0_.refs_5_, bf16[1024,256]{1,0:T(8,128)(2,1)S(1)} %collective-permute-done.6.refs_1_.refs_6_, f32[1024,256]{1,0:T(8,128)S(1)} %get-tuple-element.57.refs_2_, ...), custom_call_target="tpu_custom_call" | custom-call | flops 1 | bytes 1 | tf_op jit(solution)/shard_map/pallas_call | solution.py:58
  31.6 1.3 %collective-permute-start.9 = (bf16[1024,256]{1,0:T(8,128)(2,1)S(1)}, bf16[1024,256]{1,0:T(8,128)(2,1)S(1)}, u32[]{:S(2)}, u32[]{:S(2)}) collective-permute-start(bf16[1024,256]{1,0:T(8,128)(2,1)S(1)} %get-tuple-element.67), channel_id=1, source_target_pairs={{4,0},{6,2},{8,4},{10,6},{12,8},{14,10},{5,1},{7,3},{9,5},{11,7},{... | collective-permute-start | bytes 1572872 | tf_op jit(solution)/shard_map/ppermute | solution.py:285
  32.9 0.6 shard_map.80
  33.5 7.6 %collective-permute-done.4.refs_0_ = bf16[1024,256]{1,0:T(8,128)(2,1)S(1)} collective-permute-done((bf16[1024,256]{1,0:T(8,128)(2,1)S(1)}, bf16[1024,256]{1,0:T(8,128)(2,1)S(1)}, u32[]{:S(2)}, u32[]{:S(2)}) %collective-permute-start.4) | collective-permute-done | bytes 524320 | tf_op jit(solution)/shard_map/ppermute | solution.py:285
  41.1 1.5 %shard_map.81.refs_4_ = f32[1024,256]{1,0:T(8,128)S(1)} custom-call(bf16[1024,256]{1,0:T(8,128)(2,1)S(1)} %collective-permute-done.4.refs_0_, bf16[1024,256]{1,0:T(8,128)(2,1)S(1)} %get-tuple-element.55.refs_4_.refs_1_.refs_0_, bf16[1024,256]{1,0:T(8,128)(2,1)S(1)} %collective-permute-done.5.refs_5_.refs_2_, ...), custom_call_target="tpu_custom_call" | custom-call | flops 1 | bytes 1 | tf_op jit(solution)/shard_map/pallas_call | solution.py:58
  42.6 0.0 collective-permute-done.3.refs_1_
  42.6 3.2 %shard_map.82 = (bf16[1024,256]{1,0:T(8,128)(2,1)S(1)}, bf16[1024,512]{1,0:T(8,128)(2,1)S(1)}, bf16[1024,256]{1,0:T(8,128)(2,1)S(1)}, bf16[1024,128]{1,0:T(8,128...) custom-call(bf16[1024,256]{1,0:T(8,128)(2,1)S(1)} %get-tuple-element, ...), custom_call_target="tpu_custom_call" | custom-call | flops 1 | bytes 1 | tf_op jit(solution)/shard_map/pallas_call | solution.py:58
  45.8 1.6 %shard_map.83 = (f32[1280,128]{1,0:T(8,128)S(1)}, bf16[1280,128]{1,0:T(8,128)(2,1)S(1)}) custom-call(bf16[1024,256]{1,0:T(8,128)(2,1)S(1)} %get-tuple-element.55.refs_4_.refs_1_.refs_0_, bf16[1024,256]{1,0:T(8,128)(2,1)S(1)} %collective-permute-done.3.refs_1_, bf16[1024,512]{1,0:T(8,128)(2,1)S(1)} %get-tuple-element.70.refs_2_, ...), custom_call_target="tpu_custom_call" | custom-call | flops 1 | bytes 1 | tf_op jit(solution)/shard_map/pallas_call | solution.py:58
  47.4 0.1 collective-permute-start.11
  47.5 1.5 %collective-permute-start.10 = (bf16[1024,256]{1,0:T(8,128)(2,1)S(1)}, bf16[1024,256]{1,0:T(8,128)(2,1)S(1)}, u32[]{:S(2)}, u32[]{:S(2)}) collective-permute-start(bf16[1024,256]{1,0:T(8,128)(2,1)S(1)} %get-tuple-element.74), channel_id=1, source_target_pairs={{2,0},{4,2},{6,4},{8,6},{10,8},{12,10},{14,12},{3,1},{5,3},{7,5},{... | collective-permute-start | bytes 1572872 | tf_op jit(solution)/shard_map/ppermute | solution.py:285
  48.9 1.2 %collective-permute-done.9.refs_1_ = bf16[1024,256]{1,0:T(8,128)(2,1)S(1)} collective-permute-done((bf16[1024,256]{1,0:T(8,128)(2,1)S(1)}, bf16[1024,256]{1,0:T(8,128)(2,1)S(1)}, u32[]{:S(2)}, u32[]{:S(2)}) %collective-permute-start.9) | collective-permute-done | bytes 524320 | tf_op jit(solution)/shard_map/ppermute | solution.py:285
  50.1 1.3 %shard_map.84 = (bf16[1024,128]{1,0:T(8,128)(2,1)S(1)}, bf16[1024,128]{1,0:T(8,128)(2,1)S(1)}, bf16[1024,256]{1,0:T(8,128)(2,1)S(1)}, bf16[1024,512]{1,0:T(8,128)(2,1)S(1)}, f32[1024,256]{1,0:T(8,128)S(1)}) custom-call(f32[1024,256]{1,0:T(8,128)S(1)} %get-tuple-element.61.refs_5_.refs_0_, bf16[1024,256]{1,0:T(8,128)(2,1)S(1)} %collective-permute-done.9.refs_1_, ...), custom_call_target="tpu_custom_call" | custom-call | flops 1 | bytes 1 | tf_op jit(solution)/shard_map/pallas_call | solution.py:58
  51.4 0.0 collective-permute-done.11.refs_1_
  51.4 0.1 shard_map.85
  51.5 1.6 %shard_map.86 = (f32[1280,128]{1,0:T(8,128)S(1)}, bf16[1280,128]{1,0:T(8,128)(2,1)S(1)}) custom-call(bf16[1024,256]{1,0:T(8,128)(2,1)S(1)} %get-tuple-element.51.refs_1_.refs_0_.refs_6_, bf16[1024,256]{1,0:T(8,128)(2,1)S(1)} %collective-permute-done.1.refs_1_, bf16[1024,512]{1,0:T(8,128)(2,1)S(1)} %get-tuple-element.78.refs_2_, ...), custom_call_target="tpu_custom_call" | custom-call | flops 1 | bytes 1 | tf_op jit(solution)/shard_map/pallas_call | solution.py:58
  53.1 0.1 collective-permute-start.13
  53.2 2.1 %collective-permute-start.12 = (bf16[640,128]{1,0:T(8,128)(2,1)S(1)}, bf16[640,128]{1,0:T(8,128)(2,1)S(1)}, u32[]{:S(2)}, u32[]{:S(2)}) collective-permute-start(bf16[640,128]{1,0:T(8,128)(2,1)S(1)} %get-tuple-element.77.refs_11_), channel_id=1, source_target_pairs={{0,2},{2,0},{4,6},{6,4},{8,10},{10,8},{12,14},{14,12},{1,3},{3,1},... | collective-permute-start | bytes 491528 | tf_op jit(solution)/shard_map/ppermute | solution.py:291
  55.3 0.1 shard_map.87
  55.4 1.3 %collective-permute-start.16 = (bf16[640,128]{1,0:T(8,128)(2,1)S(1)}, bf16[640,128]{1,0:T(8,128)(2,1)S(1)}, u32[]{:S(2)}, u32[]{:S(2)}) collective-permute-start(bf16[640,128]{1,0:T(8,128)(2,1)S(1)} %get-tuple-element.87.refs_3_), channel_id=1, source_target_pairs={{0,2},{2,0},{4,6},{6,4},{8,10},{10,8},{12,14},{14,12},{1,3},{3,1},... | collective-permute-start | bytes 491528 | tf_op jit(solution)/shard_map/ppermute | solution.py:291
  56.7 11.1 %collective-permute-done.12.refs_1_ = bf16[640,128]{1,0:T(8,128)(2,1)S(1)} collective-permute-done((bf16[640,128]{1,0:T(8,128)(2,1)S(1)}, bf16[640,128]{1,0:T(8,128)(2,1)S(1)}, u32[]{:S(2)}, u32[]{:S(2)}) %collective-permute-start.12) | collective-permute-done | bytes 163872 | tf_op jit(solution)/shard_map/ppermute | solution.py:291
  67.8 2.5 %collective-permute-start.18 = (bf16[320,128]{1,0:T(8,128)(2,1)S(1)}, bf16[320,128]{1,0:T(8,128)(2,1)S(1)}, u32[]{:S(2)}, u32[]{:S(2)}) collective-permute-start(bf16[320,128]{1,0:T(8,128)(2,1)S(1)} %get-tuple-element.89.refs_3_), channel_id=1, source_target_pairs={{0,4},{2,6},{4,0},{6,2},{8,12},{10,14},{12,8},{14,10},{1,5},{3,7},... | collective-permute-start | bytes 245768 | tf_op jit(solution)/shard_map/ppermute | solution.py:291
  70.4 0.0 collective-permute-done.10.refs_1_
  70.4 0.2 shard_map.89
  70.6 0.7 collective-permute-done.16.refs_1_
  71.3 2.5 %collective-permute-start.17 = (bf16[320,128]{1,0:T(8,128)(2,1)S(1)}, bf16[320,128]{1,0:T(8,128)(2,1)S(1)}, u32[]{:S(2)}, u32[]{:S(2)}) collective-permute-start(bf16[320,128]{1,0:T(8,128)(2,1)S(1)} %get-tuple-element.95.refs_3_), channel_id=1, source_target_pairs={{0,4},{2,6},{4,0},{6,2},{8,12},{10,14},{12,8},{14,10},{1,5},{3,7},... | collective-permute-start | bytes 245768 | tf_op jit(solution)/shard_map/ppermute | solution.py:291
  73.8 2.1 %collective-permute-start.20 = (bf16[320,128]{1,0:T(8,128)(2,1)S(1)}, bf16[320,128]{1,0:T(8,128)(2,1)S(1)}, u32[]{:S(2)}, u32[]{:S(2)}) collective-permute-start(bf16[320,128]{1,0:T(8,128)(2,1)S(1)} %shard_map.93.refs_2_.refs_0_), channel_id=1, source_target_pairs={{0,8},{2,10},{4,12},{6,14},{8,0},{10,2},{12,4},{14,6},{1,9},{3,11}... | collective-permute-start | bytes 245768 | tf_op jit(solution)/shard_map/ppermute | solution.py:291
  75.9 0.5 collective-permute-done.17.refs_1_
  76.5 3.7 %collective-permute-start.19 = (bf16[320,128]{1,0:T(8,128)(2,1)S(1)}, bf16[320,128]{1,0:T(8,128)(2,1)S(1)}, u32[]{:S(2)}, u32[]{:S(2)}) collective-permute-start(bf16[320,128]{1,0:T(8,128)(2,1)S(1)} %shard_map.94.refs_2_.refs_0_), channel_id=1, source_target_pairs={{0,8},{2,10},{4,12},{6,14},{8,0},{10,2},{12,4},{14,6},{1,9},{3,11}... | collective-permute-start | bytes 245768 | tf_op jit(solution)/shard_map/ppermute | solution.py:291
  80.2 1.7 %collective-permute-done.20.refs_1_ = bf16[320,128]{1,0:T(8,128)(2,1)S(1)} collective-permute-done((bf16[320,128]{1,0:T(8,128)(2,1)S(1)}, bf16[320,128]{1,0:T(8,128)(2,1)S(1)}, u32[]{:S(2)}, u32[]{:S(2)}) %collective-permute-start.20) | collective-permute-done | bytes 81952 | tf_op jit(solution)/shard_map/ppermute | solution.py:291
  81.9 0.1 collective-permute-start.22
  82.0 2.2 %collective-permute-done.19.refs_1_ = bf16[320,128]{1,0:T(8,128)(2,1)S(1)} collective-permute-done((bf16[320,128]{1,0:T(8,128)(2,1)S(1)}, bf16[320,128]{1,0:T(8,128)(2,1)S(1)}, u32[]{:S(2)}, u32[]{:S(2)}) %collective-permute-start.19) | collective-permute-done | bytes 81952 | tf_op jit(solution)/shard_map/ppermute | solution.py:291
  84.3 0.1 collective-permute-start.21
  84.3 2.1 %collective-permute-done.22.refs_1_.refs_4_ = bf16[320,128]{1,0:T(8,128)(2,1)S(1)} collective-permute-done((bf16[320,128]{1,0:T(8,128)(2,1)S(1)}, bf16[320,128]{1,0:T(8,128)(2,1)S(1)}, u32[]{:S(2)}, u32[]{:S(2)}) %collective-permute-start.22) | collective-permute-done | bytes 81952 | tf_op jit(solution)/shard_map/ppermute | solution.py:291
  86.4 2.6 %collective-permute-start.23 = (bf16[640,128]{1,0:T(8,128)(2,1)S(1)}, bf16[640,128]{1,0:T(8,128)(2,1)S(1)}, u32[]{:S(2)}, u32[]{:S(2)}) collective-permute-start(bf16[640,128]{1,0:T(8,128)(2,1)S(1)} %shard_map.97), channel_id=1, source_target_pairs={{0,2},{2,0},{4,6},{6,4},{8,10},{10,8},{12,14},{14,12},{1,3},{3,1},... | collective-permute-start | bytes 491528 | tf_op jit(solution)/shard_map/ppermute | solution.py:291
  89.0 0.0 collective-permute-start.8
  89.0 0.5 collective-permute-start.7
  89.5 0.0 collective-permute-start.14
  89.5 0.0 collective-permute-done.21.refs_1_
  89.5 0.5 collective-permute-start.15
  90.0 2.3 %collective-permute-done.23.refs_2_.refs_5_ = bf16[640,128]{1,0:T(8,128)(2,1)S(1)} collective-permute-done((bf16[640,128]{1,0:T(8,128)(2,1)S(1)}, bf16[640,128]{1,0:T(8,128)(2,1)S(1)}, u32[]{:S(2)}, u32[]{:S(2)}) %collective-permute-start.23) | collective-permute-done | bytes 163872 | tf_op jit(solution)/shard_map/ppermute | solution.py:291
  92.3 2.1 %collective-permute-start.24 = (bf16[640,128]{1,0:T(8,128)(2,1)S(1)}, bf16[640,128]{1,0:T(8,128)(2,1)S(1)}, u32[]{:S(2)}, u32[]{:S(2)}) collective-permute-start(bf16[640,128]{1,0:T(8,128)(2,1)S(1)} %shard_map.98), channel_id=1, source_target_pairs={{0,2},{2,0},{4,6},{6,4},{8,10},{10,8},{12,14},{14,12},{1,3},{3,1},... | collective-permute-start | bytes 491528 | tf_op jit(solution)/shard_map/ppermute | solution.py:291
  94.4 0.0 collective-permute-done.8.refs_3_
  94.4 0.0 collective-permute-done.7.refs_1_
  94.4 1.0 %shard_map.90 = bf16[4096,128]{1,0:T(8,128)(2,1)} custom-call(bf16[1024,128]{1,0:T(8,128)(2,1)S(1)} %get-tuple-element.63.refs_0_, bf16[1024,128]{1,0:T(8,128)(2,1)S(1)} %collective-permute-done.7.refs_1_, bf16[1024,128]{1,0:T(8,128)(2,1)S(1)} %get-tuple-element.65.refs_2_, bf16[1024,128]{1,0:T(8,128)(2,1)S(1)} %collective-permute-done.8.refs_3_, ...), custom_call_target="tpu_custom_call" | custom-call | flops 1 | bytes 1 | tf_op jit(solution)/shard_map/pallas_call | solution.py:58
  95.5 1.0 %shard_map.91 = bf16[4096,128]{1,0:T(8,128)(2,1)} custom-call(bf16[1024,128]{1,0:T(8,128)(2,1)S(1)} %get-tuple-element.91.refs_0_, bf16[1024,128]{1,0:T(8,128)(2,1)S(1)} %collective-permute-done.14.refs_1_, bf16[1024,128]{1,0:T(8,128)(2,1)S(1)} %get-tuple-element.90.refs_4_.refs_2_, bf16[1024,128]{1,0:T(8,128)(2,1)S(1)} %collective-permute-done.15.refs_3_), custom_call_target="tpu_custom_call" | custom-call | flops 1 | bytes 1 | tf_op jit(solution)/shard_map/pallas_call | solution.py:58
  96.5 1.2 %collective-permute-done.24.refs_2_ = bf16[640,128]{1,0:T(8,128)(2,1)S(1)} collective-permute-done((bf16[640,128]{1,0:T(8,128)(2,1)S(1)}, bf16[640,128]{1,0:T(8,128)(2,1)S(1)}, u32[]{:S(2)}, u32[]{:S(2)}) %collective-permute-start.24) | collective-permute-done | bytes 163872 | tf_op jit(solution)/shard_map/ppermute | solution.py:291
  97.7 1.3 %shard_map.99 = (f32[2048,128]{1,0:T(8,128)}, f32[512,128]{1,0:T(8,128)}) custom-call(bf16[320,128]{1,0:T(8,128)(2,1)S(1)} %shard_map.96.refs_2_.refs_0_, bf16[320,128]{1,0:T(8,128)(2,1)S(1)} %collective-permute-done.21.refs_1_, bf16[640,128]{1,0:T(8,128)(2,1)S(1)} %collective-permute-done.24.refs_2_, ...), custom_call_target="tpu_custom_call" | custom-call | flops 1 | bytes 1 | tf_op jit(solution)/shard_map/pallas_call | solution.py:58
  (18 shorter events, 0.2 us)
Async XLA Ops:
  0.6 3.7 %copy-start.1 = (bf16[4096,128]{1,0:T(8,128)(2,1)S(1)}, bf16[4096,128]{1,0:T(8,128)(2,1)}, u32[]{:S(2)}) copy-start(bf16[4096,128]{1,0:T(8,128)(2,1)} %refs_0_.2) | copy-start | bytes 3145732
  0.6 3.7 %collective-permute-start = (bf16[4096,128]{1,0:T(8,128)(2,1)}, bf16[4096,128]{1,0:T(8,128)(2,1)S(1)}, u32[]{:S(2)}, u32[]{:S(2)}) collective-permute-start(bf16[4096,128]{1,0:T(8,128)(2,1)} %refs_0_.2), channel_id=1, source_target_pairs={{0,1},{1,0},{2,3},{3,2},{4,5},{5,4},{6,7},{7,6},{8,9},{9,8},{10,11... | collective-permute-start | bytes 3145736 | tf_op jit(solution)/shard_map/ppermute | solution.py:295
  1.2 8.2 %collective-permute-start.2 = (bf16[4096,128]{1,0:T(8,128)(2,1)}, bf16[4096,128]{1,0:T(8,128)(2,1)}, u32[]{:S(2)}, u32[]{:S(2)}) collective-permute-start(bf16[4096,128]{1,0:T(8,128)(2,1)} %refs_0_.3), channel_id=1, source_target_pairs={{0,1},{1,0},{2,3},{3,2},{4,5},{5,4},{6,7},{7,6},{8,9},{9,8},{10,11... | collective-permute-start | bytes 3145736 | tf_op jit(solution)/shard_map/ppermute | solution.py:295
  3.0 6.4 %copy-start = (bf16[2,256,256]{2,1,0:T(8,128)(2,1)S(1)}, bf16[2,256,256]{2,1,0:T(8,128)(2,1)}, u32[]{:S(2)}) copy-start(bf16[2,256,256]{2,1,0:T(8,128)(2,1)} %refs_5_.3) | copy-start | bytes 786436
  3.0 6.4 %copy-start.2 = (bf16[4096,128]{1,0:T(8,128)(2,1)S(1)}, bf16[4096,128]{1,0:T(8,128)(2,1)}, u32[]{:S(2)}) copy-start(bf16[4096,128]{1,0:T(8,128)(2,1)} %refs_0_.3) | copy-start | bytes 3145732
  4.5 16.3 %collective-permute-start.1 = (bf16[1024,256]{1,0:T(8,128)(2,1)S(1)}, bf16[1024,256]{1,0:T(8,128)(2,1)S(1)}, u32[]{:S(2)}, u32[]{:S(2)}) collective-permute-start(bf16[1024,256]{1,0:T(8,128)(2,1)S(1)} %get-tuple-element.52.refs_3_.refs_0_.refs_5_), channel_id=1, source_target_pairs={{0,2},{2,4},{4,6},{6,8},{8,10},{10,12},{12,14},{1,3},{3,5},{5,7},{... | collective-permute-start | bytes 1572872 | tf_op jit(solution)/shard_map/ppermute | solution.py:285
  11.1 19.2 %collective-permute-start.5 = (bf16[1024,256]{1,0:T(8,128)(2,1)S(1)}, bf16[1024,256]{1,0:T(8,128)(2,1)S(1)}, u32[]{:S(2)}, u32[]{:S(2)}) collective-permute-start(bf16[1024,256]{1,0:T(8,128)(2,1)S(1)} %get-tuple-element.53.refs_4_.refs_2_), channel_id=1, source_target_pairs={{4,0},{6,2},{8,4},{10,6},{12,8},{14,10},{5,1},{7,3},{9,5},{11,7},{... | collective-permute-start | bytes 1572872 | tf_op jit(solution)/shard_map/ppermute | solution.py:285
  13.7 16.5 %collective-permute-start.6 = (bf16[1024,256]{1,0:T(8,128)(2,1)S(1)}, bf16[1024,256]{1,0:T(8,128)(2,1)S(1)}, u32[]{:S(2)}, u32[]{:S(2)}) collective-permute-start(bf16[1024,256]{1,0:T(8,128)(2,1)S(1)} %get-tuple-element.54.refs_4_.refs_0_.refs_5_), channel_id=1, source_target_pairs={{0,4},{2,6},{4,8},{6,10},{8,12},{10,14},{1,5},{3,7},{5,9},{7,11},{... | collective-permute-start | bytes 1572872 | tf_op jit(solution)/shard_map/ppermute | solution.py:285
  22.1 19.0 %collective-permute-start.4 = (bf16[1024,256]{1,0:T(8,128)(2,1)S(1)}, bf16[1024,256]{1,0:T(8,128)(2,1)S(1)}, u32[]{:S(2)}, u32[]{:S(2)}) collective-permute-start(bf16[1024,256]{1,0:T(8,128)(2,1)S(1)} %get-tuple-element.55.refs_4_.refs_1_.refs_0_), channel_id=1, source_target_pairs={{4,0},{6,2},{8,4},{10,6},{12,8},{14,10},{5,1},{7,3},{9,5},{11,7},{... | collective-permute-start | bytes 1572872 | tf_op jit(solution)/shard_map/ppermute | solution.py:285
  23.4 19.2 %collective-permute-start.3 = (bf16[1024,256]{1,0:T(8,128)(2,1)S(1)}, bf16[1024,256]{1,0:T(8,128)(2,1)S(1)}, u32[]{:S(2)}, u32[]{:S(2)}) collective-permute-start(bf16[1024,256]{1,0:T(8,128)(2,1)S(1)} %get-tuple-element.55.refs_4_.refs_1_.refs_0_), channel_id=1, source_target_pairs={{0,4},{2,6},{4,8},{6,10},{8,12},{10,14},{1,5},{3,7},{5,9},{7,11},{... | collective-permute-start | bytes 1572872 | tf_op jit(solution)/shard_map/ppermute | solution.py:285
  31.6 18.5 %collective-permute-start.9 = (bf16[1024,256]{1,0:T(8,128)(2,1)S(1)}, bf16[1024,256]{1,0:T(8,128)(2,1)S(1)}, u32[]{:S(2)}, u32[]{:S(2)}) collective-permute-start(bf16[1024,256]{1,0:T(8,128)(2,1)S(1)} %get-tuple-element.67), channel_id=1, source_target_pairs={{4,0},{6,2},{8,4},{10,6},{12,8},{14,10},{5,1},{7,3},{9,5},{11,7},{... | collective-permute-start | bytes 1572872 | tf_op jit(solution)/shard_map/ppermute | solution.py:285
  47.4 4.0 %collective-permute-start.11 = (bf16[1280,128]{1,0:T(8,128)(2,1)S(1)}, bf16[1280,128]{1,0:T(8,128)(2,1)S(1)}, u32[]{:S(2)}, u32[]{:S(2)}) collective-permute-start(bf16[1280,128]{1,0:T(8,128)(2,1)S(1)} %get-tuple-element.75), channel_id=1, source_target_pairs={{0,1},{1,0},{2,3},{3,2},{4,5},{5,4},{6,7},{7,6},{8,9},{9,8},{10,11... | collective-permute-start | bytes 983048 | tf_op jit(solution)/shard_map/ppermute | solution.py:295
  47.5 22.9 %collective-permute-start.10 = (bf16[1024,256]{1,0:T(8,128)(2,1)S(1)}, bf16[1024,256]{1,0:T(8,128)(2,1)S(1)}, u32[]{:S(2)}, u32[]{:S(2)}) collective-permute-start(bf16[1024,256]{1,0:T(8,128)(2,1)S(1)} %get-tuple-element.74), channel_id=1, source_target_pairs={{2,0},{4,2},{6,4},{8,6},{10,8},{12,10},{14,12},{3,1},{5,3},{7,5},{... | collective-permute-start | bytes 1572872 | tf_op jit(solution)/shard_map/ppermute | solution.py:285
  53.1 2.2 %collective-permute-start.13 = (bf16[1280,128]{1,0:T(8,128)(2,1)S(1)}, bf16[1280,128]{1,0:T(8,128)(2,1)S(1)}, u32[]{:S(2)}, u32[]{:S(2)}) collective-permute-start(bf16[1280,128]{1,0:T(8,128)(2,1)S(1)} %get-tuple-element.85), channel_id=1, source_target_pairs={{0,1},{1,0},{2,3},{3,2},{4,5},{5,4},{6,7},{7,6},{8,9},{9,8},{10,11... | collective-permute-start | bytes 983048 | tf_op jit(solution)/shard_map/ppermute | solution.py:295
  53.2 14.6 %collective-permute-start.12 = (bf16[640,128]{1,0:T(8,128)(2,1)S(1)}, bf16[640,128]{1,0:T(8,128)(2,1)S(1)}, u32[]{:S(2)}, u32[]{:S(2)}) collective-permute-start(bf16[640,128]{1,0:T(8,128)(2,1)S(1)} %get-tuple-element.77.refs_11_), channel_id=1, source_target_pairs={{0,2},{2,0},{4,6},{6,4},{8,10},{10,8},{12,14},{14,12},{1,3},{3,1},... | collective-permute-start | bytes 491528 | tf_op jit(solution)/shard_map/ppermute | solution.py:291
  55.4 15.8 %collective-permute-start.16 = (bf16[640,128]{1,0:T(8,128)(2,1)S(1)}, bf16[640,128]{1,0:T(8,128)(2,1)S(1)}, u32[]{:S(2)}, u32[]{:S(2)}) collective-permute-start(bf16[640,128]{1,0:T(8,128)(2,1)S(1)} %get-tuple-element.87.refs_3_), channel_id=1, source_target_pairs={{0,2},{2,0},{4,6},{6,4},{8,10},{10,8},{12,14},{14,12},{1,3},{3,1},... | collective-permute-start | bytes 491528 | tf_op jit(solution)/shard_map/ppermute | solution.py:291
  67.8 6.0 %collective-permute-start.18 = (bf16[320,128]{1,0:T(8,128)(2,1)S(1)}, bf16[320,128]{1,0:T(8,128)(2,1)S(1)}, u32[]{:S(2)}, u32[]{:S(2)}) collective-permute-start(bf16[320,128]{1,0:T(8,128)(2,1)S(1)} %get-tuple-element.89.refs_3_), channel_id=1, source_target_pairs={{0,4},{2,6},{4,0},{6,2},{8,12},{10,14},{12,8},{14,10},{1,5},{3,7},... | collective-permute-start | bytes 245768 | tf_op jit(solution)/shard_map/ppermute | solution.py:291
  71.3 5.2 %collective-permute-start.17 = (bf16[320,128]{1,0:T(8,128)(2,1)S(1)}, bf16[320,128]{1,0:T(8,128)(2,1)S(1)}, u32[]{:S(2)}, u32[]{:S(2)}) collective-permute-start(bf16[320,128]{1,0:T(8,128)(2,1)S(1)} %get-tuple-element.95.refs_3_), channel_id=1, source_target_pairs={{0,4},{2,6},{4,0},{6,2},{8,12},{10,14},{12,8},{14,10},{1,5},{3,7},... | collective-permute-start | bytes 245768 | tf_op jit(solution)/shard_map/ppermute | solution.py:291
  73.8 8.1 %collective-permute-start.20 = (bf16[320,128]{1,0:T(8,128)(2,1)S(1)}, bf16[320,128]{1,0:T(8,128)(2,1)S(1)}, u32[]{:S(2)}, u32[]{:S(2)}) collective-permute-start(bf16[320,128]{1,0:T(8,128)(2,1)S(1)} %shard_map.93.refs_2_.refs_0_), channel_id=1, source_target_pairs={{0,8},{2,10},{4,12},{6,14},{8,0},{10,2},{12,4},{14,6},{1,9},{3,11}... | collective-permute-start | bytes 245768 | tf_op jit(solution)/shard_map/ppermute | solution.py:291
  76.5 7.8 %collective-permute-start.19 = (bf16[320,128]{1,0:T(8,128)(2,1)S(1)}, bf16[320,128]{1,0:T(8,128)(2,1)S(1)}, u32[]{:S(2)}, u32[]{:S(2)}) collective-permute-start(bf16[320,128]{1,0:T(8,128)(2,1)S(1)} %shard_map.94.refs_2_.refs_0_), channel_id=1, source_target_pairs={{0,8},{2,10},{4,12},{6,14},{8,0},{10,2},{12,4},{14,6},{1,9},{3,11}... | collective-permute-start | bytes 245768 | tf_op jit(solution)/shard_map/ppermute | solution.py:291
  81.9 4.5 %collective-permute-start.22 = (bf16[320,128]{1,0:T(8,128)(2,1)S(1)}, bf16[320,128]{1,0:T(8,128)(2,1)S(1)}, u32[]{:S(2)}, u32[]{:S(2)}) collective-permute-start(bf16[320,128]{1,0:T(8,128)(2,1)S(1)} %shard_map.95.refs_2_.refs_0_.refs_3_), channel_id=1, source_target_pairs={{0,4},{2,6},{4,0},{6,2},{8,12},{10,14},{12,8},{14,10},{1,5},{3,7},... | collective-permute-start | bytes 245768 | tf_op jit(solution)/shard_map/ppermute | solution.py:291
  84.3 5.3 %collective-permute-start.21 = (bf16[320,128]{1,0:T(8,128)(2,1)S(1)}, bf16[320,128]{1,0:T(8,128)(2,1)S(1)}, u32[]{:S(2)}, u32[]{:S(2)}) collective-permute-start(bf16[320,128]{1,0:T(8,128)(2,1)S(1)} %shard_map.96.refs_2_.refs_0_), channel_id=1, source_target_pairs={{0,4},{2,6},{4,0},{6,2},{8,12},{10,14},{12,8},{14,10},{1,5},{3,7},... | collective-permute-start | bytes 245768 | tf_op jit(solution)/shard_map/ppermute | solution.py:291
  86.4 5.9 %collective-permute-start.23 = (bf16[640,128]{1,0:T(8,128)(2,1)S(1)}, bf16[640,128]{1,0:T(8,128)(2,1)S(1)}, u32[]{:S(2)}, u32[]{:S(2)}) collective-permute-start(bf16[640,128]{1,0:T(8,128)(2,1)S(1)} %shard_map.97), channel_id=1, source_target_pairs={{0,2},{2,0},{4,6},{6,4},{8,10},{10,8},{12,14},{14,12},{1,3},{3,1},... | collective-permute-start | bytes 491528 | tf_op jit(solution)/shard_map/ppermute | solution.py:291
  89.0 5.4 %collective-permute-start.8 = (bf16[1024,128]{1,0:T(8,128)(2,1)S(1)}, bf16[1024,128]{1,0:T(8,128)(2,1)S(1)}, u32[]{:S(2)}, u32[]{:S(2)}) collective-permute-start(bf16[1024,128]{1,0:T(8,128)(2,1)S(1)} %get-tuple-element.66), channel_id=1, source_target_pairs={{0,1},{1,0},{2,3},{3,2},{4,5},{5,4},{6,7},{7,6},{8,9},{9,8},{10,11... | collective-permute-start | bytes 786440 | tf_op jit(solution)/shard_map/ppermute | solution.py:295
  89.0 5.4 %collective-permute-start.7 = (bf16[1024,128]{1,0:T(8,128)(2,1)S(1)}, bf16[1024,128]{1,0:T(8,128)(2,1)S(1)}, u32[]{:S(2)}, u32[]{:S(2)}) collective-permute-start(bf16[1024,128]{1,0:T(8,128)(2,1)S(1)} %get-tuple-element.64), channel_id=1, source_target_pairs={{0,1},{1,0},{2,3},{3,2},{4,5},{5,4},{6,7},{7,6},{8,9},{9,8},{10,11... | collective-permute-start | bytes 786440 | tf_op jit(solution)/shard_map/ppermute | solution.py:295
  89.5 5.9 %collective-permute-start.14 = (bf16[1024,128]{1,0:T(8,128)(2,1)S(1)}, bf16[1024,128]{1,0:T(8,128)(2,1)S(1)}, u32[]{:S(2)}, u32[]{:S(2)}) collective-permute-start(bf16[1024,128]{1,0:T(8,128)(2,1)S(1)} %get-tuple-element.92), channel_id=1, source_target_pairs={{0,1},{1,0},{2,3},{3,2},{4,5},{5,4},{6,7},{7,6},{8,9},{9,8},{10,11... | collective-permute-start | bytes 786440 | tf_op jit(solution)/shard_map/ppermute | solution.py:295
  89.5 5.9 %collective-permute-start.15 = (bf16[1024,128]{1,0:T(8,128)(2,1)S(1)}, bf16[1024,128]{1,0:T(8,128)(2,1)S(1)}, u32[]{:S(2)}, u32[]{:S(2)}) collective-permute-start(bf16[1024,128]{1,0:T(8,128)(2,1)S(1)} %get-tuple-element.93), channel_id=1, source_target_pairs={{0,1},{1,0},{2,3},{3,2},{4,5},{5,4},{6,7},{7,6},{8,9},{9,8},{10,11... | collective-permute-start | bytes 786440 | tf_op jit(solution)/shard_map/ppermute | solution.py:295
  92.3 5.4 %collective-permute-start.24 = (bf16[640,128]{1,0:T(8,128)(2,1)S(1)}, bf16[640,128]{1,0:T(8,128)(2,1)S(1)}, u32[]{:S(2)}, u32[]{:S(2)}) collective-permute-start(bf16[640,128]{1,0:T(8,128)(2,1)S(1)} %shard_map.98), channel_id=1, source_target_pairs={{0,2},{2,0},{4,6},{6,4},{8,10},{10,8},{12,14},{14,12},{1,3},{3,1},... | collective-permute-start | bytes 491528 | tf_op jit(solution)/shard_map/ppermute | solution.py:291

commit v6 on v5

--- a/solution.py
+++ b/solution.py
@@ -249,15 +249,16 @@
     both_o[rows:, :] = second[...]
 
 
-def place_body(cuts, ids, *refs):
+def place_body(cuts, first, ids, *refs):
     conv_o, out_o = refs[-2:]
     pieces = 1 << cuts
     rows = refs[0].shape[0]
+    layers = (refs[:first], refs[first:-2])
     conv_rows = conv_o.shape[0] // 2
     out_rows = out_o.shape[0] // 2
     for layer in (0, 1):
         held = []
-        for ref in refs[layer * (cuts + 1) : (layer + 1) * (cuts + 1)]:
+        for ref in layers[layer]:
             held += [ref[r : r + rows, :] for r in range(0, ref.shape[0], rows)]
         for bit in range(cuts):
             swap = side(ids, cuts - 1 - bit) == 1
@@ -353,10 +354,12 @@
         return both[:, : 4 * channels], both[:, 4 * channels :]
     cols = sums0[0].shape[1]
     late = spread(ids, cuts, sums1[0], [sums0[0]])
+    own = sums0[0]
+    soon = [own] + [crossed(own, partner) for partner in ((2, 1, 3) if cuts == 2 else (1,))]
     return run(
-        functools.partial(place_body, cuts),
-        ids,
-        spread(ids, cuts, sums0[0], [late[-1]]) + late,
+        functools.partial(place_body, cuts, len(soon)),
+        ids,
+        soon + late,
         [((8 * channels, cols), F32), ((2 * channels, cols), F32)],
     )
 

time: 99.3 us -> 99 us (level)
  waiting for transfers between devices: 34.4 us -> 33.4 us
    ppermute x10 -> x11, starting transfers between devices: 19.1 us -> 20.3 us  [crossed(): lax.ppermute(values, 'tm', [(i, i ^ bit) for i in range(lax.axis_size('tm...]
    ppermute x10 -> x11, waiting for transfers between devices: 21.8 us -> 20.7 us  [crossed(): lax.ppermute(values, 'tm', [(i, i ^ bit) for i in range(lax.axis_size('tm...]
    pallas_call x25 -> x24, Pallas kernels: 19.5 us -> 19.5 us  [run(): pl.pallas_call(kernel, in_specs=[pl.BlockSpec(memory_space=pltpu.VMEM)] *...]
  transfers between devices with their start and end apart: 25 -> 26, of which waited for: 12 -> 10; matrix products, arithmetic and copies ran while one was open for 2% -> 2% of each run, Pallas kernels for 18% -> 18%
where the time goes in v6:
time: 99 us; the launch traced here: 98.7 us
  starting transfers between devices  43.1 us (44%)
  waiting for transfers between devices  33.4 us (34%)
  Pallas kernels  19.5 us (20%)
  local copies, waits for them, and re-layouts  1.75 us (2%)
    ppermute x7, starting transfers between devices, moved_by(): lax.ppermute(values, 'tm', [(i, i + distance) for i in devices if i + dis...  21.6 us
    ppermute x11, waiting for transfers between devices, crossed(): lax.ppermute(values, 'tm', [(i, i ^ bit) for i in range(lax.axis_size('tm...  20.7 us
    ppermute x11, starting transfers between devices, crossed(): lax.ppermute(values, 'tm', [(i, i ^ bit) for i in range(lax.axis_size('tm...  20.3 us
    pallas_call x24, Pallas kernels, run(): pl.pallas_call(kernel, in_specs=[pl.BlockSpec(memory_space=pltpu.VMEM)] *...  19.5 us
    ppermute x7, waiting for transfers between devices, moved_by(): lax.ppermute(values, 'tm', [(i, i + distance) for i in devices if i + dis...  11.2 us
  transfers between devices with their start and end apart: 26, of which 10 were waited for; matrix products, arithmetic and copies ran while one was open for 2% of the time, Pallas kernels for 18%

profile of v6, /device:TPU:0, one launch (start us, length us, event | category | flops | bytes accessed | tf_op | source)
XLA Modules:
  0.0 98.7 jit_solution(9757947680399135300)
XLA Ops:
  0.6 0.5 collective-permute-start
  1.2 0.1 collective-permute-start.2
  1.2 1.7 %reshape.17.refs_2_.refs_3_.refs_4_.refs_6_ = bf16[2,2,256,512]{3,2,1,0:T(8,128)(2,1)S(1)} reshape(bf16[2,2,256,2,256]{4,3,2,1,0:T(2,128)(2,1)} %param.6) | data formatting | bytes 2097152 | tf_op jit(solution)/shard_map/reshape | solution.py:375
  3.0 0.0 copy-start
  3.0 0.0 copy-start.2
  3.0 1.4 %collective-permute-done.refs_1_ = bf16[4096,128]{1,0:T(8,128)(2,1)S(1)} collective-permute-done((bf16[4096,128]{1,0:T(8,128)(2,1)}, bf16[4096,128]{1,0:T(8,128)(2,1)S(1)}, u32[]{:S(2)}, u32[]{:S(2)}) %collective-permute-start) | collective-permute-done | bytes 1048608 | tf_op jit(solution)/shard_map/ppermute | solution.py:296
  4.4 0.1 shard_map.75
  4.5 4.8 %collective-permute-start.1 = (bf16[1024,256]{1,0:T(8,128)(2,1)S(1)}, bf16[1024,256]{1,0:T(8,128)(2,1)S(1)}, u32[]{:S(2)}, u32[]{:S(2)}) collective-permute-start(bf16[1024,256]{1,0:T(8,128)(2,1)S(1)} %get-tuple-element.52.refs_3_.refs_0_.refs_5_), channel_id=1, source_target_pairs={{0,2},{2,4},{4,6},{6,8},{8,10},{10,12},{12,14},{1,3},{3,5},{5,7},{... | collective-permute-start | bytes 1572872 | tf_op jit(solution)/shard_map/ppermute | solution.py:286
  9.4 1.7 %shard_map.76 = (bf16[1024,256]{1,0:T(8,128)(2,1)S(1)}, bf16[1024,256]{1,0:T(8,128)(2,1)S(1)}, f32[1024,256]{1,0:T(8,128)S(1)}, f32[1024,256]{1,0:T(8,128)S(1)}) custom-call(bf16[4096,128]{1,0:T(8,128)(2,1)S(1)} %copy-done.2, bf16[4096,128]{1,0:T(8,128)(2,1)} %collective-permute-done.2.refs_1_, bf16[2,256,256]{2,1,0:T(8,128)(2,1)S(1)} %copy-done, ...), custom_call_target="tpu_custom_call" | custom-call | flops 1 | bytes 1 | tf_op jit(solution)/shard_map/pallas_call | solution.py:58
  11.1 1.3 %collective-permute-start.5 = (bf16[1024,256]{1,0:T(8,128)(2,1)S(1)}, bf16[1024,256]{1,0:T(8,128)(2,1)S(1)}, u32[]{:S(2)}, u32[]{:S(2)}) collective-permute-start(bf16[1024,256]{1,0:T(8,128)(2,1)S(1)} %get-tuple-element.53.refs_4_.refs_2_), channel_id=1, source_target_pairs={{4,0},{6,2},{8,4},{10,6},{12,8},{14,10},{5,1},{7,3},{9,5},{11,7},{... | collective-permute-start | bytes 1572872 | tf_op jit(solution)/shard_map/ppermute | solution.py:286
  12.4 1.4 %shard_map.77 = (bf16[1024,256]{1,0:T(8,128)(2,1)S(1)}, bf16[1024,256]{1,0:T(8,128)(2,1)S(1)}, f32[1024,512]{1,0:T(8,128)S(1)}) custom-call(bf16[1024,256]{1,0:T(8,128)(2,1)S(1)} %get-tuple-element.52.refs_3_.refs_0_.refs_5_, bf16[1024,256]{1,0:T(8,128)(2,1)S(1)} %get-tuple-element.51.refs_1_.refs_0_.refs_6_, ...), custom_call_target="tpu_custom_call" | custom-call | flops 1 | bytes 1 | tf_op jit(solution)/shard_map/pallas_call | solution.py:58
  13.7 4.6 %collective-permute-start.6 = (bf16[1024,256]{1,0:T(8,128)(2,1)S(1)}, bf16[1024,256]{1,0:T(8,128)(2,1)S(1)}, u32[]{:S(2)}, u32[]{:S(2)}) collective-permute-start(bf16[1024,256]{1,0:T(8,128)(2,1)S(1)} %get-tuple-element.54.refs_4_.refs_0_.refs_5_), channel_id=1, source_target_pairs={{0,4},{2,6},{4,8},{6,10},{8,12},{10,14},{1,5},{3,7},{5,9},{7,11},{... | collective-permute-start | bytes 1572872 | tf_op jit(solution)/shard_map/ppermute | solution.py:286
  18.3 2.4 %collective-permute-done.1.refs_1_ = bf16[1024,256]{1,0:T(8,128)(2,1)S(1)} collective-permute-done((bf16[1024,256]{1,0:T(8,128)(2,1)S(1)}, bf16[1024,256]{1,0:T(8,128)(2,1)S(1)}, u32[]{:S(2)}, u32[]{:S(2)}) %collective-permute-start.1) | collective-permute-done | bytes 524320 | tf_op jit(solution)/shard_map/ppermute | solution.py:286
  20.8 1.4 %shard_map.78 = (bf16[1024,256]{1,0:T(8,128)(2,1)S(1)}, bf16[1024,256]{1,0:T(8,128)(2,1)S(1)}, f32[1024,512]{1,0:T(8,128)S(1)}) custom-call(bf16[1024,256]{1,0:T(8,128)(2,1)S(1)} %get-tuple-element.51.refs_1_.refs_0_.refs_6_, bf16[1024,256]{1,0:T(8,128)(2,1)S(1)} %collective-permute-done.1.refs_1_, ...), custom_call_target="tpu_custom_call" | custom-call | flops 1 | bytes 1 | tf_op jit(solution)/shard_map/pallas_call | solution.py:58
  22.1 1.3 %collective-permute-start.4 = (bf16[1024,256]{1,0:T(8,128)(2,1)S(1)}, bf16[1024,256]{1,0:T(8,128)(2,1)S(1)}, u32[]{:S(2)}, u32[]{:S(2)}) collective-permute-start(bf16[1024,256]{1,0:T(8,128)(2,1)S(1)} %get-tuple-element.55.refs_4_.refs_1_.refs_0_), channel_id=1, source_target_pairs={{4,0},{6,2},{8,4},{10,6},{12,8},{14,10},{5,1},{7,3},{9,5},{11,7},{... | collective-permute-start | bytes 1572872 | tf_op jit(solution)/shard_map/ppermute | solution.py:286
  23.4 6.8 %collective-permute-start.3 = (bf16[1024,256]{1,0:T(8,128)(2,1)S(1)}, bf16[1024,256]{1,0:T(8,128)(2,1)S(1)}, u32[]{:S(2)}, u32[]{:S(2)}) collective-permute-start(bf16[1024,256]{1,0:T(8,128)(2,1)S(1)} %get-tuple-element.55.refs_4_.refs_1_.refs_0_), channel_id=1, source_target_pairs={{0,4},{2,6},{4,8},{6,10},{8,12},{10,14},{1,5},{3,7},{5,9},{7,11},{... | collective-permute-start | bytes 1572872 | tf_op jit(solution)/shard_map/ppermute | solution.py:286
  30.2 0.0 collective-permute-done.5.refs_5_.refs_2_
  30.2 0.0 collective-permute-done.6.refs_1_.refs_6_
  30.3 1.3 %shard_map.79 = (bf16[1024,512]{1,0:T(8,128)(2,1)S(1)}, bf16[1024,256]{1,0:T(8,128)(2,1)S(1)}, bf16[1024,256]{1,0:T(8,128)(2,1)S(1)}) custom-call(bf16[1024,256]{1,0:T(8,128)(2,1)S(1)} %get-tuple-element.54.refs_4_.refs_0_.refs_5_, bf16[1024,256]{1,0:T(8,128)(2,1)S(1)} %collective-permute-done.6.refs_1_.refs_6_, f32[1024,256]{1,0:T(8,128)S(1)} %get-tuple-element.57.refs_2_, ...), custom_call_target="tpu_custom_call" | custom-call | flops 1 | bytes 1 | tf_op jit(solution)/shard_map/pallas_call | solution.py:58
  31.6 1.3 %collective-permute-start.9 = (bf16[1024,256]{1,0:T(8,128)(2,1)S(1)}, bf16[1024,256]{1,0:T(8,128)(2,1)S(1)}, u32[]{:S(2)}, u32[]{:S(2)}) collective-permute-start(bf16[1024,256]{1,0:T(8,128)(2,1)S(1)} %get-tuple-element.67), channel_id=1, source_target_pairs={{4,0},{6,2},{8,4},{10,6},{12,8},{14,10},{5,1},{7,3},{9,5},{11,7},{... | collective-permute-start | bytes 1572872 | tf_op jit(solution)/shard_map/ppermute | solution.py:286
  32.9 0.6 shard_map.80
  33.5 7.6 %collective-permute-done.4.refs_0_ = bf16[1024,256]{1,0:T(8,128)(2,1)S(1)} collective-permute-done((bf16[1024,256]{1,0:T(8,128)(2,1)S(1)}, bf16[1024,256]{1,0:T(8,128)(2,1)S(1)}, u32[]{:S(2)}, u32[]{:S(2)}) %collective-permute-start.4) | collective-permute-done | bytes 524320 | tf_op jit(solution)/shard_map/ppermute | solution.py:286
  41.1 1.5 %shard_map.81.refs_4_ = f32[1024,256]{1,0:T(8,128)S(1)} custom-call(bf16[1024,256]{1,0:T(8,128)(2,1)S(1)} %collective-permute-done.4.refs_0_, bf16[1024,256]{1,0:T(8,128)(2,1)S(1)} %get-tuple-element.55.refs_4_.refs_1_.refs_0_, bf16[1024,256]{1,0:T(8,128)(2,1)S(1)} %collective-permute-done.5.refs_5_.refs_2_, ...), custom_call_target="tpu_custom_call" | custom-call | flops 1 | bytes 1 | tf_op jit(solution)/shard_map/pallas_call | solution.py:58
  42.6 0.0 collective-permute-done.3.refs_1_
  42.6 3.2 %shard_map.82 = (bf16[1024,256]{1,0:T(8,128)(2,1)S(1)}, bf16[1024,512]{1,0:T(8,128)(2,1)S(1)}, bf16[1024,256]{1,0:T(8,128)(2,1)S(1)}, bf16[1024,128]{1,0:T(8,128...) custom-call(bf16[1024,256]{1,0:T(8,128)(2,1)S(1)} %get-tuple-element, ...), custom_call_target="tpu_custom_call" | custom-call | flops 1 | bytes 1 | tf_op jit(solution)/shard_map/pallas_call | solution.py:58
  45.8 1.6 %shard_map.83 = (f32[1280,128]{1,0:T(8,128)S(1)}, bf16[1280,128]{1,0:T(8,128)(2,1)S(1)}) custom-call(bf16[1024,256]{1,0:T(8,128)(2,1)S(1)} %get-tuple-element.55.refs_4_.refs_1_.refs_0_, bf16[1024,256]{1,0:T(8,128)(2,1)S(1)} %collective-permute-done.3.refs_1_, bf16[1024,512]{1,0:T(8,128)(2,1)S(1)} %get-tuple-element.70.refs_2_, ...), custom_call_target="tpu_custom_call" | custom-call | flops 1 | bytes 1 | tf_op jit(solution)/shard_map/pallas_call | solution.py:58
  47.4 0.1 collective-permute-start.11
  47.5 1.5 %collective-permute-start.10 = (bf16[1024,256]{1,0:T(8,128)(2,1)S(1)}, bf16[1024,256]{1,0:T(8,128)(2,1)S(1)}, u32[]{:S(2)}, u32[]{:S(2)}) collective-permute-start(bf16[1024,256]{1,0:T(8,128)(2,1)S(1)} %get-tuple-element.74), channel_id=1, source_target_pairs={{2,0},{4,2},{6,4},{8,6},{10,8},{12,10},{14,12},{3,1},{5,3},{7,5},{... | collective-permute-start | bytes 1572872 | tf_op jit(solution)/shard_map/ppermute | solution.py:286
  48.9 1.2 %collective-permute-done.9.refs_1_ = bf16[1024,256]{1,0:T(8,128)(2,1)S(1)} collective-permute-done((bf16[1024,256]{1,0:T(8,128)(2,1)S(1)}, bf16[1024,256]{1,0:T(8,128)(2,1)S(1)}, u32[]{:S(2)}, u32[]{:S(2)}) %collective-permute-start.9) | collective-permute-done | bytes 524320 | tf_op jit(solution)/shard_map/ppermute | solution.py:286
  50.1 1.3 %shard_map.84 = (bf16[1024,128]{1,0:T(8,128)(2,1)S(1)}, bf16[1024,128]{1,0:T(8,128)(2,1)S(1)}, bf16[1024,256]{1,0:T(8,128)(2,1)S(1)}, bf16[1024,512]{1,0:T(8,128)(2,1)S(1)}, f32[1024,256]{1,0:T(8,128)S(1)}) custom-call(f32[1024,256]{1,0:T(8,128)S(1)} %get-tuple-element.61.refs_5_.refs_0_, bf16[1024,256]{1,0:T(8,128)(2,1)S(1)} %collective-permute-done.9.refs_1_, ...), custom_call_target="tpu_custom_call" | custom-call | flops 1 | bytes 1 | tf_op jit(solution)/shard_map/pallas_call | solution.py:58
  51.4 0.1 shard_map.85
  51.5 1.6 %shard_map.86 = (f32[1280,128]{1,0:T(8,128)S(1)}, bf16[1280,128]{1,0:T(8,128)(2,1)S(1)}) custom-call(bf16[1024,256]{1,0:T(8,128)(2,1)S(1)} %get-tuple-element.51.refs_1_.refs_0_.refs_6_, bf16[1024,256]{1,0:T(8,128)(2,1)S(1)} %collective-permute-done.1.refs_1_, bf16[1024,512]{1,0:T(8,128)(2,1)S(1)} %get-tuple-element.78.refs_2_, ...), custom_call_target="tpu_custom_call" | custom-call | flops 1 | bytes 1 | tf_op jit(solution)/shard_map/pallas_call | solution.py:58
  53.1 0.1 collective-permute-start.13
  53.2 2.1 %collective-permute-start.12 = (bf16[640,128]{1,0:T(8,128)(2,1)S(1)}, bf16[640,128]{1,0:T(8,128)(2,1)S(1)}, u32[]{:S(2)}, u32[]{:S(2)}) collective-permute-start(bf16[640,128]{1,0:T(8,128)(2,1)S(1)} %get-tuple-element.77.refs_11_), channel_id=1, source_target_pairs={{0,2},{2,0},{4,6},{6,4},{8,10},{10,8},{12,14},{14,12},{1,3},{3,1},... | collective-permute-start | bytes 491528 | tf_op jit(solution)/shard_map/ppermute | solution.py:292
  55.3 0.0 collective-permute-done.13.refs_1_
  55.3 0.1 shard_map.87
  55.4 1.3 %collective-permute-start.16 = (bf16[640,128]{1,0:T(8,128)(2,1)S(1)}, bf16[640,128]{1,0:T(8,128)(2,1)S(1)}, u32[]{:S(2)}, u32[]{:S(2)}) collective-permute-start(bf16[640,128]{1,0:T(8,128)(2,1)S(1)} %get-tuple-element.87.refs_3_), channel_id=1, source_target_pairs={{0,2},{2,0},{4,6},{6,4},{8,10},{10,8},{12,14},{14,12},{1,3},{3,1},... | collective-permute-start | bytes 491528 | tf_op jit(solution)/shard_map/ppermute | solution.py:292
  56.7 11.1 %collective-permute-done.12.refs_1_ = bf16[640,128]{1,0:T(8,128)(2,1)S(1)} collective-permute-done((bf16[640,128]{1,0:T(8,128)(2,1)S(1)}, bf16[640,128]{1,0:T(8,128)(2,1)S(1)}, u32[]{:S(2)}, u32[]{:S(2)}) %collective-permute-start.12) | collective-permute-done | bytes 163872 | tf_op jit(solution)/shard_map/ppermute | solution.py:292
  67.8 2.5 %collective-permute-start.18 = (bf16[320,128]{1,0:T(8,128)(2,1)S(1)}, bf16[320,128]{1,0:T(8,128)(2,1)S(1)}, u32[]{:S(2)}, u32[]{:S(2)}) collective-permute-start(bf16[320,128]{1,0:T(8,128)(2,1)S(1)} %get-tuple-element.89.refs_3_), channel_id=1, source_target_pairs={{0,4},{2,6},{4,0},{6,2},{8,12},{10,14},{12,8},{14,10},{1,5},{3,7},... | collective-permute-start | bytes 245768 | tf_op jit(solution)/shard_map/ppermute | solution.py:292
  70.4 0.0 collective-permute-done.10.refs_1_
  70.4 0.2 shard_map.89
  70.6 0.7 collective-permute-done.16.refs_1_
  71.3 2.5 %collective-permute-start.17 = (bf16[320,128]{1,0:T(8,128)(2,1)S(1)}, bf16[320,128]{1,0:T(8,128)(2,1)S(1)}, u32[]{:S(2)}, u32[]{:S(2)}) collective-permute-start(bf16[320,128]{1,0:T(8,128)(2,1)S(1)} %get-tuple-element.95.refs_3_), channel_id=1, source_target_pairs={{0,4},{2,6},{4,0},{6,2},{8,12},{10,14},{12,8},{14,10},{1,5},{3,7},... | collective-permute-start | bytes 245768 | tf_op jit(solution)/shard_map/ppermute | solution.py:292
  73.8 2.1 %collective-permute-start.20 = (bf16[320,128]{1,0:T(8,128)(2,1)S(1)}, bf16[320,128]{1,0:T(8,128)(2,1)S(1)}, u32[]{:S(2)}, u32[]{:S(2)}) collective-permute-start(bf16[320,128]{1,0:T(8,128)(2,1)S(1)} %shard_map.93.refs_2_.refs_0_), channel_id=1, source_target_pairs={{0,8},{2,10},{4,12},{6,14},{8,0},{10,2},{12,4},{14,6},{1,9},{3,11}... | collective-permute-start | bytes 245768 | tf_op jit(solution)/shard_map/ppermute | solution.py:292
  75.9 0.5 collective-permute-start.7
  76.4 0.0 collective-permute-start.14
  76.4 0.0 collective-permute-done.17.refs_1_
  76.5 3.7 %collective-permute-start.19 = (bf16[320,128]{1,0:T(8,128)(2,1)S(1)}, bf16[320,128]{1,0:T(8,128)(2,1)S(1)}, u32[]{:S(2)}, u32[]{:S(2)}) collective-permute-start(bf16[320,128]{1,0:T(8,128)(2,1)S(1)} %shard_map.94.refs_2_.refs_0_), channel_id=1, source_target_pairs={{0,8},{2,10},{4,12},{6,14},{8,0},{10,2},{12,4},{14,6},{1,9},{3,11}... | collective-permute-start | bytes 245768 | tf_op jit(solution)/shard_map/ppermute | solution.py:292
  80.2 0.6 collective-permute-done.20.refs_1_
  80.8 0.0 collective-permute-start.15
  80.8 3.4 %collective-permute-done.19.refs_1_ = bf16[320,128]{1,0:T(8,128)(2,1)S(1)} collective-permute-done((bf16[320,128]{1,0:T(8,128)(2,1)S(1)}, bf16[320,128]{1,0:T(8,128)(2,1)S(1)}, u32[]{:S(2)}, u32[]{:S(2)}) %collective-permute-start.19) | collective-permute-done | bytes 81952 | tf_op jit(solution)/shard_map/ppermute | solution.py:292
  84.2 0.0 collective-permute-start.24
  84.2 4.4 %collective-permute-done.24.refs_1_.refs_5_ = bf16[320,128]{1,0:T(8,128)(2,1)S(1)} collective-permute-done((bf16[320,128]{1,0:T(8,128)(2,1)S(1)}, bf16[320,128]{1,0:T(8,128)(2,1)S(1)}, u32[]{:S(2)}, u32[]{:S(2)}) %collective-permute-start.24) | collective-permute-done | bytes 81952 | tf_op jit(solution)/shard_map/ppermute | solution.py:292
  88.6 2.6 %collective-permute-start.25 = (bf16[640,128]{1,0:T(8,128)(2,1)S(1)}, bf16[640,128]{1,0:T(8,128)(2,1)S(1)}, u32[]{:S(2)}, u32[]{:S(2)}) collective-permute-start(bf16[640,128]{1,0:T(8,128)(2,1)S(1)} %shard_map.97), channel_id=1, source_target_pairs={{0,2},{2,0},{4,6},{6,4},{8,10},{10,8},{12,14},{14,12},{1,3},{3,1},... | collective-permute-start | bytes 491528 | tf_op jit(solution)/shard_map/ppermute | solution.py:292
  91.2 0.0 collective-permute-done.7.refs_1_
  91.2 1.7 %collective-permute-start.22 = (bf16[320,128]{1,0:T(8,128)(2,1)S(1)}, bf16[320,128]{1,0:T(8,128)(2,1)S(1)}, u32[]{:S(2)}, u32[]{:S(2)}) collective-permute-start(bf16[320,128]{1,0:T(8,128)(2,1)S(1)} %shard_map.96.refs_2_.refs_0_), channel_id=1, source_target_pairs={{0,2},{2,0},{4,6},{6,4},{8,10},{10,8},{12,14},{14,12},{1,3},{3,1},... | collective-permute-start | bytes 245768 | tf_op jit(solution)/shard_map/ppermute | solution.py:292
  92.9 1.8 %collective-permute-start.21 = (bf16[320,128]{1,0:T(8,128)(2,1)S(1)}, bf16[320,128]{1,0:T(8,128)(2,1)S(1)}, u32[]{:S(2)}, u32[]{:S(2)}) collective-permute-start(bf16[320,128]{1,0:T(8,128)(2,1)S(1)} %shard_map.96.refs_2_.refs_0_), channel_id=1, source_target_pairs={{0,4},{2,6},{4,0},{6,2},{8,12},{10,14},{12,8},{14,10},{1,5},{3,7},... | collective-permute-start | bytes 245768 | tf_op jit(solution)/shard_map/ppermute | solution.py:292
  94.7 1.0 %shard_map.90 = bf16[4096,128]{1,0:T(8,128)(2,1)} custom-call(bf16[1024,128]{1,0:T(8,128)(2,1)S(1)} %get-tuple-element.63.refs_0_, bf16[1024,128]{1,0:T(8,128)(2,1)S(1)} %collective-permute-done.7.refs_1_, bf16[1024,128]{1,0:T(8,128)(2,1)S(1)} %get-tuple-element.65.refs_2_, bf16[1024,128]{1,0:T(8,128)(2,1)S(1)} %collective-permute-done.8.refs_3_, ...), custom_call_target="tpu_custom_call" | custom-call | flops 1 | bytes 1 | tf_op jit(solution)/shard_map/pallas_call | solution.py:58
  95.7 0.0 collective-permute-done.15.refs_3_
  95.7 1.0 %shard_map.91 = bf16[4096,128]{1,0:T(8,128)(2,1)} custom-call(bf16[1024,128]{1,0:T(8,128)(2,1)S(1)} %get-tuple-element.91.refs_0_, bf16[1024,128]{1,0:T(8,128)(2,1)S(1)} %collective-permute-done.14.refs_1_, bf16[1024,128]{1,0:T(8,128)(2,1)S(1)} %get-tuple-element.90.refs_4_.refs_2_, bf16[1024,128]{1,0:T(8,128)(2,1)S(1)} %collective-permute-done.15.refs_3_), custom_call_target="tpu_custom_call" | custom-call | flops 1 | bytes 1 | tf_op jit(solution)/shard_map/pallas_call | solution.py:58
  96.8 0.0 collective-permute-done.23.refs_3_
  96.8 0.0 collective-permute-done.22.refs_2_
  96.8 0.5 collective-permute-done.21.refs_1_
  97.4 1.3 %shard_map.98 = (f32[2048,128]{1,0:T(8,128)}, f32[512,128]{1,0:T(8,128)}) custom-call(bf16[320,128]{1,0:T(8,128)(2,1)S(1)} %shard_map.96.refs_2_.refs_0_, bf16[320,128]{1,0:T(8,128)(2,1)S(1)} %collective-permute-done.21.refs_1_, bf16[320,128]{1,0:T(8,128)(2,1)S(1)} %collective-permute-done.22.refs_2_, bf16[320,128]{1,0:T(8,128)(2,1)S(1)} %collective-permute-done.23.refs_3_, ...), custom_call_target="tpu_custom_call" | custom-call | flops 1 | bytes 1 | tf_op jit(solution)/shard_map/pallas_call | solution.py:58
  (19 shorter events, 0.2 us)
Async XLA Ops:
  0.6 3.7 %copy-start.1 = (bf16[4096,128]{1,0:T(8,128)(2,1)S(1)}, bf16[4096,128]{1,0:T(8,128)(2,1)}, u32[]{:S(2)}) copy-start(bf16[4096,128]{1,0:T(8,128)(2,1)} %refs_0_.2) | copy-start | bytes 3145732
  0.6 3.7 %collective-permute-start = (bf16[4096,128]{1,0:T(8,128)(2,1)}, bf16[4096,128]{1,0:T(8,128)(2,1)S(1)}, u32[]{:S(2)}, u32[]{:S(2)}) collective-permute-start(bf16[4096,128]{1,0:T(8,128)(2,1)} %refs_0_.2), channel_id=1, source_target_pairs={{0,1},{1,0},{2,3},{3,2},{4,5},{5,4},{6,7},{7,6},{8,9},{9,8},{10,11... | collective-permute-start | bytes 3145736 | tf_op jit(solution)/shard_map/ppermute | solution.py:296
  1.2 8.2 %collective-permute-start.2 = (bf16[4096,128]{1,0:T(8,128)(2,1)}, bf16[4096,128]{1,0:T(8,128)(2,1)}, u32[]{:S(2)}, u32[]{:S(2)}) collective-permute-start(bf16[4096,128]{1,0:T(8,128)(2,1)} %refs_0_.3), channel_id=1, source_target_pairs={{0,1},{1,0},{2,3},{3,2},{4,5},{5,4},{6,7},{7,6},{8,9},{9,8},{10,11... | collective-permute-start | bytes 3145736 | tf_op jit(solution)/shard_map/ppermute | solution.py:296
  3.0 6.4 %copy-start = (bf16[2,256,256]{2,1,0:T(8,128)(2,1)S(1)}, bf16[2,256,256]{2,1,0:T(8,128)(2,1)}, u32[]{:S(2)}) copy-start(bf16[2,256,256]{2,1,0:T(8,128)(2,1)} %refs_5_.3) | copy-start | bytes 786436
  3.0 6.4 %copy-start.2 = (bf16[4096,128]{1,0:T(8,128)(2,1)S(1)}, bf16[4096,128]{1,0:T(8,128)(2,1)}, u32[]{:S(2)}) copy-start(bf16[4096,128]{1,0:T(8,128)(2,1)} %refs_0_.3) | copy-start | bytes 3145732
  4.5 16.3 %collective-permute-start.1 = (bf16[1024,256]{1,0:T(8,128)(2,1)S(1)}, bf16[1024,256]{1,0:T(8,128)(2,1)S(1)}, u32[]{:S(2)}, u32[]{:S(2)}) collective-permute-start(bf16[1024,256]{1,0:T(8,128)(2,1)S(1)} %get-tuple-element.52.refs_3_.refs_0_.refs_5_), channel_id=1, source_target_pairs={{0,2},{2,4},{4,6},{6,8},{8,10},{10,12},{12,14},{1,3},{3,5},{5,7},{... | collective-permute-start | bytes 1572872 | tf_op jit(solution)/shard_map/ppermute | solution.py:286
  11.1 19.2 %collective-permute-start.5 = (bf16[1024,256]{1,0:T(8,128)(2,1)S(1)}, bf16[1024,256]{1,0:T(8,128)(2,1)S(1)}, u32[]{:S(2)}, u32[]{:S(2)}) collective-permute-start(bf16[1024,256]{1,0:T(8,128)(2,1)S(1)} %get-tuple-element.53.refs_4_.refs_2_), channel_id=1, source_target_pairs={{4,0},{6,2},{8,4},{10,6},{12,8},{14,10},{5,1},{7,3},{9,5},{11,7},{... | collective-permute-start | bytes 1572872 | tf_op jit(solution)/shard_map/ppermute | solution.py:286
  13.7 16.5 %collective-permute-start.6 = (bf16[1024,256]{1,0:T(8,128)(2,1)S(1)}, bf16[1024,256]{1,0:T(8,128)(2,1)S(1)}, u32[]{:S(2)}, u32[]{:S(2)}) collective-permute-start(bf16[1024,256]{1,0:T(8,128)(2,1)S(1)} %get-tuple-element.54.refs_4_.refs_0_.refs_5_), channel_id=1, source_target_pairs={{0,4},{2,6},{4,8},{6,10},{8,12},{10,14},{1,5},{3,7},{5,9},{7,11},{... | collective-permute-start | bytes 1572872 | tf_op jit(solution)/shard_map/ppermute | solution.py:286
  22.1 19.0 %collective-permute-start.4 = (bf16[1024,256]{1,0:T(8,128)(2,1)S(1)}, bf16[1024,256]{1,0:T(8,128)(2,1)S(1)}, u32[]{:S(2)}, u32[]{:S(2)}) collective-permute-start(bf16[1024,256]{1,0:T(8,128)(2,1)S(1)} %get-tuple-element.55.refs_4_.refs_1_.refs_0_), channel_id=1, source_target_pairs={{4,0},{6,2},{8,4},{10,6},{12,8},{14,10},{5,1},{7,3},{9,5},{11,7},{... | collective-permute-start | bytes 1572872 | tf_op jit(solution)/shard_map/ppermute | solution.py:286
  23.4 19.2 %collective-permute-start.3 = (bf16[1024,256]{1,0:T(8,128)(2,1)S(1)}, bf16[1024,256]{1,0:T(8,128)(2,1)S(1)}, u32[]{:S(2)}, u32[]{:S(2)}) collective-permute-start(bf16[1024,256]{1,0:T(8,128)(2,1)S(1)} %get-tuple-element.55.refs_4_.refs_1_.refs_0_), channel_id=1, source_target_pairs={{0,4},{2,6},{4,8},{6,10},{8,12},{10,14},{1,5},{3,7},{5,9},{7,11},{... | collective-permute-start | bytes 1572872 | tf_op jit(solution)/shard_map/ppermute | solution.py:286
  31.6 18.5 %collective-permute-start.9 = (bf16[1024,256]{1,0:T(8,128)(2,1)S(1)}, bf16[1024,256]{1,0:T(8,128)(2,1)S(1)}, u32[]{:S(2)}, u32[]{:S(2)}) collective-permute-start(bf16[1024,256]{1,0:T(8,128)(2,1)S(1)} %get-tuple-element.67), channel_id=1, source_target_pairs={{4,0},{6,2},{8,4},{10,6},{12,8},{14,10},{5,1},{7,3},{9,5},{11,7},{... | collective-permute-start | bytes 1572872 | tf_op jit(solution)/shard_map/ppermute | solution.py:286
  47.4 4.0 %collective-permute-start.11 = (bf16[1280,128]{1,0:T(8,128)(2,1)S(1)}, bf16[1280,128]{1,0:T(8,128)(2,1)S(1)}, u32[]{:S(2)}, u32[]{:S(2)}) collective-permute-start(bf16[1280,128]{1,0:T(8,128)(2,1)S(1)} %get-tuple-element.75), channel_id=1, source_target_pairs={{0,1},{1,0},{2,3},{3,2},{4,5},{5,4},{6,7},{7,6},{8,9},{9,8},{10,11... | collective-permute-start | bytes 983048 | tf_op jit(solution)/shard_map/ppermute | solution.py:296
  47.5 22.9 %collective-permute-start.10 = (bf16[1024,256]{1,0:T(8,128)(2,1)S(1)}, bf16[1024,256]{1,0:T(8,128)(2,1)S(1)}, u32[]{:S(2)}, u32[]{:S(2)}) collective-permute-start(bf16[1024,256]{1,0:T(8,128)(2,1)S(1)} %get-tuple-element.74), channel_id=1, source_target_pairs={{2,0},{4,2},{6,4},{8,6},{10,8},{12,10},{14,12},{3,1},{5,3},{7,5},{... | collective-permute-start | bytes 1572872 | tf_op jit(solution)/shard_map/ppermute | solution.py:286
  53.1 2.2 %collective-permute-start.13 = (bf16[1280,128]{1,0:T(8,128)(2,1)S(1)}, bf16[1280,128]{1,0:T(8,128)(2,1)S(1)}, u32[]{:S(2)}, u32[]{:S(2)}) collective-permute-start(bf16[1280,128]{1,0:T(8,128)(2,1)S(1)} %get-tuple-element.85), channel_id=1, source_target_pairs={{0,1},{1,0},{2,3},{3,2},{4,5},{5,4},{6,7},{7,6},{8,9},{9,8},{10,11... | collective-permute-start | bytes 983048 | tf_op jit(solution)/shard_map/ppermute | solution.py:296
  53.2 14.6 %collective-permute-start.12 = (bf16[640,128]{1,0:T(8,128)(2,1)S(1)}, bf16[640,128]{1,0:T(8,128)(2,1)S(1)}, u32[]{:S(2)}, u32[]{:S(2)}) collective-permute-start(bf16[640,128]{1,0:T(8,128)(2,1)S(1)} %get-tuple-element.77.refs_11_), channel_id=1, source_target_pairs={{0,2},{2,0},{4,6},{6,4},{8,10},{10,8},{12,14},{14,12},{1,3},{3,1},... | collective-permute-start | bytes 491528 | tf_op jit(solution)/shard_map/ppermute | solution.py:292
  55.4 15.8 %collective-permute-start.16 = (bf16[640,128]{1,0:T(8,128)(2,1)S(1)}, bf16[640,128]{1,0:T(8,128)(2,1)S(1)}, u32[]{:S(2)}, u32[]{:S(2)}) collective-permute-start(bf16[640,128]{1,0:T(8,128)(2,1)S(1)} %get-tuple-element.87.refs_3_), channel_id=1, source_target_pairs={{0,2},{2,0},{4,6},{6,4},{8,10},{10,8},{12,14},{14,12},{1,3},{3,1},... | collective-permute-start | bytes 491528 | tf_op jit(solution)/shard_map/ppermute | solution.py:292
  67.8 6.0 %collective-permute-start.18 = (bf16[320,128]{1,0:T(8,128)(2,1)S(1)}, bf16[320,128]{1,0:T(8,128)(2,1)S(1)}, u32[]{:S(2)}, u32[]{:S(2)}) collective-permute-start(bf16[320,128]{1,0:T(8,128)(2,1)S(1)} %get-tuple-element.89.refs_3_), channel_id=1, source_target_pairs={{0,4},{2,6},{4,0},{6,2},{8,12},{10,14},{12,8},{14,10},{1,5},{3,7},... | collective-permute-start | bytes 245768 | tf_op jit(solution)/shard_map/ppermute | solution.py:292
  71.3 5.2 %collective-permute-start.17 = (bf16[320,128]{1,0:T(8,128)(2,1)S(1)}, bf16[320,128]{1,0:T(8,128)(2,1)S(1)}, u32[]{:S(2)}, u32[]{:S(2)}) collective-permute-start(bf16[320,128]{1,0:T(8,128)(2,1)S(1)} %get-tuple-element.95.refs_3_), channel_id=1, source_target_pairs={{0,4},{2,6},{4,0},{6,2},{8,12},{10,14},{12,8},{14,10},{1,5},{3,7},... | collective-permute-start | bytes 245768 | tf_op jit(solution)/shard_map/ppermute | solution.py:292
  73.8 6.9 %collective-permute-start.20 = (bf16[320,128]{1,0:T(8,128)(2,1)S(1)}, bf16[320,128]{1,0:T(8,128)(2,1)S(1)}, u32[]{:S(2)}, u32[]{:S(2)}) collective-permute-start(bf16[320,128]{1,0:T(8,128)(2,1)S(1)} %shard_map.93.refs_2_.refs_0_), channel_id=1, source_target_pairs={{0,8},{2,10},{4,12},{6,14},{8,0},{10,2},{12,4},{14,6},{1,9},{3,11}... | collective-permute-start | bytes 245768 | tf_op jit(solution)/shard_map/ppermute | solution.py:292
  75.9 15.3 %collective-permute-start.8 = (bf16[1024,128]{1,0:T(8,128)(2,1)S(1)}, bf16[1024,128]{1,0:T(8,128)(2,1)S(1)}, u32[]{:S(2)}, u32[]{:S(2)}) collective-permute-start(bf16[1024,128]{1,0:T(8,128)(2,1)S(1)} %get-tuple-element.66), channel_id=1, source_target_pairs={{0,1},{1,0},{2,3},{3,2},{4,5},{5,4},{6,7},{7,6},{8,9},{9,8},{10,11... | collective-permute-start | bytes 786440 | tf_op jit(solution)/shard_map/ppermute | solution.py:296
  75.9 15.3 %collective-permute-start.7 = (bf16[1024,128]{1,0:T(8,128)(2,1)S(1)}, bf16[1024,128]{1,0:T(8,128)(2,1)S(1)}, u32[]{:S(2)}, u32[]{:S(2)}) collective-permute-start(bf16[1024,128]{1,0:T(8,128)(2,1)S(1)} %get-tuple-element.64), channel_id=1, source_target_pairs={{0,1},{1,0},{2,3},{3,2},{4,5},{5,4},{6,7},{7,6},{8,9},{9,8},{10,11... | collective-permute-start | bytes 786440 | tf_op jit(solution)/shard_map/ppermute | solution.py:296
  76.4 16.5 %collective-permute-start.14 = (bf16[1024,128]{1,0:T(8,128)(2,1)S(1)}, bf16[1024,128]{1,0:T(8,128)(2,1)S(1)}, u32[]{:S(2)}, u32[]{:S(2)}) collective-permute-start(bf16[1024,128]{1,0:T(8,128)(2,1)S(1)} %get-tuple-element.92), channel_id=1, source_target_pairs={{0,1},{1,0},{2,3},{3,2},{4,5},{5,4},{6,7},{7,6},{8,9},{9,8},{10,11... | collective-permute-start | bytes 786440 | tf_op jit(solution)/shard_map/ppermute | solution.py:296
  76.5 7.7 %collective-permute-start.19 = (bf16[320,128]{1,0:T(8,128)(2,1)S(1)}, bf16[320,128]{1,0:T(8,128)(2,1)S(1)}, u32[]{:S(2)}, u32[]{:S(2)}) collective-permute-start(bf16[320,128]{1,0:T(8,128)(2,1)S(1)} %shard_map.94.refs_2_.refs_0_), channel_id=1, source_target_pairs={{0,8},{2,10},{4,12},{6,14},{8,0},{10,2},{12,4},{14,6},{1,9},{3,11}... | collective-permute-start | bytes 245768 | tf_op jit(solution)/shard_map/ppermute | solution.py:292
  80.8 15.0 %collective-permute-start.15 = (bf16[1024,128]{1,0:T(8,128)(2,1)S(1)}, bf16[1024,128]{1,0:T(8,128)(2,1)S(1)}, u32[]{:S(2)}, u32[]{:S(2)}) collective-permute-start(bf16[1024,128]{1,0:T(8,128)(2,1)S(1)} %get-tuple-element.93), channel_id=1, source_target_pairs={{0,1},{1,0},{2,3},{3,2},{4,5},{5,4},{6,7},{7,6},{8,9},{9,8},{10,11... | collective-permute-start | bytes 786440 | tf_op jit(solution)/shard_map/ppermute | solution.py:296
  84.2 4.4 %collective-permute-start.24 = (bf16[320,128]{1,0:T(8,128)(2,1)S(1)}, bf16[320,128]{1,0:T(8,128)(2,1)S(1)}, u32[]{:S(2)}, u32[]{:S(2)}) collective-permute-start(bf16[320,128]{1,0:T(8,128)(2,1)S(1)} %shard_map.95.refs_2_.refs_0_.refs_4_), channel_id=1, source_target_pairs={{0,4},{2,6},{4,0},{6,2},{8,12},{10,14},{12,8},{14,10},{1,5},{3,7},... | collective-permute-start | bytes 245768 | tf_op jit(solution)/shard_map/ppermute | solution.py:292
  88.6 8.7 %collective-permute-start.25 = (bf16[640,128]{1,0:T(8,128)(2,1)S(1)}, bf16[640,128]{1,0:T(8,128)(2,1)S(1)}, u32[]{:S(2)}, u32[]{:S(2)}) collective-permute-start(bf16[640,128]{1,0:T(8,128)(2,1)S(1)} %shard_map.97), channel_id=1, source_target_pairs={{0,2},{2,0},{4,6},{6,4},{8,10},{10,8},{12,14},{14,12},{1,3},{3,1},... | collective-permute-start | bytes 491528 | tf_op jit(solution)/shard_map/ppermute | solution.py:292
  91.2 5.6 %collective-permute-start.23 = (bf16[320,128]{1,0:T(8,128)(2,1)S(1)}, bf16[320,128]{1,0:T(8,128)(2,1)S(1)}, u32[]{:S(2)}, u32[]{:S(2)}) collective-permute-start(bf16[320,128]{1,0:T(8,128)(2,1)S(1)} %shard_map.96.refs_2_.refs_0_), channel_id=1, source_target_pairs={{0,6},{2,4},{4,2},{6,0},{8,14},{10,12},{12,10},{14,8},{1,7},{3,5},... | collective-permute-start | bytes 245768 | tf_op jit(solution)/shard_map/ppermute | solution.py:292
  91.2 5.6 %collective-permute-start.22 = (bf16[320,128]{1,0:T(8,128)(2,1)S(1)}, bf16[320,128]{1,0:T(8,128)(2,1)S(1)}, u32[]{:S(2)}, u32[]{:S(2)}) collective-permute-start(bf16[320,128]{1,0:T(8,128)(2,1)S(1)} %shard_map.96.refs_2_.refs_0_), channel_id=1, source_target_pairs={{0,2},{2,0},{4,6},{6,4},{8,10},{10,8},{12,14},{14,12},{1,3},{3,1},... | collective-permute-start | bytes 245768 | tf_op jit(solution)/shard_map/ppermute | solution.py:292
  92.9 4.4 %collective-permute-start.21 = (bf16[320,128]{1,0:T(8,128)(2,1)S(1)}, bf16[320,128]{1,0:T(8,128)(2,1)S(1)}, u32[]{:S(2)}, u32[]{:S(2)}) collective-permute-start(bf16[320,128]{1,0:T(8,128)(2,1)S(1)} %shard_map.96.refs_2_.refs_0_), channel_id=1, source_target_pairs={{0,4},{2,6},{4,0},{6,2},{8,12},{10,14},{12,8},{14,10},{1,5},{3,7},... | collective-permute-start | bytes 245768 | tf_op jit(solution)/shard_map/ppermute | solution.py:292

commit v7 on v6

--- a/solution.py
+++ b/solution.py
@@ -353,7 +353,7 @@
         both = jnp.stack([lax.psum(sums[0], "tm") for sums in (sums0, sums1)])
         return both[:, : 4 * channels], both[:, 4 * channels :]
     cols = sums0[0].shape[1]
-    late = spread(ids, cuts, sums1[0], [sums0[0]])
+    late = spread(ids, cuts, sums1[0], ())
     own = sums0[0]
     soon = [own] + [crossed(own, partner) for partner in ((2, 1, 3) if cuts == 2 else (1,))]
     return run(

time: 99 us -> 101 us (1.020)
  waiting for transfers between devices: 33.4 us -> 38 us
  starting transfers between devices: 43.1 us -> 40.9 us
    ppermute x11, waiting for transfers between devices: 20.7 us -> 25.4 us  [crossed(): lax.ppermute(values, 'tm', [(i, i ^ bit) for i in range(lax.axis_size('tm...]
    ppermute x11, starting transfers between devices: 20.3 us -> 18.1 us  [crossed(): lax.ppermute(values, 'tm', [(i, i ^ bit) for i in range(lax.axis_size('tm...]
where the time goes in v7:
time: 101 us
  starting transfers between devices  40.9 us (40%)
  waiting for transfers between devices  38 us (38%)
  Pallas kernels  19.5 us (19%)
  local copies, waits for them, and re-layouts  1.75 us (2%)
    ppermute x11, waiting for transfers between devices, crossed(): lax.ppermute(values, 'tm', [(i, i ^ bit) for i in range(lax.axis_size('tm...  25.4 us
    ppermute x7, starting transfers between devices, moved_by(): lax.ppermute(values, 'tm', [(i, i + distance) for i in devices if i + dis...  21.6 us
    pallas_call x24, Pallas kernels, run(): pl.pallas_call(kernel, in_specs=[pl.BlockSpec(memory_space=pltpu.VMEM)] *...  19.5 us
    ppermute x11, starting transfers between devices, crossed(): lax.ppermute(values, 'tm', [(i, i ^ bit) for i in range(lax.axis_size('tm...  18.1 us
    ppermute x7, waiting for transfers between devices, moved_by(): lax.ppermute(values, 'tm', [(i, i + distance) for i in devices if i + dis...  11.2 us
  transfers between devices with their start and end apart: 26, of which 10 were waited for; matrix products, arithmetic and copies ran while one was open for 2% of the time, Pallas kernels for 18%

profile of v7, /device:TPU:0, one launch (start us, length us, event | category | flops | bytes accessed | tf_op | source)
XLA Modules:
  0.0 101.0 jit_solution(5878010421017397202)
XLA Ops:
  0.6 0.5 collective-permute-start
  1.2 0.1 collective-permute-start.2
  1.2 1.7 %reshape.17.refs_2_.refs_3_.refs_4_.refs_6_ = bf16[2,2,256,512]{3,2,1,0:T(8,128)(2,1)S(1)} reshape(bf16[2,2,256,2,256]{4,3,2,1,0:T(2,128)(2,1)} %param.6) | data formatting | bytes 2097152 | tf_op jit(solution)/shard_map/reshape | solution.py:375
  3.0 0.0 copy-start
  3.0 0.0 copy-start.2
  3.0 1.4 %collective-permute-done.refs_1_ = bf16[4096,128]{1,0:T(8,128)(2,1)S(1)} collective-permute-done((bf16[4096,128]{1,0:T(8,128)(2,1)}, bf16[4096,128]{1,0:T(8,128)(2,1)S(1)}, u32[]{:S(2)}, u32[]{:S(2)}) %collective-permute-start) | collective-permute-done | bytes 1048608 | tf_op jit(solution)/shard_map/ppermute | solution.py:296
  4.4 0.1 shard_map.75
  4.5 4.8 %collective-permute-start.1 = (bf16[1024,256]{1,0:T(8,128)(2,1)S(1)}, bf16[1024,256]{1,0:T(8,128)(2,1)S(1)}, u32[]{:S(2)}, u32[]{:S(2)}) collective-permute-start(bf16[1024,256]{1,0:T(8,128)(2,1)S(1)} %get-tuple-element.52.refs_3_.refs_0_.refs_5_), channel_id=1, source_target_pairs={{0,2},{2,4},{4,6},{6,8},{8,10},{10,12},{12,14},{1,3},{3,5},{5,7},{... | collective-permute-start | bytes 1572872 | tf_op jit(solution)/shard_map/ppermute | solution.py:286
  9.4 1.7 %shard_map.76 = (bf16[1024,256]{1,0:T(8,128)(2,1)S(1)}, bf16[1024,256]{1,0:T(8,128)(2,1)S(1)}, f32[1024,256]{1,0:T(8,128)S(1)}, f32[1024,256]{1,0:T(8,128)S(1)}) custom-call(bf16[4096,128]{1,0:T(8,128)(2,1)S(1)} %copy-done.2, bf16[4096,128]{1,0:T(8,128)(2,1)} %collective-permute-done.2.refs_1_, bf16[2,256,256]{2,1,0:T(8,128)(2,1)S(1)} %copy-done, ...), custom_call_target="tpu_custom_call" | custom-call | flops 1 | bytes 1 | tf_op jit(solution)/shard_map/pallas_call | solution.py:58
  11.1 1.3 %collective-permute-start.5 = (bf16[1024,256]{1,0:T(8,128)(2,1)S(1)}, bf16[1024,256]{1,0:T(8,128)(2,1)S(1)}, u32[]{:S(2)}, u32[]{:S(2)}) collective-permute-start(bf16[1024,256]{1,0:T(8,128)(2,1)S(1)} %get-tuple-element.53.refs_4_.refs_2_), channel_id=1, source_target_pairs={{4,0},{6,2},{8,4},{10,6},{12,8},{14,10},{5,1},{7,3},{9,5},{11,7},{... | collective-permute-start | bytes 1572872 | tf_op jit(solution)/shard_map/ppermute | solution.py:286
  12.4 1.4 %shard_map.77 = (bf16[1024,256]{1,0:T(8,128)(2,1)S(1)}, bf16[1024,256]{1,0:T(8,128)(2,1)S(1)}, f32[1024,512]{1,0:T(8,128)S(1)}) custom-call(bf16[1024,256]{1,0:T(8,128)(2,1)S(1)} %get-tuple-element.52.refs_3_.refs_0_.refs_5_, bf16[1024,256]{1,0:T(8,128)(2,1)S(1)} %get-tuple-element.51.refs_1_.refs_0_.refs_6_, ...), custom_call_target="tpu_custom_call" | custom-call | flops 1 | bytes 1 | tf_op jit(solution)/shard_map/pallas_call | solution.py:58
  13.7 4.6 %collective-permute-start.6 = (bf16[1024,256]{1,0:T(8,128)(2,1)S(1)}, bf16[1024,256]{1,0:T(8,128)(2,1)S(1)}, u32[]{:S(2)}, u32[]{:S(2)}) collective-permute-start(bf16[1024,256]{1,0:T(8,128)(2,1)S(1)} %get-tuple-element.54.refs_4_.refs_0_.refs_5_), channel_id=1, source_target_pairs={{0,4},{2,6},{4,8},{6,10},{8,12},{10,14},{1,5},{3,7},{5,9},{7,11},{... | collective-permute-start | bytes 1572872 | tf_op jit(solution)/shard_map/ppermute | solution.py:286
  18.3 2.4 %collective-permute-done.1.refs_1_ = bf16[1024,256]{1,0:T(8,128)(2,1)S(1)} collective-permute-done((bf16[1024,256]{1,0:T(8,128)(2,1)S(1)}, bf16[1024,256]{1,0:T(8,128)(2,1)S(1)}, u32[]{:S(2)}, u32[]{:S(2)}) %collective-permute-start.1) | collective-permute-done | bytes 524320 | tf_op jit(solution)/shard_map/ppermute | solution.py:286
  20.8 1.4 %shard_map.78 = (bf16[1024,256]{1,0:T(8,128)(2,1)S(1)}, bf16[1024,256]{1,0:T(8,128)(2,1)S(1)}, f32[1024,512]{1,0:T(8,128)S(1)}) custom-call(bf16[1024,256]{1,0:T(8,128)(2,1)S(1)} %get-tuple-element.51.refs_1_.refs_0_.refs_6_, bf16[1024,256]{1,0:T(8,128)(2,1)S(1)} %collective-permute-done.1.refs_1_, ...), custom_call_target="tpu_custom_call" | custom-call | flops 1 | bytes 1 | tf_op jit(solution)/shard_map/pallas_call | solution.py:58
  22.1 1.3 %collective-permute-start.4 = (bf16[1024,256]{1,0:T(8,128)(2,1)S(1)}, bf16[1024,256]{1,0:T(8,128)(2,1)S(1)}, u32[]{:S(2)}, u32[]{:S(2)}) collective-permute-start(bf16[1024,256]{1,0:T(8,128)(2,1)S(1)} %get-tuple-element.55.refs_4_.refs_1_.refs_0_), channel_id=1, source_target_pairs={{4,0},{6,2},{8,4},{10,6},{12,8},{14,10},{5,1},{7,3},{9,5},{11,7},{... | collective-permute-start | bytes 1572872 | tf_op jit(solution)/shard_map/ppermute | solution.py:286
  23.4 6.8 %collective-permute-start.3 = (bf16[1024,256]{1,0:T(8,128)(2,1)S(1)}, bf16[1024,256]{1,0:T(8,128)(2,1)S(1)}, u32[]{:S(2)}, u32[]{:S(2)}) collective-permute-start(bf16[1024,256]{1,0:T(8,128)(2,1)S(1)} %get-tuple-element.55.refs_4_.refs_1_.refs_0_), channel_id=1, source_target_pairs={{0,4},{2,6},{4,8},{6,10},{8,12},{10,14},{1,5},{3,7},{5,9},{7,11},{... | collective-permute-start | bytes 1572872 | tf_op jit(solution)/shard_map/ppermute | solution.py:286
  30.2 0.0 collective-permute-done.6.refs_1_.refs_6_
  30.3 1.3 %shard_map.79 = (bf16[1024,512]{1,0:T(8,128)(2,1)S(1)}, bf16[1024,256]{1,0:T(8,128)(2,1)S(1)}, bf16[1024,256]{1,0:T(8,128)(2,1)S(1)}) custom-call(bf16[1024,256]{1,0:T(8,128)(2,1)S(1)} %get-tuple-element.54.refs_4_.refs_0_.refs_5_, bf16[1024,256]{1,0:T(8,128)(2,1)S(1)} %collective-permute-done.6.refs_1_.refs_6_, f32[1024,256]{1,0:T(8,128)S(1)} %get-tuple-element.57.refs_2_, ...), custom_call_target="tpu_custom_call" | custom-call | flops 1 | bytes 1 | tf_op jit(solution)/shard_map/pallas_call | solution.py:58
  31.6 1.3 %collective-permute-start.9 = (bf16[1024,256]{1,0:T(8,128)(2,1)S(1)}, bf16[1024,256]{1,0:T(8,128)(2,1)S(1)}, u32[]{:S(2)}, u32[]{:S(2)}) collective-permute-start(bf16[1024,256]{1,0:T(8,128)(2,1)S(1)} %get-tuple-element.67), channel_id=1, source_target_pairs={{4,0},{6,2},{8,4},{10,6},{12,8},{14,10},{5,1},{7,3},{9,5},{11,7},{... | collective-permute-start | bytes 1572872 | tf_op jit(solution)/shard_map/ppermute | solution.py:286
  32.9 0.6 shard_map.80
  33.5 7.6 %collective-permute-done.4.refs_0_ = bf16[1024,256]{1,0:T(8,128)(2,1)S(1)} collective-permute-done((bf16[1024,256]{1,0:T(8,128)(2,1)S(1)}, bf16[1024,256]{1,0:T(8,128)(2,1)S(1)}, u32[]{:S(2)}, u32[]{:S(2)}) %collective-permute-start.4) | collective-permute-done | bytes 524320 | tf_op jit(solution)/shard_map/ppermute | solution.py:286
  41.1 1.5 %shard_map.81.refs_4_ = f32[1024,256]{1,0:T(8,128)S(1)} custom-call(bf16[1024,256]{1,0:T(8,128)(2,1)S(1)} %collective-permute-done.4.refs_0_, bf16[1024,256]{1,0:T(8,128)(2,1)S(1)} %get-tuple-element.55.refs_4_.refs_1_.refs_0_, bf16[1024,256]{1,0:T(8,128)(2,1)S(1)} %collective-permute-done.5.refs_5_.refs_2_, ...), custom_call_target="tpu_custom_call" | custom-call | flops 1 | bytes 1 | tf_op jit(solution)/shard_map/pallas_call | solution.py:58
  42.6 0.0 collective-permute-done.3.refs_1_
  42.6 3.2 %shard_map.82 = (bf16[1024,256]{1,0:T(8,128)(2,1)S(1)}, bf16[1024,512]{1,0:T(8,128)(2,1)S(1)}, bf16[1024,256]{1,0:T(8,128)(2,1)S(1)}, bf16[1024,128]{1,0:T(8,128...) custom-call(bf16[1024,256]{1,0:T(8,128)(2,1)S(1)} %get-tuple-element, ...), custom_call_target="tpu_custom_call" | custom-call | flops 1 | bytes 1 | tf_op jit(solution)/shard_map/pallas_call | solution.py:58
  45.8 1.6 %shard_map.83 = (f32[1280,128]{1,0:T(8,128)S(1)}, bf16[1280,128]{1,0:T(8,128)(2,1)S(1)}) custom-call(bf16[1024,256]{1,0:T(8,128)(2,1)S(1)} %get-tuple-element.55.refs_4_.refs_1_.refs_0_, bf16[1024,256]{1,0:T(8,128)(2,1)S(1)} %collective-permute-done.3.refs_1_, bf16[1024,512]{1,0:T(8,128)(2,1)S(1)} %get-tuple-element.70.refs_2_, ...), custom_call_target="tpu_custom_call" | custom-call | flops 1 | bytes 1 | tf_op jit(solution)/shard_map/pallas_call | solution.py:58
  47.4 0.1 collective-permute-start.11
  47.5 1.5 %collective-permute-start.10 = (bf16[1024,256]{1,0:T(8,128)(2,1)S(1)}, bf16[1024,256]{1,0:T(8,128)(2,1)S(1)}, u32[]{:S(2)}, u32[]{:S(2)}) collective-permute-start(bf16[1024,256]{1,0:T(8,128)(2,1)S(1)} %get-tuple-element.74), channel_id=1, source_target_pairs={{2,0},{4,2},{6,4},{8,6},{10,8},{12,10},{14,12},{3,1},{5,3},{7,5},{... | collective-permute-start | bytes 1572872 | tf_op jit(solution)/shard_map/ppermute | solution.py:286
  48.9 1.2 %collective-permute-done.9.refs_1_ = bf16[1024,256]{1,0:T(8,128)(2,1)S(1)} collective-permute-done((bf16[1024,256]{1,0:T(8,128)(2,1)S(1)}, bf16[1024,256]{1,0:T(8,128)(2,1)S(1)}, u32[]{:S(2)}, u32[]{:S(2)}) %collective-permute-start.9) | collective-permute-done | bytes 524320 | tf_op jit(solution)/shard_map/ppermute | solution.py:286
  50.1 1.3 %shard_map.84 = (bf16[1024,128]{1,0:T(8,128)(2,1)S(1)}, bf16[1024,128]{1,0:T(8,128)(2,1)S(1)}, bf16[1024,256]{1,0:T(8,128)(2,1)S(1)}, bf16[1024,512]{1,0:T(8,128)(2,1)S(1)}, f32[1024,256]{1,0:T(8,128)S(1)}) custom-call(f32[1024,256]{1,0:T(8,128)S(1)} %get-tuple-element.61.refs_5_.refs_0_, bf16[1024,256]{1,0:T(8,128)(2,1)S(1)} %collective-permute-done.9.refs_1_, ...), custom_call_target="tpu_custom_call" | custom-call | flops 1 | bytes 1 | tf_op jit(solution)/shard_map/pallas_call | solution.py:58
  51.4 0.1 shard_map.85
  51.5 1.6 %shard_map.86 = (f32[1280,128]{1,0:T(8,128)S(1)}, bf16[1280,128]{1,0:T(8,128)(2,1)S(1)}) custom-call(bf16[1024,256]{1,0:T(8,128)(2,1)S(1)} %get-tuple-element.51.refs_1_.refs_0_.refs_6_, bf16[1024,256]{1,0:T(8,128)(2,1)S(1)} %collective-permute-done.1.refs_1_, bf16[1024,512]{1,0:T(8,128)(2,1)S(1)} %get-tuple-element.78.refs_2_, ...), custom_call_target="tpu_custom_call" | custom-call | flops 1 | bytes 1 | tf_op jit(solution)/shard_map/pallas_call | solution.py:58
  53.1 0.1 collective-permute-start.13
  53.2 2.1 %collective-permute-start.12 = (bf16[640,128]{1,0:T(8,128)(2,1)S(1)}, bf16[640,128]{1,0:T(8,128)(2,1)S(1)}, u32[]{:S(2)}, u32[]{:S(2)}) collective-permute-start(bf16[640,128]{1,0:T(8,128)(2,1)S(1)} %get-tuple-element.77.refs_11_), channel_id=1, source_target_pairs={{0,2},{2,0},{4,6},{6,4},{8,10},{10,8},{12,14},{14,12},{1,3},{3,1},... | collective-permute-start | bytes 491528 | tf_op jit(solution)/shard_map/ppermute | solution.py:292
  55.3 0.1 shard_map.87
  55.4 1.3 %collective-permute-start.16 = (bf16[640,128]{1,0:T(8,128)(2,1)S(1)}, bf16[640,128]{1,0:T(8,128)(2,1)S(1)}, u32[]{:S(2)}, u32[]{:S(2)}) collective-permute-start(bf16[640,128]{1,0:T(8,128)(2,1)S(1)} %get-tuple-element.87.refs_3_), channel_id=1, source_target_pairs={{0,2},{2,0},{4,6},{6,4},{8,10},{10,8},{12,14},{14,12},{1,3},{3,1},... | collective-permute-start | bytes 491528 | tf_op jit(solution)/shard_map/ppermute | solution.py:292
  56.7 11.1 %collective-permute-done.12.refs_1_ = bf16[640,128]{1,0:T(8,128)(2,1)S(1)} collective-permute-done((bf16[640,128]{1,0:T(8,128)(2,1)S(1)}, bf16[640,128]{1,0:T(8,128)(2,1)S(1)}, u32[]{:S(2)}, u32[]{:S(2)}) %collective-permute-start.12) | collective-permute-done | bytes 163872 | tf_op jit(solution)/shard_map/ppermute | solution.py:292
  67.8 2.5 %collective-permute-start.18 = (bf16[320,128]{1,0:T(8,128)(2,1)S(1)}, bf16[320,128]{1,0:T(8,128)(2,1)S(1)}, u32[]{:S(2)}, u32[]{:S(2)}) collective-permute-start(bf16[320,128]{1,0:T(8,128)(2,1)S(1)} %get-tuple-element.89.refs_3_), channel_id=1, source_target_pairs={{0,4},{2,6},{4,0},{6,2},{8,12},{10,14},{12,8},{14,10},{1,5},{3,7},... | collective-permute-start | bytes 245768 | tf_op jit(solution)/shard_map/ppermute | solution.py:292
  70.4 0.0 collective-permute-done.10.refs_1_
  70.4 0.2 shard_map.89
  70.6 0.7 collective-permute-done.16.refs_1_
  71.3 2.5 %collective-permute-start.17 = (bf16[320,128]{1,0:T(8,128)(2,1)S(1)}, bf16[320,128]{1,0:T(8,128)(2,1)S(1)}, u32[]{:S(2)}, u32[]{:S(2)}) collective-permute-start(bf16[320,128]{1,0:T(8,128)(2,1)S(1)} %get-tuple-element.95.refs_3_), channel_id=1, source_target_pairs={{0,4},{2,6},{4,0},{6,2},{8,12},{10,14},{12,8},{14,10},{1,5},{3,7},... | collective-permute-start | bytes 245768 | tf_op jit(solution)/shard_map/ppermute | solution.py:292
  73.8 2.1 %collective-permute-start.20 = (bf16[320,128]{1,0:T(8,128)(2,1)S(1)}, bf16[320,128]{1,0:T(8,128)(2,1)S(1)}, u32[]{:S(2)}, u32[]{:S(2)}) collective-permute-start(bf16[320,128]{1,0:T(8,128)(2,1)S(1)} %shard_map.93.refs_2_.refs_0_), channel_id=1, source_target_pairs={{0,8},{2,10},{4,12},{6,14},{8,0},{10,2},{12,4},{14,6},{1,9},{3,11}... | collective-permute-start | bytes 245768 | tf_op jit(solution)/shard_map/ppermute | solution.py:292
  75.9 0.5 collective-permute-start.7
  76.4 0.0 collective-permute-start.14
  76.4 0.0 collective-permute-done.17.refs_1_
  76.5 4.2 %collective-permute-done.20.refs_1_ = bf16[320,128]{1,0:T(8,128)(2,1)S(1)} collective-permute-done((bf16[320,128]{1,0:T(8,128)(2,1)S(1)}, bf16[320,128]{1,0:T(8,128)(2,1)S(1)}, u32[]{:S(2)}, u32[]{:S(2)}) %collective-permute-start.20) | collective-permute-done | bytes 81952 | tf_op jit(solution)/shard_map/ppermute | solution.py:292
  80.7 0.4 collective-permute-start.24
  81.1 4.1 %collective-permute-done.24.refs_1_.refs_5_ = bf16[320,128]{1,0:T(8,128)(2,1)S(1)} collective-permute-done((bf16[320,128]{1,0:T(8,128)(2,1)S(1)}, bf16[320,128]{1,0:T(8,128)(2,1)S(1)}, u32[]{:S(2)}, u32[]{:S(2)}) %collective-permute-start.24) | collective-permute-done | bytes 81952 | tf_op jit(solution)/shard_map/ppermute | solution.py:292
  85.2 1.0 %collective-permute-start.19 = (bf16[320,128]{1,0:T(8,128)(2,1)S(1)}, bf16[320,128]{1,0:T(8,128)(2,1)S(1)}, u32[]{:S(2)}, u32[]{:S(2)}) collective-permute-start(bf16[320,128]{1,0:T(8,128)(2,1)S(1)} %shard_map.94.refs_2_.refs_0_), channel_id=1, source_target_pairs={{0,8},{2,10},{4,12},{6,14},{8,0},{10,2},{12,4},{14,6},{1,9},{3,11}... | collective-permute-start | bytes 245768 | tf_op jit(solution)/shard_map/ppermute | solution.py:292
  86.2 4.9 %collective-permute-done.19.refs_1_ = bf16[320,128]{1,0:T(8,128)(2,1)S(1)} collective-permute-done((bf16[320,128]{1,0:T(8,128)(2,1)S(1)}, bf16[320,128]{1,0:T(8,128)(2,1)S(1)}, u32[]{:S(2)}, u32[]{:S(2)}) %collective-permute-start.19) | collective-permute-done | bytes 81952 | tf_op jit(solution)/shard_map/ppermute | solution.py:292
  91.2 2.6 %collective-permute-start.25 = (bf16[640,128]{1,0:T(8,128)(2,1)S(1)}, bf16[640,128]{1,0:T(8,128)(2,1)S(1)}, u32[]{:S(2)}, u32[]{:S(2)}) collective-permute-start(bf16[640,128]{1,0:T(8,128)(2,1)S(1)} %shard_map.97), channel_id=1, source_target_pairs={{0,2},{2,0},{4,6},{6,4},{8,10},{10,8},{12,14},{14,12},{1,3},{3,1},... | collective-permute-start | bytes 491528 | tf_op jit(solution)/shard_map/ppermute | solution.py:292
  93.8 0.0 collective-permute-done.8.refs_3_
  93.8 0.1 collective-permute-start.23
  93.8 0.0 collective-permute-done.7.refs_1_
  93.9 1.1 %collective-permute-start.22 = (bf16[320,128]{1,0:T(8,128)(2,1)S(1)}, bf16[320,128]{1,0:T(8,128)(2,1)S(1)}, u32[]{:S(2)}, u32[]{:S(2)}) collective-permute-start(bf16[320,128]{1,0:T(8,128)(2,1)S(1)} %shard_map.96.refs_0_), channel_id=1, source_target_pairs={{0,2},{2,0},{4,6},{6,4},{8,10},{10,8},{12,14},{14,12},{1,3},{3,1},... | collective-permute-start | bytes 245768 | tf_op jit(solution)/shard_map/ppermute | solution.py:292
  95.0 2.4 %collective-permute-start.21 = (bf16[320,128]{1,0:T(8,128)(2,1)S(1)}, bf16[320,128]{1,0:T(8,128)(2,1)S(1)}, u32[]{:S(2)}, u32[]{:S(2)}) collective-permute-start(bf16[320,128]{1,0:T(8,128)(2,1)S(1)} %shard_map.96.refs_0_), channel_id=1, source_target_pairs={{0,4},{2,6},{4,0},{6,2},{8,12},{10,14},{12,8},{14,10},{1,5},{3,7},... | collective-permute-start | bytes 245768 | tf_op jit(solution)/shard_map/ppermute | solution.py:292
  97.3 1.0 %shard_map.90 = bf16[4096,128]{1,0:T(8,128)(2,1)} custom-call(bf16[1024,128]{1,0:T(8,128)(2,1)S(1)} %get-tuple-element.63.refs_0_, bf16[1024,128]{1,0:T(8,128)(2,1)S(1)} %collective-permute-done.7.refs_1_, bf16[1024,128]{1,0:T(8,128)(2,1)S(1)} %get-tuple-element.65.refs_2_, bf16[1024,128]{1,0:T(8,128)(2,1)S(1)} %collective-permute-done.8.refs_3_, ...), custom_call_target="tpu_custom_call" | custom-call | flops 1 | bytes 1 | tf_op jit(solution)/shard_map/pallas_call | solution.py:58
  98.4 0.0 collective-permute-done.15.refs_3_
  98.4 1.0 %shard_map.91 = bf16[4096,128]{1,0:T(8,128)(2,1)} custom-call(bf16[1024,128]{1,0:T(8,128)(2,1)S(1)} %get-tuple-element.91.refs_0_, bf16[1024,128]{1,0:T(8,128)(2,1)S(1)} %collective-permute-done.14.refs_1_, bf16[1024,128]{1,0:T(8,128)(2,1)S(1)} %get-tuple-element.90.refs_4_.refs_2_, bf16[1024,128]{1,0:T(8,128)(2,1)S(1)} %collective-permute-done.15.refs_3_), custom_call_target="tpu_custom_call" | custom-call | flops 1 | bytes 1 | tf_op jit(solution)/shard_map/pallas_call | solution.py:58
  99.4 0.0 collective-permute-done.23.refs_3_
  99.4 0.0 collective-permute-done.22.refs_2_
  99.4 0.3 collective-permute-done.21.refs_1_
  99.8 0.0 collective-permute-done.25.refs_6_
  99.8 1.3 %shard_map.98 = (f32[2048,128]{1,0:T(8,128)}, f32[512,128]{1,0:T(8,128)}) custom-call(bf16[320,128]{1,0:T(8,128)(2,1)S(1)} %shard_map.96.refs_0_, bf16[320,128]{1,0:T(8,128)(2,1)S(1)} %collective-permute-done.21.refs_1_, bf16[320,128]{1,0:T(8,128)(2,1)S(1)} %collective-permute-done.22.refs_2_, bf16[320,128]{1,0:T(8,128)(2,1)S(1)} %collective-permute-done.23.refs_3_, ...), custom_call_target="tpu_custom_call" | custom-call | flops 1 | bytes 1 | tf_op jit(solution)/shard_map/pallas_call | solution.py:58
  (19 shorter events, 0.2 us)
Async XLA Ops:
  0.6 3.7 %copy-start.1 = (bf16[4096,128]{1,0:T(8,128)(2,1)S(1)}, bf16[4096,128]{1,0:T(8,128)(2,1)}, u32[]{:S(2)}) copy-start(bf16[4096,128]{1,0:T(8,128)(2,1)} %refs_0_.2) | copy-start | bytes 3145732
  0.6 3.7 %collective-permute-start = (bf16[4096,128]{1,0:T(8,128)(2,1)}, bf16[4096,128]{1,0:T(8,128)(2,1)S(1)}, u32[]{:S(2)}, u32[]{:S(2)}) collective-permute-start(bf16[4096,128]{1,0:T(8,128)(2,1)} %refs_0_.2), channel_id=1, source_target_pairs={{0,1},{1,0},{2,3},{3,2},{4,5},{5,4},{6,7},{7,6},{8,9},{9,8},{10,11... | collective-permute-start | bytes 3145736 | tf_op jit(solution)/shard_map/ppermute | solution.py:296
  1.2 8.2 %collective-permute-start.2 = (bf16[4096,128]{1,0:T(8,128)(2,1)}, bf16[4096,128]{1,0:T(8,128)(2,1)}, u32[]{:S(2)}, u32[]{:S(2)}) collective-permute-start(bf16[4096,128]{1,0:T(8,128)(2,1)} %refs_0_.3), channel_id=1, source_target_pairs={{0,1},{1,0},{2,3},{3,2},{4,5},{5,4},{6,7},{7,6},{8,9},{9,8},{10,11... | collective-permute-start | bytes 3145736 | tf_op jit(solution)/shard_map/ppermute | solution.py:296
  3.0 6.4 %copy-start = (bf16[2,256,256]{2,1,0:T(8,128)(2,1)S(1)}, bf16[2,256,256]{2,1,0:T(8,128)(2,1)}, u32[]{:S(2)}) copy-start(bf16[2,256,256]{2,1,0:T(8,128)(2,1)} %refs_5_.3) | copy-start | bytes 786436
  3.0 6.4 %copy-start.2 = (bf16[4096,128]{1,0:T(8,128)(2,1)S(1)}, bf16[4096,128]{1,0:T(8,128)(2,1)}, u32[]{:S(2)}) copy-start(bf16[4096,128]{1,0:T(8,128)(2,1)} %refs_0_.3) | copy-start | bytes 3145732
  4.5 16.3 %collective-permute-start.1 = (bf16[1024,256]{1,0:T(8,128)(2,1)S(1)}, bf16[1024,256]{1,0:T(8,128)(2,1)S(1)}, u32[]{:S(2)}, u32[]{:S(2)}) collective-permute-start(bf16[1024,256]{1,0:T(8,128)(2,1)S(1)} %get-tuple-element.52.refs_3_.refs_0_.refs_5_), channel_id=1, source_target_pairs={{0,2},{2,4},{4,6},{6,8},{8,10},{10,12},{12,14},{1,3},{3,5},{5,7},{... | collective-permute-start | bytes 1572872 | tf_op jit(solution)/shard_map/ppermute | solution.py:286
  11.1 19.2 %collective-permute-start.5 = (bf16[1024,256]{1,0:T(8,128)(2,1)S(1)}, bf16[1024,256]{1,0:T(8,128)(2,1)S(1)}, u32[]{:S(2)}, u32[]{:S(2)}) collective-permute-start(bf16[1024,256]{1,0:T(8,128)(2,1)S(1)} %get-tuple-element.53.refs_4_.refs_2_), channel_id=1, source_target_pairs={{4,0},{6,2},{8,4},{10,6},{12,8},{14,10},{5,1},{7,3},{9,5},{11,7},{... | collective-permute-start | bytes 1572872 | tf_op jit(solution)/shard_map/ppermute | solution.py:286
  13.7 16.5 %collective-permute-start.6 = (bf16[1024,256]{1,0:T(8,128)(2,1)S(1)}, bf16[1024,256]{1,0:T(8,128)(2,1)S(1)}, u32[]{:S(2)}, u32[]{:S(2)}) collective-permute-start(bf16[1024,256]{1,0:T(8,128)(2,1)S(1)} %get-tuple-element.54.refs_4_.refs_0_.refs_5_), channel_id=1, source_target_pairs={{0,4},{2,6},{4,8},{6,10},{8,12},{10,14},{1,5},{3,7},{5,9},{7,11},{... | collective-permute-start | bytes 1572872 | tf_op jit(solution)/shard_map/ppermute | solution.py:286
  22.1 19.0 %collective-permute-start.4 = (bf16[1024,256]{1,0:T(8,128)(2,1)S(1)}, bf16[1024,256]{1,0:T(8,128)(2,1)S(1)}, u32[]{:S(2)}, u32[]{:S(2)}) collective-permute-start(bf16[1024,256]{1,0:T(8,128)(2,1)S(1)} %get-tuple-element.55.refs_4_.refs_1_.refs_0_), channel_id=1, source_target_pairs={{4,0},{6,2},{8,4},{10,6},{12,8},{14,10},{5,1},{7,3},{9,5},{11,7},{... | collective-permute-start | bytes 1572872 | tf_op jit(solution)/shard_map/ppermute | solution.py:286
  23.4 19.2 %collective-permute-start.3 = (bf16[1024,256]{1,0:T(8,128)(2,1)S(1)}, bf16[1024,256]{1,0:T(8,128)(2,1)S(1)}, u32[]{:S(2)}, u32[]{:S(2)}) collective-permute-start(bf16[1024,256]{1,0:T(8,128)(2,1)S(1)} %get-tuple-element.55.refs_4_.refs_1_.refs_0_), channel_id=1, source_target_pairs={{0,4},{2,6},{4,8},{6,10},{8,12},{10,14},{1,5},{3,7},{5,9},{7,11},{... | collective-permute-start | bytes 1572872 | tf_op jit(solution)/shard_map/ppermute | solution.py:286
  31.6 18.5 %collective-permute-start.9 = (bf16[1024,256]{1,0:T(8,128)(2,1)S(1)}, bf16[1024,256]{1,0:T(8,128)(2,1)S(1)}, u32[]{:S(2)}, u32[]{:S(2)}) collective-permute-start(bf16[1024,256]{1,0:T(8,128)(2,1)S(1)} %get-tuple-element.67), channel_id=1, source_target_pairs={{4,0},{6,2},{8,4},{10,6},{12,8},{14,10},{5,1},{7,3},{9,5},{11,7},{... | collective-permute-start | bytes 1572872 | tf_op jit(solution)/shard_map/ppermute | solution.py:286
  47.4 4.0 %collective-permute-start.11 = (bf16[1280,128]{1,0:T(8,128)(2,1)S(1)}, bf16[1280,128]{1,0:T(8,128)(2,1)S(1)}, u32[]{:S(2)}, u32[]{:S(2)}) collective-permute-start(bf16[1280,128]{1,0:T(8,128)(2,1)S(1)} %get-tuple-element.75), channel_id=1, source_target_pairs={{0,1},{1,0},{2,3},{3,2},{4,5},{5,4},{6,7},{7,6},{8,9},{9,8},{10,11... | collective-permute-start | bytes 983048 | tf_op jit(solution)/shard_map/ppermute | solution.py:296
  47.5 22.9 %collective-permute-start.10 = (bf16[1024,256]{1,0:T(8,128)(2,1)S(1)}, bf16[1024,256]{1,0:T(8,128)(2,1)S(1)}, u32[]{:S(2)}, u32[]{:S(2)}) collective-permute-start(bf16[1024,256]{1,0:T(8,128)(2,1)S(1)} %get-tuple-element.74), channel_id=1, source_target_pairs={{2,0},{4,2},{6,4},{8,6},{10,8},{12,10},{14,12},{3,1},{5,3},{7,5},{... | collective-permute-start | bytes 1572872 | tf_op jit(solution)/shard_map/ppermute | solution.py:286
  53.1 2.2 %collective-permute-start.13 = (bf16[1280,128]{1,0:T(8,128)(2,1)S(1)}, bf16[1280,128]{1,0:T(8,128)(2,1)S(1)}, u32[]{:S(2)}, u32[]{:S(2)}) collective-permute-start(bf16[1280,128]{1,0:T(8,128)(2,1)S(1)} %get-tuple-element.85), channel_id=1, source_target_pairs={{0,1},{1,0},{2,3},{3,2},{4,5},{5,4},{6,7},{7,6},{8,9},{9,8},{10,11... | collective-permute-start | bytes 983048 | tf_op jit(solution)/shard_map/ppermute | solution.py:296
  53.2 14.6 %collective-permute-start.12 = (bf16[640,128]{1,0:T(8,128)(2,1)S(1)}, bf16[640,128]{1,0:T(8,128)(2,1)S(1)}, u32[]{:S(2)}, u32[]{:S(2)}) collective-permute-start(bf16[640,128]{1,0:T(8,128)(2,1)S(1)} %get-tuple-element.77.refs_11_), channel_id=1, source_target_pairs={{0,2},{2,0},{4,6},{6,4},{8,10},{10,8},{12,14},{14,12},{1,3},{3,1},... | collective-permute-start | bytes 491528 | tf_op jit(solution)/shard_map/ppermute | solution.py:292
  55.4 15.8 %collective-permute-start.16 = (bf16[640,128]{1,0:T(8,128)(2,1)S(1)}, bf16[640,128]{1,0:T(8,128)(2,1)S(1)}, u32[]{:S(2)}, u32[]{:S(2)}) collective-permute-start(bf16[640,128]{1,0:T(8,128)(2,1)S(1)} %get-tuple-element.87.refs_3_), channel_id=1, source_target_pairs={{0,2},{2,0},{4,6},{6,4},{8,10},{10,8},{12,14},{14,12},{1,3},{3,1},... | collective-permute-start | bytes 491528 | tf_op jit(solution)/shard_map/ppermute | solution.py:292
  67.8 6.0 %collective-permute-start.18 = (bf16[320,128]{1,0:T(8,128)(2,1)S(1)}, bf16[320,128]{1,0:T(8,128)(2,1)S(1)}, u32[]{:S(2)}, u32[]{:S(2)}) collective-permute-start(bf16[320,128]{1,0:T(8,128)(2,1)S(1)} %get-tuple-element.89.refs_3_), channel_id=1, source_target_pairs={{0,4},{2,6},{4,0},{6,2},{8,12},{10,14},{12,8},{14,10},{1,5},{3,7},... | collective-permute-start | bytes 245768 | tf_op jit(solution)/shard_map/ppermute | solution.py:292
  71.3 5.2 %collective-permute-start.17 = (bf16[320,128]{1,0:T(8,128)(2,1)S(1)}, bf16[320,128]{1,0:T(8,128)(2,1)S(1)}, u32[]{:S(2)}, u32[]{:S(2)}) collective-permute-start(bf16[320,128]{1,0:T(8,128)(2,1)S(1)} %get-tuple-element.95.refs_3_), channel_id=1, source_target_pairs={{0,4},{2,6},{4,0},{6,2},{8,12},{10,14},{12,8},{14,10},{1,5},{3,7},... | collective-permute-start | bytes 245768 | tf_op jit(solution)/shard_map/ppermute | solution.py:292
  73.8 6.8 %collective-permute-start.20 = (bf16[320,128]{1,0:T(8,128)(2,1)S(1)}, bf16[320,128]{1,0:T(8,128)(2,1)S(1)}, u32[]{:S(2)}, u32[]{:S(2)}) collective-permute-start(bf16[320,128]{1,0:T(8,128)(2,1)S(1)} %shard_map.93.refs_2_.refs_0_), channel_id=1, source_target_pairs={{0,8},{2,10},{4,12},{6,14},{8,0},{10,2},{12,4},{14,6},{1,9},{3,11}... | collective-permute-start | bytes 245768 | tf_op jit(solution)/shard_map/ppermute | solution.py:292
  75.9 17.9 %collective-permute-start.8 = (bf16[1024,128]{1,0:T(8,128)(2,1)S(1)}, bf16[1024,128]{1,0:T(8,128)(2,1)S(1)}, u32[]{:S(2)}, u32[]{:S(2)}) collective-permute-start(bf16[1024,128]{1,0:T(8,128)(2,1)S(1)} %get-tuple-element.66), channel_id=1, source_target_pairs={{0,1},{1,0},{2,3},{3,2},{4,5},{5,4},{6,7},{7,6},{8,9},{9,8},{10,11... | collective-permute-start | bytes 786440 | tf_op jit(solution)/shard_map/ppermute | solution.py:296
  75.9 17.9 %collective-permute-start.7 = (bf16[1024,128]{1,0:T(8,128)(2,1)S(1)}, bf16[1024,128]{1,0:T(8,128)(2,1)S(1)}, u32[]{:S(2)}, u32[]{:S(2)}) collective-permute-start(bf16[1024,128]{1,0:T(8,128)(2,1)S(1)} %get-tuple-element.64), channel_id=1, source_target_pairs={{0,1},{1,0},{2,3},{3,2},{4,5},{5,4},{6,7},{7,6},{8,9},{9,8},{10,11... | collective-permute-start | bytes 786440 | tf_op jit(solution)/shard_map/ppermute | solution.py:296
  76.4 18.5 %collective-permute-start.14 = (bf16[1024,128]{1,0:T(8,128)(2,1)S(1)}, bf16[1024,128]{1,0:T(8,128)(2,1)S(1)}, u32[]{:S(2)}, u32[]{:S(2)}) collective-permute-start(bf16[1024,128]{1,0:T(8,128)(2,1)S(1)} %get-tuple-element.92), channel_id=1, source_target_pairs={{0,1},{1,0},{2,3},{3,2},{4,5},{5,4},{6,7},{7,6},{8,9},{9,8},{10,11... | collective-permute-start | bytes 786440 | tf_op jit(solution)/shard_map/ppermute | solution.py:296
  80.7 4.5 %collective-permute-start.24 = (bf16[320,128]{1,0:T(8,128)(2,1)S(1)}, bf16[320,128]{1,0:T(8,128)(2,1)S(1)}, u32[]{:S(2)}, u32[]{:S(2)}) collective-permute-start(bf16[320,128]{1,0:T(8,128)(2,1)S(1)} %shard_map.95.refs_2_.refs_0_.refs_4_), channel_id=1, source_target_pairs={{0,4},{2,6},{4,0},{6,2},{8,12},{10,14},{12,8},{14,10},{1,5},{3,7},... | collective-permute-start | bytes 245768 | tf_op jit(solution)/shard_map/ppermute | solution.py:292
  81.1 17.3 %collective-permute-start.15 = (bf16[1024,128]{1,0:T(8,128)(2,1)S(1)}, bf16[1024,128]{1,0:T(8,128)(2,1)S(1)}, u32[]{:S(2)}, u32[]{:S(2)}) collective-permute-start(bf16[1024,128]{1,0:T(8,128)(2,1)S(1)} %get-tuple-element.93), channel_id=1, source_target_pairs={{0,1},{1,0},{2,3},{3,2},{4,5},{5,4},{6,7},{7,6},{8,9},{9,8},{10,11... | collective-permute-start | bytes 786440 | tf_op jit(solution)/shard_map/ppermute | solution.py:296
  85.2 6.0 %collective-permute-start.19 = (bf16[320,128]{1,0:T(8,128)(2,1)S(1)}, bf16[320,128]{1,0:T(8,128)(2,1)S(1)}, u32[]{:S(2)}, u32[]{:S(2)}) collective-permute-start(bf16[320,128]{1,0:T(8,128)(2,1)S(1)} %shard_map.94.refs_2_.refs_0_), channel_id=1, source_target_pairs={{0,8},{2,10},{4,12},{6,14},{8,0},{10,2},{12,4},{14,6},{1,9},{3,11}... | collective-permute-start | bytes 245768 | tf_op jit(solution)/shard_map/ppermute | solution.py:292
  91.2 8.6 %collective-permute-start.25 = (bf16[640,128]{1,0:T(8,128)(2,1)S(1)}, bf16[640,128]{1,0:T(8,128)(2,1)S(1)}, u32[]{:S(2)}, u32[]{:S(2)}) collective-permute-start(bf16[640,128]{1,0:T(8,128)(2,1)S(1)} %shard_map.97), channel_id=1, source_target_pairs={{0,2},{2,0},{4,6},{6,4},{8,10},{10,8},{12,14},{14,12},{1,3},{3,1},... | collective-permute-start | bytes 491528 | tf_op jit(solution)/shard_map/ppermute | solution.py:292
  93.8 5.7 %collective-permute-start.23 = (bf16[320,128]{1,0:T(8,128)(2,1)S(1)}, bf16[320,128]{1,0:T(8,128)(2,1)S(1)}, u32[]{:S(2)}, u32[]{:S(2)}) collective-permute-start(bf16[320,128]{1,0:T(8,128)(2,1)S(1)} %shard_map.96.refs_0_), channel_id=1, source_target_pairs={{0,6},{2,4},{4,2},{6,0},{8,14},{10,12},{12,10},{14,8},{1,7},{3,5},... | collective-permute-start | bytes 245768 | tf_op jit(solution)/shard_map/ppermute | solution.py:292
  93.9 5.6 %collective-permute-start.22 = (bf16[320,128]{1,0:T(8,128)(2,1)S(1)}, bf16[320,128]{1,0:T(8,128)(2,1)S(1)}, u32[]{:S(2)}, u32[]{:S(2)}) collective-permute-start(bf16[320,128]{1,0:T(8,128)(2,1)S(1)} %shard_map.96.refs_0_), channel_id=1, source_target_pairs={{0,2},{2,0},{4,6},{6,4},{8,10},{10,8},{12,14},{14,12},{1,3},{3,1},... | collective-permute-start | bytes 245768 | tf_op jit(solution)/shard_map/ppermute | solution.py:292
  95.0 4.8 %collective-permute-start.21 = (bf16[320,128]{1,0:T(8,128)(2,1)S(1)}, bf16[320,128]{1,0:T(8,128)(2,1)S(1)}, u32[]{:S(2)}, u32[]{:S(2)}) collective-permute-start(bf16[320,128]{1,0:T(8,128)(2,1)S(1)} %shard_map.96.refs_0_), channel_id=1, source_target_pairs={{0,4},{2,6},{4,0},{6,2},{8,12},{10,14},{12,8},{14,10},{1,5},{3,7},... | collective-permute-start | bytes 245768 | tf_op jit(solution)/shard_map/ppermute | solution.py:292
